TPU v7x, 32 devices: a whole 2x2x4 slice. The times are simulated.
32 devices in a mesh: tensor: 2 (over core), req: 4 (over z), seq: 4 (over y, x).
Axes of the slice: x: 2, y: 2, z: 4, core: 2. Of those that a mesh axis runs over, the one named last changes fastest.
Arguments:
- incoming_activations: bfloat16 [8, 1024, 4096], P('req', 'seq'), may hold values from -6 to 6
- standardize_scaling: float32 [4096], replicated, may hold values from 0.1 to 1.9
- lagged_blending_weights: float32 [4, 4096], replicated, may hold values from 0 to 1
- learner_line_permutation: int32 [4096], replicated, may hold values from 0 to 4095, each once
- learner_acceptor_lookup_slices: float32 [3, 4096, 2048], P(None, ('req', 'seq'), 'tensor'), may hold values from -0.09375 to 0.09375
- learner_projection_slices: float32 [2048, 4096], P('tensor', ('req', 'seq')), may hold values from -0.125 to 0.125
- fading_left_matrix: bfloat16 [4096, 128], replicated, may hold values from -0.09375 to 0.09375
- fading_right_matrix: bfloat16 [128, 2048], P(None, 'tensor'), may hold values from -0.5 to 0.5
- feature_fading_speed: float32 [2048], P('tensor'), may hold values from 0.0002 to 0.08
- self_reward: float32 [2048], P('tensor'), may hold values from -3 to 3
- cluster_scaling_vector: float32 [2048], P('tensor'), may hold values from 0.1 to 1.9
- prompt_extents: int32 [8], P('req'), may hold values from 128 to 1024, as said below
Outputs:
- hidden_out: bfloat16 [8, 1024, 4096], P('req', 'seq', 'tensor')
- stretch_states: float32 [8, 4, 32, 4096], P('req', 'seq', 'tensor')
Inputs may be any that keep to these rules, and one draw needn't show every extreme that they name: `prompt_extents`: it counts the valid tokens of each prompt from its start; prompt 0 is always full. learner_line_permutation names each of the 4096 input rows once.
All inputs are finite; a program needn't handle non-finite values.
Results may differ from a plain program's by a relative error of at most 0.013.
Values may be sent and summed in bfloat16 or wider, within the bound.
No kernel may reach another device: no remote copies, remote signals or barrier semaphores. Data moves between devices by JAX's collectives and lax.ppermute only.
A program may use at most 192 MiB of HBM per device.

v0:
```python
import functools

import jax
import jax.numpy as jnp
import numpy as np
from jax import lax
from jax.experimental import pallas as pl
from jax.experimental.pallas import tpu as pltpu
from jax.sharding import PartitionSpec as P

ATTEND_DIM = 64
CHUNK = 64
LEVELS = 6
PREFIX = 8

eps = 1e-05
bf16 = jnp.bfloat16
f32 = jnp.float32


def dot(a, b):
    return jnp.dot(a, b, preferred_element_type=f32)


def dot_nt(a, b):
    return lax.dot_general(a, b, (((1,), (1,)), ((), ())), preferred_element_type=f32)


def dot_tn(a, b):
    return lax.dot_general(a, b, (((0,), (0,)), ((), ())), preferred_element_type=f32)


def swapped(value, axis, by):
    peers = lax.axis_size(axis)
    return lax.ppermute(value, axis, [(i, i ^ by) for i in range(peers)])


def vmem(mib):
    return pltpu.CompilerParams(vmem_limit_bytes=mib * 2**20)


def order_kernel(x_ref, gain_ref, coeff_ref, perm_ref, out_ref, coeff_out_ref, cur_ref):
    rows, width = x_ref.shape
    block = out_ref.shape[1]
    depth = 256

    @pl.when(pl.program_id(0) == 0)
    def _():
        x = x_ref[...].astype(f32)
        mean = jnp.mean(x, axis=-1, keepdims=True)
        centred = x - mean
        spread = jnp.mean(centred * centred, axis=-1, keepdims=True)
        cur_ref[:rows, :] = (centred * lax.rsqrt(spread + eps) * gain_ref[...]).astype(bf16)
        c = coeff_ref[...]
        high = c.astype(bf16)
        cur_ref[rows:, :] = jnp.concatenate([high, (c - high.astype(f32)).astype(bf16)], axis=0)

    perm = perm_ref[...]
    total = jnp.zeros((rows + 2 * PREFIX, block), f32)
    for k in range(width // depth):
        lines = lax.broadcasted_iota(jnp.int32, (depth, block), 0) + k * depth
        chosen = jnp.where(lines == perm, 1.0, 0.0).astype(bf16)
        total += dot(cur_ref[:, k * depth : (k + 1) * depth], chosen)
    out_ref[...] = total[:rows].astype(bf16)
    coeff_out_ref[...] = total[rows : rows + PREFIX] + total[rows + PREFIX :]


def ordered(x, gain, coeffs, perm):
    rows, width = x.shape
    block = 512
    return pl.pallas_call(
        order_kernel,
        grid=(width // block,),
        in_specs=[
            pl.BlockSpec((rows, width), lambda n: (0, 0)),
            pl.BlockSpec((1, width), lambda n: (0, 0)),
            pl.BlockSpec((PREFIX, width), lambda n: (0, 0)),
            pl.BlockSpec((1, block), lambda n: (0, n)),
        ],
        out_specs=[
            pl.BlockSpec((rows, block), lambda n: (0, n)),
            pl.BlockSpec((PREFIX, block), lambda n: (0, n)),
        ],
        out_shape=[
            jax.ShapeDtypeStruct((rows, width), bf16),
            jax.ShapeDtypeStruct((PREFIX, width), f32),
        ],
        scratch_shapes=[pltpu.VMEM((rows + 2 * PREFIX, width), bf16)],
        compiler_params=vmem(40),
        cost_estimate=pl.CostEstimate(
            flops=2 * rows * width * width, bytes_accessed=4 * rows * width, transcendentals=0
        ),
    )(x, gain, coeffs, perm)


def mix_kernel(where_ref, act_ref, before_ref, coeff_ref, left_ref, mixed_ref, lora_ref):
    rows, width = act_ref.shape[2:]
    block = 512
    first = (pl.program_id(1) == 0) & (pl.program_id(2) == 0)
    inner = jnp.zeros((rows, left_ref.shape[1]), f32)
    top = lax.broadcasted_iota(jnp.int32, (rows, block), 0) == 0
    for n in range(width // block):
        cols = slice(n * block, (n + 1) * block)
        cur = act_ref[0, 0, :, cols].astype(f32)
        last = before_ref[0, 0, :, cols].astype(f32)[15:16]
        last = jnp.where(first, jnp.zeros_like(last), last)
        delta = jnp.where(top, last, pltpu.roll(cur, 1, 0)) - cur
        for j in range(3):
            mixed_ref[j, 0, 0, :, cols] = (cur + delta * coeff_ref[j : j + 1, cols]).astype(bf16)
        inner += dot((cur + delta * coeff_ref[3:4, cols]).astype(bf16), left_ref[cols, :])
    lora_ref[0, 0] = jnp.tanh(inner).astype(bf16)


def shifted(where, act, coeffs, left):
    stretches, prompts, span, width = act.shape
    inner = left.shape[1]
    rows = 128
    tiles = span // rows
    groups = rows // 16

    def before(p, b, i, where):
        block = jnp.where(i == 0, jnp.maximum(b - 1, 0), b)
        return (block ^ where[0], p, jnp.where(i == 0, tiles, i) * groups - 1, 0)

    return pl.pallas_call(
        mix_kernel,
        grid_spec=pltpu.PrefetchScalarGridSpec(
            num_scalar_prefetch=1,
            grid=(prompts, stretches, tiles),
            in_specs=[
                pl.BlockSpec((1, 1, rows, width), lambda p, b, i, w: (b ^ w[0], p, i, 0)),
                pl.BlockSpec((1, 1, 16, width), before),
                pl.BlockSpec((PREFIX, width), lambda p, b, i, w: (0, 0)),
                pl.BlockSpec((width, inner), lambda p, b, i, w: (0, 0)),
            ],
            out_specs=[
                pl.BlockSpec((3, 1, 1, rows, width), lambda p, b, i, w: (0, p, b, i, 0)),
                pl.BlockSpec((1, 1, rows, inner), lambda p, b, i, w: (p, b, i, 0)),
            ],
        ),
        out_shape=[
            jax.ShapeDtypeStruct((3, prompts, stretches, span, width), bf16),
            jax.ShapeDtypeStruct((prompts, stretches, span, inner), bf16),
        ],
        compiler_params=vmem(40),
        cost_estimate=pl.CostEstimate(
            flops=24 * act.size, bytes_accessed=8 * act.size, transcendentals=0
        ),
    )(where, act, act, coeffs, left)


def project_kernel(where_ref, act_ref, *refs):
    *weights, out_ref, total_ref = refs
    depth = weights[0].shape[2]
    r = pl.program_id(1)

    @pl.when(r == 0)
    def _():
        total_ref[...] = jnp.zeros_like(total_ref)

    for d, w_ref in enumerate(weights):
        cols = pl.ds(pl.multiple_of((where_ref[0] ^ d) * depth, depth), depth)
        total_ref[...] += dot(act_ref[0, :, cols], w_ref[0, 0])

    @pl.when(r == pl.num_programs(1) - 1)
    def _():
        out_ref[0] = total_ref[...].astype(bf16)


def projected(where, mixed, weights):
    reqs, kinds, depth, cols = weights[0].shape
    tokens, width = mixed.shape[1:]
    stretches = len(weights)
    if depth % 128:
        order = jnp.arange(stretches) ^ where[0]
        lines = jnp.stack(weights)[order]
        lines = jnp.transpose(lines, (2, 1, 0, 3, 4)).reshape(kinds, width, cols)
        return jnp.einsum("jtk,jkc->jtc", mixed, lines, preferred_element_type=f32).astype(bf16)
    share = stretches * depth
    return pl.pallas_call(
        project_kernel,
        grid_spec=pltpu.PrefetchScalarGridSpec(
            num_scalar_prefetch=1,
            grid=(kinds, reqs),
            in_specs=[pl.BlockSpec((1, tokens, share), lambda j, r, w: (j, 0, r))]
            + [pl.BlockSpec((1, 1, depth, cols), lambda j, r, w: (r, j, 0, 0))] * stretches,
            out_specs=pl.BlockSpec((1, tokens, cols), lambda j, r, w: (j, 0, 0)),
            scratch_shapes=[pltpu.VMEM((tokens, cols), f32)],
        ),
        out_shape=jax.ShapeDtypeStruct((kinds, tokens, cols), bf16),
        compiler_params=vmem(40),
        cost_estimate=pl.CostEstimate(
            flops=2 * kinds * tokens * width * cols,
            bytes_accessed=2 * (mixed.size + kinds * width * cols),
            transcendentals=0,
        ),
    )(where, mixed, *weights)


def decay_sums():
    place = np.arange(CHUNK)
    of, by = place[:, None], place[None, :]
    parts = []
    for level in range(LEVELS):
        half = 1 << level
        middle = (of // (2 * half)) * 2 * half + half - 1
        later = (of % (2 * half)) >= half
        parts.append(np.where(later, (by > middle) & (by < of), (by > of) & (by <= middle)))
    parts += [by < of, by > of, np.ones((8, CHUNK), bool)]
    sums = np.concatenate(parts).astype(np.float32)
    return np.concatenate([sums, sums], axis=1)


def pair_levels(heads):
    of, by = np.arange(CHUNK)[:, None], np.arange(CHUNK)[None, :]
    level = np.full((CHUNK, CHUNK), -1.0, np.float32)
    for bit in range(LEVELS):
        level[((of ^ by) >> bit) == 1] = bit
    return np.tile(np.where(of > by, level, -1.0).astype(np.float32), (1, heads))


def wkv_kernel(
    extent_ref, where_ref, own_ref, own_lora_ref, far_ref, far_lora_ref, right_ref, speed_ref, reward_ref,
    scale_ref, sums_ref, level_ref, same_ref, normed_ref, state_ref, memory_ref,
):
    chunk = pl.program_id(0)
    prompts = own_ref.shape[1]
    cols = own_ref.shape[3]
    heads = cols // ATTEND_DIM
    per_block = pl.num_programs(0) // lax.axis_size("seq")
    same = same_ref[...]
    same_f32 = same.astype(f32)
    level = level_ref[...]
    at = chunk * CHUNK + lax.broadcasted_iota(jnp.int32, (CHUNK, cols), 0)

    @pl.when(chunk == 0)
    def _():
        memory_ref[...] = jnp.zeros_like(memory_ref)

    for side, (proj_ref, lora_ref) in enumerate(((own_ref, own_lora_ref), (far_ref, far_lora_ref))):
        for p in range(prompts):
            prompt = (where_ref[1] ^ side) * prompts + p
            valid = jnp.where(at < extent_ref[prompt], 1.0, 0.0)
            r = proj_ref[0, p].astype(f32)
            k = proj_ref[1, p].astype(f32) * valid
            v = proj_ref[2, p]
            decay = -speed_ref[...] * jnp.exp(dot(lora_ref[p], right_ref[...])) * valid
            high = decay.astype(bf16)
            low = (decay - high.astype(f32)).astype(bf16)
            kept = jnp.exp(dot(sums_ref[...], jnp.concatenate([high, low], axis=0)))
            scores = jnp.zeros((CHUNK, heads * CHUNK), f32)
            for bit in range(LEVELS):
                part = kept[bit * CHUNK : (bit + 1) * CHUNK]
                lookup = (k * part).astype(bf16)
                lookup = jnp.concatenate([lookup] * heads, axis=0) * same
                found = dot_nt((r * part).astype(bf16), lookup)
                scores = jnp.where(level == bit, found, scores)
            v_heads = jnp.concatenate([v] * heads, axis=0) * same
            memory = memory_ref[side * prompts + p]
            from_start = (r * kept[LEVELS * CHUNK : (LEVELS + 1) * CHUNK]).astype(bf16)
            to_end = (k * kept[(LEVELS + 1) * CHUNK : (LEVELS + 2) * CHUNK]).astype(bf16)
            own = dot((r * reward_ref[...] * k).astype(bf16), same)
            y = dot_nt(from_start, memory.astype(bf16)) + dot(scores.astype(bf16), v_heads)
            y += own * v.astype(f32)
            whole = kept[(LEVELS + 2) * CHUNK : (LEVELS + 2) * CHUNK + 1]
            memory = memory * whole + same_f32 * dot_tn(v, to_end)
            memory_ref[side * prompts + p] = memory

            y_high = y.astype(bf16)
            y_low = (y - y_high.astype(f32)).astype(bf16)
            centred = y - (dot(y_high, same) + dot(y_low, same)) * (1.0 / ATTEND_DIM)
            spread = dot((centred * centred).astype(bf16), same) * (1.0 / ATTEND_DIM)
            normed = centred * lax.rsqrt(spread + eps) * scale_ref[...] * valid
            normed_ref[0, pl.ds(prompt, 1)] = normed.astype(bf16)[None]

            @pl.when(chunk % per_block == per_block - 1)
            def _():
                folded = memory[:ATTEND_DIM]
                for h in range(1, heads):
                    folded += memory[h * ATTEND_DIM : (h + 1) * ATTEND_DIM]
                state_ref[0, pl.ds(prompt, 1)] = folded[None]


def recurrence(extents, where, own, own_lora, far, far_lora, right, speed, reward, scale, stretches, span):
    _, prompts, length, cols = own.shape
    inner = own_lora.shape[-1]
    heads = cols // ATTEND_DIM
    reqs = 2 * prompts
    per_block = span // CHUNK
    sums = jnp.asarray(decay_sums(), bf16)
    level = jnp.asarray(pair_levels(heads), f32)
    head = np.arange(cols) // ATTEND_DIM
    same = jnp.asarray(head[:, None] == head[None, :], bf16)

    def fixed(array):
        return pl.BlockSpec(array.shape, lambda c, e, w: (0,) * array.ndim)

    proj_spec = pl.BlockSpec((3, prompts, CHUNK, cols), lambda c, e, w: (0, 0, c, 0))
    lora_spec = pl.BlockSpec((prompts, CHUNK, inner), lambda c, e, w: (0, c, 0))
    tables = (right, speed, reward, scale, sums, level, same)
    return pl.pallas_call(
        wkv_kernel,
        grid_spec=pltpu.PrefetchScalarGridSpec(
            num_scalar_prefetch=2,
            grid=(length // CHUNK,),
            in_specs=[proj_spec, lora_spec, proj_spec, lora_spec] + [fixed(a) for a in tables],
            out_specs=[
                pl.BlockSpec(
                    (1, reqs, CHUNK, cols), lambda c, e, w: (c // per_block, 0, c % per_block, 0)
                ),
                pl.BlockSpec(
                    (1, reqs, ATTEND_DIM, cols), lambda c, e, w: (c // per_block, 0, 0, 0)
                ),
            ],
            scratch_shapes=[pltpu.VMEM((reqs, cols, cols), f32)],
        ),
        out_shape=[
            jax.ShapeDtypeStruct((stretches, reqs, span, cols), bf16),
            jax.ShapeDtypeStruct((stretches, reqs, ATTEND_DIM, cols), f32),
        ],
        compiler_params=vmem(40),
        cost_estimate=pl.CostEstimate(
            flops=reqs * length * cols * 8000, bytes_accessed=20 * length * cols, transcendentals=0
        ),
    )(extents, where, own, own_lora, far, far_lora, *tables)


def finish_kernel(where_ref, x_ref, own_ref, far_ref, *refs):
    *weights, out_ref = refs
    stretches, rows, cols = own_ref.shape
    chunk = weights[0].shape[-1]
    for e in range(stretches):
        total = x_ref[:, pl.ds(pl.multiple_of((where_ref[0] ^ e) * chunk, chunk), chunk)].astype(f32)
        for side, lines_ref in enumerate((own_ref, far_ref)):
            w_ref = weights[2 * e + side]
            for d in range(stretches):
                at = pl.ds(pl.multiple_of((where_ref[0] ^ d) * cols, cols), cols)
                total += dot(lines_ref[d], w_ref[0, at, :])
        out_ref[:, pl.ds(pl.multiple_of((where_ref[0] ^ e) * chunk, chunk), chunk)] = total.astype(bf16)


def finished(where, x, own, far, weights):
    stretches, rows, cols = own.shape
    width = x.shape[1]
    groups, depth, chunk = weights[0].shape
    share = groups * stretches * chunk
    if chunk % 128:
        order = jnp.arange(stretches) ^ where[0]
        total = lax.dynamic_slice_in_dim(x, where[1] * share, share, 1).astype(f32)
        for side, lines in enumerate((own, far)):
            w = jnp.transpose(jnp.stack(weights[side::2])[order], (2, 1, 0, 3)).reshape(depth, share)
            lines = jnp.transpose(lines[order], (1, 0, 2)).reshape(rows, depth)
            total += dot(lines, w)
        return total.astype(bf16)
    block = stretches * chunk
    whole = pl.BlockSpec((stretches, rows, cols), lambda g, w: (0, 0, 0))
    return pl.pallas_call(
        finish_kernel,
        grid_spec=pltpu.PrefetchScalarGridSpec(
            num_scalar_prefetch=1,
            grid=(groups,),
            in_specs=[pl.BlockSpec((rows, block), lambda g, w: (0, w[1] * groups + g)), whole, whole]
            + [pl.BlockSpec((1, depth, chunk), lambda g, w: (g, 0, 0))] * len(weights),
            out_specs=pl.BlockSpec((rows, block), lambda g, w: (0, g)),
        ),
        out_shape=jax.ShapeDtypeStruct((rows, share), bf16),
        compiler_params=vmem(48),
        cost_estimate=pl.CostEstimate(
            flops=4 * rows * depth * share, bytes_accessed=4 * depth * share, transcendentals=0
        ),
    )(where, x, own, far, *weights)


def over_plane(value):
    peers = lax.axis_size("seq")
    if peers != 4:
        got = [value] + [swapped(value, "seq", d) for d in range(1, peers)]
        half = got[-1].shape[0] // 2
        return got[:-1] + [(got[-1][:half], got[-1][half:])]
    near, other = swapped(value, "seq", 1), swapped(value, "seq", 2)
    half = value.shape[0] // 2
    return [value, near, other, (swapped(near[:half], "seq", 2), swapped(other[half:], "seq", 1))]


def local(
    incoming_activations,
    standardize_scaling,
    lagged_blending_weights,
    learner_line_permutation,
    learner_acceptor_lookup_slices,
    learner_projection_slices,
    fading_left_matrix,
    fading_right_matrix,
    feature_fading_speed,
    self_reward,
    cluster_scaling_vector,
    prompt_extents,
):
    reqs, span, width = incoming_activations.shape
    rows = reqs * span
    stretches = lax.axis_size("seq")
    cores = lax.axis_size("tensor")
    prompts = reqs // cores
    local_width = feature_fading_speed.shape[0]
    cols = local_width // stretches
    t, s = lax.axis_index("tensor"), lax.axis_index("seq")
    where = jnp.stack([s, t]).astype(jnp.int32)

    out_half = learner_projection_slices.astype(bf16)
    out_lines = lax.all_gather(out_half, "req", axis=0, tiled=False)

    pieces = []
    for d in range(stretches):
        piece = lax.dynamic_slice_in_dim(learner_acceptor_lookup_slices, (s ^ d) * cols, cols, 2).astype(bf16)
        pieces.append(swapped(piece, "seq", d) if d else piece)
    weights = [lax.all_gather(piece, "req", axis=0, tiled=False) for piece in pieces]

    x = incoming_activations.reshape(rows, width)
    part = prompts * span
    own_x = lax.dynamic_slice_in_dim(x, t * part, part, 0)
    coeffs = jnp.pad(lagged_blending_weights, ((0, PREFIX - 4), (0, 0)))
    act, coeffs = ordered(own_x, standardize_scaling.reshape(1, width), coeffs, learner_line_permutation.reshape(1, width))
    perm, act = lax.optimization_barrier((learner_line_permutation, act))
    left = fading_left_matrix[perm]
    arrived = over_plane(act)
    acts = jnp.concatenate([*arrived[:-1], *arrived[-1]], axis=0).reshape(stretches, prompts, span, width)
    far_acts = swapped(acts, "tensor", 1)

    groups = out_lines.shape[0] // cores
    kept = lax.dynamic_slice_in_dim(out_lines, t * groups, groups, 0)
    given = lax.dynamic_slice_in_dim(out_lines, (1 - t) * groups, groups, 0)
    out_lines = jnp.stack([kept, swapped(given, "tensor", 1)])
    arrived = over_plane(out_lines)
    out_weights = []
    for pair in arrived[:-1]:
        out_weights += [pair[0], pair[1]]
    out_weights += [half[0] for half in arrived[-1]]

    sides = []
    for values in (acts, far_acts):
        mixed, lora = shifted(where, values, coeffs, left)
        proj = projected(where, mixed.reshape(3, part * stretches, width), weights)
        sides += [proj.reshape(3, prompts, stretches * span, cols), lora.reshape(prompts, stretches * span, -1)]

    def mine(array):
        return lax.dynamic_slice_in_dim(array, s * cols, cols, array.ndim - 1).reshape(-1, cols)

    normed, states = recurrence(
        prompt_extents, where, *sides, mine(fading_right_matrix), mine(feature_fading_speed), mine(self_reward),
        mine(cluster_scaling_vector), stretches, span,
    )

    sent = jnp.concatenate(
        [normed.reshape(stretches, rows, cols), states.reshape(stretches, -1, cols).astype(bf16)], axis=1
    )
    blocks = []
    for d in range(stretches):
        block = lax.dynamic_index_in_dim(sent, s ^ d, 0, keepdims=False)
        blocks.append(swapped(block, "seq", d) if d else block)
    blocks = jnp.stack(blocks)
    own_lines = blocks[:, :rows]
    far_lines = swapped(own_lines, "tensor", 1)
    hidden_out = finished(where, x, own_lines, far_lines, out_weights).reshape(reqs, span, width // cores)

    heads = cols // ATTEND_DIM
    states = blocks[jnp.arange(stretches) ^ s, rows:].reshape(stretches, reqs, ATTEND_DIM, heads, ATTEND_DIM)
    states = jnp.transpose(states, (1, 0, 3, 4, 2)).astype(f32)
    stretch_states = states.reshape(reqs, 1, stretches * heads, ATTEND_DIM * ATTEND_DIM)
    return (hidden_out, stretch_states)


def solution(mesh):
    in_specs = (
        P("req", "seq", None),
        P(),
        P(),
        P(),
        P(None, ("req", "seq"), "tensor"),
        P("tensor", ("req", "seq")),
        P(),
        P(None, "tensor"),
        P("tensor"),
        P("tensor"),
        P("tensor"),
        P("req"),
    )
    out_specs = (P("req", "seq", "tensor"), P("req", "seq", "tensor", None))
    return jax.shard_map(local, mesh=mesh, in_specs=in_specs, out_specs=out_specs, check_vma=False)
```

profile of v0, /device:TPU:0, one launch (start us, length us, event | category | flops | bytes accessed | tf_op | source)
XLA Modules:
  0.0 381.6 jit_solution(12662899984759948267)
XLA Ops:
  7.2 2.1 convert_element_type.36
  9.5 1.8 constant_dynamic-slice_fusion.3.x_ref
  11.4 12.6 %shard_map.158 = (bf16[256,4096]{1,0:T(8,128)(2,1)S(1)}, f32[8,4096]{1,0:T(8,128)S(1)}) custom-call(bf16[256,4096]{1,0:T(8,128)(2,1)S(1)} %constant_dynamic-slice_fusion.3.x_ref, f32[1,4096]{1,0:T(1,128)S(1)} %bitcast.70, f32[8,4096]{1,0:T(8,128)S(1)} %pad.5.coeff_ref, s32[1,4096]{1,0:T(1,128)S(1)} %bitcast.64), custom_call_target="tpu_custom_call" | custom-call | flops 8589934592 | bytes 4194304 | tf_op jit(solution)/shard_map/pallas_call | solution.py:71
  24.0 3.0 collective-permute-start
  27.0 1.5 collective-permute-start.1
  28.6 3.1 dynamic-slice_convert_fusion
  31.7 41.1 %collective-permute-done = bf16[256,4096]{1,0:T(8,128)(2,1)} collective-permute-done((bf16[256,4096]{1,0:T(8,128)(2,1)S(1)}, bf16[256,4096]{1,0:T(8,128)(2,1)}, u32[]{:S(2)}, u32[]{:S(2)}) %collective-permute-start) | collective-permute-done | bytes 2097184 | tf_op jit(solution)/shard_map/ppermute | solution.py:35
  74.1 1.8 collective-permute-start.2
  75.9 1.5 constant_dynamic-update-slice_fusion.4
  77.4 1.3 slice.35
  78.7 1.6 collective-permute-start.3
  80.3 3.2 constant_dynamic-update-slice_fusion.3
  83.5 3.1 constant_dynamic-update-slice_fusion.2
  86.6 11.9 %collective-permute-done.2 = bf16[128,4096]{1,0:T(8,128)(2,1)S(1)} collective-permute-done((bf16[128,4096]{1,0:T(8,128)(2,1)S(1)}, bf16[128,4096]{1,0:T(8,128)(2,1)S(1)}, u32[]{:S(2)}, u32[]{:S(2)}) %collective-permute-start.2) | collective-permute-done | bytes 1048608 | tf_op jit(solution)/shard_map/ppermute | solution.py:35
  99.6 3.0 collective-permute-done.3
  103.6 1.5 collective-permute-start.4
  105.1 10.0 %collective-permute-done.4 = bf16[3,256,256]{2,1,0:T(8,128)(2,1)S(1)} collective-permute-done((bf16[3,256,256]{2,1,0:T(8,128)(2,1)S(1)}, bf16[3,256,256]{2,1,0:T(8,128)(2,1)S(1)}, u32[]{:S(2)}, u32[]{:S(2)}) %collective-permute-start.4) | collective-permute-done | bytes 393248 | tf_op jit(solution)/shard_map/ppermute | solution.py:35
  116.6 10.2 %collective-permute-done.5 = bf16[3,256,256]{2,1,0:T(8,128)(2,1)S(1)} collective-permute-done((bf16[3,256,256]{2,1,0:T(8,128)(2,1)S(1)}, bf16[3,256,256]{2,1,0:T(8,128)(2,1)S(1)}, u32[]{:S(2)}, u32[]{:S(2)}) %collective-permute-start.5) | collective-permute-done | bytes 393248 | tf_op jit(solution)/shard_map/ppermute | solution.py:35
  127.6 1.5 collective-permute-start.6
  129.1 9.3 %collective-permute-done.6 = bf16[3,256,256]{2,1,0:T(8,128)(2,1)S(1)} collective-permute-done((bf16[3,256,256]{2,1,0:T(8,128)(2,1)S(1)}, bf16[3,256,256]{2,1,0:T(8,128)(2,1)S(1)}, u32[]{:S(2)}, u32[]{:S(2)}) %collective-permute-start.6) | collective-permute-done | bytes 393248 | tf_op jit(solution)/shard_map/ppermute | solution.py:35
  139.2 2.7 constant_dynamic-slice_fusion
  144.8 1.6 pad_maximum_fusion
  146.4 1.5 collective-permute-start.13
  147.9 12.3 %gather_fusion = bf16[4096,128]{1,0:T(8,128)(2,1)S(1)} fusion(bf16[4096,128]{1,0:T(8,128)(2,1)S(1)} %copy-done, s32[4096]{0:T(1024)S(1)} %fusion.7), kind=kCustom, calls=%fused_computation | custom fusion | bytes 2113536 | tf_op jit(solution)/shard_map/gather | solution.py:424
  161.7 16.8 %shard_map.159 = (bf16[3,1,4,256,4096]{4,3,2,1,0:T(8,128)(2,1)}, bf16[1,4,256,128]{3,2,1,0:T(8,128)(2,1)S(1)}) custom-call(s32[2]{0:T(128)S(1)} %pad_add_fusion.where_ref, bf16[4,1,256,4096]{3,2,1,0:T(8,128)(2,1)} %bitcast.5.act_ref.before_ref, bf16[4,1,256,4096]{3,2,1,0:T(8,128)(2,1)} %bitcast.5.act_ref.before_ref, ...), custom_call_target="tpu_custom_call" | custom-call | flops 100663296 | bytes 33554432 | tf_op jit(solution)/shard_map/pallas_call | solution.py:125
  178.5 12.3 %all-gather.15.cloned.1.call-done = bf16[12,256,256]{2,1,0:T(8,128)(2,1)} async-done(((bf16[3,256,256]{2,1,0:T(8,128)(2,1)}), bf16[12,256,256]{2,1,0:T(8,128)(2,1)}) %all-gather.15.cloned.1.call-update) | async-done | bytes 1572880 | tf_op jit(solution)/shard_map/all_gather | solution.py:416
  190.9 37.4 %all-gather.17.cloned.1.call-done = bf16[12,256,256]{2,1,0:T(8,128)(2,1)} async-done(((bf16[3,256,256]{2,1,0:T(8,128)(2,1)}), bf16[12,256,256]{2,1,0:T(8,128)(2,1)}) %all-gather.17.cloned.1.call-update) | async-done | bytes 1572880 | tf_op jit(solution)/shard_map/all_gather | solution.py:416
  228.3 1.4 copy-done.2
  229.7 1.4 copy-done.4
  231.1 1.4 copy-done.6
  232.5 1.4 copy-done.8
  233.9 16.1 %shard_map.160 = bf16[3,1024,256]{2,1,0:T(8,128)(2,1)S(1)} custom-call(s32[2]{0:T(128)S(1)} %pad_add_fusion.where_ref, bf16[3,1024,4096]{2,1,0:T(8,128)(2,1)} %bitcast.71, bf16[4,3,256,256]{3,2,1,0:T(8,128)(2,1)S(1)} %bitcast.52, bf16[4,3,256,256]{3,2,1,0:T(8,128)(2,1)S(1)} %bitcast.54, bf16[4,3,256,256]{3,2,1,0:T(8,128)(2,1)S(1)} %bitcast.56, ...), custom_call_target="tpu_custom_call" | custom-call | flops 6442450944 | bytes 31457280 | tf_op jit(solution)/shard_map/pallas_call | solution.py:180
  250.1 17.1 %shard_map.161 = (bf16[3,1,4,256,4096]{4,3,2,1,0:T(8,128)(2,1)}, bf16[1,4,256,128]{3,2,1,0:T(8,128)(2,1)S(1)}) custom-call(s32[2]{0:T(128)S(1)} %pad_add_fusion.where_ref, bf16[4,1,256,4096]{3,2,1,0:T(8,128)(2,1)} %collective-permute-done.7.act_ref.before_ref, bf16[4,1,256,4096]{3,2,1,0:T(8,128)(2,1)} %collective-permute-done.7.act_ref.before_ref, ...), custom_call_target="tpu_custom_call" | custom-call | flops 100663296 | bytes 33554432 | tf_op jit(solution)/shard_map/pallas_call | solution.py:125
  267.3 16.1 %shard_map.162 = bf16[3,1024,256]{2,1,0:T(8,128)(2,1)S(1)} custom-call(s32[2]{0:T(128)S(1)} %pad_add_fusion.where_ref, bf16[3,1024,4096]{2,1,0:T(8,128)(2,1)} %bitcast.72, bf16[4,3,256,256]{3,2,1,0:T(8,128)(2,1)S(1)} %bitcast.53, bf16[4,3,256,256]{3,2,1,0:T(8,128)(2,1)S(1)} %bitcast.55, bf16[4,3,256,256]{3,2,1,0:T(8,128)(2,1)S(1)} %bitcast.57, ...), custom_call_target="tpu_custom_call" | custom-call | flops 6442450944 | bytes 31457280 | tf_op jit(solution)/shard_map/pallas_call | solution.py:180
  283.4 40.0 %shard_map.163 = (bf16[4,2,256,256]{3,2,1,0:T(8,128)(2,1)S(1)}, f32[4,2,64,256]{3,2,1,0:T(8,128)S(1)}) custom-call(s32[2]{0:T(128)S(1)} %copy-done.16, s32[2]{0:T(128)S(1)} %pad_add_fusion.where_ref, bf16[3,1,1024,256]{3,2,1,0:T(8,128)(2,1)S(1)} %bitcast.61, bf16[1,1024,128]{2,1,0:T(8,128)(2,1)S(1)} %bitcast.68, bf16[3,1,1024,256]{3,2,1,0:T(8,128)(2,1)S(1)} %bitcast.62, ...), custom_call_target="tpu_custom_call" | custom-call | flops 4194304000 | bytes 5242880 | tf_op jit(solution)/shard_map/pallas_call | solution.py:301
  323.6 2.4 collective-permute-start.10
  327.2 3.1 fusion.13
  330.2 1.4 collective-permute-start.15
  331.7 3.4 fusion.12
  335.1 1.5 collective-permute-start.16
  336.6 4.4 %collective-permute-done.9 = bf16[640,256]{1,0:T(8,128)(2,1)S(1)} collective-permute-done((bf16[640,256]{1,0:T(8,128)(2,1)S(1)}, bf16[640,256]{1,0:T(8,128)(2,1)S(1)}, u32[]{:S(2)}, u32[]{:S(2)}) %collective-permute-start.9) | collective-permute-done | bytes 327712 | tf_op jit(solution)/shard_map/ppermute | solution.py:35
  342.6 2.1 copy.19
  344.6 2.5 gather_fusion.1
  347.2 1.4 reshape.97
  348.6 2.6 copy.20
  351.2 2.4 reshape.94
  353.6 9.9 %collective-permute-done.15 = bf16[1,2,1024,256]{3,2,1,0:T(8,128)(2,1)} collective-permute-done((bf16[1,2,1024,256]{3,2,1,0:T(8,128)(2,1)}, bf16[1,2,1024,256]{3,2,1,0:T(8,128)(2,1)}, u32[]{:S(2)}, u32[]{:S(2)}) %collective-permute-start.15) | collective-permute-done | bytes 1048608 | tf_op jit(solution)/shard_map/ppermute | solution.py:35
  366.0 9.1 %shard_map.164 = bf16[512,2048]{1,0:T(8,128)(2,1)} custom-call(s32[2]{0:T(128)S(1)} %pad_add_fusion.where_ref, bf16[512,4096]{1,0:T(8,128)(2,1)} %bitcast.74, bf16[4,512,256]{2,1,0:T(8,128)(2,1)S(1)} %copy-done.11, bf16[4,512,256]{2,1,0:T(8,128)(2,1)} %collective-permute-done.11.far_ref, bf16[2,1024,256]{2,1,0:T(8,128)(2,1)S(1)} %get-tuple-element.33.refs_0_, ...), custom_call_target="tpu_custom_call" | custom-call | flops 4294967296 | bytes 8388608 | tf_op jit(solution)/shard_map/pallas_call | solution.py:357
  (94 shorter events, 16.3 us)
Async XLA Ops:
  7.2 140.8 %copy-start = (bf16[4096,128]{1,0:T(8,128)(2,1)S(1)}, bf16[4096,128]{1,0:T(8,128)(2,1)}, u32[]{:S(2)}) copy-start(bf16[4096,128]{1,0:T(8,128)(2,1)} %param.21) | copy-start | bytes 3145732
  7.2 132.0 %all-gather.19.cloned.1.call-start = ((), (), s32[]{:S(2)}) async-start(), calls=%async_computation.4 | async-start | bytes 2621440 | tf_op jit(solution)/shard_map/all_gather | solution.py:410
  9.4 169.1 %all-gather.11.cloned.1.call-start = ((), (), s32[]{:S(2)}) async-start(), calls=%async_computation | async-start | bytes 1966080 | tf_op jit(solution)/shard_map/all_gather | solution.py:416
  9.5 1.9 copy-start.26
  9.5 1.9 copy-start.14
  9.5 1.9 copy-start.15
  24.0 48.7 %collective-permute-start = (bf16[256,4096]{1,0:T(8,128)(2,1)S(1)}, bf16[256,4096]{1,0:T(8,128)(2,1)}, u32[]{:S(2)}, u32[]{:S(2)}) collective-permute-start(bf16[256,4096]{1,0:T(8,128)(2,1)S(1)} %get-tuple-element.13), channel_id=1, source_target_pairs={{0,1},{1,0},{2,3},{3,2},{4,5},{5,4},{6,7},{7,6},{8,9},{9,8},{10,11... | collective-permute-start | bytes 6291464 | tf_op jit(solution)/shard_map/ppermute | solution.py:35
  27.0 50.4 %collective-permute-start.1 = (bf16[256,4096]{1,0:T(8,128)(2,1)S(1)}, bf16[256,4096]{1,0:T(8,128)(2,1)}, u32[]{:S(2)}, u32[]{:S(2)}) collective-permute-start(bf16[256,4096]{1,0:T(8,128)(2,1)S(1)} %get-tuple-element.13), channel_id=1, source_target_pairs={{0,2},{1,3},{2,0},{3,1},{4,6},{5,7},{6,4},{7,5},{8,10},{9,11},{10,... | collective-permute-start | bytes 6291464 | tf_op jit(solution)/shard_map/ppermute | solution.py:35
  31.7 146.9 %all-gather.13.cloned.1.call-start = ((), (), s32[]{:S(2)}) async-start(), calls=%async_computation.1 | async-start | bytes 1966080 | tf_op jit(solution)/shard_map/all_gather | solution.py:416
  74.1 24.4 %collective-permute-start.2 = (bf16[128,4096]{1,0:T(8,128)(2,1)S(1)}, bf16[128,4096]{1,0:T(8,128)(2,1)S(1)}, u32[]{:S(2)}, u32[]{:S(2)}) collective-permute-start(bf16[128,4096]{1,0:T(8,128)(2,1)S(1)} %slice.34), channel_id=1, source_target_pairs={{0,2},{1,3},{2,0},{3,1},{4,6},{5,7},{6,4},{7,5},{8,10},{9,11},{10,... | collective-permute-start | bytes 3145736 | tf_op jit(solution)/shard_map/ppermute | solution.py:35
  78.7 23.8 %collective-permute-start.3 = (bf16[128,4096]{1,0:T(8,128)(2,1)S(1)}, bf16[128,4096]{1,0:T(8,128)(2,1)S(1)}, u32[]{:S(2)}, u32[]{:S(2)}) collective-permute-start(bf16[128,4096]{1,0:T(8,128)(2,1)S(1)} %slice.35), channel_id=1, source_target_pairs={{0,1},{1,0},{2,3},{3,2},{4,5},{5,4},{6,7},{7,6},{8,9},{9,8},{10,11... | collective-permute-start | bytes 3145736 | tf_op jit(solution)/shard_map/ppermute | solution.py:35
  86.6 17.0 %copy-start.25 = (bf16[3,256,256]{2,1,0:T(8,128)(2,1)S(1)}, bf16[3,256,256]{2,1,0:T(8,128)(2,1)}, u32[]{:S(2)}) copy-start(bf16[3,256,256]{2,1,0:T(8,128)(2,1)} %get-tuple-element.23) | copy-start | bytes 1179652
  86.6 29.3 %copy-start.24 = (bf16[3,256,256]{2,1,0:T(8,128)(2,1)S(1)}, bf16[3,256,256]{2,1,0:T(8,128)(2,1)}, u32[]{:S(2)}) copy-start(bf16[3,256,256]{2,1,0:T(8,128)(2,1)} %get-tuple-element.25) | copy-start | bytes 1179652
  86.6 41.0 %copy-start.23 = (bf16[3,256,256]{2,1,0:T(8,128)(2,1)S(1)}, bf16[3,256,256]{2,1,0:T(8,128)(2,1)}, u32[]{:S(2)}) copy-start(bf16[3,256,256]{2,1,0:T(8,128)(2,1)} %get-tuple-element.22) | copy-start | bytes 1179652
  103.6 146.5 %collective-permute-start.7 = (bf16[4,1,256,4096]{3,2,1,0:T(8,128)(2,1)}, bf16[4,1,256,4096]{3,2,1,0:T(8,128)(2,1)}, u32[]{:S(2)}, u32[]{:S(2)}) collective-permute-start(bf16[4,1,256,4096]{3,2,1,0:T(8,128)(2,1)} %bitcast.5.act_ref.before_ref), channel_id=1, source_target_pairs={{0,16},{16,0},{1,17},{17,1},{2,18},{18,2},{3,19},{19,3},{4,20},{20... | collective-permute-start | bytes 25165832 | tf_op jit(solution)/shard_map/ppermute | solution.py:35
  103.6 11.5 %collective-permute-start.4 = (bf16[3,256,256]{2,1,0:T(8,128)(2,1)S(1)}, bf16[3,256,256]{2,1,0:T(8,128)(2,1)S(1)}, u32[]{:S(2)}, u32[]{:S(2)}) collective-permute-start(bf16[3,256,256]{2,1,0:T(8,128)(2,1)S(1)} %copy-done.25), channel_id=1, source_target_pairs={{0,1},{1,0},{2,3},{3,2},{4,5},{5,4},{6,7},{7,6},{8,9},{9,8},{10,11... | collective-permute-start | bytes 1179656 | tf_op jit(solution)/shard_map/ppermute | solution.py:35
  115.9 75.0 %all-gather.15.cloned.1.call-start = ((), (), s32[]{:S(2)}) async-start(), calls=%async_computation.2 | async-start | bytes 1966080 | tf_op jit(solution)/shard_map/all_gather | solution.py:416
  115.9 10.8 %collective-permute-start.5 = (bf16[3,256,256]{2,1,0:T(8,128)(2,1)S(1)}, bf16[3,256,256]{2,1,0:T(8,128)(2,1)S(1)}, u32[]{:S(2)}, u32[]{:S(2)}) collective-permute-start(bf16[3,256,256]{2,1,0:T(8,128)(2,1)S(1)} %copy-done.24), channel_id=1, source_target_pairs={{0,2},{1,3},{2,0},{3,1},{4,6},{5,7},{6,4},{7,5},{8,10},{9,11},{10,... | collective-permute-start | bytes 1179656 | tf_op jit(solution)/shard_map/ppermute | solution.py:35
  126.8 0.8 copy-start.21
  127.5 100.7 %all-gather.17.cloned.1.call-start = ((), (), s32[]{:S(2)}) async-start(), calls=%async_computation.3 | async-start | bytes 1966080 | tf_op jit(solution)/shard_map/all_gather | solution.py:416
  127.6 10.8 %collective-permute-start.6 = (bf16[3,256,256]{2,1,0:T(8,128)(2,1)S(1)}, bf16[3,256,256]{2,1,0:T(8,128)(2,1)S(1)}, u32[]{:S(2)}, u32[]{:S(2)}) collective-permute-start(bf16[3,256,256]{2,1,0:T(8,128)(2,1)S(1)} %copy-done.23), channel_id=1, source_target_pairs={{0,3},{1,2},{2,1},{3,0},{4,7},{5,6},{6,5},{7,4},{8,11},{9,10},{10,... | collective-permute-start | bytes 1179656 | tf_op jit(solution)/shard_map/ppermute | solution.py:35
  138.4 0.7 copy-start.22
  141.9 2.9 collective-permute-start.12
  144.8 1.7 copy-start.12
  146.4 180.7 %collective-permute-start.13 = (bf16[2,2,1024,256]{3,2,1,0:T(8,128)(2,1)}, bf16[2,2,1024,256]{3,2,1,0:T(8,128)(2,1)}, u32[]{:S(2)}, u32[]{:S(2)}) collective-permute-start(bf16[2,2,1024,256]{3,2,1,0:T(8,128)(2,1)} %pad_maximum_fusion), channel_id=1, source_target_pairs={{0,1},{1,0},{2,3},{3,2},{4,5},{5,4},{6,7},{7,6},{8,9},{9,8},{10,11... | collective-permute-start | bytes 6291464 | tf_op jit(solution)/shard_map/ppermute | solution.py:35
  161.1 170.5 %collective-permute-start.14 = (bf16[2,2,1024,256]{3,2,1,0:T(8,128)(2,1)}, bf16[2,2,1024,256]{3,2,1,0:T(8,128)(2,1)}, u32[]{:S(2)}, u32[]{:S(2)}) collective-permute-start(bf16[2,2,1024,256]{3,2,1,0:T(8,128)(2,1)} %pad_maximum_fusion), channel_id=1, source_target_pairs={{0,2},{1,3},{2,0},{3,1},{4,6},{5,7},{6,4},{7,5},{8,10},{9,11},{10,... | collective-permute-start | bytes 6291464 | tf_op jit(solution)/shard_map/ppermute | solution.py:35
  228.3 1.4 copy-start.2
  229.7 1.4 copy-start.4
  231.1 1.4 copy-start.6
  232.5 1.4 copy-start.8
  250.0 17.2 %copy-start.3 = (bf16[12,256,256]{2,1,0:T(8,128)(2,1)S(1)}, bf16[12,256,256]{2,1,0:T(8,128)(2,1)}, u32[]{:S(2)}) copy-start(bf16[12,256,256]{2,1,0:T(8,128)(2,1)} %all-gather.11.cloned.1.call-done) | copy-start | bytes 4718596
  250.0 17.2 %copy-start.5 = (bf16[12,256,256]{2,1,0:T(8,128)(2,1)S(1)}, bf16[12,256,256]{2,1,0:T(8,128)(2,1)}, u32[]{:S(2)}) copy-start(bf16[12,256,256]{2,1,0:T(8,128)(2,1)} %all-gather.13.cloned.1.call-done) | copy-start | bytes 4718596
  250.0 17.2 %copy-start.7 = (bf16[12,256,256]{2,1,0:T(8,128)(2,1)S(1)}, bf16[12,256,256]{2,1,0:T(8,128)(2,1)}, u32[]{:S(2)}) copy-start(bf16[12,256,256]{2,1,0:T(8,128)(2,1)} %all-gather.15.cloned.1.call-done) | copy-start | bytes 4718596
  250.1 17.2 %copy-start.9 = (bf16[12,256,256]{2,1,0:T(8,128)(2,1)S(1)}, bf16[12,256,256]{2,1,0:T(8,128)(2,1)}, u32[]{:S(2)}) copy-start(bf16[12,256,256]{2,1,0:T(8,128)(2,1)} %all-gather.17.cloned.1.call-done) | copy-start | bytes 4718596
  267.2 16.2 %copy-start.16 = (s32[2]{0:T(128)S(1)}, s32[2]{0:T(128)}, u32[]{:S(2)}) copy-start(s32[2]{0:T(128)} %extent_ref.1) | copy-start | bytes 28
  267.2 16.2 %copy-start.17 = (bf16[520,128]{1,0:T(8,128)(2,1)S(1)}, bf16[520,128]{1,0:T(8,128)(2,1)}, u32[]{:S(2)}) copy-start(bf16[520,128]{1,0:T(8,128)(2,1)} %constant.50.clone.sums_ref) | copy-start | bytes 399364
  267.2 16.2 %copy-start.18 = (bf16[256,256]{1,0:T(8,128)(2,1)S(1)}, bf16[256,256]{1,0:T(8,128)(2,1)}, u32[]{:S(2)}) copy-start(bf16[256,256]{1,0:T(8,128)(2,1)} %constant.52.clone.same_ref) | copy-start | bytes 393220
  267.3 16.2 %copy-start.19 = (f32[64,256]{1,0:T(8,128)S(1)}, f32[64,256]{1,0:T(8,128)}, u32[]{:S(2)}) copy-start(f32[64,256]{1,0:T(8,128)} %constant.51.clone.level_ref) | copy-start | bytes 196612
  323.6 13.0 %collective-permute-start.10 = (bf16[640,256]{1,0:T(8,128)(2,1)S(1)}, bf16[640,256]{1,0:T(8,128)(2,1)S(1)}, u32[]{:S(2)}, u32[]{:S(2)}) collective-permute-start(bf16[640,256]{1,0:T(8,128)(2,1)S(1)} %get-tuple-element.37), channel_id=1, source_target_pairs={{0,3},{1,2},{2,1},{3,0},{4,7},{5,6},{6,5},{7,4},{8,11},{9,10},{10,... | collective-permute-start | bytes 983048 | tf_op jit(solution)/shard_map/ppermute | solution.py:35
  326.0 15.0 %collective-permute-start.9 = (bf16[640,256]{1,0:T(8,128)(2,1)S(1)}, bf16[640,256]{1,0:T(8,128)(2,1)S(1)}, u32[]{:S(2)}, u32[]{:S(2)}) collective-permute-start(bf16[640,256]{1,0:T(8,128)(2,1)S(1)} %get-tuple-element.36), channel_id=1, source_target_pairs={{0,2},{1,3},{2,0},{3,1},{4,6},{5,7},{6,4},{7,5},{8,10},{9,11},{10,... | collective-permute-start | bytes 983048 | tf_op jit(solution)/shard_map/ppermute | solution.py:35
  326.6 15.6 %collective-permute-start.8 = (bf16[640,256]{1,0:T(8,128)(2,1)S(1)}, bf16[640,256]{1,0:T(8,128)(2,1)S(1)}, u32[]{:S(2)}, u32[]{:S(2)}) collective-permute-start(bf16[640,256]{1,0:T(8,128)(2,1)S(1)} %get-tuple-element.35), channel_id=1, source_target_pairs={{0,1},{1,0},{2,3},{3,2},{4,5},{5,4},{6,7},{7,6},{8,9},{9,8},{10,11... | collective-permute-start | bytes 983048 | tf_op jit(solution)/shard_map/ppermute | solution.py:35
  330.2 33.3 %collective-permute-start.15 = (bf16[1,2,1024,256]{3,2,1,0:T(8,128)(2,1)}, bf16[1,2,1024,256]{3,2,1,0:T(8,128)(2,1)}, u32[]{:S(2)}, u32[]{:S(2)}) collective-permute-start(bf16[1,2,1024,256]{3,2,1,0:T(8,128)(2,1)} %get-tuple-element.29), channel_id=1, source_target_pairs={{0,2},{1,3},{2,0},{3,1},{4,6},{5,7},{6,4},{7,5},{8,10},{9,11},{10,... | collective-permute-start | bytes 3145736 | tf_op jit(solution)/shard_map/ppermute | solution.py:35
  335.1 28.4 %collective-permute-start.16 = (bf16[1,2,1024,256]{3,2,1,0:T(8,128)(2,1)}, bf16[1,2,1024,256]{3,2,1,0:T(8,128)(2,1)}, u32[]{:S(2)}, u32[]{:S(2)}) collective-permute-start(bf16[1,2,1024,256]{3,2,1,0:T(8,128)(2,1)} %get-tuple-element.26), channel_id=1, source_target_pairs={{0,1},{1,0},{2,3},{3,2},{4,5},{5,4},{6,7},{7,6},{8,9},{9,8},{10,11... | collective-permute-start | bytes 3145736 | tf_op jit(solution)/shard_map/ppermute | solution.py:35
  342.5 4.7 %copy-start.10 = (bf16[4,512,256]{2,1,0:T(8,128)(2,1)}, bf16[4,512,256]{2,1,0:T(8,128)(2,1)S(1)}, u32[]{:S(2)}) copy-start(bf16[4,512,256]{2,1,0:T(8,128)(2,1)S(1)} %slice.36.own_ref) | copy-start | bytes 3145732
  342.5 21.0 %collective-permute-start.11 = (bf16[4,512,256]{2,1,0:T(8,128)(2,1)S(1)}, bf16[4,512,256]{2,1,0:T(8,128)(2,1)}, u32[]{:S(2)}, u32[]{:S(2)}) collective-permute-start(bf16[4,512,256]{2,1,0:T(8,128)(2,1)S(1)} %slice.36.own_ref), channel_id=1, source_target_pairs={{0,16},{16,0},{1,17},{17,1},{2,18},{18,2},{3,19},{19,3},{4,20},{20... | collective-permute-start | bytes 3145736 | tf_op jit(solution)/shard_map/ppermute | solution.py:35
  363.5 1.2 copy-start.11
  364.7 1.2 copy-start.13
  366.0 9.1 %copy-start.1 = (bf16[4096,128]{1,0:T(8,128)(2,1)S(1)}, bf16[4096,128]{1,0:T(8,128)(2,1)}, u32[]{:S(2)}) copy-start(bf16[4096,128]{1,0:T(8,128)(2,1)} %param.21) | copy-start | bytes 3145732
  (1 other events, 0.7 us)
Sparse Core Ops, SparseCore 0:
  10.2 48.6 all-gather.18
  60.4 35.7 all-gather.10
  116.0 37.3 all-gather.12
  154.9 35.9 all-gather.14
  192.3 35.9 all-gather.16
where the time goes:
time: 383 us; the launch traced here: 382 us
  waiting for transfers between devices  151 us (39%)
  Pallas kernels  128 us (33%)
  local copies, waits for them, and re-layouts  63.6 us (17%)
  starting transfers between devices  20.3 us (5%)
  between operations  14.2 us (4%)
  other arithmetic  4.17 us (1%)
    ppermute x17, waiting for transfers between devices, swapped(): return lax.ppermute(value, axis, [(i, i ^ by) for i in range(peers)])  102 us
    all_gather x4, waiting for transfers between devices, local(): lax.all_gather(piece, 'req', axis=0, tiled=False)  49.7 us
    pallas_call x1, Pallas kernels, recurrence(): pl.pallas_call(wkv_kernel, grid_spec=pltpu.PrefetchScalarGridSpec(num_sca...  40 us
    pallas_call x2, Pallas kernels, shifted(): pl.pallas_call(mix_kernel, grid_spec=pltpu.PrefetchScalarGridSpec(num_sca...  34 us
    pallas_call x2, Pallas kernels, projected(): pl.pallas_call(project_kernel, grid_spec=pltpu.PrefetchScalarGridSpec(num...  32.3 us
    ppermute x17, starting transfers between devices, swapped(): return lax.ppermute(value, axis, [(i, i ^ by) for i in range(peers)])  20.1 us
    unnamed x58, local copies, waits for them, and re-layouts  19.3 us
    pallas_call x1, Pallas kernels, ordered(): pl.pallas_call(order_kernel, grid=(width // block,), in_specs=[pl.BlockSp...  12.6 us
  transfers between devices with their start and end apart: 22, of which 12 were waited for; matrix products, arithmetic and copies ran while one was open for 14% of the time, Pallas kernels for 31%

commit v1 on v0

v1 whole, which is shorter than its diff:
```python
import functools

import jax
import jax.numpy as jnp
import numpy as np
from jax import lax
from jax.experimental import pallas as pl
from jax.experimental.pallas import tpu as pltpu
from jax.sharding import PartitionSpec as P

ATTEND_DIM = 64
CHUNK = 64
LEVELS = 6
PREFIX = 8
PAST = 16

eps = 1e-05
bf16 = jnp.bfloat16
f32 = jnp.float32


def dot(a, b):
    return jnp.dot(a, b, preferred_element_type=f32)


def dot_nt(a, b):
    return lax.dot_general(a, b, (((1,), (1,)), ((), ())), preferred_element_type=f32)


def dot_tn(a, b):
    return lax.dot_general(a, b, (((0,), (0,)), ((), ())), preferred_element_type=f32)


def swapped(value, axis, by):
    peers = lax.axis_size(axis)
    return lax.ppermute(value, axis, [(i, i ^ by) for i in range(peers)])


def vmem(mib):
    return pltpu.CompilerParams(vmem_limit_bytes=mib * 2**20)


def order_kernel(x_ref, gain_ref, coeff_ref, perm_ref, out_ref, coeff_out_ref, cur_ref):
    rows, width = x_ref.shape
    block = out_ref.shape[1]
    depth = 256

    @pl.when(pl.program_id(0) == 0)
    def _():
        x = x_ref[...].astype(f32)
        mean = jnp.mean(x, axis=-1, keepdims=True)
        centred = x - mean
        spread = jnp.mean(centred * centred, axis=-1, keepdims=True)
        cur_ref[:rows, :] = (centred * lax.rsqrt(spread + eps) * gain_ref[...]).astype(bf16)
        c = coeff_ref[...]
        high = c.astype(bf16)
        cur_ref[rows:, :] = jnp.concatenate([high, (c - high.astype(f32)).astype(bf16)], axis=0)

    perm = perm_ref[...]
    total = jnp.zeros((rows + 2 * PREFIX, block), f32)
    for k in range(width // depth):
        lines = lax.broadcasted_iota(jnp.int32, (depth, block), 0) + k * depth
        chosen = jnp.where(lines == perm, 1.0, 0.0).astype(bf16)
        total += dot(cur_ref[:, k * depth : (k + 1) * depth], chosen)
    out_ref[...] = total[:rows].astype(bf16)
    coeff_out_ref[...] = total[rows : rows + PREFIX] + total[rows + PREFIX :]


def ordered(x, gain, coeffs, perm):
    rows, width = x.shape
    block = 512
    return pl.pallas_call(
        order_kernel,
        grid=(width // block,),
        in_specs=[
            pl.BlockSpec((rows, width), lambda n: (0, 0)),
            pl.BlockSpec((1, width), lambda n: (0, 0)),
            pl.BlockSpec((PREFIX, width), lambda n: (0, 0)),
            pl.BlockSpec((1, block), lambda n: (0, n)),
        ],
        out_specs=[
            pl.BlockSpec((rows, block), lambda n: (0, n)),
            pl.BlockSpec((PREFIX, block), lambda n: (0, n)),
        ],
        out_shape=[
            jax.ShapeDtypeStruct((rows, width), bf16),
            jax.ShapeDtypeStruct((PREFIX, width), f32),
        ],
        scratch_shapes=[pltpu.VMEM((rows + 2 * PREFIX, width), bf16)],
        compiler_params=vmem(40),
        cost_estimate=pl.CostEstimate(
            flops=2 * rows * width * width, bytes_accessed=4 * rows * width, transcendentals=0
        ),
    )(x, gain, coeffs, perm)


def mix_kernel(where_ref, act_ref, coeff_ref, left_ref, *refs):
    mixed_ref, lora_ref, inner_ref = refs[-3:]
    rows, block = mixed_ref.shape[-2:]
    width = 512
    n = pl.program_id(0)
    inner = jnp.zeros(inner_ref.shape, f32)
    for c in range(block // width):
        cols = slice(c * width, (c + 1) * width)
        act = act_ref[:, cols].astype(f32)
        cur = act[PAST:]
        delta = pltpu.roll(act, 1, 0)[PAST:] - cur
        for j in range(3):
            mixed_ref[j, 0, 0, :, cols] = (cur + delta * coeff_ref[j : j + 1, cols]).astype(bf16)
        inner += dot((cur + delta * coeff_ref[3:4, cols]).astype(bf16), left_ref[cols, :])

    @pl.when(n == 0)
    def _():
        inner_ref[...] = inner

    @pl.when(n > 0)
    def _():
        inner_ref[...] += inner

    @pl.when(n == pl.num_programs(0) - 1)
    def _():
        lora_ref[0, 0] = jnp.tanh(inner_ref[...]).astype(bf16)


def shifted(where, act, coeffs, left, side, apart, stretches, earlier):
    span, width = act.shape[0] - PAST, act.shape[1]
    inner = left.shape[1]
    block = 1024
    kept = pl.BlockSpec(memory_space=pl.ANY)
    return pl.pallas_call(
        mix_kernel,
        grid_spec=pltpu.PrefetchScalarGridSpec(
            num_scalar_prefetch=1,
            grid=(width // block,),
            in_specs=[
                pl.BlockSpec((span + PAST, block), lambda n, w: (0, n)),
                pl.BlockSpec((PREFIX, block), lambda n, w: (0, n)),
                pl.BlockSpec((block, inner), lambda n, w: (n, 0)),
            ]
            + [kept] * len(earlier),
            out_specs=[
                pl.BlockSpec((3, 1, 1, span, block), lambda n, w: (0, side, w[0] ^ apart, 0, n)),
                pl.BlockSpec((1, 1, span, inner), lambda n, w: (side, w[0] ^ apart, 0, 0)),
            ],
            scratch_shapes=[pltpu.VMEM((span, inner), f32)],
        ),
        out_shape=[
            jax.ShapeDtypeStruct((3, 2, stretches, span, width), bf16),
            jax.ShapeDtypeStruct((2, stretches, span, inner), bf16),
        ],
        input_output_aliases={4: 0, 5: 1} if earlier else {},
        compiler_params=vmem(32),
        cost_estimate=pl.CostEstimate(
            flops=24 * act.size, bytes_accessed=8 * act.size, transcendentals=0
        ),
    )(where, act, coeffs, left, *earlier)


def project_kernel(where_ref, act_ref, gathered_ref, *refs):
    *pieces, out_ref, lines_ref = refs
    reqs, depth = gathered_ref.shape[0], gathered_ref.shape[2]
    stretches = 1 + len(pieces) // reqs

    @pl.when(pl.program_id(1) == 0)
    def _():
        for r in range(reqs):
            at = (r * stretches + where_ref[0]) * depth
            lines_ref[pl.ds(pl.multiple_of(at, depth), depth), :] = gathered_ref[r, 0]
        for i, piece_ref in enumerate(pieces):
            d, k = 1 + i // reqs, i % reqs
            at = (lax.rem(where_ref[2] + k, reqs) * stretches + (where_ref[0] ^ d)) * depth
            lines_ref[pl.ds(pl.multiple_of(at, depth), depth), :] = piece_ref[0]

    out_ref[0, 0, 0] = dot(act_ref[0, 0, 0], lines_ref[...]).astype(bf16)


def projected(where, mixed, gathered, pieces):
    reqs, kinds, depth, cols = gathered.shape
    _, sides, stretches, span, width = mixed.shape
    if depth % 128:
        order = jnp.arange(stretches) ^ where[0]
        lines = jnp.stack([gathered, *pieces])[order]
        lines = jnp.transpose(lines, (2, 1, 0, 3, 4)).reshape(kinds, width, cols)
        return jnp.einsum("jxbtk,jkc->jxbtc", mixed, lines, preferred_element_type=f32).astype(bf16)
    return pl.pallas_call(
        project_kernel,
        grid_spec=pltpu.PrefetchScalarGridSpec(
            num_scalar_prefetch=1,
            grid=(kinds, sides * stretches),
            in_specs=[
                pl.BlockSpec((1, 1, 1, span, width), lambda j, m, w: (j, m // stretches, m % stretches, 0, 0)),
                pl.BlockSpec((reqs, 1, depth, cols), lambda j, m, w: (0, j, 0, 0)),
            ]
            + [pl.BlockSpec((1, depth, cols), lambda j, m, w: (j, 0, 0))] * len(pieces),
            out_specs=pl.BlockSpec((1, 1, 1, span, cols), lambda j, m, w: (j, m // stretches, m % stretches, 0, 0)),
            scratch_shapes=[pltpu.VMEM((width, cols), bf16)],
        ),
        out_shape=jax.ShapeDtypeStruct((kinds, sides, stretches, span, cols), bf16),
        compiler_params=vmem(40),
        cost_estimate=pl.CostEstimate(
            flops=2 * mixed.size * cols,
            bytes_accessed=2 * (mixed.size + kinds * width * cols),
            transcendentals=0,
        ),
    )(where, mixed, gathered, *pieces)


def decay_sums():
    place = np.arange(CHUNK)
    of, by = place[:, None], place[None, :]
    parts = []
    for level in range(LEVELS):
        half = 1 << level
        middle = (of // (2 * half)) * 2 * half + half - 1
        later = (of % (2 * half)) >= half
        parts.append(np.where(later, (by > middle) & (by < of), (by > of) & (by <= middle)))
    parts += [by < of, by > of, np.ones((8, CHUNK), bool)]
    sums = np.concatenate(parts).astype(np.float32)
    return np.concatenate([sums, sums], axis=1)


def pair_levels(heads):
    of, by = np.arange(CHUNK)[:, None], np.arange(CHUNK)[None, :]
    level = np.full((CHUNK, CHUNK), -1.0, np.float32)
    for bit in range(LEVELS):
        level[((of ^ by) >> bit) == 1] = bit
    return np.tile(np.where(of > by, level, -1.0).astype(np.float32), (1, heads))


def wkv_kernel(
    extent_ref, where_ref, proj_ref, lora_ref, right_ref, speed_ref, reward_ref, scale_ref, sums_ref, level_ref,
    same_ref, normed_ref, state_ref, memory_ref,
):
    step = pl.program_id(0)
    tokens, cols = proj_ref.shape[3:]
    heads = cols // ATTEND_DIM
    per_block = pl.num_programs(0) // lax.axis_size("seq")
    same = same_ref[...]
    same_f32 = same.astype(f32)
    level = level_ref[...]

    @pl.when(step == 0)
    def _():
        memory_ref[...] = jnp.zeros_like(memory_ref)

    memories = [memory_ref[0], memory_ref[1]]
    for sub in range(tokens // CHUNK):
        lines = slice(sub * CHUNK, (sub + 1) * CHUNK)
        at = step * tokens + sub * CHUNK + lax.broadcasted_iota(jnp.int32, (CHUNK, cols), 0)
        for side in range(2):
            prompt = where_ref[1] ^ side
            valid = jnp.where(at < extent_ref[prompt], 1.0, 0.0)
            r = proj_ref[0, side, 0, lines].astype(f32)
            k = proj_ref[1, side, 0, lines].astype(f32) * valid
            v = proj_ref[2, side, 0, lines]
            decay = -speed_ref[...] * jnp.exp(dot(lora_ref[side, 0, lines], right_ref[...])) * valid
            high = decay.astype(bf16)
            low = (decay - high.astype(f32)).astype(bf16)
            kept = jnp.exp(dot(sums_ref[...], jnp.concatenate([high, low], axis=0)))
            scores = jnp.zeros((CHUNK, heads * CHUNK), f32)
            for bit in range(LEVELS):
                part = kept[bit * CHUNK : (bit + 1) * CHUNK]
                lookup = (k * part).astype(bf16)
                lookup = jnp.concatenate([lookup] * heads, axis=0) * same
                found = dot_nt((r * part).astype(bf16), lookup)
                scores = jnp.where(level == bit, found, scores)
            v_heads = jnp.concatenate([v] * heads, axis=0) * same
            memory = memories[side]
            from_start = (r * kept[LEVELS * CHUNK : (LEVELS + 1) * CHUNK]).astype(bf16)
            to_end = (k * kept[(LEVELS + 1) * CHUNK : (LEVELS + 2) * CHUNK]).astype(bf16)
            own = dot((r * reward_ref[...] * k).astype(bf16), same)
            y = dot_nt(from_start, memory.astype(bf16)) + dot(scores.astype(bf16), v_heads)
            y += own * v.astype(f32)
            whole = kept[(LEVELS + 2) * CHUNK : (LEVELS + 2) * CHUNK + 1]
            memories[side] = memory * whole + same_f32 * dot_tn(v, to_end)

            y_high = y.astype(bf16)
            y_low = (y - y_high.astype(f32)).astype(bf16)
            centred = y - (dot(y_high, same) + dot(y_low, same)) * (1.0 / ATTEND_DIM)
            spread = dot((centred * centred).astype(bf16), same) * (1.0 / ATTEND_DIM)
            normed = centred * lax.rsqrt(spread + eps) * scale_ref[...] * valid
            normed_ref[0, pl.ds(prompt, 1), lines] = normed.astype(bf16)[None]
    for side in range(2):
        memory_ref[side] = memories[side]

    @pl.when(step % per_block == per_block - 1)
    def _():
        for side in range(2):
            folded = memory_ref[side, :ATTEND_DIM]
            for h in range(1, heads):
                folded += memory_ref[side, h * ATTEND_DIM : (h + 1) * ATTEND_DIM]
            state_ref[0, pl.ds(where_ref[1] ^ side, 1)] = folded[None]


def recurrence(extents, where, proj, lora, right, speed, reward, scale):
    _, reqs, stretches, span, cols = proj.shape
    inner = lora.shape[-1]
    heads = cols // ATTEND_DIM
    tokens = 2 * CHUNK
    per_block = span // tokens
    sums = jnp.asarray(decay_sums(), bf16)
    level = jnp.asarray(pair_levels(heads), f32)
    head = np.arange(cols) // ATTEND_DIM
    same = jnp.asarray(head[:, None] == head[None, :], bf16)

    def fixed(array):
        return pl.BlockSpec(array.shape, lambda c, e, w: (0,) * array.ndim)

    tables = (right, speed, reward, scale, sums, level, same)
    return pl.pallas_call(
        wkv_kernel,
        grid_spec=pltpu.PrefetchScalarGridSpec(
            num_scalar_prefetch=2,
            grid=(stretches * per_block,),
            in_specs=[
                pl.BlockSpec((3, reqs, 1, tokens, cols), lambda c, e, w: (0, 0, c // per_block, c % per_block, 0)),
                pl.BlockSpec((reqs, 1, tokens, inner), lambda c, e, w: (0, c // per_block, c % per_block, 0)),
            ]
            + [fixed(a) for a in tables],
            out_specs=[
                pl.BlockSpec((1, reqs, tokens, cols), lambda c, e, w: (c // per_block, 0, c % per_block, 0)),
                pl.BlockSpec((1, reqs, ATTEND_DIM, cols), lambda c, e, w: (c // per_block, 0, 0, 0)),
            ],
            scratch_shapes=[pltpu.VMEM((reqs, cols, cols), f32)],
        ),
        out_shape=[
            jax.ShapeDtypeStruct((stretches, reqs, span, cols), bf16),
            jax.ShapeDtypeStruct((stretches, reqs, ATTEND_DIM, cols), f32),
        ],
        compiler_params=vmem(40),
        cost_estimate=pl.CostEstimate(
            flops=proj.size * 3000, bytes_accessed=4 * proj.size, transcendentals=0
        ),
    )(extents, where, proj, lora, *tables)


def finish_kernel(where_ref, x_ref, own_ref, far_ref, *refs):
    *weights, out_ref = refs
    stretches, rows, cols = own_ref.shape
    chunk = weights[0].shape[-1]
    for e in range(stretches):
        total = x_ref[:, pl.ds(pl.multiple_of((where_ref[0] ^ e) * chunk, chunk), chunk)].astype(f32)
        for side, lines_ref in enumerate((own_ref, far_ref)):
            w_ref = weights[e]
            for d in range(stretches):
                at = pl.ds(pl.multiple_of((where_ref[0] ^ d) * cols, cols), cols)
                total += dot(lines_ref[d], w_ref[side, 0, at, :])
        out_ref[:, pl.ds(pl.multiple_of((where_ref[0] ^ e) * chunk, chunk), chunk)] = total.astype(bf16)


def finished(where, x, own, far, weights):
    stretches, rows, cols = own.shape
    width = x.shape[1]
    _, groups, depth, chunk = weights[0].shape
    share = groups * stretches * chunk
    if chunk % 128:
        order = jnp.arange(stretches) ^ where[0]
        total = lax.dynamic_slice_in_dim(x, where[1] * share, share, 1).astype(f32)
        for side, lines in enumerate((own, far)):
            w = jnp.transpose(jnp.stack([w[side] for w in weights])[order], (2, 1, 0, 3)).reshape(depth, share)
            lines = jnp.transpose(lines[order], (1, 0, 2)).reshape(rows, depth)
            total += dot(lines, w)
        return total.astype(bf16)
    block = stretches * chunk
    whole = pl.BlockSpec((stretches, rows, cols), lambda g, w: (0, 0, 0))
    return pl.pallas_call(
        finish_kernel,
        grid_spec=pltpu.PrefetchScalarGridSpec(
            num_scalar_prefetch=1,
            grid=(groups,),
            in_specs=[pl.BlockSpec((rows, block), lambda g, w: (0, w[1] * groups + g)), whole, whole]
            + [pl.BlockSpec((2, 1, depth, chunk), lambda g, w: (0, g, 0, 0))] * len(weights),
            out_specs=pl.BlockSpec((rows, block), lambda g, w: (0, g)),
        ),
        out_shape=jax.ShapeDtypeStruct((rows, share), bf16),
        compiler_params=vmem(48),
        cost_estimate=pl.CostEstimate(
            flops=4 * rows * depth * share, bytes_accessed=4 * depth * share, transcendentals=0
        ),
    )(where, x, own, far, *weights)


def over_plane(value, cut):
    peers = lax.axis_size("seq")
    if peers != 4 or not cut:
        return [value] + [swapped(value, "seq", d) for d in range(1, peers)]
    near, other = swapped(value, "seq", 1), swapped(value, "seq", 2)
    across = [swapped(near[:cut], "seq", 2), swapped(other[cut:], "seq", 1)]
    return [value, near, other, jnp.concatenate(across, axis=0)]


def ahead(value, axis, by):
    peers = lax.axis_size(axis)
    return lax.ppermute(value, axis, [((i + by) % peers, i) for i in range(peers)])


def local(
    incoming_activations,
    standardize_scaling,
    lagged_blending_weights,
    learner_line_permutation,
    learner_acceptor_lookup_slices,
    learner_projection_slices,
    fading_left_matrix,
    fading_right_matrix,
    feature_fading_speed,
    self_reward,
    cluster_scaling_vector,
    prompt_extents,
):
    reqs, span, width = incoming_activations.shape
    rows = reqs * span
    stretches = lax.axis_size("seq")
    cores = lax.axis_size("tensor")
    groups = lax.axis_size("req")
    assert reqs == cores == 2
    local_width = feature_fading_speed.shape[0]
    cols = local_width // stretches
    t, s = lax.axis_index("tensor"), lax.axis_index("seq")
    where = jnp.stack([s, t, lax.axis_index("req")]).astype(jnp.int32)

    x = incoming_activations.reshape(rows, width)
    own_x = lax.dynamic_slice_in_dim(x, t * span, span, 0)
    past = lax.ppermute(own_x[span - PAST :], "seq", [(i, i + 1) for i in range(stretches - 1)])
    pieces = [
        lax.dynamic_slice_in_dim(learner_acceptor_lookup_slices, (s ^ d) * cols, cols, 2).astype(bf16)
        for d in range(stretches)
    ]
    out_half = learner_projection_slices.astype(bf16)
    out_lines = lax.all_gather(out_half, "req", axis=0, tiled=False)
    gathered = lax.all_gather(pieces[0], "req", axis=0, tiled=False)
    got = [swapped(pieces[d], "seq", d) for d in range(1, stretches)]

    own_x, past, *_ = lax.optimization_barrier((own_x, past, *pieces))
    coeffs = jnp.pad(lagged_blending_weights, ((0, PREFIX - 4), (0, 0)))
    act, coeffs = ordered(
        jnp.concatenate([past, own_x], axis=0),
        standardize_scaling.reshape(1, width),
        coeffs,
        learner_line_permutation.reshape(1, width),
    )
    act, perm, *got = lax.optimization_barrier((act, learner_line_permutation, *got))
    if pieces[0].shape[1] % 128:
        weights = [lax.all_gather(piece, "req", axis=0, tiled=False) for piece in got]
    else:
        weights = [ahead(piece, "req", k) if k else piece for piece in got for k in range(groups)]
    left = fading_left_matrix[perm]

    acts = over_plane(act, (span + PAST) // 32 * 16)
    results = ()
    for d, block in enumerate(acts):
        for side, values in enumerate((block, swapped(block, "tensor", 1))):
            results = shifted(where, values, coeffs, left, side, d, stretches, results)
    mixed, lora = results

    share = groups // cores
    kept = lax.dynamic_slice_in_dim(out_lines, t * share, share, 0)
    given = lax.dynamic_slice_in_dim(out_lines, (1 - t) * share, share, 0)
    out_lines = jnp.stack([kept, swapped(given, "tensor", 1)])
    out_lines, _ = lax.optimization_barrier((out_lines, acts[-1]))
    out_weights = over_plane(out_lines, 0)

    proj = projected(where, mixed, gathered, weights)

    def mine(array):
        return lax.dynamic_slice_in_dim(array, s * cols, cols, array.ndim - 1).reshape(-1, cols)

    normed, states = recurrence(
        prompt_extents, where, proj, lora, mine(fading_right_matrix), mine(feature_fading_speed), mine(self_reward),
        mine(cluster_scaling_vector),
    )

    sent = jnp.concatenate(
        [normed.reshape(stretches, rows, cols), states.reshape(stretches, -1, cols).astype(bf16)], axis=1
    )
    blocks = []
    for d in range(stretches):
        block = lax.dynamic_index_in_dim(sent, s ^ d, 0, keepdims=False)
        blocks.append(swapped(block, "seq", d) if d else block)
    blocks = jnp.stack(blocks)
    own_lines = blocks[:, :rows]
    far_lines = swapped(own_lines, "tensor", 1)
    hidden_out = finished(where, x, own_lines, far_lines, out_weights).reshape(reqs, span, width // cores)

    heads = cols // ATTEND_DIM
    states = blocks[jnp.arange(stretches) ^ s, rows:].reshape(stretches, reqs, ATTEND_DIM, heads, ATTEND_DIM)
    states = jnp.transpose(states, (1, 0, 3, 4, 2)).astype(f32)
    stretch_states = states.reshape(reqs, 1, stretches * heads, ATTEND_DIM * ATTEND_DIM)
    return (hidden_out, stretch_states)


def solution(mesh):
    in_specs = (
        P("req", "seq", None),
        P(),
        P(),
        P(),
        P(None, ("req", "seq"), "tensor"),
        P("tensor", ("req", "seq")),
        P(),
        P(None, "tensor"),
        P("tensor"),
        P("tensor"),
        P("tensor"),
        P("req"),
    )
    out_specs = (P("req", "seq", "tensor"), P("req", "seq", "tensor", None))
    return jax.shard_map(local, mesh=mesh, in_specs=in_specs, out_specs=out_specs, check_vma=False)
```

time: 383 us -> 379 us (0.990)
  waiting for transfers between devices: 151 us -> 128 us
  starting transfers between devices: 20.3 us -> 42.2 us
  local copies, waits for them, and re-layouts: 63.6 us -> 45.2 us
  Pallas kernels: 128 us -> 143 us
    all_gather x4 -> x1, waiting for transfers between devices: 49.7 us -> 0.01 us  [local(): gathered = lax.all_gather(pieces[0], 'req', axis=0, tiled=False)]
    ppermute x0 -> x10, waiting for transfers between devices: none -> 32.2 us  [the longest x9 32.2 us: ahead(): lax.ppermute(value, axis, [((i + by) % peers, i) for i in range(peers)])]
    ppermute x0 -> x10, starting transfers between devices: none -> 26.9 us  [the longest x9 22.1 us: ahead(): lax.ppermute(value, axis, [((i + by) % peers, i) for i in range(peers)])]
    pallas_call x2 -> x8, Pallas kernels: 34 us -> 52.4 us  [shifted(): pl.pallas_call(mix_kernel, grid_spec=pltpu.PrefetchScalarGridSpec(num_sca...]
    unnamed x58 -> x41, local copies, waits for them, and re-layouts: 19.3 us -> 5.28 us
    ppermute x17 -> x19, waiting for transfers between devices: 102 us -> 95.8 us  [swapped(): return lax.ppermute(value, axis, [(i, i ^ by) for i in range(peers)])]
    slice x4 -> x3, local copies, waits for them, and re-layouts: 9.09 us -> 3.67 us  [the longest x2 2.67 us: over_plane(): across = [swapped(near[:cut], 'seq', 2), swapped(other[cut:], 'seq', 1)]]
    ppermute x17 -> x19, starting transfers between devices: 20.1 us -> 15.2 us  [swapped(): return lax.ppermute(value, axis, [(i, i ^ by) for i in range(peers)])]
  transfers between devices with their start and end apart: 22 -> 31, of which waited for: 12 -> 8; matrix products, arithmetic and copies ran while one was open for 14% -> 12% of each run, Pallas kernels for 31% -> 36%
where the time goes in v1:
time: 379 us; the launch traced here: 377 us
  Pallas kernels  143 us (38%)
  waiting for transfers between devices  128 us (34%)
  local copies, waits for them, and re-layouts  45.2 us (12%)
  starting transfers between devices  42.2 us (11%)
  between operations  14.4 us (4%)
  other arithmetic  4.52 us (1%)
    ppermute x19, waiting for transfers between devices, swapped(): return lax.ppermute(value, axis, [(i, i ^ by) for i in range(peers)])  95.8 us
    pallas_call x8, Pallas kernels, shifted(): pl.pallas_call(mix_kernel, grid_spec=pltpu.PrefetchScalarGridSpec(num_sca...  52.4 us
    pallas_call x1, Pallas kernels, recurrence(): pl.pallas_call(wkv_kernel, grid_spec=pltpu.PrefetchScalarGridSpec(num_sca...  36.6 us
    ppermute x9, waiting for transfers between devices, ahead(): lax.ppermute(value, axis, [((i + by) % peers, i) for i in range(peers)])  32.2 us
    pallas_call x1, Pallas kernels, projected(): pl.pallas_call(project_kernel, grid_spec=pltpu.PrefetchScalarGridSpec(num...  31.4 us
    ppermute x9, starting transfers between devices, ahead(): lax.ppermute(value, axis, [((i + by) % peers, i) for i in range(peers)])  22.1 us
    ppermute x19, starting transfers between devices, swapped(): return lax.ppermute(value, axis, [(i, i ^ by) for i in range(peers)])  15.2 us
    pallas_call x1, Pallas kernels, ordered(): pl.pallas_call(order_kernel, grid=(width // block,), in_specs=[pl.BlockSp...  13.9 us
  transfers between devices with their start and end apart: 31, of which 8 were waited for; matrix products, arithmetic and copies ran while one was open for 12% of the time, Pallas kernels for 36%

profile of v1, /device:TPU:0, one launch (start us, length us, event | category | flops | bytes accessed | tf_op | source)
XLA Modules:
  0.0 377.5 jit_solution(174242192082363192)
XLA Ops:
  8.2 4.8 %collective-permute-start = (bf16[16,4096]{1,0:T(8,128)(2,1)S(1)}, bf16[16,4096]{1,0:T(8,128)(2,1)S(1)}, u32[]{:S(2)}, u32[]{:S(2)}) collective-permute-start(bf16[16,4096]{1,0:T(8,128)(2,1)S(1)} %constant_dynamic-slice_fusion), channel_id=1, source_target_pairs={{0,1},{1,2},{2,3},{4,5},{5,6},{6,7},{8,9},{9,10},{10,11},{12,13},{... | collective-permute-start | bytes 393224 | tf_op jit(solution)/shard_map/ppermute | solution.py:424
  13.1 2.9 dynamic-slice_convert_fusion
  16.0 1.5 collective-permute-start.1
  17.6 2.0 collective-permute-start.3
  19.5 3.1 constant_dynamic-slice_fusion.3
  22.7 1.8 pad_maximum_fusion.x_ref
  24.6 13.9 %shard_map.158 = (bf16[272,4096]{1,0:T(8,128)(2,1)}, f32[8,4096]{1,0:T(8,128)S(1)}) custom-call(bf16[272,4096]{1,0:T(8,128)(2,1)S(1)} %pad_maximum_fusion.x_ref, f32[1,4096]{1,0:T(1,128)S(1)} %bitcast.39, f32[8,4096]{1,0:T(8,128)S(1)} %pad.5.coeff_ref, s32[1,4096]{1,0:T(1,128)S(1)} %bitcast.35), custom_call_target="tpu_custom_call" | custom-call | flops 9126805504 | bytes 4456448 | tf_op jit(solution)/shard_map/pallas_call | solution.py:72
  38.5 1.6 collective-permute-start.4
  41.1 46.9 %collective-permute-done.4.act_ref = bf16[272,4096]{1,0:T(8,128)(2,1)} collective-permute-done((bf16[272,4096]{1,0:T(8,128)(2,1)}, bf16[272,4096]{1,0:T(8,128)(2,1)}, u32[]{:S(2)}, u32[]{:S(2)}) %collective-permute-start.4) | collective-permute-done | bytes 2228256 | tf_op jit(solution)/shard_map/ppermute | solution.py:36
  88.0 1.3 slice.20
  89.3 1.6 collective-permute-start.5
  90.9 1.4 slice.21
  92.6 3.6 collective-permute-start.12
  96.2 16.0 %collective-permute-done.5 = bf16[128,4096]{1,0:T(8,128)(2,1)S(1)} collective-permute-done((bf16[128,4096]{1,0:T(8,128)(2,1)S(1)}, bf16[128,4096]{1,0:T(8,128)(2,1)S(1)}, u32[]{:S(2)}, u32[]{:S(2)}) %collective-permute-start.5) | collective-permute-done | bytes 1048608 | tf_op jit(solution)/shard_map/ppermute | solution.py:36
  113.3 4.4 %collective-permute-done.7 = bf16[144,4096]{1,0:T(8,128)(2,1)S(1)} collective-permute-done((bf16[144,4096]{1,0:T(8,128)(2,1)S(1)}, bf16[144,4096]{1,0:T(8,128)(2,1)S(1)}, u32[]{:S(2)}, u32[]{:S(2)}) %collective-permute-start.7) | collective-permute-done | bytes 1179680 | tf_op jit(solution)/shard_map/ppermute | solution.py:36
  117.7 1.1 constant_dynamic-update-slice_fusion.act_ref
  119.4 2.6 collective-permute-done.13.refs_2_
  122.9 15.6 %collective-permute-done.14.refs_3_ = bf16[3,256,256]{2,1,0:T(8,128)(2,1)S(1)} collective-permute-done((bf16[3,256,256]{2,1,0:T(8,128)(2,1)S(1)}, bf16[3,256,256]{2,1,0:T(8,128)(2,1)S(1)}, u32[]{:S(2)}, u32[]{:S(2)}) %collective-permute-start.14) | collective-permute-done | bytes 393248 | tf_op jit(solution)/shard_map/ppermute | solution.py:394
  139.2 12.1 %collective-permute-start.15 = (bf16[3,256,256]{2,1,0:T(8,128)(2,1)S(1)}, bf16[3,256,256]{2,1,0:T(8,128)(2,1)}, u32[]{:S(2)}, u32[]{:S(2)}) collective-permute-start(bf16[3,256,256]{2,1,0:T(8,128)(2,1)S(1)} %collective-permute-done.2.refs_4_), channel_id=1, source_target_pairs={{4,0},{8,4},{12,8},{0,12},{5,1},{9,5},{13,9},{1,13},{6,2},{10,6},{... | collective-permute-start | bytes 1179656 | tf_op jit(solution)/shard_map/ppermute | solution.py:394
  151.2 3.0 dynamic-slice_bitcast_fusion
  154.3 14.1 %collective-permute-done.15.refs_5_ = bf16[3,256,256]{2,1,0:T(8,128)(2,1)} collective-permute-done((bf16[3,256,256]{2,1,0:T(8,128)(2,1)S(1)}, bf16[3,256,256]{2,1,0:T(8,128)(2,1)}, u32[]{:S(2)}, u32[]{:S(2)}) %collective-permute-start.15) | collective-permute-done | bytes 393248 | tf_op jit(solution)/shard_map/ppermute | solution.py:394
  171.6 1.2 collective-permute-start.17
  172.8 2.6 collective-permute-start.18
  177.2 12.1 %gather_fusion = bf16[4096,128]{1,0:T(8,128)(2,1)S(1)} fusion(bf16[4096,128]{1,0:T(8,128)(2,1)S(1)} %copy-done, s32[4096]{0:T(1024)S(1)} %fusion.7), kind=kCustom, calls=%fused_computation | custom fusion | bytes 2113536 | tf_op jit(solution)/shard_map/gather | solution.py:447
  189.3 6.5 %shard_map.159 = (bf16[3,2,4,256,4096]{4,3,2,1,0:T(8,128)(2,1)}, bf16[2,4,256,128]{3,2,1,0:T(8,128)(2,1)S(1)}) custom-call(s32[3]{0:T(128)S(1)} %pad_add_fusion.where_ref, bf16[272,4096]{1,0:T(8,128)(2,1)} %get-tuple-element.33.act_ref, f32[8,4096]{1,0:T(8,128)S(1)} %get-tuple-element.34.coeff_ref, bf16[4096,128]{1,0:T(8,128)(2,1)S(1)} %gather_fusion), custom_call_target="tpu_custom_call" | custom-call | flops 26738688 | bytes 8912896 | tf_op jit(solution)/shard_map/pallas_call | solution.py:130
  195.8 6.6 %shard_map.160 = (bf16[3,2,4,256,4096]{4,3,2,1,0:T(8,128)(2,1)}, bf16[2,4,256,128]{3,2,1,0:T(8,128)(2,1)S(1)}) custom-call(s32[3]{0:T(128)S(1)} %pad_add_fusion.where_ref, bf16[272,4096]{1,0:T(8,128)(2,1)} %collective-permute-done.11.act_ref, f32[8,4096]{1,0:T(8,128)S(1)} %get-tuple-element.34.coeff_ref, ...), custom_call_target="tpu_custom_call", output_to_operand_aliasing={{0}: (4, {}), {1}: (5, {})} | custom-call | flops 26738688 | bytes 8912896 | tf_op jit(solution)/shard_map/pallas_call | solution.py:130
  202.4 6.6 %shard_map.161 = (bf16[3,2,4,256,4096]{4,3,2,1,0:T(8,128)(2,1)}, bf16[2,4,256,128]{3,2,1,0:T(8,128)(2,1)S(1)}) custom-call(s32[3]{0:T(128)S(1)} %pad_add_fusion.where_ref, bf16[272,4096]{1,0:T(8,128)(2,1)} %collective-permute-done.4.act_ref, f32[8,4096]{1,0:T(8,128)S(1)} %get-tuple-element.34.coeff_ref, ...), custom_call_target="tpu_custom_call", output_to_operand_aliasing={{0}: (4, {}), {1}: (5, {})} | custom-call | flops 26738688 | bytes 8912896 | tf_op jit(solution)/shard_map/pallas_call | solution.py:130
  209.0 1.5 pad_maximum_fusion.1.refs_0_
  210.5 6.5 %shard_map.162 = (bf16[3,2,4,256,4096]{4,3,2,1,0:T(8,128)(2,1)}, bf16[2,4,256,128]{3,2,1,0:T(8,128)(2,1)S(1)}) custom-call(s32[3]{0:T(128)S(1)} %pad_add_fusion.where_ref, bf16[272,4096]{1,0:T(8,128)(2,1)} %collective-permute-done.10.act_ref, f32[8,4096]{1,0:T(8,128)S(1)} %get-tuple-element.34.coeff_ref, ...), custom_call_target="tpu_custom_call", output_to_operand_aliasing={{0}: (4, {}), {1}: (5, {})} | custom-call | flops 26738688 | bytes 8912896 | tf_op jit(solution)/shard_map/pallas_call | solution.py:130
  217.0 6.5 %shard_map.163 = (bf16[3,2,4,256,4096]{4,3,2,1,0:T(8,128)(2,1)}, bf16[2,4,256,128]{3,2,1,0:T(8,128)(2,1)S(1)}) custom-call(s32[3]{0:T(128)S(1)} %pad_add_fusion.where_ref, bf16[272,4096]{1,0:T(8,128)(2,1)} %collective-permute-done.6.act_ref, f32[8,4096]{1,0:T(8,128)S(1)} %get-tuple-element.34.coeff_ref, ...), custom_call_target="tpu_custom_call", output_to_operand_aliasing={{0}: (4, {}), {1}: (5, {})} | custom-call | flops 26738688 | bytes 8912896 | tf_op jit(solution)/shard_map/pallas_call | solution.py:130
  223.5 6.5 %shard_map.164 = (bf16[3,2,4,256,4096]{4,3,2,1,0:T(8,128)(2,1)}, bf16[2,4,256,128]{3,2,1,0:T(8,128)(2,1)S(1)}) custom-call(s32[3]{0:T(128)S(1)} %pad_add_fusion.where_ref, bf16[272,4096]{1,0:T(8,128)(2,1)} %collective-permute-done.9.act_ref, f32[8,4096]{1,0:T(8,128)S(1)} %get-tuple-element.34.coeff_ref, ...), custom_call_target="tpu_custom_call", output_to_operand_aliasing={{0}: (4, {}), {1}: (5, {})} | custom-call | flops 26738688 | bytes 8912896 | tf_op jit(solution)/shard_map/pallas_call | solution.py:130
  230.0 6.6 %shard_map.165 = (bf16[3,2,4,256,4096]{4,3,2,1,0:T(8,128)(2,1)}, bf16[2,4,256,128]{3,2,1,0:T(8,128)(2,1)S(1)}) custom-call(s32[3]{0:T(128)S(1)} %pad_add_fusion.where_ref, bf16[272,4096]{1,0:T(8,128)(2,1)} %constant_dynamic-update-slice_fusion.act_ref, f32[8,4096]{1,0:T(8,128)S(1)} %get-tuple-element.34.coeff_ref, ...), custom_call_target="tpu_custom_call", output_to_operand_aliasing={{0}: (4, {}), {1}: (5, {})} | custom-call | flops 26738688 | bytes 8912896 | tf_op jit(solution)/shard_map/pallas_call | solution.py:130
  236.6 6.5 %shard_map.166 = (bf16[3,2,4,256,4096]{4,3,2,1,0:T(8,128)(2,1)}, bf16[2,4,256,128]{3,2,1,0:T(8,128)(2,1)S(1)}) custom-call(s32[3]{0:T(128)S(1)} %pad_add_fusion.where_ref, bf16[272,4096]{1,0:T(8,128)(2,1)} %collective-permute-done.8.act_ref, f32[8,4096]{1,0:T(8,128)S(1)} %get-tuple-element.34.coeff_ref, ...), custom_call_target="tpu_custom_call", output_to_operand_aliasing={{0}: (4, {}), {1}: (5, {})} | custom-call | flops 26738688 | bytes 8912896 | tf_op jit(solution)/shard_map/pallas_call | solution.py:130
  243.1 1.7 collective-permute-start.26
  245.4 1.2 collective-permute-start.28
  246.7 1.4 copy-done.2
  250.1 31.4 %shard_map.167.proj_ref = bf16[3,2,4,256,256]{4,3,2,1,0:T(8,128)(2,1)S(1)} custom-call(s32[3]{0:T(128)S(1)} %pad_add_fusion.where_ref, bf16[3,2,4,256,4096]{4,3,2,1,0:T(8,128)(2,1)} %get-tuple-element.50.act_ref, bf16[4,3,256,256]{3,2,1,0:T(8,128)(2,1)S(1)} %bitcast.33, bf16[3,256,256]{2,1,0:T(8,128)(2,1)S(1)} %collective-permute-done.1.refs_0_, ...), custom_call_target="tpu_custom_call" | custom-call | flops 12884901888 | bytes 56623104 | tf_op jit(solution)/shard_map/pallas_call | solution.py:185
  281.5 36.6 %shard_map.168 = (bf16[4,2,256,256]{3,2,1,0:T(8,128)(2,1)S(1)}, f32[4,2,64,256]{3,2,1,0:T(8,128)S(1)}) custom-call(s32[2]{0:T(128)S(1)} %copy-done.11, s32[3]{0:T(128)S(1)} %pad_add_fusion.where_ref, bf16[3,2,4,256,256]{4,3,2,1,0:T(8,128)(2,1)S(1)} %shard_map.167.proj_ref, bf16[2,4,256,128]{3,2,1,0:T(8,128)(2,1)S(1)} %get-tuple-element.54.lora_ref, ...), custom_call_target="tpu_custom_call" | custom-call | flops 4718592000 | bytes 6291456 | tf_op jit(solution)/shard_map/pallas_call | solution.py:310
  318.2 1.8 collective-permute-start.21
  320.5 21.5 %collective-permute-done.21 = bf16[640,256]{1,0:T(8,128)(2,1)S(1)} collective-permute-done((bf16[640,256]{1,0:T(8,128)(2,1)S(1)}, bf16[640,256]{1,0:T(8,128)(2,1)S(1)}, u32[]{:S(2)}, u32[]{:S(2)}) %collective-permute-start.21) | collective-permute-done | bytes 327712 | tf_op jit(solution)/shard_map/ppermute | solution.py:36
  342.0 1.7 collective-permute-start.23
  343.7 7.0 %collective-permute-done.23 = bf16[640,256]{1,0:T(8,128)(2,1)S(1)} collective-permute-done((bf16[640,256]{1,0:T(8,128)(2,1)S(1)}, bf16[640,256]{1,0:T(8,128)(2,1)S(1)}, u32[]{:S(2)}, u32[]{:S(2)}) %collective-permute-start.23) | collective-permute-done | bytes 327712 | tf_op jit(solution)/shard_map/ppermute | solution.py:36
  351.0 2.1 copy.33
  353.1 3.3 gather_fusion.1
  356.4 1.4 reshape.69
  357.8 1.5 copy.34
  359.3 2.4 reshape.66
  361.7 8.9 %shard_map.169 = bf16[512,2048]{1,0:T(8,128)(2,1)} custom-call(s32[3]{0:T(128)S(1)} %pad_add_fusion.where_ref, bf16[512,4096]{1,0:T(8,128)(2,1)} %bitcast.42, bf16[4,512,256]{2,1,0:T(8,128)(2,1)S(1)} %slice.22.own_ref, bf16[4,512,256]{2,1,0:T(8,128)(2,1)S(1)} %collective-permute-done.24.far_ref, bf16[2,2,1024,256]{3,2,1,0:T(8,128)(2,1)} %pad_maximum_fusion.1.refs_0_, ...), custom_call_target="tpu_custom_call" | custom-call | flops 4294967296 | bytes 8388608 | tf_op jit(solution)/shard_map/pallas_call | solution.py:366
  (97 shorter events, 14.1 us)
Async XLA Ops:
  7.2 170.0 %copy-start = (bf16[4096,128]{1,0:T(8,128)(2,1)S(1)}, bf16[4096,128]{1,0:T(8,128)(2,1)}, u32[]{:S(2)}) copy-start(bf16[4096,128]{1,0:T(8,128)(2,1)} %param.21) | copy-start | bytes 3145732
  7.2 144.0 %all-gather.7.cloned.1.call-start = ((), (), s32[]{:S(2)}) async-start(), calls=%async_computation.1 | async-start | bytes 2621440 | tf_op jit(solution)/shard_map/all_gather | solution.py:430
  8.2 14.5 %collective-permute-start = (bf16[16,4096]{1,0:T(8,128)(2,1)S(1)}, bf16[16,4096]{1,0:T(8,128)(2,1)S(1)}, u32[]{:S(2)}, u32[]{:S(2)}) collective-permute-start(bf16[16,4096]{1,0:T(8,128)(2,1)S(1)} %constant_dynamic-slice_fusion), channel_id=1, source_target_pairs={{0,1},{1,2},{2,3},{4,5},{5,6},{6,7},{8,9},{9,10},{10,11},{12,13},{... | collective-permute-start | bytes 393224 | tf_op jit(solution)/shard_map/ppermute | solution.py:424
  16.0 22.5 %collective-permute-start.1 = (bf16[3,256,256]{2,1,0:T(8,128)(2,1)}, bf16[3,256,256]{2,1,0:T(8,128)(2,1)S(1)}, u32[]{:S(2)}, u32[]{:S(2)}) collective-permute-start(bf16[3,256,256]{2,1,0:T(8,128)(2,1)} %get-tuple-element.59), channel_id=1, source_target_pairs={{0,1},{1,0},{2,3},{3,2},{4,5},{5,4},{6,7},{7,6},{8,9},{9,8},{10,11... | collective-permute-start | bytes 1179656 | tf_op jit(solution)/shard_map/ppermute | solution.py:36
  17.5 21.0 %collective-permute-start.2 = (bf16[3,256,256]{2,1,0:T(8,128)(2,1)S(1)}, bf16[3,256,256]{2,1,0:T(8,128)(2,1)S(1)}, u32[]{:S(2)}, u32[]{:S(2)}) collective-permute-start(bf16[3,256,256]{2,1,0:T(8,128)(2,1)S(1)} %get-tuple-element.61), channel_id=1, source_target_pairs={{0,2},{1,3},{2,0},{3,1},{4,6},{5,7},{6,4},{7,5},{8,10},{9,11},{10,... | collective-permute-start | bytes 1179656 | tf_op jit(solution)/shard_map/ppermute | solution.py:36
  17.6 5.1 %copy-start.19 = (f32[4,4096]{1,0:T(4,128)S(1)}, f32[4,4096]{1,0:T(4,128)}, u32[]{:S(2)}) copy-start(f32[4,4096]{1,0:T(4,128)} %param.17) | copy-start | bytes 196612
  17.6 21.0 %collective-permute-start.3 = (bf16[3,256,256]{2,1,0:T(8,128)(2,1)S(1)}, bf16[3,256,256]{2,1,0:T(8,128)(2,1)S(1)}, u32[]{:S(2)}, u32[]{:S(2)}) collective-permute-start(bf16[3,256,256]{2,1,0:T(8,128)(2,1)S(1)} %get-tuple-element.58), channel_id=1, source_target_pairs={{0,3},{1,2},{2,1},{3,0},{4,7},{5,6},{6,5},{7,4},{8,11},{9,10},{10,... | collective-permute-start | bytes 1179656 | tf_op jit(solution)/shard_map/ppermute | solution.py:36
  22.7 1.9 copy-start.9
  22.7 1.9 copy-start.10
  24.6 15.6 %copy-start.16 = (f32[1024,256]{1,0:T(8,128)S(1)}, f32[1024,256]{1,0:T(8,128)}, u32[]{:S(2)}) copy-start(f32[1024,256]{1,0:T(8,128)} %param.20) | copy-start | bytes 3145732
  38.5 49.4 %collective-permute-start.4 = (bf16[272,4096]{1,0:T(8,128)(2,1)}, bf16[272,4096]{1,0:T(8,128)(2,1)}, u32[]{:S(2)}, u32[]{:S(2)}) collective-permute-start(bf16[272,4096]{1,0:T(8,128)(2,1)} %get-tuple-element.33.act_ref), channel_id=1, source_target_pairs={{0,1},{1,0},{2,3},{3,2},{4,5},{5,4},{6,7},{7,6},{8,9},{9,8},{10,11... | collective-permute-start | bytes 6684680 | tf_op jit(solution)/shard_map/ppermute | solution.py:36
  40.1 50.8 %collective-permute-start.6 = (bf16[272,4096]{1,0:T(8,128)(2,1)}, bf16[272,4096]{1,0:T(8,128)(2,1)}, u32[]{:S(2)}, u32[]{:S(2)}) collective-permute-start(bf16[272,4096]{1,0:T(8,128)(2,1)} %get-tuple-element.33.act_ref), channel_id=1, source_target_pairs={{0,2},{1,3},{2,0},{3,1},{4,6},{5,7},{6,4},{7,5},{8,10},{9,11},{10,... | collective-permute-start | bytes 6684680 | tf_op jit(solution)/shard_map/ppermute | solution.py:36
  41.1 205.6 %all-gather.5.cloned.1.call-start = ((), (), s32[]{:S(2)}) async-start(), calls=%async_computation | async-start | bytes 1966080 | tf_op jit(solution)/shard_map/all_gather | solution.py:431
  89.3 22.9 %collective-permute-start.5 = (bf16[128,4096]{1,0:T(8,128)(2,1)S(1)}, bf16[128,4096]{1,0:T(8,128)(2,1)S(1)}, u32[]{:S(2)}, u32[]{:S(2)}) collective-permute-start(bf16[128,4096]{1,0:T(8,128)(2,1)S(1)} %slice.20), channel_id=1, source_target_pairs={{0,2},{1,3},{2,0},{3,1},{4,6},{5,7},{6,4},{7,5},{8,10},{9,11},{10,... | collective-permute-start | bytes 3145736 | tf_op jit(solution)/shard_map/ppermute | solution.py:36
  92.3 25.5 %collective-permute-start.7 = (bf16[144,4096]{1,0:T(8,128)(2,1)S(1)}, bf16[144,4096]{1,0:T(8,128)(2,1)S(1)}, u32[]{:S(2)}, u32[]{:S(2)}) collective-permute-start(bf16[144,4096]{1,0:T(8,128)(2,1)S(1)} %slice.21), channel_id=1, source_target_pairs={{0,1},{1,0},{2,3},{3,2},{4,5},{5,4},{6,7},{7,6},{8,9},{9,8},{10,11... | collective-permute-start | bytes 3538952 | tf_op jit(solution)/shard_map/ppermute | solution.py:36
  92.6 78.9 %collective-permute-start.11 = (bf16[272,4096]{1,0:T(8,128)(2,1)}, bf16[272,4096]{1,0:T(8,128)(2,1)}, u32[]{:S(2)}, u32[]{:S(2)}) collective-permute-start(bf16[272,4096]{1,0:T(8,128)(2,1)} %get-tuple-element.33.act_ref), channel_id=1, source_target_pairs={{0,16},{16,0},{1,17},{17,1},{2,18},{18,2},{3,19},{19,3},{4,20},{20... | collective-permute-start | bytes 6684680 | tf_op jit(solution)/shard_map/ppermute | solution.py:36
  92.6 26.2 %collective-permute-start.12 = (bf16[3,256,256]{2,1,0:T(8,128)(2,1)S(1)}, bf16[3,256,256]{2,1,0:T(8,128)(2,1)S(1)}, u32[]{:S(2)}, u32[]{:S(2)}) collective-permute-start(bf16[3,256,256]{2,1,0:T(8,128)(2,1)S(1)} %collective-permute-done.1.refs_0_), channel_id=1, source_target_pairs={{4,0},{8,4},{12,8},{0,12},{5,1},{9,5},{13,9},{1,13},{6,2},{10,6},{... | collective-permute-start | bytes 1179656 | tf_op jit(solution)/shard_map/ppermute | solution.py:394
  96.2 25.8 %collective-permute-start.13 = (bf16[3,256,256]{2,1,0:T(8,128)(2,1)S(1)}, bf16[3,256,256]{2,1,0:T(8,128)(2,1)S(1)}, u32[]{:S(2)}, u32[]{:S(2)}) collective-permute-start(bf16[3,256,256]{2,1,0:T(8,128)(2,1)S(1)} %collective-permute-done.1.refs_0_), channel_id=1, source_target_pairs={{8,0},{12,4},{0,8},{4,12},{9,1},{13,5},{1,9},{5,13},{10,2},{14,6},... | collective-permute-start | bytes 1179656 | tf_op jit(solution)/shard_map/ppermute | solution.py:394
  112.2 60.6 %collective-permute-start.10 = (bf16[272,4096]{1,0:T(8,128)(2,1)}, bf16[272,4096]{1,0:T(8,128)(2,1)}, u32[]{:S(2)}, u32[]{:S(2)}) collective-permute-start(bf16[272,4096]{1,0:T(8,128)(2,1)} %collective-permute-done.4.act_ref), channel_id=1, source_target_pairs={{0,16},{16,0},{1,17},{17,1},{2,18},{18,2},{3,19},{19,3},{4,20},{20... | collective-permute-start | bytes 6684680 | tf_op jit(solution)/shard_map/ppermute | solution.py:36
  117.7 57.7 %collective-permute-start.9 = (bf16[272,4096]{1,0:T(8,128)(2,1)}, bf16[272,4096]{1,0:T(8,128)(2,1)}, u32[]{:S(2)}, u32[]{:S(2)}) collective-permute-start(bf16[272,4096]{1,0:T(8,128)(2,1)} %collective-permute-done.6.act_ref), channel_id=1, source_target_pairs={{0,16},{16,0},{1,17},{17,1},{2,18},{18,2},{3,19},{19,3},{4,20},{20... | collective-permute-start | bytes 6684680 | tf_op jit(solution)/shard_map/ppermute | solution.py:36
  118.9 35.4 %copy-start.3 = (bf16[3,256,256]{2,1,0:T(8,128)(2,1)}, bf16[3,256,256]{2,1,0:T(8,128)(2,1)S(1)}, u32[]{:S(2)}) copy-start(bf16[3,256,256]{2,1,0:T(8,128)(2,1)S(1)} %collective-permute-done.12.refs_1_) | copy-start | bytes 1179652
  118.9 57.6 %collective-permute-start.8 = (bf16[272,4096]{1,0:T(8,128)(2,1)}, bf16[272,4096]{1,0:T(8,128)(2,1)}, u32[]{:S(2)}, u32[]{:S(2)}) collective-permute-start(bf16[272,4096]{1,0:T(8,128)(2,1)} %constant_dynamic-update-slice_fusion.act_ref), channel_id=1, source_target_pairs={{0,16},{16,0},{1,17},{17,1},{2,18},{18,2},{3,19},{19,3},{4,20},{20... | collective-permute-start | bytes 6684680 | tf_op jit(solution)/shard_map/ppermute | solution.py:36
  122.0 32.3 %copy-start.5 = (bf16[3,256,256]{2,1,0:T(8,128)(2,1)}, bf16[3,256,256]{2,1,0:T(8,128)(2,1)S(1)}, u32[]{:S(2)}) copy-start(bf16[3,256,256]{2,1,0:T(8,128)(2,1)S(1)} %collective-permute-done.13.refs_2_) | copy-start | bytes 1179652
  122.0 16.4 %collective-permute-start.14 = (bf16[3,256,256]{2,1,0:T(8,128)(2,1)S(1)}, bf16[3,256,256]{2,1,0:T(8,128)(2,1)S(1)}, u32[]{:S(2)}, u32[]{:S(2)}) collective-permute-start(bf16[3,256,256]{2,1,0:T(8,128)(2,1)S(1)} %collective-permute-done.1.refs_0_), channel_id=1, source_target_pairs={{12,0},{0,4},{4,8},{8,12},{13,1},{1,5},{5,9},{9,13},{14,2},{2,6},{... | collective-permute-start | bytes 1179656 | tf_op jit(solution)/shard_map/ppermute | solution.py:394
  139.2 29.2 %collective-permute-start.15 = (bf16[3,256,256]{2,1,0:T(8,128)(2,1)S(1)}, bf16[3,256,256]{2,1,0:T(8,128)(2,1)}, u32[]{:S(2)}, u32[]{:S(2)}) collective-permute-start(bf16[3,256,256]{2,1,0:T(8,128)(2,1)S(1)} %collective-permute-done.2.refs_4_), channel_id=1, source_target_pairs={{4,0},{8,4},{12,8},{0,12},{5,1},{9,5},{13,9},{1,13},{6,2},{10,6},{... | collective-permute-start | bytes 1179656 | tf_op jit(solution)/shard_map/ppermute | solution.py:394
  168.3 3.2 collective-permute-start.25
  171.5 71.6 %collective-permute-start.16 = (bf16[3,256,256]{2,1,0:T(8,128)(2,1)S(1)}, bf16[3,256,256]{2,1,0:T(8,128)(2,1)}, u32[]{:S(2)}, u32[]{:S(2)}) collective-permute-start(bf16[3,256,256]{2,1,0:T(8,128)(2,1)S(1)} %collective-permute-done.2.refs_4_), channel_id=1, source_target_pairs={{8,0},{12,4},{0,8},{4,12},{9,1},{13,5},{1,9},{5,13},{10,2},{14,6},... | collective-permute-start | bytes 1179656 | tf_op jit(solution)/shard_map/ppermute | solution.py:394
  171.6 5.6 %copy-start.17 = (bf16[2,1024,256]{2,1,0:T(8,128)(2,1)}, bf16[2,1024,256]{2,1,0:T(8,128)(2,1)S(1)}, u32[]{:S(2)}) copy-start(bf16[2,1024,256]{2,1,0:T(8,128)(2,1)S(1)} %collective-permute-done.25) | copy-start | bytes 3145732
  171.6 73.3 %collective-permute-start.17 = (bf16[3,256,256]{2,1,0:T(8,128)(2,1)S(1)}, bf16[3,256,256]{2,1,0:T(8,128)(2,1)}, u32[]{:S(2)}, u32[]{:S(2)}) collective-permute-start(bf16[3,256,256]{2,1,0:T(8,128)(2,1)S(1)} %collective-permute-done.2.refs_4_), channel_id=1, source_target_pairs={{12,0},{0,4},{4,8},{8,12},{13,1},{1,5},{5,9},{9,13},{14,2},{2,6},{... | collective-permute-start | bytes 1179656 | tf_op jit(solution)/shard_map/ppermute | solution.py:394
  172.8 72.6 %collective-permute-start.18 = (bf16[3,256,256]{2,1,0:T(8,128)(2,1)S(1)}, bf16[3,256,256]{2,1,0:T(8,128)(2,1)}, u32[]{:S(2)}, u32[]{:S(2)}) collective-permute-start(bf16[3,256,256]{2,1,0:T(8,128)(2,1)S(1)} %collective-permute-done.3.refs_8_), channel_id=1, source_target_pairs={{4,0},{8,4},{12,8},{0,12},{5,1},{9,5},{13,9},{1,13},{6,2},{10,6},{... | collective-permute-start | bytes 1179656 | tf_op jit(solution)/shard_map/ppermute | solution.py:394
  175.5 71.2 %collective-permute-start.19 = (bf16[3,256,256]{2,1,0:T(8,128)(2,1)S(1)}, bf16[3,256,256]{2,1,0:T(8,128)(2,1)}, u32[]{:S(2)}, u32[]{:S(2)}) collective-permute-start(bf16[3,256,256]{2,1,0:T(8,128)(2,1)S(1)} %collective-permute-done.3.refs_8_), channel_id=1, source_target_pairs={{8,0},{12,4},{0,8},{4,12},{9,1},{13,5},{1,9},{5,13},{10,2},{14,6},... | collective-permute-start | bytes 1179656 | tf_op jit(solution)/shard_map/ppermute | solution.py:394
  176.5 70.1 %collective-permute-start.20 = (bf16[3,256,256]{2,1,0:T(8,128)(2,1)S(1)}, bf16[3,256,256]{2,1,0:T(8,128)(2,1)}, u32[]{:S(2)}, u32[]{:S(2)}) collective-permute-start(bf16[3,256,256]{2,1,0:T(8,128)(2,1)S(1)} %collective-permute-done.3.refs_8_), channel_id=1, source_target_pairs={{12,0},{0,4},{4,8},{8,12},{13,1},{1,5},{5,9},{9,13},{14,2},{2,6},{... | collective-permute-start | bytes 1179656 | tf_op jit(solution)/shard_map/ppermute | solution.py:394
  202.4 6.6 %copy-start.15 = (bf16[1,2,1024,256]{3,2,1,0:T(8,128)(2,1)S(1)}, bf16[1,2,1024,256]{3,2,1,0:T(8,128)(2,1)}, u32[]{:S(2)}) copy-start(bf16[1,2,1024,256]{3,2,1,0:T(8,128)(2,1)} %get-tuple-element.62) | copy-start | bytes 3145732
  202.4 6.6 %copy-start.18 = (bf16[2,1024,256]{2,1,0:T(8,128)(2,1)S(1)}, bf16[2,1024,256]{2,1,0:T(8,128)(2,1)}, u32[]{:S(2)}) copy-start(bf16[2,1024,256]{2,1,0:T(8,128)(2,1)} %copy-done.17) | copy-start | bytes 3145732
  236.6 10.0 %copy-start.4 = (bf16[3,256,256]{2,1,0:T(8,128)(2,1)S(1)}, bf16[3,256,256]{2,1,0:T(8,128)(2,1)}, u32[]{:S(2)}) copy-start(bf16[3,256,256]{2,1,0:T(8,128)(2,1)} %copy-done.3) | copy-start | bytes 1179652
  243.1 118.5 %collective-permute-start.26 = (bf16[2,2,1024,256]{3,2,1,0:T(8,128)(2,1)}, bf16[2,2,1024,256]{3,2,1,0:T(8,128)(2,1)}, u32[]{:S(2)}, u32[]{:S(2)}) collective-permute-start(bf16[2,2,1024,256]{3,2,1,0:T(8,128)(2,1)} %pad_maximum_fusion.1.refs_0_), channel_id=1, source_target_pairs={{0,1},{1,0},{2,3},{3,2},{4,5},{5,4},{6,7},{7,6},{8,9},{9,8},{10,11... | collective-permute-start | bytes 6291464 | tf_op jit(solution)/shard_map/ppermute | solution.py:36
  244.9 116.8 %collective-permute-start.27 = (bf16[2,2,1024,256]{3,2,1,0:T(8,128)(2,1)}, bf16[2,2,1024,256]{3,2,1,0:T(8,128)(2,1)}, u32[]{:S(2)}, u32[]{:S(2)}) collective-permute-start(bf16[2,2,1024,256]{3,2,1,0:T(8,128)(2,1)} %pad_maximum_fusion.1.refs_0_), channel_id=1, source_target_pairs={{0,2},{1,3},{2,0},{3,1},{4,6},{5,7},{6,4},{7,5},{8,10},{9,11},{10,... | collective-permute-start | bytes 6291464 | tf_op jit(solution)/shard_map/ppermute | solution.py:36
  245.4 116.3 %collective-permute-start.28 = (bf16[2,2,1024,256]{3,2,1,0:T(8,128)(2,1)}, bf16[2,2,1024,256]{3,2,1,0:T(8,128)(2,1)}, u32[]{:S(2)}, u32[]{:S(2)}) collective-permute-start(bf16[2,2,1024,256]{3,2,1,0:T(8,128)(2,1)} %pad_maximum_fusion.1.refs_0_), channel_id=1, source_target_pairs={{0,3},{1,2},{2,1},{3,0},{4,7},{5,6},{6,5},{7,4},{8,11},{9,10},{10,... | collective-permute-start | bytes 6291464 | tf_op jit(solution)/shard_map/ppermute | solution.py:36
  246.7 1.4 copy-start.2
  250.1 31.4 %copy-start.11 = (s32[2]{0:T(128)S(1)}, s32[2]{0:T(128)}, u32[]{:S(2)}) copy-start(s32[2]{0:T(128)} %extent_ref.1) | copy-start | bytes 28
  250.1 31.4 %copy-start.12 = (bf16[520,128]{1,0:T(8,128)(2,1)S(1)}, bf16[520,128]{1,0:T(8,128)(2,1)}, u32[]{:S(2)}) copy-start(bf16[520,128]{1,0:T(8,128)(2,1)} %constant.53.clone.sums_ref) | copy-start | bytes 399364
  250.1 31.4 %copy-start.13 = (bf16[256,256]{1,0:T(8,128)(2,1)S(1)}, bf16[256,256]{1,0:T(8,128)(2,1)}, u32[]{:S(2)}) copy-start(bf16[256,256]{1,0:T(8,128)(2,1)} %constant.55.clone.same_ref) | copy-start | bytes 393220
  250.1 31.4 %copy-start.14 = (f32[64,256]{1,0:T(8,128)S(1)}, f32[64,256]{1,0:T(8,128)}, u32[]{:S(2)}) copy-start(f32[64,256]{1,0:T(8,128)} %constant.54.clone.level_ref) | copy-start | bytes 196612
  318.2 23.8 %collective-permute-start.21 = (bf16[640,256]{1,0:T(8,128)(2,1)S(1)}, bf16[640,256]{1,0:T(8,128)(2,1)S(1)}, u32[]{:S(2)}, u32[]{:S(2)}) collective-permute-start(bf16[640,256]{1,0:T(8,128)(2,1)S(1)} %get-tuple-element.65), channel_id=1, source_target_pairs={{0,1},{1,0},{2,3},{3,2},{4,5},{5,4},{6,7},{7,6},{8,9},{9,8},{10,11... | collective-permute-start | bytes 983048 | tf_op jit(solution)/shard_map/ppermute | solution.py:36
  320.0 23.7 %collective-permute-start.22 = (bf16[640,256]{1,0:T(8,128)(2,1)S(1)}, bf16[640,256]{1,0:T(8,128)(2,1)S(1)}, u32[]{:S(2)}, u32[]{:S(2)}) collective-permute-start(bf16[640,256]{1,0:T(8,128)(2,1)S(1)} %get-tuple-element.66), channel_id=1, source_target_pairs={{0,2},{1,3},{2,0},{3,1},{4,6},{5,7},{6,4},{7,5},{8,10},{9,11},{10,... | collective-permute-start | bytes 983048 | tf_op jit(solution)/shard_map/ppermute | solution.py:36
  342.0 8.7 %collective-permute-start.23 = (bf16[640,256]{1,0:T(8,128)(2,1)S(1)}, bf16[640,256]{1,0:T(8,128)(2,1)S(1)}, u32[]{:S(2)}, u32[]{:S(2)}) collective-permute-start(bf16[640,256]{1,0:T(8,128)(2,1)S(1)} %get-tuple-element.67), channel_id=1, source_target_pairs={{0,3},{1,2},{2,1},{3,0},{4,7},{5,6},{6,5},{7,4},{8,11},{9,10},{10,... | collective-permute-start | bytes 983048 | tf_op jit(solution)/shard_map/ppermute | solution.py:36
  351.0 10.8 %collective-permute-start.24 = (bf16[4,512,256]{2,1,0:T(8,128)(2,1)S(1)}, bf16[4,512,256]{2,1,0:T(8,128)(2,1)S(1)}, u32[]{:S(2)}, u32[]{:S(2)}) collective-permute-start(bf16[4,512,256]{2,1,0:T(8,128)(2,1)S(1)} %slice.22.own_ref), channel_id=1, source_target_pairs={{0,16},{16,0},{1,17},{17,1},{2,18},{18,2},{3,19},{19,3},{4,20},{20... | collective-permute-start | bytes 3145736 | tf_op jit(solution)/shard_map/ppermute | solution.py:36
  361.7 8.9 %copy-start.1 = (bf16[4096,128]{1,0:T(8,128)(2,1)S(1)}, bf16[4096,128]{1,0:T(8,128)(2,1)}, u32[]{:S(2)}) copy-start(bf16[4096,128]{1,0:T(8,128)(2,1)} %param.21) | copy-start | bytes 3145732
  (3 other events, 2.7 us)
Sparse Core Ops, SparseCore 0:
  41.2 46.6 all-gather.6
  119.5 49.0 all-gather.4

commit v2 on v1

--- a/solution.py
+++ b/solution.py
@@ -13,6 +13,8 @@
 LEVELS = 6
 PREFIX = 8
 PAST = 16
+
+SMALL = pl.CostEstimate(flops=1024, bytes_accessed=1024, transcendentals=0)
 
 eps = 1e-05
 bf16 = jnp.bfloat16
@@ -88,9 +90,7 @@
         ],
         scratch_shapes=[pltpu.VMEM((rows + 2 * PREFIX, width), bf16)],
         compiler_params=vmem(40),
-        cost_estimate=pl.CostEstimate(
-            flops=2 * rows * width * width, bytes_accessed=4 * rows * width, transcendentals=0
-        ),
+        cost_estimate=SMALL,
     )(x, gain, coeffs, perm)
 
 
@@ -102,12 +102,11 @@
     inner = jnp.zeros(inner_ref.shape, f32)
     for c in range(block // width):
         cols = slice(c * width, (c + 1) * width)
-        act = act_ref[:, cols].astype(f32)
-        cur = act[PAST:]
-        delta = pltpu.roll(act, 1, 0)[PAST:] - cur
+        cur = act_ref[PAST:, cols]
+        delta = pltpu.roll(act_ref[:, cols].astype(f32), 1, 0)[PAST:].astype(bf16) - cur
         for j in range(3):
-            mixed_ref[j, 0, 0, :, cols] = (cur + delta * coeff_ref[j : j + 1, cols]).astype(bf16)
-        inner += dot((cur + delta * coeff_ref[3:4, cols]).astype(bf16), left_ref[cols, :])
+            mixed_ref[j, 0, 0, :, cols] = cur + delta * coeff_ref[j : j + 1, cols].astype(bf16)
+        inner += dot(cur + delta * coeff_ref[3:4, cols].astype(bf16), left_ref[cols, :])
 
     @pl.when(n == 0)
     def _():
@@ -150,9 +149,7 @@
         ],
         input_output_aliases={4: 0, 5: 1} if earlier else {},
         compiler_params=vmem(32),
-        cost_estimate=pl.CostEstimate(
-            flops=24 * act.size, bytes_accessed=8 * act.size, transcendentals=0
-        ),
+        cost_estimate=SMALL,
     )(where, act, coeffs, left, *earlier)
 
 
@@ -171,7 +168,8 @@
             at = (lax.rem(where_ref[2] + k, reqs) * stretches + (where_ref[0] ^ d)) * depth
             lines_ref[pl.ds(pl.multiple_of(at, depth), depth), :] = piece_ref[0]
 
-    out_ref[0, 0, 0] = dot(act_ref[0, 0, 0], lines_ref[...]).astype(bf16)
+    act = act_ref[0, 0].reshape(-1, act_ref.shape[-1])
+    out_ref[0, 0] = dot(act, lines_ref[...]).astype(bf16).reshape(out_ref.shape[2:])
 
 
 def projected(where, mixed, gathered, pieces):
@@ -186,22 +184,18 @@
         project_kernel,
         grid_spec=pltpu.PrefetchScalarGridSpec(
             num_scalar_prefetch=1,
-            grid=(kinds, sides * stretches),
+            grid=(kinds, sides),
             in_specs=[
-                pl.BlockSpec((1, 1, 1, span, width), lambda j, m, w: (j, m // stretches, m % stretches, 0, 0)),
+                pl.BlockSpec((1, 1, stretches, span, width), lambda j, m, w: (j, m, 0, 0, 0)),
                 pl.BlockSpec((reqs, 1, depth, cols), lambda j, m, w: (0, j, 0, 0)),
             ]
             + [pl.BlockSpec((1, depth, cols), lambda j, m, w: (j, 0, 0))] * len(pieces),
-            out_specs=pl.BlockSpec((1, 1, 1, span, cols), lambda j, m, w: (j, m // stretches, m % stretches, 0, 0)),
+            out_specs=pl.BlockSpec((1, 1, stretches, span, cols), lambda j, m, w: (j, m, 0, 0, 0)),
             scratch_shapes=[pltpu.VMEM((width, cols), bf16)],
         ),
         out_shape=jax.ShapeDtypeStruct((kinds, sides, stretches, span, cols), bf16),
         compiler_params=vmem(40),
-        cost_estimate=pl.CostEstimate(
-            flops=2 * mixed.size * cols,
-            bytes_accessed=2 * (mixed.size + kinds * width * cols),
-            transcendentals=0,
-        ),
+        cost_estimate=SMALL,
     )(where, mixed, gathered, *pieces)
 
 
@@ -328,9 +322,7 @@
             jax.ShapeDtypeStruct((stretches, reqs, ATTEND_DIM, cols), f32),
         ],
         compiler_params=vmem(40),
-        cost_estimate=pl.CostEstimate(
-            flops=proj.size * 3000, bytes_accessed=4 * proj.size, transcendentals=0
-        ),
+        cost_estimate=SMALL,
     )(extents, where, proj, lora, *tables)
 
 
@@ -374,19 +366,8 @@
         ),
         out_shape=jax.ShapeDtypeStruct((rows, share), bf16),
         compiler_params=vmem(48),
-        cost_estimate=pl.CostEstimate(
-            flops=4 * rows * depth * share, bytes_accessed=4 * depth * share, transcendentals=0
-        ),
+        cost_estimate=SMALL,
     )(where, x, own, far, *weights)
-
-
-def over_plane(value, cut):
-    peers = lax.axis_size("seq")
-    if peers != 4 or not cut:
-        return [value] + [swapped(value, "seq", d) for d in range(1, peers)]
-    near, other = swapped(value, "seq", 1), swapped(value, "seq", 2)
-    across = [swapped(near[:cut], "seq", 2), swapped(other[cut:], "seq", 1)]
-    return [value, near, other, jnp.concatenate(across, axis=0)]
 
 
 def ahead(value, axis, by):
@@ -413,7 +394,7 @@
     stretches = lax.axis_size("seq")
     cores = lax.axis_size("tensor")
     groups = lax.axis_size("req")
-    assert reqs == cores == 2
+    assert reqs == cores == 2 and stretches == 4
     local_width = feature_fading_speed.shape[0]
     cols = local_width // stretches
     t, s = lax.axis_index("tensor"), lax.axis_index("seq")
@@ -431,7 +412,10 @@
     gathered = lax.all_gather(pieces[0], "req", axis=0, tiled=False)
     got = [swapped(pieces[d], "seq", d) for d in range(1, stretches)]
 
-    own_x, past, *_ = lax.optimization_barrier((own_x, past, *pieces))
+    def tied(*values):
+        return lax.optimization_barrier(values)
+
+    own_x, past, *_ = tied(own_x, past, out_half, *pieces)
     coeffs = jnp.pad(lagged_blending_weights, ((0, PREFIX - 4), (0, 0)))
     act, coeffs = ordered(
         jnp.concatenate([past, own_x], axis=0),
@@ -439,28 +423,49 @@
         coeffs,
         learner_line_permutation.reshape(1, width),
     )
-    act, perm, *got = lax.optimization_barrier((act, learner_line_permutation, *got))
-    if pieces[0].shape[1] % 128:
-        weights = [lax.all_gather(piece, "req", axis=0, tiled=False) for piece in got]
-    else:
-        weights = [ahead(piece, "req", k) if k else piece for piece in got for k in range(groups)]
+    act, perm, *got = tied(act, learner_line_permutation, *got)
+    direct = pieces[0].shape[1] % 128 == 0
+
+    def along_z(piece):
+        if not direct:
+            return [lax.all_gather(piece, "req", axis=0, tiled=False)]
+        return [ahead(piece, "req", k) if k else piece for k in range(groups)]
+
+    def mixed_in(values, side, apart, earlier):
+        return shifted(where, values, coeffs, left, side, apart, stretches, earlier)
+
     left = fading_left_matrix[perm]
-
-    acts = over_plane(act, (span + PAST) // 32 * 16)
-    results = ()
-    for d, block in enumerate(acts):
-        for side, values in enumerate((block, swapped(block, "tensor", 1))):
-            results = shifted(where, values, coeffs, left, side, d, stretches, results)
-    mixed, lora = results
-
+    cut = (span + PAST) // 32 * 16
+    near, other = swapped(act, "seq", 1), swapped(act, "seq", 2)
+    lines = along_z(got[0])
+    results = mixed_in(act, 0, 0, ())
+    results = mixed_in(swapped(act, "tensor", 1), 1, 0, results)
+    near, other, *rest = tied(near, other, *results, *lines, *got[1:])
+    results, lines, got = tuple(rest[:2]), rest[2:-2], rest[-2:]
+
+    across = [swapped(near[:cut], "seq", 2), swapped(other[cut:], "seq", 1)]
+    more = along_z(got[0])
+    results = mixed_in(near, 0, 1, results)
+    results = mixed_in(other, 0, 2, results)
+    far = swapped(jnp.stack([near, other]), "tensor", 1)
     share = groups // cores
     kept = lax.dynamic_slice_in_dim(out_lines, t * share, share, 0)
     given = lax.dynamic_slice_in_dim(out_lines, (1 - t) * share, share, 0)
     out_lines = jnp.stack([kept, swapped(given, "tensor", 1)])
-    out_lines, _ = lax.optimization_barrier((out_lines, acts[-1]))
-    out_weights = over_plane(out_lines, 0)
-
-    proj = projected(where, mixed, gathered, weights)
+    across = jnp.concatenate(across, axis=0)
+    across, out_lines, far, *rest = tied(across, out_lines, far, *results, *more, got[1])
+    results, got = tuple(rest[:2]), rest[-1]
+    lines += rest[2:-1]
+
+    lines += along_z(got)
+    out_weights = [out_lines] + [swapped(out_lines, "seq", d) for d in range(1, stretches)]
+    last = swapped(across, "tensor", 1)
+    results = mixed_in(across, 0, 3, results)
+    results = mixed_in(far[0], 1, 1, results)
+    results = mixed_in(far[1], 1, 2, results)
+    mixed, lora = mixed_in(last, 1, 3, results)
+
+    proj = projected(where, mixed, gathered, lines)
 
     def mine(array):
         return lax.dynamic_slice_in_dim(array, s * cols, cols, array.ndim - 1).reshape(-1, cols)

time: 379 us -> 350 us (0.923)
  waiting for transfers between devices: 128 us -> 108 us
  Pallas kernels: 143 us -> 127 us
  other arithmetic: 4.52 us -> 12.5 us
  local copies, waits for them, and re-layouts: 45.2 us -> 51.2 us
  starting transfers between devices: 42.2 us -> 36.5 us
    ppermute x19 -> x18, waiting for transfers between devices: 95.8 us -> 26 us  [swapped(): return lax.ppermute(value, axis, [(i, i ^ by) for i in range(peers)])]
    ppermute x9, waiting for transfers between devices: 32.2 us -> 65.6 us  [ahead(): lax.ppermute(value, axis, [((i + by) % peers, i) for i in range(peers)])]
    all_gather x1, waiting for transfers between devices: 0.01 us -> 16.1 us  [local(): gathered = lax.all_gather(pieces[0], 'req', axis=0, tiled=False)]
    pallas_call x1, Pallas kernels: 31.4 us -> 21.2 us  [projected(): pl.pallas_call(project_kernel, grid_spec=pltpu.PrefetchScalarGridSpec(num...]
    pallas_call x8, Pallas kernels: 52.4 us -> 46.3 us  [shifted(): pl.pallas_call(mix_kernel, grid_spec=pltpu.PrefetchScalarGridSpec(num_sca...]
    another operation x0 -> x1, other arithmetic: none -> 4.77 us  [local(): far = swapped(jnp.stack([near, other]), 'tensor', 1)]
    unnamed x41 -> x44, local copies, waits for them, and re-layouts: 5.28 us -> 8.58 us
    ppermute x19 -> x18, starting transfers between devices: 15.2 us -> 13.2 us  [swapped(): return lax.ppermute(value, axis, [(i, i ^ by) for i in range(peers)])]
  transfers between devices with their start and end apart: 31 -> 30, of which waited for: 8 -> 7; matrix products, arithmetic and copies ran while one was open for 12% -> 16% of each run, Pallas kernels for 36% -> 34%
where the time goes in v2:
time: 350 us; the launch traced here: 349 us
  Pallas kernels  127 us (36%)
  waiting for transfers between devices  108 us (31%)
  local copies, waits for them, and re-layouts  51.2 us (15%)
  starting transfers between devices  36.5 us (10%)
  between operations  14.4 us (4%)
  other arithmetic  12.5 us (4%)
    ppermute x9, waiting for transfers between devices, ahead(): lax.ppermute(value, axis, [((i + by) % peers, i) for i in range(peers)])  65.6 us
    pallas_call x8, Pallas kernels, shifted(): pl.pallas_call(mix_kernel, grid_spec=pltpu.PrefetchScalarGridSpec(num_sca...  46.3 us
    pallas_call x1, Pallas kernels, recurrence(): pl.pallas_call(wkv_kernel, grid_spec=pltpu.PrefetchScalarGridSpec(num_sca...  36.4 us
    ppermute x18, waiting for transfers between devices, swapped(): return lax.ppermute(value, axis, [(i, i ^ by) for i in range(peers)])  26 us
    pallas_call x1, Pallas kernels, projected(): pl.pallas_call(project_kernel, grid_spec=pltpu.PrefetchScalarGridSpec(num...  21.2 us
    ppermute x9, starting transfers between devices, ahead(): lax.ppermute(value, axis, [((i + by) % peers, i) for i in range(peers)])  18.4 us
    all_gather x1, waiting for transfers between devices, local(): gathered = lax.all_gather(pieces[0], 'req', axis=0, tiled=False)  16.1 us
    pallas_call x1, Pallas kernels, ordered(): pl.pallas_call(order_kernel, grid=(width // block,), in_specs=[pl.BlockSp...  13.9 us
  transfers between devices with their start and end apart: 30, of which 7 were waited for; matrix products, arithmetic and copies ran while one was open for 16% of the time, Pallas kernels for 34%

profile of v2, /device:TPU:0, one launch (start us, length us, event | category | flops | bytes accessed | tf_op | source)
XLA Modules:
  0.0 349.1 jit_solution(14444746832228459805)
XLA Ops:
  8.2 4.8 %collective-permute-start = (bf16[16,4096]{1,0:T(8,128)(2,1)S(1)}, bf16[16,4096]{1,0:T(8,128)(2,1)S(1)}, u32[]{:S(2)}, u32[]{:S(2)}) collective-permute-start(bf16[16,4096]{1,0:T(8,128)(2,1)S(1)} %constant_dynamic-slice_fusion), channel_id=1, source_target_pairs={{0,1},{1,2},{2,3},{4,5},{5,6},{6,7},{8,9},{9,10},{10,11},{12,13},{... | collective-permute-start | bytes 393224 | tf_op jit(solution)/shard_map/ppermute | solution.py:405
  13.1 3.0 dynamic-slice_convert_fusion
  16.1 1.5 collective-permute-start.1
  17.6 1.9 collective-permute-start.3
  19.6 3.1 constant_dynamic-slice_fusion.3
  23.6 1.8 pad_maximum_fusion.1.x_ref
  25.5 13.9 %shard_map.158 = (bf16[272,4096]{1,0:T(8,128)(2,1)}, f32[8,4096]{1,0:T(8,128)S(1)}) custom-call(bf16[272,4096]{1,0:T(8,128)(2,1)S(1)} %pad_maximum_fusion.1.x_ref, f32[1,4096]{1,0:T(1,128)S(1)} %bitcast.42, f32[8,4096]{1,0:T(8,128)S(1)} %pad.5.coeff_ref, s32[1,4096]{1,0:T(1,128)S(1)} %bitcast.41), custom_call_target="tpu_custom_call" | custom-call | flops 1024 | bytes 1024 | tf_op jit(solution)/shard_map/pallas_call | solution.py:74
  39.5 1.6 collective-permute-start.4
  41.1 3.6 %collective-permute-start.7 = (bf16[3,256,256]{2,1,0:T(8,128)(2,1)S(1)}, bf16[3,256,256]{2,1,0:T(8,128)(2,1)}, u32[]{:S(2)}, u32[]{:S(2)}) collective-permute-start(bf16[3,256,256]{2,1,0:T(8,128)(2,1)S(1)} %collective-permute-done.1.refs_0_), channel_id=1, source_target_pairs={{4,0},{8,4},{12,8},{0,12},{5,1},{9,5},{13,9},{1,13},{6,2},{10,6},{... | collective-permute-start | bytes 1179656 | tf_op jit(solution)/shard_map/ppermute | solution.py:375
  44.8 1.4 copy-done.5
  47.3 12.1 %gather_fusion = bf16[4096,128]{1,0:T(8,128)(2,1)S(1)} fusion(bf16[4096,128]{1,0:T(8,128)(2,1)S(1)} %copy-done, s32[4096]{0:T(1024)S(1)} %fusion.7), kind=kCustom, calls=%fused_computation | custom fusion | bytes 2113536 | tf_op jit(solution)/shard_map/gather | solution.py:437
  59.5 6.4 %shard_map.159 = (bf16[3,2,4,256,4096]{4,3,2,1,0:T(8,128)(2,1)}, bf16[2,4,256,128]{3,2,1,0:T(8,128)(2,1)S(1)}) custom-call(s32[3]{0:T(128)S(1)} %pad_add_fusion.where_ref, bf16[272,4096]{1,0:T(8,128)(2,1)} %get-tuple-element.52.act_ref, f32[8,4096]{1,0:T(8,128)S(1)} %get-tuple-element.53.coeff_ref, bf16[4096,128]{1,0:T(8,128)(2,1)S(1)} %gather_fusion), custom_call_target="tpu_custom_call" | custom-call | flops 1024 | bytes 1024 | tf_op jit(solution)/shard_map/pallas_call | solution.py:129
  65.9 4.9 %shard_map.160 = (bf16[3,2,4,256,4096]{4,3,2,1,0:T(8,128)(2,1)}, bf16[2,4,256,128]{3,2,1,0:T(8,128)(2,1)S(1)}) custom-call(s32[3]{0:T(128)S(1)} %pad_add_fusion.where_ref, bf16[272,4096]{1,0:T(8,128)(2,1)S(1)} %copy-done.6, f32[8,4096]{1,0:T(8,128)S(1)} %get-tuple-element.53.coeff_ref, ...), custom_call_target="tpu_custom_call", output_to_operand_aliasing={{0}: (4, {}), {1}: (5, {})} | custom-call | flops 1024 | bytes 1024 | tf_op jit(solution)/shard_map/pallas_call | solution.py:129
  70.8 31.5 %collective-permute-done.8.refs_2_ = bf16[3,256,256]{2,1,0:T(8,128)(2,1)} collective-permute-done((bf16[3,256,256]{2,1,0:T(8,128)(2,1)S(1)}, bf16[3,256,256]{2,1,0:T(8,128)(2,1)}, u32[]{:S(2)}, u32[]{:S(2)}) %collective-permute-start.8) | collective-permute-done | bytes 393248 | tf_op jit(solution)/shard_map/ppermute | solution.py:375
  102.3 4.8 %pad_maximum_fusion = bf16[2,272,4096]{2,1,0:T(8,128)(2,1)} fusion(bf16[1,272,4096]{2,1,0:T(8,128)(2,1)} %bitcast.10, bf16[1,272,4096]{2,1,0:T(8,128)(2,1)} %bitcast.9), kind=kLoop, calls=%fused_computation.2 | loop fusion | flops 2228224 | bytes 8912896 | tf_op jit(solution)/shard_map/stack | solution.py:450
  107.1 2.4 slice.20
  109.5 3.4 collective-permute-start.11
  112.9 2.3 slice.19
  115.7 1.7 dynamic-slice_bitcast_fusion
  118.1 6.3 %shard_map.161 = (bf16[3,2,4,256,4096]{4,3,2,1,0:T(8,128)(2,1)}, bf16[2,4,256,128]{3,2,1,0:T(8,128)(2,1)S(1)}) custom-call(s32[3]{0:T(128)S(1)} %pad_add_fusion.where_ref, bf16[272,4096]{1,0:T(8,128)(2,1)} %collective-permute-done.4.act_ref, f32[8,4096]{1,0:T(8,128)S(1)} %get-tuple-element.53.coeff_ref, ...), custom_call_target="tpu_custom_call", output_to_operand_aliasing={{0}: (4, {}), {1}: (5, {})} | custom-call | flops 1024 | bytes 1024 | tf_op jit(solution)/shard_map/pallas_call | solution.py:129
  124.4 6.3 %shard_map.162 = (bf16[3,2,4,256,4096]{4,3,2,1,0:T(8,128)(2,1)}, bf16[2,4,256,128]{3,2,1,0:T(8,128)(2,1)S(1)}) custom-call(s32[3]{0:T(128)S(1)} %pad_add_fusion.where_ref, bf16[272,4096]{1,0:T(8,128)(2,1)} %collective-permute-done.5.act_ref, f32[8,4096]{1,0:T(8,128)S(1)} %get-tuple-element.53.coeff_ref, ...), custom_call_target="tpu_custom_call", output_to_operand_aliasing={{0}: (4, {}), {1}: (5, {})} | custom-call | flops 1024 | bytes 1024 | tf_op jit(solution)/shard_map/pallas_call | solution.py:129
  130.7 10.1 %collective-permute-done.10 = bf16[128,4096]{1,0:T(8,128)(2,1)} collective-permute-done((bf16[128,4096]{1,0:T(8,128)(2,1)}, bf16[128,4096]{1,0:T(8,128)(2,1)}, u32[]{:S(2)}, u32[]{:S(2)}) %collective-permute-start.10) | collective-permute-done | bytes 1048608 | tf_op jit(solution)/shard_map/ppermute | solution.py:38
  140.8 11.1 %collective-permute-start.15 = (bf16[3,256,256]{2,1,0:T(8,128)(2,1)S(1)}, bf16[3,256,256]{2,1,0:T(8,128)(2,1)S(1)}, u32[]{:S(2)}, u32[]{:S(2)}) collective-permute-start(bf16[3,256,256]{2,1,0:T(8,128)(2,1)S(1)} %collective-permute-done.2.refs_4_), channel_id=1, source_target_pairs={{8,0},{12,4},{0,8},{4,12},{9,1},{13,5},{1,9},{5,13},{10,2},{14,6},... | collective-permute-start | bytes 1179656 | tf_op jit(solution)/shard_map/ppermute | solution.py:375
  152.0 3.2 pad_maximum_fusion.2.act_ref
  155.1 1.5 pad_maximum_fusion.3.refs_0_
  156.7 20.6 %collective-permute-done.15.refs_6_ = bf16[3,256,256]{2,1,0:T(8,128)(2,1)S(1)} collective-permute-done((bf16[3,256,256]{2,1,0:T(8,128)(2,1)S(1)}, bf16[3,256,256]{2,1,0:T(8,128)(2,1)S(1)}, u32[]{:S(2)}, u32[]{:S(2)}) %collective-permute-start.15) | collective-permute-done | bytes 393248 | tf_op jit(solution)/shard_map/ppermute | solution.py:375
  182.0 2.0 collective-permute-start.20
  184.3 13.5 %collective-permute-done.18.refs_9_ = bf16[3,256,256]{2,1,0:T(8,128)(2,1)} collective-permute-done((bf16[3,256,256]{2,1,0:T(8,128)(2,1)S(1)}, bf16[3,256,256]{2,1,0:T(8,128)(2,1)}, u32[]{:S(2)}, u32[]{:S(2)}) %collective-permute-start.18) | collective-permute-done | bytes 393248 | tf_op jit(solution)/shard_map/ppermute | solution.py:375
  197.8 2.8 slice_bitcast_fusion
  200.7 6.4 %shard_map.163 = (bf16[3,2,4,256,4096]{4,3,2,1,0:T(8,128)(2,1)}, bf16[2,4,256,128]{3,2,1,0:T(8,128)(2,1)S(1)}) custom-call(s32[3]{0:T(128)S(1)} %pad_add_fusion.where_ref, bf16[272,4096]{1,0:T(8,128)(2,1)} %pad_maximum_fusion.2.act_ref, f32[8,4096]{1,0:T(8,128)S(1)} %get-tuple-element.53.coeff_ref, ...), custom_call_target="tpu_custom_call", output_to_operand_aliasing={{0}: (4, {}), {1}: (5, {})} | custom-call | flops 1024 | bytes 1024 | tf_op jit(solution)/shard_map/pallas_call | solution.py:129
  207.1 4.8 %shard_map.164 = (bf16[3,2,4,256,4096]{4,3,2,1,0:T(8,128)(2,1)}, bf16[2,4,256,128]{3,2,1,0:T(8,128)(2,1)S(1)}) custom-call(s32[3]{0:T(128)S(1)} %pad_add_fusion.where_ref, bf16[272,4096]{1,0:T(8,128)(2,1)S(1)} %get-tuple-element.96.act_ref, f32[8,4096]{1,0:T(8,128)S(1)} %get-tuple-element.53.coeff_ref, ...), custom_call_target="tpu_custom_call", output_to_operand_aliasing={{0}: (4, {}), {1}: (5, {})} | custom-call | flops 1024 | bytes 1024 | tf_op jit(solution)/shard_map/pallas_call | solution.py:129
  211.9 4.8 %shard_map.165 = (bf16[3,2,4,256,4096]{4,3,2,1,0:T(8,128)(2,1)}, bf16[2,4,256,128]{3,2,1,0:T(8,128)(2,1)S(1)}) custom-call(s32[3]{0:T(128)S(1)} %pad_add_fusion.where_ref, bf16[272,4096]{1,0:T(8,128)(2,1)S(1)} %get-tuple-element.97.act_ref, f32[8,4096]{1,0:T(8,128)S(1)} %get-tuple-element.53.coeff_ref, ...), custom_call_target="tpu_custom_call", output_to_operand_aliasing={{0}: (4, {}), {1}: (5, {})} | custom-call | flops 1024 | bytes 1024 | tf_op jit(solution)/shard_map/pallas_call | solution.py:129
  216.7 6.3 %shard_map.166 = (bf16[3,2,4,256,4096]{4,3,2,1,0:T(8,128)(2,1)}, bf16[2,4,256,128]{3,2,1,0:T(8,128)(2,1)S(1)}) custom-call(s32[3]{0:T(128)S(1)} %pad_add_fusion.where_ref, bf16[272,4096]{1,0:T(8,128)(2,1)} %collective-permute-done.17.act_ref, f32[8,4096]{1,0:T(8,128)S(1)} %get-tuple-element.53.coeff_ref, ...), custom_call_target="tpu_custom_call", output_to_operand_aliasing={{0}: (4, {}), {1}: (5, {})} | custom-call | flops 1024 | bytes 1024 | tf_op jit(solution)/shard_map/pallas_call | solution.py:129
  223.0 16.1 %all-gather.7.cloned.1.call-done = bf16[12,256,256]{2,1,0:T(8,128)(2,1)} async-done(((bf16[3,256,256]{2,1,0:T(8,128)(2,1)}), bf16[12,256,256]{2,1,0:T(8,128)(2,1)}) %all-gather.7.cloned.1.call-update) | async-done | bytes 1572880 | tf_op jit(solution)/shard_map/all_gather | solution.py:412
  239.1 1.4 copy-done.7
  243.5 21.2 %shard_map.167.proj_ref = bf16[3,2,4,256,256]{4,3,2,1,0:T(8,128)(2,1)S(1)} custom-call(s32[3]{0:T(128)S(1)} %pad_add_fusion.where_ref, bf16[3,2,4,256,4096]{4,3,2,1,0:T(8,128)(2,1)} %get-tuple-element.82.act_ref, bf16[4,3,256,256]{3,2,1,0:T(8,128)(2,1)S(1)} %bitcast.39, bf16[3,256,256]{2,1,0:T(8,128)(2,1)S(1)} %collective-permute-done.1.refs_0_, ...), custom_call_target="tpu_custom_call" | custom-call | flops 1024 | bytes 1024 | tf_op jit(solution)/shard_map/pallas_call | solution.py:183
  264.7 36.4 %shard_map.168 = (bf16[4,2,256,256]{3,2,1,0:T(8,128)(2,1)S(1)}, f32[4,2,64,256]{3,2,1,0:T(8,128)S(1)}) custom-call(s32[2]{0:T(128)S(1)} %copy-done.19, s32[3]{0:T(128)S(1)} %pad_add_fusion.where_ref, bf16[3,2,4,256,256]{4,3,2,1,0:T(8,128)(2,1)S(1)} %shard_map.167.proj_ref, bf16[2,4,256,128]{3,2,1,0:T(8,128)(2,1)S(1)} %get-tuple-element.92.lora_ref, ...), custom_call_target="tpu_custom_call" | custom-call | flops 1024 | bytes 1024 | tf_op jit(solution)/shard_map/pallas_call | solution.py:304
  301.7 1.7 collective-permute-start.22
  303.3 7.6 %collective-permute-done.21 = bf16[640,256]{1,0:T(8,128)(2,1)S(1)} collective-permute-done((bf16[640,256]{1,0:T(8,128)(2,1)S(1)}, bf16[640,256]{1,0:T(8,128)(2,1)S(1)}, u32[]{:S(2)}, u32[]{:S(2)}) %collective-permute-start.21) | collective-permute-done | bytes 327712 | tf_op jit(solution)/shard_map/ppermute | solution.py:38
  311.0 1.5 collective-permute-start.23
  312.5 8.2 %collective-permute-done.23 = bf16[640,256]{1,0:T(8,128)(2,1)S(1)} collective-permute-done((bf16[640,256]{1,0:T(8,128)(2,1)S(1)}, bf16[640,256]{1,0:T(8,128)(2,1)S(1)}, u32[]{:S(2)}, u32[]{:S(2)}) %collective-permute-start.23) | collective-permute-done | bytes 327712 | tf_op jit(solution)/shard_map/ppermute | solution.py:38
  321.0 1.0 copy.33
  322.0 2.4 gather_fusion.1
  324.5 2.6 reshape.69
  327.1 2.6 copy.34
  329.7 2.4 reshape.66
  332.1 1.2 copy-done.4
  333.3 8.9 %shard_map.169 = bf16[512,2048]{1,0:T(8,128)(2,1)} custom-call(s32[3]{0:T(128)S(1)} %pad_add_fusion.where_ref, bf16[512,4096]{1,0:T(8,128)(2,1)} %bitcast.48, bf16[4,512,256]{2,1,0:T(8,128)(2,1)S(1)} %copy-done.4, bf16[4,512,256]{2,1,0:T(8,128)(2,1)} %collective-permute-done.24.far_ref, bf16[2,2,1024,256]{3,2,1,0:T(8,128)(2,1)S(1)} %copy-done.2, ...), custom_call_target="tpu_custom_call" | custom-call | flops 1024 | bytes 1024 | tf_op jit(solution)/shard_map/pallas_call | solution.py:358
  (100 shorter events, 13.5 us)
Async XLA Ops:
  7.2 40.1 %copy-start = (bf16[4096,128]{1,0:T(8,128)(2,1)S(1)}, bf16[4096,128]{1,0:T(8,128)(2,1)}, u32[]{:S(2)}) copy-start(bf16[4096,128]{1,0:T(8,128)(2,1)} %param.21) | copy-start | bytes 3145732
  7.2 108.6 %all-gather.5.cloned.1.call-start = ((), (), s32[]{:S(2)}) async-start(), calls=%async_computation | async-start | bytes 2621440 | tf_op jit(solution)/shard_map/all_gather | solution.py:411
  8.2 15.3 %collective-permute-start = (bf16[16,4096]{1,0:T(8,128)(2,1)S(1)}, bf16[16,4096]{1,0:T(8,128)(2,1)S(1)}, u32[]{:S(2)}, u32[]{:S(2)}) collective-permute-start(bf16[16,4096]{1,0:T(8,128)(2,1)S(1)} %constant_dynamic-slice_fusion), channel_id=1, source_target_pairs={{0,1},{1,2},{2,3},{4,5},{5,6},{6,7},{8,9},{9,10},{10,11},{12,13},{... | collective-permute-start | bytes 393224 | tf_op jit(solution)/shard_map/ppermute | solution.py:405
  16.1 6.6 %copy-start.20 = (f32[1024,256]{1,0:T(8,128)S(1)}, f32[1024,256]{1,0:T(8,128)}, u32[]{:S(2)}) copy-start(f32[1024,256]{1,0:T(8,128)} %param.20) | copy-start | bytes 3145732
  16.1 23.3 %collective-permute-start.1 = (bf16[3,256,256]{2,1,0:T(8,128)(2,1)}, bf16[3,256,256]{2,1,0:T(8,128)(2,1)S(1)}, u32[]{:S(2)}, u32[]{:S(2)}) collective-permute-start(bf16[3,256,256]{2,1,0:T(8,128)(2,1)} %get-tuple-element.99), channel_id=1, source_target_pairs={{0,1},{1,0},{2,3},{3,2},{4,5},{5,4},{6,7},{7,6},{8,9},{9,8},{10,11... | collective-permute-start | bytes 1179656 | tf_op jit(solution)/shard_map/ppermute | solution.py:38
  17.6 21.8 %collective-permute-start.2 = (bf16[3,256,256]{2,1,0:T(8,128)(2,1)S(1)}, bf16[3,256,256]{2,1,0:T(8,128)(2,1)S(1)}, u32[]{:S(2)}, u32[]{:S(2)}) collective-permute-start(bf16[3,256,256]{2,1,0:T(8,128)(2,1)S(1)} %get-tuple-element.101), channel_id=1, source_target_pairs={{0,2},{1,3},{2,0},{3,1},{4,6},{5,7},{6,4},{7,5},{8,10},{9,11},{10,... | collective-permute-start | bytes 1179656 | tf_op jit(solution)/shard_map/ppermute | solution.py:38
  17.6 5.9 %copy-start.21 = (f32[4,4096]{1,0:T(4,128)S(1)}, f32[4,4096]{1,0:T(4,128)}, u32[]{:S(2)}) copy-start(f32[4,4096]{1,0:T(4,128)} %param.17) | copy-start | bytes 196612
  17.6 21.8 %collective-permute-start.3 = (bf16[3,256,256]{2,1,0:T(8,128)(2,1)S(1)}, bf16[3,256,256]{2,1,0:T(8,128)(2,1)S(1)}, u32[]{:S(2)}, u32[]{:S(2)}) collective-permute-start(bf16[3,256,256]{2,1,0:T(8,128)(2,1)S(1)} %get-tuple-element.98), channel_id=1, source_target_pairs={{0,3},{1,2},{2,1},{3,0},{4,7},{5,6},{6,5},{7,4},{8,11},{9,10},{10,... | collective-permute-start | bytes 1179656 | tf_op jit(solution)/shard_map/ppermute | solution.py:38
  23.6 1.9 copy-start.17
  23.6 1.9 copy-start.18
  39.4 5.3 %collective-permute-start.6 = (bf16[272,4096]{1,0:T(8,128)(2,1)}, bf16[272,4096]{1,0:T(8,128)(2,1)S(1)}, u32[]{:S(2)}, u32[]{:S(2)}) collective-permute-start(bf16[272,4096]{1,0:T(8,128)(2,1)} %get-tuple-element.52.act_ref), channel_id=1, source_target_pairs={{0,16},{16,0},{1,17},{17,1},{2,18},{18,2},{3,19},{19,3},{4,20},{20... | collective-permute-start | bytes 6684680 | tf_op jit(solution)/shard_map/ppermute | solution.py:38
  39.5 62.9 %collective-permute-start.4 = (bf16[272,4096]{1,0:T(8,128)(2,1)}, bf16[272,4096]{1,0:T(8,128)(2,1)}, u32[]{:S(2)}, u32[]{:S(2)}) collective-permute-start(bf16[272,4096]{1,0:T(8,128)(2,1)} %get-tuple-element.52.act_ref), channel_id=1, source_target_pairs={{0,1},{1,0},{2,3},{3,2},{4,5},{5,4},{6,7},{7,6},{8,9},{9,8},{10,11... | collective-permute-start | bytes 6684680 | tf_op jit(solution)/shard_map/ppermute | solution.py:38
  41.0 61.3 %collective-permute-start.5 = (bf16[272,4096]{1,0:T(8,128)(2,1)}, bf16[272,4096]{1,0:T(8,128)(2,1)}, u32[]{:S(2)}, u32[]{:S(2)}) collective-permute-start(bf16[272,4096]{1,0:T(8,128)(2,1)} %get-tuple-element.52.act_ref), channel_id=1, source_target_pairs={{0,2},{1,3},{2,0},{3,1},{4,6},{5,7},{6,4},{7,5},{8,10},{9,11},{10,... | collective-permute-start | bytes 6684680 | tf_op jit(solution)/shard_map/ppermute | solution.py:38
  41.1 29.7 %collective-permute-start.7 = (bf16[3,256,256]{2,1,0:T(8,128)(2,1)S(1)}, bf16[3,256,256]{2,1,0:T(8,128)(2,1)}, u32[]{:S(2)}, u32[]{:S(2)}) collective-permute-start(bf16[3,256,256]{2,1,0:T(8,128)(2,1)S(1)} %collective-permute-done.1.refs_0_), channel_id=1, source_target_pairs={{4,0},{8,4},{12,8},{0,12},{5,1},{9,5},{13,9},{1,13},{6,2},{10,6},{... | collective-permute-start | bytes 1179656 | tf_op jit(solution)/shard_map/ppermute | solution.py:375
  44.7 57.6 %collective-permute-start.8 = (bf16[3,256,256]{2,1,0:T(8,128)(2,1)S(1)}, bf16[3,256,256]{2,1,0:T(8,128)(2,1)}, u32[]{:S(2)}, u32[]{:S(2)}) collective-permute-start(bf16[3,256,256]{2,1,0:T(8,128)(2,1)S(1)} %collective-permute-done.1.refs_0_), channel_id=1, source_target_pairs={{8,0},{12,4},{0,8},{4,12},{9,1},{13,5},{1,9},{5,13},{10,2},{14,6},... | collective-permute-start | bytes 1179656 | tf_op jit(solution)/shard_map/ppermute | solution.py:375
  44.8 1.4 copy-start.5
  46.1 56.2 %collective-permute-start.9 = (bf16[3,256,256]{2,1,0:T(8,128)(2,1)S(1)}, bf16[3,256,256]{2,1,0:T(8,128)(2,1)}, u32[]{:S(2)}, u32[]{:S(2)}) collective-permute-start(bf16[3,256,256]{2,1,0:T(8,128)(2,1)S(1)} %collective-permute-done.1.refs_0_), channel_id=1, source_target_pairs={{12,0},{0,4},{4,8},{8,12},{13,1},{1,5},{5,9},{9,13},{14,2},{2,6},{... | collective-permute-start | bytes 1179656 | tf_op jit(solution)/shard_map/ppermute | solution.py:375
  47.2 191.9 %all-gather.7.cloned.1.call-start = ((), (), s32[]{:S(2)}) async-start(), calls=%async_computation.1 | async-start | bytes 1966080 | tf_op jit(solution)/shard_map/all_gather | solution.py:412
  59.5 6.5 %copy-start.6 = (bf16[272,4096]{1,0:T(8,128)(2,1)S(1)}, bf16[272,4096]{1,0:T(8,128)(2,1)}, u32[]{:S(2)}) copy-start(bf16[272,4096]{1,0:T(8,128)(2,1)} %copy-done.5) | copy-start | bytes 6684676
  107.1 71.7 %collective-permute-start.13 = (bf16[2,272,4096]{2,1,0:T(8,128)(2,1)}, bf16[2,272,4096]{2,1,0:T(8,128)(2,1)}, u32[]{:S(2)}, u32[]{:S(2)}) collective-permute-start(bf16[2,272,4096]{2,1,0:T(8,128)(2,1)} %pad_maximum_fusion), channel_id=1, source_target_pairs={{0,16},{16,0},{1,17},{17,1},{2,18},{18,2},{3,19},{19,3},{4,20},{20... | collective-permute-start | bytes 13369352 | tf_op jit(solution)/shard_map/ppermute | solution.py:38
  109.5 42.5 %collective-permute-start.11 = (bf16[144,4096]{1,0:T(8,128)(2,1)}, bf16[144,4096]{1,0:T(8,128)(2,1)}, u32[]{:S(2)}, u32[]{:S(2)}) collective-permute-start(bf16[144,4096]{1,0:T(8,128)(2,1)} %slice.20), channel_id=1, source_target_pairs={{0,1},{1,0},{2,3},{3,2},{4,5},{5,4},{6,7},{7,6},{8,9},{9,8},{10,11... | collective-permute-start | bytes 3538952 | tf_op jit(solution)/shard_map/ppermute | solution.py:38
  115.2 25.6 %collective-permute-start.10 = (bf16[128,4096]{1,0:T(8,128)(2,1)}, bf16[128,4096]{1,0:T(8,128)(2,1)}, u32[]{:S(2)}, u32[]{:S(2)}) collective-permute-start(bf16[128,4096]{1,0:T(8,128)(2,1)} %slice.19), channel_id=1, source_target_pairs={{0,2},{1,3},{2,0},{3,1},{4,6},{5,7},{6,4},{7,5},{8,10},{9,11},{10,... | collective-permute-start | bytes 3145736 | tf_op jit(solution)/shard_map/ppermute | solution.py:38
  117.4 37.7 %collective-permute-start.12 = (bf16[2,1024,256]{2,1,0:T(8,128)(2,1)S(1)}, bf16[2,1024,256]{2,1,0:T(8,128)(2,1)S(1)}, u32[]{:S(2)}, u32[]{:S(2)}) collective-permute-start(bf16[2,1024,256]{2,1,0:T(8,128)(2,1)S(1)} %get-tuple-element.103), channel_id=1, source_target_pairs={{0,16},{16,0},{1,17},{17,1},{2,18},{18,2},{3,19},{19,3},{4,20},{20... | collective-permute-start | bytes 3145736 | tf_op jit(solution)/shard_map/ppermute | solution.py:38
  117.5 39.2 %collective-permute-start.14 = (bf16[3,256,256]{2,1,0:T(8,128)(2,1)S(1)}, bf16[3,256,256]{2,1,0:T(8,128)(2,1)S(1)}, u32[]{:S(2)}, u32[]{:S(2)}) collective-permute-start(bf16[3,256,256]{2,1,0:T(8,128)(2,1)S(1)} %collective-permute-done.2.refs_4_), channel_id=1, source_target_pairs={{4,0},{8,4},{12,8},{0,12},{5,1},{9,5},{13,9},{1,13},{6,2},{10,6},{... | collective-permute-start | bytes 1179656 | tf_op jit(solution)/shard_map/ppermute | solution.py:375
  140.8 36.4 %collective-permute-start.15 = (bf16[3,256,256]{2,1,0:T(8,128)(2,1)S(1)}, bf16[3,256,256]{2,1,0:T(8,128)(2,1)S(1)}, u32[]{:S(2)}, u32[]{:S(2)}) collective-permute-start(bf16[3,256,256]{2,1,0:T(8,128)(2,1)S(1)} %collective-permute-done.2.refs_4_), channel_id=1, source_target_pairs={{8,0},{12,4},{0,8},{4,12},{9,1},{13,5},{1,9},{5,13},{10,2},{14,6},... | collective-permute-start | bytes 1179656 | tf_op jit(solution)/shard_map/ppermute | solution.py:375
  152.0 26.0 %collective-permute-start.16 = (bf16[3,256,256]{2,1,0:T(8,128)(2,1)S(1)}, bf16[3,256,256]{2,1,0:T(8,128)(2,1)S(1)}, u32[]{:S(2)}, u32[]{:S(2)}) collective-permute-start(bf16[3,256,256]{2,1,0:T(8,128)(2,1)S(1)} %collective-permute-done.2.refs_4_), channel_id=1, source_target_pairs={{12,0},{0,4},{4,8},{8,12},{13,1},{1,5},{5,9},{9,13},{14,2},{2,6},{... | collective-permute-start | bytes 1179656 | tf_op jit(solution)/shard_map/ppermute | solution.py:375
  156.7 44.0 %copy-start.8 = (bf16[3,256,256]{2,1,0:T(8,128)(2,1)}, bf16[3,256,256]{2,1,0:T(8,128)(2,1)S(1)}, u32[]{:S(2)}) copy-start(bf16[3,256,256]{2,1,0:T(8,128)(2,1)S(1)} %collective-permute-done.14.refs_5_) | copy-start | bytes 1179652
  178.8 19.0 %collective-permute-start.17 = (bf16[272,4096]{1,0:T(8,128)(2,1)}, bf16[272,4096]{1,0:T(8,128)(2,1)}, u32[]{:S(2)}, u32[]{:S(2)}) collective-permute-start(bf16[272,4096]{1,0:T(8,128)(2,1)} %pad_maximum_fusion.2.act_ref), channel_id=1, source_target_pairs={{0,16},{16,0},{1,17},{17,1},{2,18},{18,2},{3,19},{19,3},{4,20},{20... | collective-permute-start | bytes 6684680 | tf_op jit(solution)/shard_map/ppermute | solution.py:38
  178.8 19.0 %collective-permute-start.18 = (bf16[3,256,256]{2,1,0:T(8,128)(2,1)S(1)}, bf16[3,256,256]{2,1,0:T(8,128)(2,1)}, u32[]{:S(2)}, u32[]{:S(2)}) collective-permute-start(bf16[3,256,256]{2,1,0:T(8,128)(2,1)S(1)} %collective-permute-done.3.refs_8_), channel_id=1, source_target_pairs={{4,0},{8,4},{12,8},{0,12},{5,1},{9,5},{13,9},{1,13},{6,2},{10,6},{... | collective-permute-start | bytes 1179656 | tf_op jit(solution)/shard_map/ppermute | solution.py:375
  182.0 57.1 %collective-permute-start.19 = (bf16[3,256,256]{2,1,0:T(8,128)(2,1)S(1)}, bf16[3,256,256]{2,1,0:T(8,128)(2,1)}, u32[]{:S(2)}, u32[]{:S(2)}) collective-permute-start(bf16[3,256,256]{2,1,0:T(8,128)(2,1)S(1)} %collective-permute-done.3.refs_8_), channel_id=1, source_target_pairs={{8,0},{12,4},{0,8},{4,12},{9,1},{13,5},{1,9},{5,13},{10,2},{14,6},... | collective-permute-start | bytes 1179656 | tf_op jit(solution)/shard_map/ppermute | solution.py:375
  182.0 57.1 %collective-permute-start.20 = (bf16[3,256,256]{2,1,0:T(8,128)(2,1)S(1)}, bf16[3,256,256]{2,1,0:T(8,128)(2,1)}, u32[]{:S(2)}, u32[]{:S(2)}) collective-permute-start(bf16[3,256,256]{2,1,0:T(8,128)(2,1)S(1)} %collective-permute-done.3.refs_8_), channel_id=1, source_target_pairs={{12,0},{0,4},{4,8},{8,12},{13,1},{1,5},{5,9},{9,13},{14,2},{2,6},{... | collective-permute-start | bytes 1179656 | tf_op jit(solution)/shard_map/ppermute | solution.py:375
  184.0 148.0 %collective-permute-start.25 = (bf16[2,2,1024,256]{3,2,1,0:T(8,128)(2,1)}, bf16[2,2,1024,256]{3,2,1,0:T(8,128)(2,1)}, u32[]{:S(2)}, u32[]{:S(2)}) collective-permute-start(bf16[2,2,1024,256]{3,2,1,0:T(8,128)(2,1)} %pad_maximum_fusion.3.refs_0_), channel_id=1, source_target_pairs={{0,1},{1,0},{2,3},{3,2},{4,5},{5,4},{6,7},{7,6},{8,9},{9,8},{10,11... | collective-permute-start | bytes 6291464 | tf_op jit(solution)/shard_map/ppermute | solution.py:38
  197.8 134.3 %collective-permute-start.26 = (bf16[2,2,1024,256]{3,2,1,0:T(8,128)(2,1)}, bf16[2,2,1024,256]{3,2,1,0:T(8,128)(2,1)}, u32[]{:S(2)}, u32[]{:S(2)}) collective-permute-start(bf16[2,2,1024,256]{3,2,1,0:T(8,128)(2,1)} %pad_maximum_fusion.3.refs_0_), channel_id=1, source_target_pairs={{0,2},{1,3},{2,0},{3,1},{4,6},{5,7},{6,4},{7,5},{8,10},{9,11},{10,... | collective-permute-start | bytes 6291464 | tf_op jit(solution)/shard_map/ppermute | solution.py:38
  197.8 134.3 %collective-permute-start.27 = (bf16[2,2,1024,256]{3,2,1,0:T(8,128)(2,1)}, bf16[2,2,1024,256]{3,2,1,0:T(8,128)(2,1)}, u32[]{:S(2)}, u32[]{:S(2)}) collective-permute-start(bf16[2,2,1024,256]{3,2,1,0:T(8,128)(2,1)} %pad_maximum_fusion.3.refs_0_), channel_id=1, source_target_pairs={{0,3},{1,2},{2,1},{3,0},{4,7},{5,6},{6,5},{7,4},{8,11},{9,10},{10,... | collective-permute-start | bytes 6291464 | tf_op jit(solution)/shard_map/ppermute | solution.py:38
  239.1 1.4 copy-start.7
  240.5 1.0 copy-start.9
  243.5 21.2 %copy-start.14 = (bf16[520,128]{1,0:T(8,128)(2,1)S(1)}, bf16[520,128]{1,0:T(8,128)(2,1)}, u32[]{:S(2)}) copy-start(bf16[520,128]{1,0:T(8,128)(2,1)} %constant.53.clone.sums_ref) | copy-start | bytes 399364
  243.5 21.2 %copy-start.15 = (bf16[256,256]{1,0:T(8,128)(2,1)S(1)}, bf16[256,256]{1,0:T(8,128)(2,1)}, u32[]{:S(2)}) copy-start(bf16[256,256]{1,0:T(8,128)(2,1)} %constant.55.clone.same_ref) | copy-start | bytes 393220
  243.5 21.2 %copy-start.16 = (f32[64,256]{1,0:T(8,128)S(1)}, f32[64,256]{1,0:T(8,128)}, u32[]{:S(2)}) copy-start(f32[64,256]{1,0:T(8,128)} %constant.54.clone.level_ref) | copy-start | bytes 196612
  243.5 21.2 %copy-start.19 = (s32[2]{0:T(128)S(1)}, s32[2]{0:T(128)}, u32[]{:S(2)}) copy-start(s32[2]{0:T(128)} %extent_ref.1) | copy-start | bytes 28
  301.3 9.7 %collective-permute-start.21 = (bf16[640,256]{1,0:T(8,128)(2,1)S(1)}, bf16[640,256]{1,0:T(8,128)(2,1)S(1)}, u32[]{:S(2)}, u32[]{:S(2)}) collective-permute-start(bf16[640,256]{1,0:T(8,128)(2,1)S(1)} %get-tuple-element.105), channel_id=1, source_target_pairs={{0,1},{1,0},{2,3},{3,2},{4,5},{5,4},{6,7},{7,6},{8,9},{9,8},{10,11... | collective-permute-start | bytes 983048 | tf_op jit(solution)/shard_map/ppermute | solution.py:38
  301.7 10.8 %collective-permute-start.22 = (bf16[640,256]{1,0:T(8,128)(2,1)S(1)}, bf16[640,256]{1,0:T(8,128)(2,1)S(1)}, u32[]{:S(2)}, u32[]{:S(2)}) collective-permute-start(bf16[640,256]{1,0:T(8,128)(2,1)S(1)} %get-tuple-element.106), channel_id=1, source_target_pairs={{0,2},{1,3},{2,0},{3,1},{4,6},{5,7},{6,4},{7,5},{8,10},{9,11},{10,... | collective-permute-start | bytes 983048 | tf_op jit(solution)/shard_map/ppermute | solution.py:38
  311.0 9.7 %collective-permute-start.23 = (bf16[640,256]{1,0:T(8,128)(2,1)S(1)}, bf16[640,256]{1,0:T(8,128)(2,1)S(1)}, u32[]{:S(2)}, u32[]{:S(2)}) collective-permute-start(bf16[640,256]{1,0:T(8,128)(2,1)S(1)} %get-tuple-element.107), channel_id=1, source_target_pairs={{0,3},{1,2},{2,1},{3,0},{4,7},{5,6},{6,5},{7,4},{8,11},{9,10},{10,... | collective-permute-start | bytes 983048 | tf_op jit(solution)/shard_map/ppermute | solution.py:38
  320.9 3.6 %copy-start.3 = (bf16[4,512,256]{2,1,0:T(8,128)(2,1)}, bf16[4,512,256]{2,1,0:T(8,128)(2,1)S(1)}, u32[]{:S(2)}) copy-start(bf16[4,512,256]{2,1,0:T(8,128)(2,1)S(1)} %slice.28.own_ref) | copy-start | bytes 3145732
  320.9 11.2 %collective-permute-start.24 = (bf16[4,512,256]{2,1,0:T(8,128)(2,1)S(1)}, bf16[4,512,256]{2,1,0:T(8,128)(2,1)}, u32[]{:S(2)}, u32[]{:S(2)}) collective-permute-start(bf16[4,512,256]{2,1,0:T(8,128)(2,1)S(1)} %slice.28.own_ref), channel_id=1, source_target_pairs={{0,16},{16,0},{1,17},{17,1},{2,18},{18,2},{3,19},{19,3},{4,20},{20... | collective-permute-start | bytes 3145736 | tf_op jit(solution)/shard_map/ppermute | solution.py:38
  324.5 7.6 %copy-start.2 = (bf16[2,2,1024,256]{3,2,1,0:T(8,128)(2,1)S(1)}, bf16[2,2,1024,256]{3,2,1,0:T(8,128)(2,1)}, u32[]{:S(2)}) copy-start(bf16[2,2,1024,256]{3,2,1,0:T(8,128)(2,1)} %pad_maximum_fusion.3.refs_0_) | copy-start | bytes 6291460
  332.1 1.2 copy-start.4
  333.3 8.9 %copy-start.1 = (bf16[4096,128]{1,0:T(8,128)(2,1)S(1)}, bf16[4096,128]{1,0:T(8,128)(2,1)}, u32[]{:S(2)}) copy-start(bf16[4096,128]{1,0:T(8,128)(2,1)} %param.21) | copy-start | bytes 3145732
  (4 other events, 3.5 us)
Sparse Core Ops, SparseCore 0:
  47.3 65.4 all-gather.4
  178.9 60.1 all-gather.6

commit v3 on v2

--- a/solution.py
+++ b/solution.py
@@ -153,50 +153,56 @@
     )(where, act, coeffs, left, *earlier)
 
 
-def project_kernel(where_ref, act_ref, gathered_ref, *refs):
-    *pieces, out_ref, lines_ref = refs
-    reqs, depth = gathered_ref.shape[0], gathered_ref.shape[2]
-    stretches = 1 + len(pieces) // reqs
+def project_kernel(where_ref, act_ref, *refs):
+    *hops, out_ref, lines_ref = refs
+    stretches, _, depth, _ = hops[0].shape
+    reqs = (len(hops) + 1) // 2
+
+    def place(hop_ref, r):
+        for d in range(stretches):
+            at = (r * stretches + (where_ref[0] ^ d)) * depth
+            lines_ref[pl.ds(pl.multiple_of(at, depth), depth), :] = hop_ref[d, 0]
 
     @pl.when(pl.program_id(1) == 0)
     def _():
-        for r in range(reqs):
-            at = (r * stretches + where_ref[0]) * depth
-            lines_ref[pl.ds(pl.multiple_of(at, depth), depth), :] = gathered_ref[r, 0]
-        for i, piece_ref in enumerate(pieces):
-            d, k = 1 + i // reqs, i % reqs
-            at = (lax.rem(where_ref[2] + k, reqs) * stretches + (where_ref[0] ^ d)) * depth
-            lines_ref[pl.ds(pl.multiple_of(at, depth), depth), :] = piece_ref[0]
+        me = where_ref[2]
+        place(hops[0], me)
+        for hop in range(1, reqs):
+
+            @pl.when(me >= hop)
+            def _():
+                place(hops[2 * hop - 1], me - hop)
+
+            @pl.when(me + hop < reqs)
+            def _():
+                place(hops[2 * hop], me + hop)
 
     act = act_ref[0, 0].reshape(-1, act_ref.shape[-1])
     out_ref[0, 0] = dot(act, lines_ref[...]).astype(bf16).reshape(out_ref.shape[2:])
 
 
-def projected(where, mixed, gathered, pieces):
-    reqs, kinds, depth, cols = gathered.shape
-    _, sides, stretches, span, width = mixed.shape
+def projected(where, mixed, hops):
+    stretches, kinds, depth, cols = hops[0].shape
+    _, sides, _, span, width = mixed.shape
     if depth % 128:
-        order = jnp.arange(stretches) ^ where[0]
-        lines = jnp.stack([gathered, *pieces])[order]
-        lines = jnp.transpose(lines, (2, 1, 0, 3, 4)).reshape(kinds, width, cols)
+        (lines,) = hops[1:]
+        lines = lines[:, jnp.arange(stretches) ^ where[0]]
+        lines = jnp.transpose(lines, (2, 0, 1, 3, 4)).reshape(kinds, width, cols)
         return jnp.einsum("jxbtk,jkc->jxbtc", mixed, lines, preferred_element_type=f32).astype(bf16)
     return pl.pallas_call(
         project_kernel,
         grid_spec=pltpu.PrefetchScalarGridSpec(
             num_scalar_prefetch=1,
             grid=(kinds, sides),
-            in_specs=[
-                pl.BlockSpec((1, 1, stretches, span, width), lambda j, m, w: (j, m, 0, 0, 0)),
-                pl.BlockSpec((reqs, 1, depth, cols), lambda j, m, w: (0, j, 0, 0)),
-            ]
-            + [pl.BlockSpec((1, depth, cols), lambda j, m, w: (j, 0, 0))] * len(pieces),
+            in_specs=[pl.BlockSpec((1, 1, stretches, span, width), lambda j, m, w: (j, m, 0, 0, 0))]
+            + [pl.BlockSpec((stretches, 1, depth, cols), lambda j, m, w: (0, j, 0, 0))] * len(hops),
             out_specs=pl.BlockSpec((1, 1, stretches, span, cols), lambda j, m, w: (j, m, 0, 0, 0)),
             scratch_shapes=[pltpu.VMEM((width, cols), bf16)],
         ),
         out_shape=jax.ShapeDtypeStruct((kinds, sides, stretches, span, cols), bf16),
-        compiler_params=vmem(40),
+        compiler_params=vmem(60),
         cost_estimate=SMALL,
-    )(where, mixed, gathered, *pieces)
+    )(where, mixed, *hops)
 
 
 def decay_sums():
@@ -370,9 +376,9 @@
     )(where, x, own, far, *weights)
 
 
-def ahead(value, axis, by):
+def moved(value, axis, by):
     peers = lax.axis_size(axis)
-    return lax.ppermute(value, axis, [((i + by) % peers, i) for i in range(peers)])
+    return lax.ppermute(value, axis, [(i, i + by) for i in range(peers) if 0 <= i + by < peers])
 
 
 def local(
@@ -402,14 +408,13 @@
 
     x = incoming_activations.reshape(rows, width)
     own_x = lax.dynamic_slice_in_dim(x, t * span, span, 0)
-    past = lax.ppermute(own_x[span - PAST :], "seq", [(i, i + 1) for i in range(stretches - 1)])
+    past = moved(own_x[span - PAST :], "seq", 1)
     pieces = [
         lax.dynamic_slice_in_dim(learner_acceptor_lookup_slices, (s ^ d) * cols, cols, 2).astype(bf16)
         for d in range(stretches)
     ]
     out_half = learner_projection_slices.astype(bf16)
     out_lines = lax.all_gather(out_half, "req", axis=0, tiled=False)
-    gathered = lax.all_gather(pieces[0], "req", axis=0, tiled=False)
     got = [swapped(pieces[d], "seq", d) for d in range(1, stretches)]
 
     def tied(*values):
@@ -424,48 +429,45 @@
         learner_line_permutation.reshape(1, width),
     )
     act, perm, *got = tied(act, learner_line_permutation, *got)
-    direct = pieces[0].shape[1] % 128 == 0
-
-    def along_z(piece):
-        if not direct:
-            return [lax.all_gather(piece, "req", axis=0, tiled=False)]
-        return [ahead(piece, "req", k) if k else piece for k in range(groups)]
+    lines = jnp.stack([pieces[0], *got])
+    chained = groups == 4
 
     def mixed_in(values, side, apart, earlier):
         return shifted(where, values, coeffs, left, side, apart, stretches, earlier)
 
     left = fading_left_matrix[perm]
-    cut = (span + PAST) // 32 * 16
     near, other = swapped(act, "seq", 1), swapped(act, "seq", 2)
-    lines = along_z(got[0])
+    hops = [moved(lines, "req", 1), moved(lines, "req", -1)] if chained else [lax.all_gather(lines, "req", axis=0)]
     results = mixed_in(act, 0, 0, ())
     results = mixed_in(swapped(act, "tensor", 1), 1, 0, results)
-    near, other, *rest = tied(near, other, *results, *lines, *got[1:])
-    results, lines, got = tuple(rest[:2]), rest[2:-2], rest[-2:]
-
-    across = [swapped(near[:cut], "seq", 2), swapped(other[cut:], "seq", 1)]
-    more = along_z(got[0])
+    near, other, out_lines, act, *rest = tied(near, other, out_lines, act, *results, *hops)
+    results, hops = tuple(rest[:2]), rest[2:]
+
+    across = swapped(act, "seq", 3)
+    if chained:
+        hops += [moved(hops[0], "req", 1), moved(hops[1], "req", -1)]
+    far = swapped(jnp.stack([near, other]), "tensor", 1)
     results = mixed_in(near, 0, 1, results)
     results = mixed_in(other, 0, 2, results)
-    far = swapped(jnp.stack([near, other]), "tensor", 1)
     share = groups // cores
     kept = lax.dynamic_slice_in_dim(out_lines, t * share, share, 0)
     given = lax.dynamic_slice_in_dim(out_lines, (1 - t) * share, share, 0)
     out_lines = jnp.stack([kept, swapped(given, "tensor", 1)])
-    across = jnp.concatenate(across, axis=0)
-    across, out_lines, far, *rest = tied(across, out_lines, far, *results, *more, got[1])
-    results, got = tuple(rest[:2]), rest[-1]
-    lines += rest[2:-1]
-
-    lines += along_z(got)
-    out_weights = [out_lines] + [swapped(out_lines, "seq", d) for d in range(1, stretches)]
+    across, out_lines, far, *rest = tied(across, out_lines, far, *results, *hops)
+    results, hops = tuple(rest[:2]), rest[2:]
+
+    if chained:
+        hops += [moved(hops[2], "req", 1), moved(hops[3], "req", -1)]
+    near, other = swapped(out_lines, "seq", 1), swapped(out_lines, "seq", 2)
     last = swapped(across, "tensor", 1)
     results = mixed_in(across, 0, 3, results)
     results = mixed_in(far[0], 1, 1, results)
     results = mixed_in(far[1], 1, 2, results)
-    mixed, lora = mixed_in(last, 1, 3, results)
-
-    proj = projected(where, mixed, gathered, lines)
+    results = mixed_in(last, 1, 3, results)
+    mixed, lora, out_lines, *hops = tied(*results, out_lines, *hops)
+    across = swapped(out_lines, "seq", 3)
+
+    proj = projected(where, mixed, [lines, *hops])
 
     def mine(array):
         return lax.dynamic_slice_in_dim(array, s * cols, cols, array.ndim - 1).reshape(-1, cols)
@@ -475,6 +477,7 @@
         mine(cluster_scaling_vector),
     )
 
+    normed, states, near, other, across = tied(normed, states, near, other, across)
     sent = jnp.concatenate(
         [normed.reshape(stretches, rows, cols), states.reshape(stretches, -1, cols).astype(bf16)], axis=1
     )
@@ -482,14 +485,16 @@
     for d in range(stretches):
         block = lax.dynamic_index_in_dim(sent, s ^ d, 0, keepdims=False)
         blocks.append(swapped(block, "seq", d) if d else block)
-    blocks = jnp.stack(blocks)
-    own_lines = blocks[:, :rows]
+    own_lines = jnp.stack([block[:rows] for block in blocks])
     far_lines = swapped(own_lines, "tensor", 1)
+    out_weights = [out_lines, near, other, across]
     hidden_out = finished(where, x, own_lines, far_lines, out_weights).reshape(reqs, span, width // cores)
 
     heads = cols // ATTEND_DIM
-    states = blocks[jnp.arange(stretches) ^ s, rows:].reshape(stretches, reqs, ATTEND_DIM, heads, ATTEND_DIM)
-    states = jnp.transpose(states, (1, 0, 3, 4, 2)).astype(f32)
+    states = jnp.stack([block[rows:] for block in blocks]).reshape(2, 2, reqs, ATTEND_DIM, heads, ATTEND_DIM)
+    states = jnp.where(s % 2 == 1, states[:, ::-1], states)
+    states = jnp.where(s // 2 == 1, states[::-1], states)
+    states = jnp.transpose(states, (2, 0, 1, 4, 5, 3)).astype(f32)
     stretch_states = states.reshape(reqs, 1, stretches * heads, ATTEND_DIM * ATTEND_DIM)
     return (hidden_out, stretch_states)
 

time: 350 us -> 311 us (0.89)
  waiting for transfers between devices: 108 us -> 76.7 us
  local copies, waits for them, and re-layouts: 51.2 us -> 36.8 us
  Pallas kernels: 127 us -> 131 us
    all_gather x1 -> x0, waiting for transfers between devices: 16.1 us -> none  [local(): gathered = lax.all_gather(pieces[0], 'req', axis=0, tiled=False)]
    ppermute x18 -> x17, waiting for transfers between devices: 26 us -> 18 us  [swapped(): return lax.ppermute(value, axis, [(i, i ^ by) for i in range(peers)])]
    ppermute x10 -> x7, waiting for transfers between devices: 65.6 us -> 58.6 us  [moved(): lax.ppermute(value, axis, [(i, i + by) for i in range(peers) if 0 <= i +...]
    unnamed x44 -> x32, local copies, waits for them, and re-layouts: 8.58 us -> 3.73 us
    slice x4 -> x3, local copies, waits for them, and re-layouts: 5.77 us -> 1.08 us  [the longest x1 1.05 us: local(): past = moved(own_x[span - PAST:], 'seq', 1)]
    pallas_call x1, Pallas kernels: 21.2 us -> 25.5 us  [projected(): pl.pallas_call(project_kernel, grid_spec=pltpu.PrefetchScalarGridSpec(num...]
    reshape x3 -> x2, local copies, waits for them, and re-layouts: 7.57 us -> 3.69 us  [local(): states.reshape(reqs, 1, stretches * heads, ATTEND_DIM * ATTEND_DIM)]
    ppermute x18 -> x17, starting transfers between devices: 13.2 us -> 16.6 us  [swapped(): return lax.ppermute(value, axis, [(i, i ^ by) for i in range(peers)])]
  transfers between devices with their start and end apart: 30 -> 25, of which waited for: 7 -> 9; matrix products, arithmetic and copies ran while one was open for 16% -> 12% of each run, Pallas kernels for 34% -> 39%
where the time goes in v3:
time: 311 us; the launch traced here: 309 us
  Pallas kernels  131 us (42%)
  waiting for transfers between devices  76.7 us (25%)
  starting transfers between devices  39.1 us (13%)
  local copies, waits for them, and re-layouts  36.8 us (12%)
  between operations  14.5 us (5%)
  other arithmetic  11.2 us (4%)
    ppermute x7, waiting for transfers between devices, moved(): lax.ppermute(value, axis, [(i, i + by) for i in range(peers) if 0 <= i +...  58.6 us
    pallas_call x8, Pallas kernels, shifted(): pl.pallas_call(mix_kernel, grid_spec=pltpu.PrefetchScalarGridSpec(num_sca...  46.3 us
    pallas_call x1, Pallas kernels, recurrence(): pl.pallas_call(wkv_kernel, grid_spec=pltpu.PrefetchScalarGridSpec(num_sca...  36.4 us
    pallas_call x1, Pallas kernels, projected(): pl.pallas_call(project_kernel, grid_spec=pltpu.PrefetchScalarGridSpec(num...  25.5 us
    ppermute x7, starting transfers between devices, moved(): lax.ppermute(value, axis, [(i, i + by) for i in range(peers) if 0 <= i +...  22.4 us
    ppermute x17, waiting for transfers between devices, swapped(): return lax.ppermute(value, axis, [(i, i ^ by) for i in range(peers)])  18 us
    ppermute x17, starting transfers between devices, swapped(): return lax.ppermute(value, axis, [(i, i ^ by) for i in range(peers)])  16.6 us
    pallas_call x1, Pallas kernels, ordered(): pl.pallas_call(order_kernel, grid=(width // block,), in_specs=[pl.BlockSp...  13.9 us
  transfers between devices with their start and end apart: 25, of which 9 were waited for; matrix products, arithmetic and copies ran while one was open for 12% of the time, Pallas kernels for 39%

profile of v3, /device:TPU:0, one launch (start us, length us, event | category | flops | bytes accessed | tf_op | source)
XLA Modules:
  0.0 309.3 jit_solution(11089431030273931956)
XLA Ops:
  8.3 4.8 %collective-permute-start = (bf16[16,4096]{1,0:T(8,128)(2,1)S(1)}, bf16[16,4096]{1,0:T(8,128)(2,1)S(1)}, u32[]{:S(2)}, u32[]{:S(2)}) collective-permute-start(bf16[16,4096]{1,0:T(8,128)(2,1)S(1)} %constant_dynamic-slice_fusion), channel_id=1, source_target_pairs={{0,1},{1,2},{2,3},{4,5},{5,6},{6,7},{8,9},{9,10},{10,11},{12,13},{... | collective-permute-start | bytes 393224 | tf_op jit(solution)/shard_map/ppermute | solution.py:381
  13.2 2.9 dynamic-slice_convert_fusion
  16.1 1.5 collective-permute-start.1
  17.6 2.0 collective-permute-start.3
  20.5 1.8 constant_dynamic-slice_fusion.3
  23.0 13.9 %shard_map.158 = (bf16[272,4096]{1,0:T(8,128)(2,1)}, f32[8,4096]{1,0:T(8,128)S(1)}) custom-call(bf16[272,4096]{1,0:T(8,128)(2,1)S(1)} %pad_maximum_fusion.1.x_ref, f32[1,4096]{1,0:T(1,128)S(1)} %bitcast.50, f32[8,4096]{1,0:T(8,128)S(1)} %pad.4.coeff_ref, s32[1,4096]{1,0:T(1,128)S(1)} %bitcast.49), custom_call_target="tpu_custom_call" | custom-call | flops 1024 | bytes 1024 | tf_op jit(solution)/shard_map/pallas_call | solution.py:74
  37.0 1.6 collective-permute-start.4
  38.7 2.3 pad_maximum_fusion.3.refs_0_
  41.0 4.7 %collective-permute-start.7 = (bf16[4,3,256,256]{3,2,1,0:T(8,128)(2,1)}, bf16[4,3,256,256]{3,2,1,0:T(8,128)(2,1)}, u32[]{:S(2)}, u32[]{:S(2)}) collective-permute-start(bf16[4,3,256,256]{3,2,1,0:T(8,128)(2,1)} %pad_maximum_fusion.3.refs_0_), channel_id=1, source_target_pairs={{0,4},{4,8},{8,12},{1,5},{5,9},{9,13},{2,6},{6,10},{10,14},{3,7},{... | collective-permute-start | bytes 4718600 | tf_op jit(solution)/shard_map/ppermute | solution.py:381
  45.6 1.3 collective-permute-start.8
  47.0 12.1 %gather_fusion = bf16[4096,128]{1,0:T(8,128)(2,1)S(1)} fusion(bf16[4096,128]{1,0:T(8,128)(2,1)S(1)} %copy-done, s32[4096]{0:T(1024)S(1)} %fusion.7), kind=kCustom, calls=%fused_computation | custom fusion | bytes 2113536 | tf_op jit(solution)/shard_map/gather | solution.py:438
  59.2 6.3 %shard_map.159 = (bf16[3,2,4,256,4096]{4,3,2,1,0:T(8,128)(2,1)}, bf16[2,4,256,128]{3,2,1,0:T(8,128)(2,1)S(1)}) custom-call(s32[3]{0:T(128)S(1)} %pad_add_fusion.where_ref, bf16[272,4096]{1,0:T(8,128)(2,1)} %get-tuple-element.73.act_ref, f32[8,4096]{1,0:T(8,128)S(1)} %get-tuple-element.64.coeff_ref, bf16[4096,128]{1,0:T(8,128)(2,1)S(1)} %gather_fusion), custom_call_target="tpu_custom_call" | custom-call | flops 1024 | bytes 1024 | tf_op jit(solution)/shard_map/pallas_call | solution.py:129
  65.5 6.3 %shard_map.160 = (bf16[3,2,4,256,4096]{4,3,2,1,0:T(8,128)(2,1)}, bf16[2,4,256,128]{3,2,1,0:T(8,128)(2,1)S(1)}) custom-call(s32[3]{0:T(128)S(1)} %pad_add_fusion.where_ref, bf16[272,4096]{1,0:T(8,128)(2,1)} %collective-permute-done.6.act_ref, f32[8,4096]{1,0:T(8,128)S(1)} %get-tuple-element.64.coeff_ref, ...), custom_call_target="tpu_custom_call", output_to_operand_aliasing={{0}: (4, {}), {1}: (5, {})} | custom-call | flops 1024 | bytes 1024 | tf_op jit(solution)/shard_map/pallas_call | solution.py:129
  71.8 25.2 %collective-permute-done.7.refs_1_ = bf16[4,3,256,256]{3,2,1,0:T(8,128)(2,1)} collective-permute-done((bf16[4,3,256,256]{3,2,1,0:T(8,128)(2,1)}, bf16[4,3,256,256]{3,2,1,0:T(8,128)(2,1)}, u32[]{:S(2)}, u32[]{:S(2)}) %collective-permute-start.7) | collective-permute-done | bytes 1572896 | tf_op jit(solution)/shard_map/ppermute | solution.py:381
  97.0 2.0 collective-permute-done.8.refs_2_
  98.9 4.7 %pad_maximum_fusion = bf16[2,272,4096]{2,1,0:T(8,128)(2,1)} fusion(bf16[1,272,4096]{2,1,0:T(8,128)(2,1)} %bitcast.14, bf16[1,272,4096]{2,1,0:T(8,128)(2,1)} %bitcast.13), kind=kLoop, calls=%fused_computation.1 | loop fusion | flops 2228224 | bytes 8912896 | tf_op jit(solution)/shard_map/stack | solution.py:449
  103.7 2.4 collective-permute-start.9
  106.1 5.0 %collective-permute-start.12 = (bf16[4,3,256,256]{3,2,1,0:T(8,128)(2,1)}, bf16[4,3,256,256]{3,2,1,0:T(8,128)(2,1)}, u32[]{:S(2)}, u32[]{:S(2)}) collective-permute-start(bf16[4,3,256,256]{3,2,1,0:T(8,128)(2,1)} %collective-permute-done.7.refs_1_), channel_id=1, source_target_pairs={{0,4},{4,8},{8,12},{1,5},{5,9},{9,13},{2,6},{6,10},{10,14},{3,7},{... | collective-permute-start | bytes 4718600 | tf_op jit(solution)/shard_map/ppermute | solution.py:381
  111.0 1.3 collective-permute-start.13
  112.3 1.7 dynamic-slice_bitcast_fusion
  114.1 6.4 %shard_map.161 = (bf16[3,2,4,256,4096]{4,3,2,1,0:T(8,128)(2,1)}, bf16[2,4,256,128]{3,2,1,0:T(8,128)(2,1)S(1)}) custom-call(s32[3]{0:T(128)S(1)} %pad_add_fusion.where_ref, bf16[272,4096]{1,0:T(8,128)(2,1)} %collective-permute-done.4.act_ref, f32[8,4096]{1,0:T(8,128)S(1)} %get-tuple-element.64.coeff_ref, ...), custom_call_target="tpu_custom_call", output_to_operand_aliasing={{0}: (4, {}), {1}: (5, {})} | custom-call | flops 1024 | bytes 1024 | tf_op jit(solution)/shard_map/pallas_call | solution.py:129
  120.5 6.4 %shard_map.162 = (bf16[3,2,4,256,4096]{4,3,2,1,0:T(8,128)(2,1)}, bf16[2,4,256,128]{3,2,1,0:T(8,128)(2,1)S(1)}) custom-call(s32[3]{0:T(128)S(1)} %pad_add_fusion.where_ref, bf16[272,4096]{1,0:T(8,128)(2,1)} %collective-permute-done.5.act_ref, f32[8,4096]{1,0:T(8,128)S(1)} %get-tuple-element.64.coeff_ref, ...), custom_call_target="tpu_custom_call", output_to_operand_aliasing={{0}: (4, {}), {1}: (5, {})} | custom-call | flops 1024 | bytes 1024 | tf_op jit(solution)/shard_map/pallas_call | solution.py:129
  126.8 1.5 pad_maximum_fusion.2.refs_0_
  128.3 15.9 %collective-permute-done.12.refs_3_ = bf16[4,3,256,256]{3,2,1,0:T(8,128)(2,1)} collective-permute-done((bf16[4,3,256,256]{3,2,1,0:T(8,128)(2,1)}, bf16[4,3,256,256]{3,2,1,0:T(8,128)(2,1)}, u32[]{:S(2)}, u32[]{:S(2)}) %collective-permute-start.12) | collective-permute-done | bytes 1572896 | tf_op jit(solution)/shard_map/ppermute | solution.py:381
  144.2 5.3 %collective-permute-done.13.refs_4_ = bf16[4,3,256,256]{3,2,1,0:T(8,128)(2,1)} collective-permute-done((bf16[4,3,256,256]{3,2,1,0:T(8,128)(2,1)}, bf16[4,3,256,256]{3,2,1,0:T(8,128)(2,1)}, u32[]{:S(2)}, u32[]{:S(2)}) %collective-permute-start.13) | collective-permute-done | bytes 1572896 | tf_op jit(solution)/shard_map/ppermute | solution.py:381
  149.5 6.3 %collective-permute-done.9.act_ref = bf16[272,4096]{1,0:T(8,128)(2,1)} collective-permute-done((bf16[272,4096]{1,0:T(8,128)(2,1)}, bf16[272,4096]{1,0:T(8,128)(2,1)}, u32[]{:S(2)}, u32[]{:S(2)}) %collective-permute-start.9) | collective-permute-done | bytes 2228256 | tf_op jit(solution)/shard_map/ppermute | solution.py:38
  155.8 3.9 %collective-permute-start.15 = (bf16[4,3,256,256]{3,2,1,0:T(8,128)(2,1)}, bf16[4,3,256,256]{3,2,1,0:T(8,128)(2,1)S(1)}, u32[]{:S(2)}, u32[]{:S(2)}) collective-permute-start(bf16[4,3,256,256]{3,2,1,0:T(8,128)(2,1)} %collective-permute-done.12.refs_3_), channel_id=1, source_target_pairs={{0,4},{4,8},{8,12},{1,5},{5,9},{9,13},{2,6},{6,10},{10,14},{3,7},{... | collective-permute-start | bytes 4718600 | tf_op jit(solution)/shard_map/ppermute | solution.py:381
  159.7 1.5 collective-permute-start.16
  161.2 1.5 collective-permute-start.17
  162.7 1.4 collective-permute-start.18
  164.1 6.4 %shard_map.163 = (bf16[3,2,4,256,4096]{4,3,2,1,0:T(8,128)(2,1)}, bf16[2,4,256,128]{3,2,1,0:T(8,128)(2,1)S(1)}) custom-call(s32[3]{0:T(128)S(1)} %pad_add_fusion.where_ref, bf16[272,4096]{1,0:T(8,128)(2,1)} %collective-permute-done.9.act_ref, f32[8,4096]{1,0:T(8,128)S(1)} %get-tuple-element.64.coeff_ref, ...), custom_call_target="tpu_custom_call", output_to_operand_aliasing={{0}: (4, {}), {1}: (5, {})} | custom-call | flops 1024 | bytes 1024 | tf_op jit(solution)/shard_map/pallas_call | solution.py:129
  170.6 2.8 slice_bitcast_fusion
  173.4 4.9 %shard_map.164 = (bf16[3,2,4,256,4096]{4,3,2,1,0:T(8,128)(2,1)}, bf16[2,4,256,128]{3,2,1,0:T(8,128)(2,1)S(1)}) custom-call(s32[3]{0:T(128)S(1)} %pad_add_fusion.where_ref, bf16[272,4096]{1,0:T(8,128)(2,1)S(1)} %get-tuple-element.118.act_ref, f32[8,4096]{1,0:T(8,128)S(1)} %get-tuple-element.64.coeff_ref, ...), custom_call_target="tpu_custom_call", output_to_operand_aliasing={{0}: (4, {}), {1}: (5, {})} | custom-call | flops 1024 | bytes 1024 | tf_op jit(solution)/shard_map/pallas_call | solution.py:129
  178.3 4.9 %shard_map.165 = (bf16[3,2,4,256,4096]{4,3,2,1,0:T(8,128)(2,1)}, bf16[2,4,256,128]{3,2,1,0:T(8,128)(2,1)S(1)}) custom-call(s32[3]{0:T(128)S(1)} %pad_add_fusion.where_ref, bf16[272,4096]{1,0:T(8,128)(2,1)S(1)} %get-tuple-element.119.act_ref, f32[8,4096]{1,0:T(8,128)S(1)} %get-tuple-element.64.coeff_ref, ...), custom_call_target="tpu_custom_call", output_to_operand_aliasing={{0}: (4, {}), {1}: (5, {})} | custom-call | flops 1024 | bytes 1024 | tf_op jit(solution)/shard_map/pallas_call | solution.py:129
  183.2 4.8 %shard_map.166 = (bf16[3,2,4,256,4096]{4,3,2,1,0:T(8,128)(2,1)}, bf16[2,4,256,128]{3,2,1,0:T(8,128)(2,1)S(1)}) custom-call(s32[3]{0:T(128)S(1)} %pad_add_fusion.where_ref, bf16[272,4096]{1,0:T(8,128)(2,1)S(1)} %collective-permute-done.14.act_ref, f32[8,4096]{1,0:T(8,128)S(1)} %get-tuple-element.64.coeff_ref, ...), custom_call_target="tpu_custom_call", output_to_operand_aliasing={{0}: (4, {}), {1}: (5, {})} | custom-call | flops 1024 | bytes 1024 | tf_op jit(solution)/shard_map/pallas_call | solution.py:129
  188.0 6.2 %collective-permute-done.15.refs_5_ = bf16[4,3,256,256]{3,2,1,0:T(8,128)(2,1)S(1)} collective-permute-done((bf16[4,3,256,256]{3,2,1,0:T(8,128)(2,1)}, bf16[4,3,256,256]{3,2,1,0:T(8,128)(2,1)S(1)}, u32[]{:S(2)}, u32[]{:S(2)}) %collective-permute-start.15) | collective-permute-done | bytes 1572896 | tf_op jit(solution)/shard_map/ppermute | solution.py:381
  194.2 4.1 %collective-permute-done.16.refs_6_ = bf16[4,3,256,256]{3,2,1,0:T(8,128)(2,1)S(1)} collective-permute-done((bf16[4,3,256,256]{3,2,1,0:T(8,128)(2,1)}, bf16[4,3,256,256]{3,2,1,0:T(8,128)(2,1)S(1)}, u32[]{:S(2)}, u32[]{:S(2)}) %collective-permute-start.16) | collective-permute-done | bytes 1572896 | tf_op jit(solution)/shard_map/ppermute | solution.py:381
  199.5 2.3 collective-permute-start.19
  205.0 25.5 %shard_map.167.proj_ref = bf16[3,2,4,256,256]{4,3,2,1,0:T(8,128)(2,1)} custom-call(s32[3]{0:T(128)} %copy-done.5, bf16[3,2,4,256,4096]{4,3,2,1,0:T(8,128)(2,1)} %get-tuple-element.102.act_ref, bf16[4,3,256,256]{3,2,1,0:T(8,128)(2,1)} %pad_maximum_fusion.3.refs_0_, bf16[4,3,256,256]{3,2,1,0:T(8,128)(2,1)} %collective-permute-done.7.refs_1_, ...), custom_call_target="tpu_custom_call" | custom-call | flops 1024 | bytes 1024 | tf_op jit(solution)/shard_map/pallas_call | solution.py:192
  230.6 1.9 copy-done.2
  232.5 36.4 %shard_map.168 = (bf16[4,2,256,256]{3,2,1,0:T(8,128)(2,1)S(1)}, f32[4,2,64,256]{3,2,1,0:T(8,128)S(1)}) custom-call(s32[2]{0:T(128)S(1)} %copy-done.10, s32[3]{0:T(128)S(1)} %copy-done.6, bf16[3,2,4,256,256]{4,3,2,1,0:T(8,128)(2,1)S(1)} %copy-done.2, bf16[2,4,256,128]{3,2,1,0:T(8,128)(2,1)S(1)} %get-tuple-element.109.lora_ref, ...), custom_call_target="tpu_custom_call" | custom-call | flops 1024 | bytes 1024 | tf_op jit(solution)/shard_map/pallas_call | solution.py:310
  270.5 1.5 collective-permute-start.21
  272.0 1.5 collective-permute-start.20
  273.5 8.3 %collective-permute-done.22 = bf16[640,256]{1,0:T(8,128)(2,1)} collective-permute-done((bf16[640,256]{1,0:T(8,128)(2,1)}, bf16[640,256]{1,0:T(8,128)(2,1)}, u32[]{:S(2)}, u32[]{:S(2)}) %collective-permute-start.22) | collective-permute-done | bytes 327712 | tf_op jit(solution)/shard_map/ppermute | solution.py:38
  282.8 3.4 %collective-permute-done.21 = bf16[640,256]{1,0:T(8,128)(2,1)} collective-permute-done((bf16[640,256]{1,0:T(8,128)(2,1)S(1)}, bf16[640,256]{1,0:T(8,128)(2,1)}, u32[]{:S(2)}, u32[]{:S(2)}) %collective-permute-start.21) | collective-permute-done | bytes 327712 | tf_op jit(solution)/shard_map/ppermute | solution.py:38
  289.9 1.3 copy.31
  291.2 2.4 reshape.55
  293.6 8.9 %shard_map.169 = bf16[512,2048]{1,0:T(8,128)(2,1)} custom-call(s32[3]{0:T(128)S(1)} %copy-done.6, bf16[512,4096]{1,0:T(8,128)(2,1)} %bitcast.56, bf16[4,512,256]{2,1,0:T(8,128)(2,1)S(1)} %pad_maximum_fusion.4.own_ref, bf16[4,512,256]{2,1,0:T(8,128)(2,1)S(1)} %collective-permute-done.23.far_ref, bf16[2,2,1024,256]{3,2,1,0:T(8,128)(2,1)} %pad_maximum_fusion.2.refs_0_, ...), custom_call_target="tpu_custom_call" | custom-call | flops 1024 | bytes 1024 | tf_op jit(solution)/shard_map/pallas_call | solution.py:364
  (82 shorter events, 13.7 us)
Async XLA Ops:
  7.2 39.9 %copy-start = (bf16[4096,128]{1,0:T(8,128)(2,1)S(1)}, bf16[4096,128]{1,0:T(8,128)(2,1)}, u32[]{:S(2)}) copy-start(bf16[4096,128]{1,0:T(8,128)(2,1)} %param.21) | copy-start | bytes 3145732
  7.2 12.4 %copy-start.14 = (f32[1024,256]{1,0:T(8,128)S(1)}, f32[1024,256]{1,0:T(8,128)}, u32[]{:S(2)}) copy-start(f32[1024,256]{1,0:T(8,128)} %param.20) | copy-start | bytes 3145732
  7.2 91.7 %all-gather.3.cloned.1.call-start = ((), (), s32[]{:S(2)}) async-start(), calls=%async_computation | async-start | bytes 2621440 | tf_op jit(solution)/shard_map/all_gather | solution.py:417
  8.3 14.0 %collective-permute-start = (bf16[16,4096]{1,0:T(8,128)(2,1)S(1)}, bf16[16,4096]{1,0:T(8,128)(2,1)S(1)}, u32[]{:S(2)}, u32[]{:S(2)}) collective-permute-start(bf16[16,4096]{1,0:T(8,128)(2,1)S(1)} %constant_dynamic-slice_fusion), channel_id=1, source_target_pairs={{0,1},{1,2},{2,3},{4,5},{5,6},{6,7},{8,9},{9,10},{10,11},{12,13},{... | collective-permute-start | bytes 393224 | tf_op jit(solution)/shard_map/ppermute | solution.py:381
  16.1 20.8 %collective-permute-start.1 = (bf16[3,256,256]{2,1,0:T(8,128)(2,1)}, bf16[3,256,256]{2,1,0:T(8,128)(2,1)S(1)}, u32[]{:S(2)}, u32[]{:S(2)}) collective-permute-start(bf16[3,256,256]{2,1,0:T(8,128)(2,1)} %get-tuple-element.121), channel_id=1, source_target_pairs={{0,1},{1,0},{2,3},{3,2},{4,5},{5,4},{6,7},{7,6},{8,9},{9,8},{10,11... | collective-permute-start | bytes 1179656 | tf_op jit(solution)/shard_map/ppermute | solution.py:38
  17.6 19.3 %collective-permute-start.2 = (bf16[3,256,256]{2,1,0:T(8,128)(2,1)}, bf16[3,256,256]{2,1,0:T(8,128)(2,1)S(1)}, u32[]{:S(2)}, u32[]{:S(2)}) collective-permute-start(bf16[3,256,256]{2,1,0:T(8,128)(2,1)} %get-tuple-element.123), channel_id=1, source_target_pairs={{0,2},{1,3},{2,0},{3,1},{4,6},{5,7},{6,4},{7,5},{8,10},{9,11},{10,... | collective-permute-start | bytes 1179656 | tf_op jit(solution)/shard_map/ppermute | solution.py:38
  17.6 19.3 %collective-permute-start.3 = (bf16[3,256,256]{2,1,0:T(8,128)(2,1)}, bf16[3,256,256]{2,1,0:T(8,128)(2,1)}, u32[]{:S(2)}, u32[]{:S(2)}) collective-permute-start(bf16[3,256,256]{2,1,0:T(8,128)(2,1)} %get-tuple-element.120), channel_id=1, source_target_pairs={{0,3},{1,2},{2,1},{3,0},{4,7},{5,6},{6,5},{7,4},{8,11},{9,10},{10,... | collective-permute-start | bytes 1179656 | tf_op jit(solution)/shard_map/ppermute | solution.py:38
  20.4 1.8 copy-start.15
  22.3 0.7 copy-start.8
  22.3 0.7 copy-start.9
  36.9 28.6 %collective-permute-start.6 = (bf16[272,4096]{1,0:T(8,128)(2,1)}, bf16[272,4096]{1,0:T(8,128)(2,1)}, u32[]{:S(2)}, u32[]{:S(2)}) collective-permute-start(bf16[272,4096]{1,0:T(8,128)(2,1)} %get-tuple-element.73.act_ref), channel_id=1, source_target_pairs={{0,16},{16,0},{1,17},{17,1},{2,18},{18,2},{3,19},{19,3},{4,20},{20... | collective-permute-start | bytes 6684680 | tf_op jit(solution)/shard_map/ppermute | solution.py:38
  37.0 61.9 %collective-permute-start.4 = (bf16[272,4096]{1,0:T(8,128)(2,1)}, bf16[272,4096]{1,0:T(8,128)(2,1)}, u32[]{:S(2)}, u32[]{:S(2)}) collective-permute-start(bf16[272,4096]{1,0:T(8,128)(2,1)} %get-tuple-element.73.act_ref), channel_id=1, source_target_pairs={{0,1},{1,0},{2,3},{3,2},{4,5},{5,4},{6,7},{7,6},{8,9},{9,8},{10,11... | collective-permute-start | bytes 6684680 | tf_op jit(solution)/shard_map/ppermute | solution.py:38
  38.5 60.4 %collective-permute-start.5 = (bf16[272,4096]{1,0:T(8,128)(2,1)}, bf16[272,4096]{1,0:T(8,128)(2,1)}, u32[]{:S(2)}, u32[]{:S(2)}) collective-permute-start(bf16[272,4096]{1,0:T(8,128)(2,1)} %get-tuple-element.73.act_ref), channel_id=1, source_target_pairs={{0,2},{1,3},{2,0},{3,1},{4,6},{5,7},{6,4},{7,5},{8,10},{9,11},{10,... | collective-permute-start | bytes 6684680 | tf_op jit(solution)/shard_map/ppermute | solution.py:38
  41.0 56.0 %collective-permute-start.7 = (bf16[4,3,256,256]{3,2,1,0:T(8,128)(2,1)}, bf16[4,3,256,256]{3,2,1,0:T(8,128)(2,1)}, u32[]{:S(2)}, u32[]{:S(2)}) collective-permute-start(bf16[4,3,256,256]{3,2,1,0:T(8,128)(2,1)} %pad_maximum_fusion.3.refs_0_), channel_id=1, source_target_pairs={{0,4},{4,8},{8,12},{1,5},{5,9},{9,13},{2,6},{6,10},{10,14},{3,7},{... | collective-permute-start | bytes 4718600 | tf_op jit(solution)/shard_map/ppermute | solution.py:381
  45.6 53.3 %collective-permute-start.8 = (bf16[4,3,256,256]{3,2,1,0:T(8,128)(2,1)}, bf16[4,3,256,256]{3,2,1,0:T(8,128)(2,1)}, u32[]{:S(2)}, u32[]{:S(2)}) collective-permute-start(bf16[4,3,256,256]{3,2,1,0:T(8,128)(2,1)} %pad_maximum_fusion.3.refs_0_), channel_id=1, source_target_pairs={{4,0},{8,4},{12,8},{5,1},{9,5},{13,9},{6,2},{10,6},{14,10},{7,3},{... | collective-permute-start | bytes 4718600 | tf_op jit(solution)/shard_map/ppermute | solution.py:381
  47.0 136.1 %copy-start.5 = (s32[3]{0:T(128)}, s32[3]{0:T(128)S(1)}, u32[]{:S(2)}) copy-start(s32[3]{0:T(128)S(1)} %pad_add_fusion.where_ref) | copy-start | bytes 40
  103.7 52.1 %collective-permute-start.11 = (bf16[2,272,4096]{2,1,0:T(8,128)(2,1)}, bf16[2,272,4096]{2,1,0:T(8,128)(2,1)}, u32[]{:S(2)}, u32[]{:S(2)}) collective-permute-start(bf16[2,272,4096]{2,1,0:T(8,128)(2,1)} %pad_maximum_fusion), channel_id=1, source_target_pairs={{0,16},{16,0},{1,17},{17,1},{2,18},{18,2},{3,19},{19,3},{4,20},{20... | collective-permute-start | bytes 13369352 | tf_op jit(solution)/shard_map/ppermute | solution.py:38
  103.7 52.1 %collective-permute-start.9 = (bf16[272,4096]{1,0:T(8,128)(2,1)}, bf16[272,4096]{1,0:T(8,128)(2,1)}, u32[]{:S(2)}, u32[]{:S(2)}) collective-permute-start(bf16[272,4096]{1,0:T(8,128)(2,1)} %get-tuple-element.73.act_ref), channel_id=1, source_target_pairs={{0,3},{1,2},{2,1},{3,0},{4,7},{5,6},{6,5},{7,4},{8,11},{9,10},{10,... | collective-permute-start | bytes 6684680 | tf_op jit(solution)/shard_map/ppermute | solution.py:38
  106.1 38.1 %collective-permute-start.12 = (bf16[4,3,256,256]{3,2,1,0:T(8,128)(2,1)}, bf16[4,3,256,256]{3,2,1,0:T(8,128)(2,1)}, u32[]{:S(2)}, u32[]{:S(2)}) collective-permute-start(bf16[4,3,256,256]{3,2,1,0:T(8,128)(2,1)} %collective-permute-done.7.refs_1_), channel_id=1, source_target_pairs={{0,4},{4,8},{8,12},{1,5},{5,9},{9,13},{2,6},{6,10},{10,14},{3,7},{... | collective-permute-start | bytes 4718600 | tf_op jit(solution)/shard_map/ppermute | solution.py:381
  111.0 38.4 %collective-permute-start.13 = (bf16[4,3,256,256]{3,2,1,0:T(8,128)(2,1)}, bf16[4,3,256,256]{3,2,1,0:T(8,128)(2,1)}, u32[]{:S(2)}, u32[]{:S(2)}) collective-permute-start(bf16[4,3,256,256]{3,2,1,0:T(8,128)(2,1)} %collective-permute-done.8.refs_2_), channel_id=1, source_target_pairs={{4,0},{8,4},{12,8},{5,1},{9,5},{13,9},{6,2},{10,6},{14,10},{7,3},{... | collective-permute-start | bytes 4718600 | tf_op jit(solution)/shard_map/ppermute | solution.py:381
  114.0 12.8 %collective-permute-start.10 = (bf16[2,1024,256]{2,1,0:T(8,128)(2,1)S(1)}, bf16[2,1024,256]{2,1,0:T(8,128)(2,1)S(1)}, u32[]{:S(2)}, u32[]{:S(2)}) collective-permute-start(bf16[2,1024,256]{2,1,0:T(8,128)(2,1)S(1)} %get-tuple-element.125), channel_id=1, source_target_pairs={{0,16},{16,0},{1,17},{17,1},{2,18},{18,2},{3,19},{19,3},{4,20},{20... | collective-permute-start | bytes 3145736 | tf_op jit(solution)/shard_map/ppermute | solution.py:38
  155.8 27.4 %collective-permute-start.14 = (bf16[272,4096]{1,0:T(8,128)(2,1)}, bf16[272,4096]{1,0:T(8,128)(2,1)S(1)}, u32[]{:S(2)}, u32[]{:S(2)}) collective-permute-start(bf16[272,4096]{1,0:T(8,128)(2,1)} %collective-permute-done.9.act_ref), channel_id=1, source_target_pairs={{0,16},{16,0},{1,17},{17,1},{2,18},{18,2},{3,19},{19,3},{4,20},{20... | collective-permute-start | bytes 6684680 | tf_op jit(solution)/shard_map/ppermute | solution.py:38
  155.8 38.5 %collective-permute-start.15 = (bf16[4,3,256,256]{3,2,1,0:T(8,128)(2,1)}, bf16[4,3,256,256]{3,2,1,0:T(8,128)(2,1)S(1)}, u32[]{:S(2)}, u32[]{:S(2)}) collective-permute-start(bf16[4,3,256,256]{3,2,1,0:T(8,128)(2,1)} %collective-permute-done.12.refs_3_), channel_id=1, source_target_pairs={{0,4},{4,8},{8,12},{1,5},{5,9},{9,13},{2,6},{6,10},{10,14},{3,7},{... | collective-permute-start | bytes 4718600 | tf_op jit(solution)/shard_map/ppermute | solution.py:381
  159.7 38.6 %collective-permute-start.16 = (bf16[4,3,256,256]{3,2,1,0:T(8,128)(2,1)}, bf16[4,3,256,256]{3,2,1,0:T(8,128)(2,1)S(1)}, u32[]{:S(2)}, u32[]{:S(2)}) collective-permute-start(bf16[4,3,256,256]{3,2,1,0:T(8,128)(2,1)} %collective-permute-done.13.refs_4_), channel_id=1, source_target_pairs={{4,0},{8,4},{12,8},{5,1},{9,5},{13,9},{6,2},{10,6},{14,10},{7,3},{... | collective-permute-start | bytes 4718600 | tf_op jit(solution)/shard_map/ppermute | solution.py:381
  161.2 107.7 %collective-permute-start.17 = (bf16[2,2,1024,256]{3,2,1,0:T(8,128)(2,1)}, bf16[2,2,1024,256]{3,2,1,0:T(8,128)(2,1)}, u32[]{:S(2)}, u32[]{:S(2)}) collective-permute-start(bf16[2,2,1024,256]{3,2,1,0:T(8,128)(2,1)} %pad_maximum_fusion.2.refs_0_), channel_id=1, source_target_pairs={{0,1},{1,0},{2,3},{3,2},{4,5},{5,4},{6,7},{7,6},{8,9},{9,8},{10,11... | collective-permute-start | bytes 6291464 | tf_op jit(solution)/shard_map/ppermute | solution.py:38
  162.7 106.2 %collective-permute-start.18 = (bf16[2,2,1024,256]{3,2,1,0:T(8,128)(2,1)}, bf16[2,2,1024,256]{3,2,1,0:T(8,128)(2,1)}, u32[]{:S(2)}, u32[]{:S(2)}) collective-permute-start(bf16[2,2,1024,256]{3,2,1,0:T(8,128)(2,1)} %pad_maximum_fusion.2.refs_0_), channel_id=1, source_target_pairs={{0,2},{1,3},{2,0},{3,1},{4,6},{5,7},{6,4},{7,5},{8,10},{9,11},{10,... | collective-permute-start | bytes 6291464 | tf_op jit(solution)/shard_map/ppermute | solution.py:38
  194.2 4.1 %copy-start.12 = (bf16[4,3,256,256]{3,2,1,0:T(8,128)(2,1)}, bf16[4,3,256,256]{3,2,1,0:T(8,128)(2,1)S(1)}, u32[]{:S(2)}) copy-start(bf16[4,3,256,256]{3,2,1,0:T(8,128)(2,1)S(1)} %collective-permute-done.15.refs_5_) | copy-start | bytes 4718596
  198.3 1.2 copy-start.13
  199.5 69.4 %collective-permute-start.19 = (bf16[2,2,1024,256]{3,2,1,0:T(8,128)(2,1)}, bf16[2,2,1024,256]{3,2,1,0:T(8,128)(2,1)S(1)}, u32[]{:S(2)}, u32[]{:S(2)}) collective-permute-start(bf16[2,2,1024,256]{3,2,1,0:T(8,128)(2,1)} %pad_maximum_fusion.2.refs_0_), channel_id=1, source_target_pairs={{0,3},{1,2},{2,1},{3,0},{4,7},{5,6},{6,5},{7,4},{8,11},{9,10},{10,... | collective-permute-start | bytes 6291464 | tf_op jit(solution)/shard_map/ppermute | solution.py:38
  205.0 25.5 %copy-start.3 = (bf16[520,128]{1,0:T(8,128)(2,1)S(1)}, bf16[520,128]{1,0:T(8,128)(2,1)}, u32[]{:S(2)}) copy-start(bf16[520,128]{1,0:T(8,128)(2,1)} %constant.70.clone.sums_ref) | copy-start | bytes 399364
  205.0 25.6 %copy-start.4 = (bf16[256,256]{1,0:T(8,128)(2,1)S(1)}, bf16[256,256]{1,0:T(8,128)(2,1)}, u32[]{:S(2)}) copy-start(bf16[256,256]{1,0:T(8,128)(2,1)} %constant.72.clone.same_ref) | copy-start | bytes 393220
  205.0 25.6 %copy-start.6 = (s32[3]{0:T(128)S(1)}, s32[3]{0:T(128)}, u32[]{:S(2)}) copy-start(s32[3]{0:T(128)} %copy-done.5) | copy-start | bytes 40
  205.0 25.6 %copy-start.7 = (f32[64,256]{1,0:T(8,128)S(1)}, f32[64,256]{1,0:T(8,128)}, u32[]{:S(2)}) copy-start(f32[64,256]{1,0:T(8,128)} %constant.71.clone.level_ref) | copy-start | bytes 196612
  205.0 25.6 %copy-start.10 = (s32[2]{0:T(128)S(1)}, s32[2]{0:T(128)}, u32[]{:S(2)}) copy-start(s32[2]{0:T(128)} %extent_ref.1) | copy-start | bytes 28
  230.6 1.9 copy-start.2
  268.9 13.9 %copy-start.11 = (bf16[2,2,1024,256]{3,2,1,0:T(8,128)(2,1)}, bf16[2,2,1024,256]{3,2,1,0:T(8,128)(2,1)S(1)}, u32[]{:S(2)}) copy-start(bf16[2,2,1024,256]{3,2,1,0:T(8,128)(2,1)S(1)} %collective-permute-done.19.refs_3_) | copy-start | bytes 6291460
  270.0 11.9 %collective-permute-start.22 = (bf16[640,256]{1,0:T(8,128)(2,1)}, bf16[640,256]{1,0:T(8,128)(2,1)}, u32[]{:S(2)}, u32[]{:S(2)}) collective-permute-start(bf16[640,256]{1,0:T(8,128)(2,1)} %get-tuple-element.129), channel_id=1, source_target_pairs={{0,3},{1,2},{2,1},{3,0},{4,7},{5,6},{6,5},{7,4},{8,11},{9,10},{10,... | collective-permute-start | bytes 983048 | tf_op jit(solution)/shard_map/ppermute | solution.py:38
  270.5 15.7 %collective-permute-start.21 = (bf16[640,256]{1,0:T(8,128)(2,1)S(1)}, bf16[640,256]{1,0:T(8,128)(2,1)}, u32[]{:S(2)}, u32[]{:S(2)}) collective-permute-start(bf16[640,256]{1,0:T(8,128)(2,1)S(1)} %get-tuple-element.128), channel_id=1, source_target_pairs={{0,2},{1,3},{2,0},{3,1},{4,6},{5,7},{6,4},{7,5},{8,10},{9,11},{10,... | collective-permute-start | bytes 983048 | tf_op jit(solution)/shard_map/ppermute | solution.py:38
  272.0 15.2 %collective-permute-start.20 = (bf16[640,256]{1,0:T(8,128)(2,1)S(1)}, bf16[640,256]{1,0:T(8,128)(2,1)S(1)}, u32[]{:S(2)}, u32[]{:S(2)}) collective-permute-start(bf16[640,256]{1,0:T(8,128)(2,1)S(1)} %get-tuple-element.127), channel_id=1, source_target_pairs={{0,1},{1,0},{2,3},{3,2},{4,5},{5,4},{6,7},{7,6},{8,9},{9,8},{10,11... | collective-permute-start | bytes 983048 | tf_op jit(solution)/shard_map/ppermute | solution.py:38
  287.4 6.2 %collective-permute-start.23 = (bf16[4,512,256]{2,1,0:T(8,128)(2,1)S(1)}, bf16[4,512,256]{2,1,0:T(8,128)(2,1)S(1)}, u32[]{:S(2)}, u32[]{:S(2)}) collective-permute-start(bf16[4,512,256]{2,1,0:T(8,128)(2,1)S(1)} %pad_maximum_fusion.4.own_ref), channel_id=1, source_target_pairs={{0,16},{16,0},{1,17},{17,1},{2,18},{18,2},{3,19},{19,3},{4,20},{20... | collective-permute-start | bytes 3145736 | tf_op jit(solution)/shard_map/ppermute | solution.py:38
  293.6 8.9 %copy-start.1 = (bf16[4096,128]{1,0:T(8,128)(2,1)S(1)}, bf16[4096,128]{1,0:T(8,128)(2,1)}, u32[]{:S(2)}) copy-start(bf16[4096,128]{1,0:T(8,128)(2,1)} %param.21) | copy-start | bytes 3145732
Sparse Core Ops, SparseCore 0:
  20.6 60.7 all-gather.2

commit v4 on v3

--- a/solution.py
+++ b/solution.py
@@ -59,11 +59,13 @@
         cur_ref[rows:, :] = jnp.concatenate([high, (c - high.astype(f32)).astype(bf16)], axis=0)
 
     perm = perm_ref[...]
+    high, low = perm // depth, (perm % depth).astype(bf16)
+    lines = lax.broadcasted_iota(jnp.int32, (depth, block), 0).astype(bf16)
+    one, none = jnp.ones((depth, block), bf16), jnp.zeros((depth, block), bf16)
     total = jnp.zeros((rows + 2 * PREFIX, block), f32)
     for k in range(width // depth):
-        lines = lax.broadcasted_iota(jnp.int32, (depth, block), 0) + k * depth
-        chosen = jnp.where(lines == perm, 1.0, 0.0).astype(bf16)
-        total += dot(cur_ref[:, k * depth : (k + 1) * depth], chosen)
+        mine = jnp.where(high == k, low, jnp.full_like(low, -1.0))
+        total += dot(cur_ref[:, k * depth : (k + 1) * depth], jnp.where(lines == mine, one, none))
     out_ref[...] = total[:rows].astype(bf16)
     coeff_out_ref[...] = total[rows : rows + PREFIX] + total[rows + PREFIX :]
 
@@ -156,39 +158,48 @@
 def project_kernel(where_ref, act_ref, *refs):
     *hops, out_ref, lines_ref = refs
     stretches, _, depth, _ = hops[0].shape
-    reqs = (len(hops) + 1) // 2
-
-    def place(hop_ref, r):
+    reqs = lines_ref.shape[0] // (stretches * depth)
+    reach = len(hops) // 2
+
+    def place(r, values):
         for d in range(stretches):
             at = (r * stretches + (where_ref[0] ^ d)) * depth
-            lines_ref[pl.ds(pl.multiple_of(at, depth), depth), :] = hop_ref[d, 0]
+            lines_ref[pl.ds(pl.multiple_of(at, depth), depth), :] = values(d)
 
     @pl.when(pl.program_id(1) == 0)
     def _():
         me = where_ref[2]
-        place(hops[0], me)
+        place(me, lambda d: hops[0][d, 0])
         for hop in range(1, reqs):
-
-            @pl.when(me >= hop)
-            def _():
-                place(hops[2 * hop - 1], me - hop)
-
-            @pl.when(me + hop < reqs)
-            def _():
-                place(hops[2 * hop], me + hop)
+            for r, ref in ((me - hop, 2 * hop - 1), (me + hop, 2 * hop)):
+
+                @pl.when((r >= 0) & (r < reqs))
+                def _():
+                    if hop > reach:
+                        place(r, lambda d: jnp.zeros_like(hops[0][d, 0]))
+                    else:
+                        place(r, lambda d: hops[ref][d, 0])
 
     act = act_ref[0, 0].reshape(-1, act_ref.shape[-1])
-    out_ref[0, 0] = dot(act, lines_ref[...]).astype(bf16).reshape(out_ref.shape[2:])
+    out_ref[0, 0] = dot(act, lines_ref[...]).reshape(out_ref.shape[2:])
+
+
+def last_kernel(where_ref, act_ref, part_ref, below_ref, above_ref, out_ref, lines_ref):
+    stretches, _, depth, _ = below_ref.shape
+
+    @pl.when(pl.program_id(1) == 0)
+    def _():
+        for d in range(stretches):
+            at = (where_ref[0] ^ d) * depth
+            lines_ref[pl.ds(pl.multiple_of(at, depth), depth), :] = below_ref[d, 0] + above_ref[d, 0]
+
+    act = act_ref[0, 0].reshape(-1, act_ref.shape[-1])
+    out_ref[0, 0] = (part_ref[0, 0] + dot(act, lines_ref[...]).reshape(out_ref.shape[2:])).astype(bf16)
 
 
 def projected(where, mixed, hops):
     stretches, kinds, depth, cols = hops[0].shape
     _, sides, _, span, width = mixed.shape
-    if depth % 128:
-        (lines,) = hops[1:]
-        lines = lines[:, jnp.arange(stretches) ^ where[0]]
-        lines = jnp.transpose(lines, (2, 0, 1, 3, 4)).reshape(kinds, width, cols)
-        return jnp.einsum("jxbtk,jkc->jxbtc", mixed, lines, preferred_element_type=f32).astype(bf16)
     return pl.pallas_call(
         project_kernel,
         grid_spec=pltpu.PrefetchScalarGridSpec(
@@ -199,10 +210,43 @@
             out_specs=pl.BlockSpec((1, 1, stretches, span, cols), lambda j, m, w: (j, m, 0, 0, 0)),
             scratch_shapes=[pltpu.VMEM((width, cols), bf16)],
         ),
+        out_shape=jax.ShapeDtypeStruct((kinds, sides, stretches, span, cols), f32),
+        compiler_params=vmem(60),
+        cost_estimate=SMALL,
+    )(where, mixed, *hops)
+
+
+def completed(where, mixed, part, below, above):
+    stretches, kinds, depth, cols = below.shape
+    _, sides, _, span, width = mixed.shape
+    share = stretches * depth
+    last = width // share - 1
+
+    def act_block(j, m, w):
+        return (j, m, 0, 0, jnp.where(w[2] == last, 0, last))
+
+    block = pl.BlockSpec((1, 1, stretches, span, cols), lambda j, m, w: (j, m, 0, 0, 0))
+    line_block = pl.BlockSpec((stretches, 1, depth, cols), lambda j, m, w: (0, j, 0, 0))
+    return pl.pallas_call(
+        last_kernel,
+        grid_spec=pltpu.PrefetchScalarGridSpec(
+            num_scalar_prefetch=1,
+            grid=(kinds, sides),
+            in_specs=[pl.BlockSpec((1, 1, stretches, span, share), act_block), block, line_block, line_block],
+            out_specs=block,
+            scratch_shapes=[pltpu.VMEM((share, cols), bf16)],
+        ),
         out_shape=jax.ShapeDtypeStruct((kinds, sides, stretches, span, cols), bf16),
         compiler_params=vmem(60),
         cost_estimate=SMALL,
-    )(where, mixed, *hops)
+    )(where, mixed, part, below, above)
+
+
+def projected_whole(where, mixed, lines):
+    _, stretches, kinds, depth, cols = lines.shape
+    lines = lines[:, jnp.arange(stretches) ^ where[0]]
+    lines = jnp.transpose(lines, (2, 0, 1, 3, 4)).reshape(kinds, mixed.shape[-1], cols)
+    return jnp.einsum("jxbtk,jkc->jxbtc", mixed, lines, preferred_element_type=f32).astype(bf16)
 
 
 def decay_sums():
@@ -229,12 +273,11 @@
 
 def wkv_kernel(
     extent_ref, where_ref, proj_ref, lora_ref, right_ref, speed_ref, reward_ref, scale_ref, sums_ref, level_ref,
-    same_ref, normed_ref, state_ref, memory_ref,
+    same_ref, normed_ref, state_ref, memory_ref, *, prompt,
 ):
     step = pl.program_id(0)
     tokens, cols = proj_ref.shape[3:]
     heads = cols // ATTEND_DIM
-    per_block = pl.num_programs(0) // lax.axis_size("seq")
     same = same_ref[...]
     same_f32 = same.astype(f32)
     level = level_ref[...]
@@ -243,61 +286,51 @@
     def _():
         memory_ref[...] = jnp.zeros_like(memory_ref)
 
-    memories = [memory_ref[0], memory_ref[1]]
+    at = step * tokens + lax.broadcasted_iota(jnp.int32, (tokens, cols), 0)
+    valid = jnp.where(at < extent_ref[prompt], 1.0, 0.0)
+    r = proj_ref[0, 0, 0]
+    k = proj_ref[1, 0, 0] * valid.astype(bf16)
+    v = proj_ref[2, 0, 0]
+    decay = -speed_ref[...] * jnp.exp(dot(lora_ref[0, 0], right_ref[...])) * valid
+    high = decay.astype(bf16)
+    low = (decay - high.astype(f32)).astype(bf16)
+    own = dot((r.astype(f32) * reward_ref[...] * k.astype(f32)).astype(bf16), same) * v.astype(f32)
+
+    memory = memory_ref[...]
+    rows = []
     for sub in range(tokens // CHUNK):
         lines = slice(sub * CHUNK, (sub + 1) * CHUNK)
-        at = step * tokens + sub * CHUNK + lax.broadcasted_iota(jnp.int32, (CHUNK, cols), 0)
-        for side in range(2):
-            prompt = where_ref[1] ^ side
-            valid = jnp.where(at < extent_ref[prompt], 1.0, 0.0)
-            r = proj_ref[0, side, 0, lines].astype(f32)
-            k = proj_ref[1, side, 0, lines].astype(f32) * valid
-            v = proj_ref[2, side, 0, lines]
-            decay = -speed_ref[...] * jnp.exp(dot(lora_ref[side, 0, lines], right_ref[...])) * valid
-            high = decay.astype(bf16)
-            low = (decay - high.astype(f32)).astype(bf16)
-            kept = jnp.exp(dot(sums_ref[...], jnp.concatenate([high, low], axis=0)))
-            scores = jnp.zeros((CHUNK, heads * CHUNK), f32)
-            for bit in range(LEVELS):
-                part = kept[bit * CHUNK : (bit + 1) * CHUNK]
-                lookup = (k * part).astype(bf16)
-                lookup = jnp.concatenate([lookup] * heads, axis=0) * same
-                found = dot_nt((r * part).astype(bf16), lookup)
-                scores = jnp.where(level == bit, found, scores)
-            v_heads = jnp.concatenate([v] * heads, axis=0) * same
-            memory = memories[side]
-            from_start = (r * kept[LEVELS * CHUNK : (LEVELS + 1) * CHUNK]).astype(bf16)
-            to_end = (k * kept[(LEVELS + 1) * CHUNK : (LEVELS + 2) * CHUNK]).astype(bf16)
-            own = dot((r * reward_ref[...] * k).astype(bf16), same)
-            y = dot_nt(from_start, memory.astype(bf16)) + dot(scores.astype(bf16), v_heads)
-            y += own * v.astype(f32)
-            whole = kept[(LEVELS + 2) * CHUNK : (LEVELS + 2) * CHUNK + 1]
-            memories[side] = memory * whole + same_f32 * dot_tn(v, to_end)
-
-            y_high = y.astype(bf16)
-            y_low = (y - y_high.astype(f32)).astype(bf16)
-            centred = y - (dot(y_high, same) + dot(y_low, same)) * (1.0 / ATTEND_DIM)
-            spread = dot((centred * centred).astype(bf16), same) * (1.0 / ATTEND_DIM)
-            normed = centred * lax.rsqrt(spread + eps) * scale_ref[...] * valid
-            normed_ref[0, pl.ds(prompt, 1), lines] = normed.astype(bf16)[None]
-    for side in range(2):
-        memory_ref[side] = memories[side]
-
-    @pl.when(step % per_block == per_block - 1)
-    def _():
-        for side in range(2):
-            folded = memory_ref[side, :ATTEND_DIM]
-            for h in range(1, heads):
-                folded += memory_ref[side, h * ATTEND_DIM : (h + 1) * ATTEND_DIM]
-            state_ref[0, pl.ds(where_ref[1] ^ side, 1)] = folded[None]
-
-
-def recurrence(extents, where, proj, lora, right, speed, reward, scale):
-    _, reqs, stretches, span, cols = proj.shape
+        r_sub, k_sub, v_sub = r[lines], k[lines], v[lines]
+        kept = jnp.exp(dot(sums_ref[...], jnp.concatenate([high[lines], low[lines]], axis=0)))
+        scores = jnp.zeros((CHUNK, heads * CHUNK), f32)
+        for bit in range(LEVELS):
+            part = kept[bit * CHUNK : (bit + 1) * CHUNK].astype(bf16)
+            lookup = jnp.concatenate([k_sub * part] * heads, axis=0) * same
+            scores = jnp.where(level == bit, dot_nt(r_sub * part, lookup), scores)
+        v_heads = jnp.concatenate([v_sub] * heads, axis=0) * same
+        from_start = r_sub * kept[LEVELS * CHUNK : (LEVELS + 1) * CHUNK].astype(bf16)
+        to_end = k_sub * kept[(LEVELS + 1) * CHUNK : (LEVELS + 2) * CHUNK].astype(bf16)
+        whole = kept[(LEVELS + 2) * CHUNK : (LEVELS + 2) * CHUNK + 1]
+        rows.append(dot_nt(from_start, memory.astype(bf16)) + dot(scores.astype(bf16), v_heads))
+        memory = memory * whole + same_f32 * dot_tn(v_sub, to_end)
+    memory_ref[...] = memory
+    folded = memory[:ATTEND_DIM]
+    for h in range(1, heads):
+        folded += memory[h * ATTEND_DIM : (h + 1) * ATTEND_DIM]
+    state_ref[0] = folded
+
+    y = jnp.concatenate(rows, axis=0) + own
+    y_high = y.astype(bf16)
+    y_low = (y - y_high.astype(f32)).astype(bf16)
+    centred = y - (dot(y_high, same) + dot(y_low, same)) * (1.0 / ATTEND_DIM)
+    spread = dot((centred * centred).astype(bf16), same) * (1.0 / ATTEND_DIM)
+    normed_ref[0] = (centred * lax.rsqrt(spread + eps) * scale_ref[...] * valid).astype(bf16)
+
+
+def recurrence(prompt, extents, where, proj, lora, right, speed, reward, scale):
+    _, _, stretches, span, cols = proj.shape
     inner = lora.shape[-1]
     heads = cols // ATTEND_DIM
-    tokens = 2 * CHUNK
-    per_block = span // tokens
     sums = jnp.asarray(decay_sums(), bf16)
     level = jnp.asarray(pair_levels(heads), f32)
     head = np.arange(cols) // ATTEND_DIM
@@ -308,24 +341,24 @@
 
     tables = (right, speed, reward, scale, sums, level, same)
     return pl.pallas_call(
-        wkv_kernel,
+        functools.partial(wkv_kernel, prompt=prompt),
         grid_spec=pltpu.PrefetchScalarGridSpec(
             num_scalar_prefetch=2,
-            grid=(stretches * per_block,),
+            grid=(stretches,),
             in_specs=[
-                pl.BlockSpec((3, reqs, 1, tokens, cols), lambda c, e, w: (0, 0, c // per_block, c % per_block, 0)),
-                pl.BlockSpec((reqs, 1, tokens, inner), lambda c, e, w: (0, c // per_block, c % per_block, 0)),
+                pl.BlockSpec((3, 1, 1, span, cols), lambda c, e, w: (0, w[1] ^ prompt, c, 0, 0)),
+                pl.BlockSpec((1, 1, span, inner), lambda c, e, w: (w[1] ^ prompt, c, 0, 0)),
             ]
             + [fixed(a) for a in tables],
             out_specs=[
-                pl.BlockSpec((1, reqs, tokens, cols), lambda c, e, w: (c // per_block, 0, c % per_block, 0)),
-                pl.BlockSpec((1, reqs, ATTEND_DIM, cols), lambda c, e, w: (c // per_block, 0, 0, 0)),
+                pl.BlockSpec((1, span, cols), lambda c, e, w: (c, 0, 0)),
+                pl.BlockSpec((1, ATTEND_DIM, cols), lambda c, e, w: (c, 0, 0)),
             ],
-            scratch_shapes=[pltpu.VMEM((reqs, cols, cols), f32)],
+            scratch_shapes=[pltpu.VMEM((cols, cols), f32)],
         ),
         out_shape=[
-            jax.ShapeDtypeStruct((stretches, reqs, span, cols), bf16),
-            jax.ShapeDtypeStruct((stretches, reqs, ATTEND_DIM, cols), f32),
+            jax.ShapeDtypeStruct((stretches, span, cols), bf16),
+            jax.ShapeDtypeStruct((stretches, ATTEND_DIM, cols), f32),
         ],
         compiler_params=vmem(40),
         cost_estimate=SMALL,
@@ -333,32 +366,32 @@
 
 
 def finish_kernel(where_ref, x_ref, own_ref, far_ref, *refs):
-    *weights, out_ref = refs
+    weights, out_ref = refs[:4], refs[-1]
     stretches, rows, cols = own_ref.shape
     chunk = weights[0].shape[-1]
     for e in range(stretches):
-        total = x_ref[:, pl.ds(pl.multiple_of((where_ref[0] ^ e) * chunk, chunk), chunk)].astype(f32)
+        places = pl.ds(pl.multiple_of((where_ref[0] ^ e) * chunk, chunk), chunk)
+        total = x_ref[:, places].astype(f32)
         for side, lines_ref in enumerate((own_ref, far_ref)):
-            w_ref = weights[e]
             for d in range(stretches):
                 at = pl.ds(pl.multiple_of((where_ref[0] ^ d) * cols, cols), cols)
-                total += dot(lines_ref[d], w_ref[side, 0, at, :])
-        out_ref[:, pl.ds(pl.multiple_of((where_ref[0] ^ e) * chunk, chunk), chunk)] = total.astype(bf16)
-
-
-def finished(where, x, own, far, weights):
+                total += dot(lines_ref[d], weights[e][side, 0, at, :])
+        out_ref[0, :, places] = total.astype(bf16)
+
+
+def finished(prompt, prompts, where, x, own, far, weights, earlier):
     stretches, rows, cols = own.shape
-    width = x.shape[1]
     _, groups, depth, chunk = weights[0].shape
     share = groups * stretches * chunk
     if chunk % 128:
         order = jnp.arange(stretches) ^ where[0]
-        total = lax.dynamic_slice_in_dim(x, where[1] * share, share, 1).astype(f32)
+        total = lax.dynamic_slice(x, (prompt * rows, where[1] * share), (rows, share)).astype(f32)
         for side, lines in enumerate((own, far)):
-            w = jnp.transpose(jnp.stack([w[side] for w in weights])[order], (2, 1, 0, 3)).reshape(depth, share)
+            w = jnp.stack([w[side] for w in weights])[order]
+            w = jnp.transpose(w, (2, 1, 0, 3)).reshape(depth, share)
             lines = jnp.transpose(lines[order], (1, 0, 2)).reshape(rows, depth)
             total += dot(lines, w)
-        return total.astype(bf16)
+        return jnp.concatenate([*earlier, total.astype(bf16)[None]], axis=0)
     block = stretches * chunk
     whole = pl.BlockSpec((stretches, rows, cols), lambda g, w: (0, 0, 0))
     return pl.pallas_call(
@@ -366,14 +399,16 @@
         grid_spec=pltpu.PrefetchScalarGridSpec(
             num_scalar_prefetch=1,
             grid=(groups,),
-            in_specs=[pl.BlockSpec((rows, block), lambda g, w: (0, w[1] * groups + g)), whole, whole]
-            + [pl.BlockSpec((2, 1, depth, chunk), lambda g, w: (0, g, 0, 0))] * len(weights),
-            out_specs=pl.BlockSpec((rows, block), lambda g, w: (0, g)),
+            in_specs=[pl.BlockSpec((rows, block), lambda g, w: (prompt, w[1] * groups + g)), whole, whole]
+            + [pl.BlockSpec((2, 1, depth, chunk), lambda g, w: (0, g, 0, 0))] * len(weights)
+            + [pl.BlockSpec(memory_space=pl.ANY)] * len(earlier),
+            out_specs=pl.BlockSpec((1, rows, block), lambda g, w: (prompt, 0, g)),
         ),
-        out_shape=jax.ShapeDtypeStruct((rows, share), bf16),
+        out_shape=jax.ShapeDtypeStruct((prompts, rows, share), bf16),
+        input_output_aliases={8: 0} if earlier else {},
         compiler_params=vmem(48),
         cost_estimate=SMALL,
-    )(where, x, own, far, *weights)
+    )(where, x, own, far, *weights, *earlier)
 
 
 def moved(value, axis, by):
@@ -440,61 +475,72 @@
     hops = [moved(lines, "req", 1), moved(lines, "req", -1)] if chained else [lax.all_gather(lines, "req", axis=0)]
     results = mixed_in(act, 0, 0, ())
     results = mixed_in(swapped(act, "tensor", 1), 1, 0, results)
+    share = groups // cores
+    out_lines, *results = tied(out_lines, *results)
+    kept = lax.dynamic_slice_in_dim(out_lines, t * share, share, 0)
+    given = lax.dynamic_slice_in_dim(out_lines, (1 - t) * share, share, 0)
+    out_lines = jnp.stack([kept, swapped(given, "tensor", 1)])
     near, other, out_lines, act, *rest = tied(near, other, out_lines, act, *results, *hops)
     results, hops = tuple(rest[:2]), rest[2:]
 
     across = swapped(act, "seq", 3)
     if chained:
         hops += [moved(hops[0], "req", 1), moved(hops[1], "req", -1)]
-    far = swapped(jnp.stack([near, other]), "tensor", 1)
     results = mixed_in(near, 0, 1, results)
     results = mixed_in(other, 0, 2, results)
-    share = groups // cores
-    kept = lax.dynamic_slice_in_dim(out_lines, t * share, share, 0)
-    given = lax.dynamic_slice_in_dim(out_lines, (1 - t) * share, share, 0)
-    out_lines = jnp.stack([kept, swapped(given, "tensor", 1)])
-    across, out_lines, far, *rest = tied(across, out_lines, far, *results, *hops)
+    results = mixed_in(swapped(near, "tensor", 1), 1, 1, results)
+    results = mixed_in(swapped(other, "tensor", 1), 1, 2, results)
+    across, out_lines, *rest = tied(across, out_lines, *results, *hops)
     results, hops = tuple(rest[:2]), rest[2:]
 
-    if chained:
-        hops += [moved(hops[2], "req", 1), moved(hops[3], "req", -1)]
     near, other = swapped(out_lines, "seq", 1), swapped(out_lines, "seq", 2)
+    ends = [moved(hops[2], "req", 1), moved(hops[3], "req", -1)] if chained else []
     last = swapped(across, "tensor", 1)
     results = mixed_in(across, 0, 3, results)
-    results = mixed_in(far[0], 1, 1, results)
-    results = mixed_in(far[1], 1, 2, results)
-    results = mixed_in(last, 1, 3, results)
-    mixed, lora, out_lines, *hops = tied(*results, out_lines, *hops)
+    mixed, lora = mixed_in(last, 1, 3, results)
+    if chained:
+        proj = projected(where, mixed, [lines, *hops])
+    else:
+        proj = projected_whole(where, mixed, *hops)
+    mixed, proj, out_lines, *ends = tied(mixed, proj, out_lines, *ends)
     across = swapped(out_lines, "seq", 3)
-
-    proj = projected(where, mixed, [lines, *hops])
+    if chained:
+        proj = completed(where, mixed, proj, *ends)
 
     def mine(array):
         return lax.dynamic_slice_in_dim(array, s * cols, cols, array.ndim - 1).reshape(-1, cols)
 
-    normed, states = recurrence(
-        prompt_extents, where, proj, lora, mine(fading_right_matrix), mine(feature_fading_speed), mine(self_reward),
-        mine(cluster_scaling_vector),
-    )
-
-    normed, states, near, other, across = tied(normed, states, near, other, across)
-    sent = jnp.concatenate(
-        [normed.reshape(stretches, rows, cols), states.reshape(stretches, -1, cols).astype(bf16)], axis=1
-    )
-    blocks = []
-    for d in range(stretches):
-        block = lax.dynamic_index_in_dim(sent, s ^ d, 0, keepdims=False)
-        blocks.append(swapped(block, "seq", d) if d else block)
-    own_lines = jnp.stack([block[:rows] for block in blocks])
-    far_lines = swapped(own_lines, "tensor", 1)
+    tables = [mine(a) for a in (fading_right_matrix, feature_fading_speed, self_reward, cluster_scaling_vector)]
+
+    def one_prompt(prompt, proj):
+        normed, states = recurrence(prompt, prompt_extents, where, proj, lora, *tables)
+        return jnp.concatenate([normed, states.astype(bf16)], axis=1)
+
+    def exchanged(block):
+        parts = [lax.dynamic_index_in_dim(block, s ^ d, 0, keepdims=False) for d in range(stretches)]
+        return parts[:1] + [swapped(parts[d], "seq", d) for d in range(1, stretches)]
+
+    def output(prompt, blocks, earlier):
+        own_lines = jnp.stack([block[:span] for block in blocks])
+        far_lines = swapped(own_lines, "tensor", 1)
+        return finished(prompt, reqs, where, x, own_lines, far_lines, out_weights, earlier)
+
+    block = one_prompt(0, proj)
+    block, near, other, proj = tied(block, near, other, proj)
+    first = exchanged(block)
+    block, across, *first = tied(one_prompt(1, proj), across, *first)
     out_weights = [out_lines, near, other, across]
-    hidden_out = finished(where, x, own_lines, far_lines, out_weights).reshape(reqs, span, width // cores)
+    second = exchanged(block)
+    hidden_out = output(0, first, ())
+    hidden_out, *second = tied(hidden_out, *second)
+    hidden_out = output(1, second, (hidden_out,))
+    stretch_blocks = [jnp.stack([block[span:] for block in blocks]) for blocks in (first, second)]
 
     heads = cols // ATTEND_DIM
-    states = jnp.stack([block[rows:] for block in blocks]).reshape(2, 2, reqs, ATTEND_DIM, heads, ATTEND_DIM)
-    states = jnp.where(s % 2 == 1, states[:, ::-1], states)
-    states = jnp.where(s // 2 == 1, states[::-1], states)
-    states = jnp.transpose(states, (2, 0, 1, 4, 5, 3)).astype(f32)
+    states = jnp.stack(stretch_blocks).reshape(reqs, 2, 2, ATTEND_DIM, heads, ATTEND_DIM)
+    states = jnp.where(s % 2 == 1, states[:, :, ::-1], states)
+    states = jnp.where(s // 2 == 1, states[:, ::-1], states)
+    states = jnp.transpose(states, (0, 1, 2, 4, 5, 3)).astype(f32)
     stretch_states = states.reshape(reqs, 1, stretches * heads, ATTEND_DIM * ATTEND_DIM)
     return (hidden_out, stretch_states)
 

time: 311 us -> 311 us (level)
  waiting for transfers between devices: 76.7 us -> 68.7 us
  other arithmetic: 11.2 us -> 5.62 us
  starting transfers between devices: 39.1 us -> 43.4 us
  local copies, waits for them, and re-layouts: 36.8 us -> 40.1 us
    ppermute x7, waiting for transfers between devices: 58.6 us -> 26 us  [moved(): lax.ppermute(value, axis, [(i, i + by) for i in range(peers) if 0 <= i +...]
    ppermute x17 -> x22, waiting for transfers between devices: 18 us -> 33.6 us  [swapped(): return lax.ppermute(value, axis, [(i, i ^ by) for i in range(peers)])]
    all_gather x1, waiting for transfers between devices: 0.01 us -> 9.15 us  [local(): out_lines = lax.all_gather(out_half, 'req', axis=0, tiled=False)]
    another operation x6 -> x15, local copies, waits for them, and re-layouts: 3.65 us -> 9.11 us  [the longest x6 4.8 us: output(): own_lines = jnp.stack([block[:span] for block in blocks])]
    another operation x3 -> x4, other arithmetic: 4.91 us -> 0.18 us  [the longest x2 0.14 us: output(): own_lines = jnp.stack([block[:span] for block in blocks])]
    pallas_call x1 -> x2, Pallas kernels: 8.9 us -> 12.8 us  [finished(): pl.pallas_call(finish_kernel, grid_spec=pltpu.PrefetchScalarGridSpec(num_...]
    ppermute x17 -> x22, starting transfers between devices: 16.6 us -> 19.8 us  [swapped(): return lax.ppermute(value, axis, [(i, i ^ by) for i in range(peers)])]
    pallas_call x1 -> x3, Pallas kernels: 36.4 us -> 37 us  [the longest x2 24.7 us: recurrence(): pl.pallas_call(functools.partial(wkv_kernel, prompt=prompt), grid_spec=pl...]
  transfers between devices with their start and end apart: 25 -> 30, of which waited for: 9 -> 8; matrix products, arithmetic and copies ran while one was open for 12% -> 10% of each run, Pallas kernels for 39% -> 42%
where the time goes in v4:
time: 311 us; the launch traced here: 307 us
  Pallas kernels  134 us (43%)
  waiting for transfers between devices  68.7 us (22%)
  starting transfers between devices  43.4 us (14%)
  local copies, waits for them, and re-layouts  40.1 us (13%)
  between operations  14.6 us (5%)
  other arithmetic  5.62 us (2%)
    pallas_call x8, Pallas kernels, shifted(): pl.pallas_call(mix_kernel, grid_spec=pltpu.PrefetchScalarGridSpec(num_sca...  45.1 us
    ppermute x22, waiting for transfers between devices, swapped(): return lax.ppermute(value, axis, [(i, i ^ by) for i in range(peers)])  33.6 us
    ppermute x7, waiting for transfers between devices, moved(): lax.ppermute(value, axis, [(i, i + by) for i in range(peers) if 0 <= i +...  26 us
    pallas_call x1, Pallas kernels, projected(): pl.pallas_call(project_kernel, grid_spec=pltpu.PrefetchScalarGridSpec(num...  25.4 us
    pallas_call x2, Pallas kernels, recurrence(): pl.pallas_call(functools.partial(wkv_kernel, prompt=prompt), grid_spec=pl...  24.7 us
    ppermute x7, starting transfers between devices, moved(): lax.ppermute(value, axis, [(i, i + by) for i in range(peers) if 0 <= i +...  23.6 us
    ppermute x22, starting transfers between devices, swapped(): return lax.ppermute(value, axis, [(i, i ^ by) for i in range(peers)])  19.8 us
    pallas_call x1, Pallas kernels, ordered(): pl.pallas_call(order_kernel, grid=(width // block,), in_specs=[pl.BlockSp...  14 us
  transfers between devices with their start and end apart: 30, of which 8 were waited for; matrix products, arithmetic and copies ran while one was open for 10% of the time, Pallas kernels for 42%

profile of v4, /device:TPU:0, one launch (start us, length us, event | category | flops | bytes accessed | tf_op | source)
XLA Modules:
  0.0 306.7 jit_solution(10376975852420137410)
XLA Ops:
  8.3 4.8 %collective-permute-start = (bf16[16,4096]{1,0:T(8,128)(2,1)S(1)}, bf16[16,4096]{1,0:T(8,128)(2,1)S(1)}, u32[]{:S(2)}, u32[]{:S(2)}) collective-permute-start(bf16[16,4096]{1,0:T(8,128)(2,1)S(1)} %constant_dynamic-slice_fusion), channel_id=1, source_target_pairs={{0,1},{1,2},{2,3},{4,5},{5,6},{6,7},{8,9},{9,10},{10,11},{12,13},{... | collective-permute-start | bytes 393224 | tf_op jit(solution)/shard_map/ppermute | solution.py:416
  13.2 2.9 dynamic-slice_convert_fusion
  16.1 1.5 collective-permute-start.1
  17.6 2.0 collective-permute-start.3
  20.5 1.8 constant_dynamic-slice_fusion.3
  23.0 14.0 %shard_map.185 = (bf16[272,4096]{1,0:T(8,128)(2,1)}, f32[8,4096]{1,0:T(8,128)S(1)}) custom-call(bf16[272,4096]{1,0:T(8,128)(2,1)S(1)} %pad_maximum_fusion.x_ref, f32[1,4096]{1,0:T(1,128)S(1)} %bitcast.70, f32[8,4096]{1,0:T(8,128)S(1)} %pad.4.coeff_ref, s32[1,4096]{1,0:T(1,128)S(1)} %bitcast.69), custom_call_target="tpu_custom_call" | custom-call | flops 1024 | bytes 1024 | tf_op jit(solution)/shard_map/pallas_call | solution.py:76
  37.1 1.6 collective-permute-start.4
  38.8 2.3 pad_maximum_fusion.2.refs_0_
  41.2 4.7 %collective-permute-start.8 = (bf16[4,3,256,256]{3,2,1,0:T(8,128)(2,1)}, bf16[4,3,256,256]{3,2,1,0:T(8,128)(2,1)}, u32[]{:S(2)}, u32[]{:S(2)}) collective-permute-start(bf16[4,3,256,256]{3,2,1,0:T(8,128)(2,1)} %pad_maximum_fusion.2.refs_0_), channel_id=1, source_target_pairs={{0,4},{4,8},{8,12},{1,5},{5,9},{9,13},{2,6},{6,10},{10,14},{3,7},{... | collective-permute-start | bytes 4718600 | tf_op jit(solution)/shard_map/ppermute | solution.py:416
  45.9 1.3 collective-permute-start.9
  47.2 12.1 %gather_fusion = bf16[4096,128]{1,0:T(8,128)(2,1)S(1)} fusion(bf16[4096,128]{1,0:T(8,128)(2,1)S(1)} %copy-done, s32[4096]{0:T(1024)S(1)} %fusion), kind=kCustom, calls=%fused_computation | custom fusion | bytes 2113536 | tf_op jit(solution)/shard_map/gather | solution.py:473
  59.3 6.4 %shard_map.186 = (bf16[3,2,4,256,4096]{4,3,2,1,0:T(8,128)(2,1)}, bf16[2,4,256,128]{3,2,1,0:T(8,128)(2,1)S(1)}) custom-call(s32[3]{0:T(128)S(1)} %pad_add_fusion.where_ref, bf16[272,4096]{1,0:T(8,128)(2,1)} %get-tuple-element.86.act_ref, f32[8,4096]{1,0:T(8,128)S(1)} %get-tuple-element.74.coeff_ref, bf16[4096,128]{1,0:T(8,128)(2,1)S(1)} %gather_fusion), custom_call_target="tpu_custom_call" | custom-call | flops 1024 | bytes 1024 | tf_op jit(solution)/shard_map/pallas_call | solution.py:131
  65.8 6.3 %shard_map.187 = (bf16[3,2,4,256,4096]{4,3,2,1,0:T(8,128)(2,1)}, bf16[2,4,256,128]{3,2,1,0:T(8,128)(2,1)S(1)}) custom-call(s32[3]{0:T(128)S(1)} %pad_add_fusion.where_ref, bf16[272,4096]{1,0:T(8,128)(2,1)} %collective-permute-done.6.act_ref, f32[8,4096]{1,0:T(8,128)S(1)} %get-tuple-element.74.coeff_ref, ...), custom_call_target="tpu_custom_call", output_to_operand_aliasing={{0}: (4, {}), {1}: (5, {})} | custom-call | flops 1024 | bytes 1024 | tf_op jit(solution)/shard_map/pallas_call | solution.py:131
  72.1 9.1 %all-gather.3.cloned.1.call-done = bf16[4096,256]{1,0:T(8,128)(2,1)} async-done(((bf16[1024,256]{1,0:T(8,128)(2,1)}), bf16[4096,256]{1,0:T(8,128)(2,1)}) %all-gather.3.cloned.1.call-update) | async-done | bytes 2097168 | tf_op jit(solution)/shard_map/all_gather | solution.py:452
  81.2 1.7 dynamic-slice_bitcast_fusion
  83.0 2.6 collective-permute-done.7
  85.6 1.5 pad_maximum_fusion.1.refs_0_
  87.1 9.9 %collective-permute-done.8.refs_1_ = bf16[4,3,256,256]{3,2,1,0:T(8,128)(2,1)} collective-permute-done((bf16[4,3,256,256]{3,2,1,0:T(8,128)(2,1)}, bf16[4,3,256,256]{3,2,1,0:T(8,128)(2,1)}, u32[]{:S(2)}, u32[]{:S(2)}) %collective-permute-start.8) | collective-permute-done | bytes 1572896 | tf_op jit(solution)/shard_map/ppermute | solution.py:416
  97.0 2.0 collective-permute-done.9.refs_2_
  99.5 2.4 collective-permute-start.10
  101.8 5.0 %collective-permute-start.13 = (bf16[4,3,256,256]{3,2,1,0:T(8,128)(2,1)}, bf16[4,3,256,256]{3,2,1,0:T(8,128)(2,1)}, u32[]{:S(2)}, u32[]{:S(2)}) collective-permute-start(bf16[4,3,256,256]{3,2,1,0:T(8,128)(2,1)} %collective-permute-done.8.refs_1_), channel_id=1, source_target_pairs={{0,4},{4,8},{8,12},{1,5},{5,9},{9,13},{2,6},{6,10},{10,14},{3,7},{... | collective-permute-start | bytes 4718600 | tf_op jit(solution)/shard_map/ppermute | solution.py:416
  108.1 6.3 %shard_map.188 = (bf16[3,2,4,256,4096]{4,3,2,1,0:T(8,128)(2,1)}, bf16[2,4,256,128]{3,2,1,0:T(8,128)(2,1)S(1)}) custom-call(s32[3]{0:T(128)S(1)} %pad_add_fusion.where_ref, bf16[272,4096]{1,0:T(8,128)(2,1)} %collective-permute-done.4.act_ref, f32[8,4096]{1,0:T(8,128)S(1)} %get-tuple-element.74.coeff_ref, ...), custom_call_target="tpu_custom_call", output_to_operand_aliasing={{0}: (4, {}), {1}: (5, {})} | custom-call | flops 1024 | bytes 1024 | tf_op jit(solution)/shard_map/pallas_call | solution.py:131
  114.4 6.3 %shard_map.189 = (bf16[3,2,4,256,4096]{4,3,2,1,0:T(8,128)(2,1)}, bf16[2,4,256,128]{3,2,1,0:T(8,128)(2,1)S(1)}) custom-call(s32[3]{0:T(128)S(1)} %pad_add_fusion.where_ref, bf16[272,4096]{1,0:T(8,128)(2,1)} %collective-permute-done.5.act_ref, f32[8,4096]{1,0:T(8,128)S(1)} %get-tuple-element.74.coeff_ref, ...), custom_call_target="tpu_custom_call", output_to_operand_aliasing={{0}: (4, {}), {1}: (5, {})} | custom-call | flops 1024 | bytes 1024 | tf_op jit(solution)/shard_map/pallas_call | solution.py:131
  120.8 5.1 %shard_map.190 = (bf16[3,2,4,256,4096]{4,3,2,1,0:T(8,128)(2,1)}, bf16[2,4,256,128]{3,2,1,0:T(8,128)(2,1)S(1)}) custom-call(s32[3]{0:T(128)S(1)} %pad_add_fusion.where_ref, bf16[272,4096]{1,0:T(8,128)(2,1)S(1)} %collective-permute-done.12.act_ref, f32[8,4096]{1,0:T(8,128)S(1)} %get-tuple-element.74.coeff_ref, ...), custom_call_target="tpu_custom_call", output_to_operand_aliasing={{0}: (4, {}), {1}: (5, {})} | custom-call | flops 1024 | bytes 1024 | tf_op jit(solution)/shard_map/pallas_call | solution.py:131
  125.8 4.9 %shard_map.191 = (bf16[3,2,4,256,4096]{4,3,2,1,0:T(8,128)(2,1)}, bf16[2,4,256,128]{3,2,1,0:T(8,128)(2,1)S(1)}) custom-call(s32[3]{0:T(128)S(1)} %pad_add_fusion.where_ref, bf16[272,4096]{1,0:T(8,128)(2,1)S(1)} %collective-permute-done.11.act_ref, f32[8,4096]{1,0:T(8,128)S(1)} %get-tuple-element.74.coeff_ref, ...), custom_call_target="tpu_custom_call", output_to_operand_aliasing={{0}: (4, {}), {1}: (5, {})} | custom-call | flops 1024 | bytes 1024 | tf_op jit(solution)/shard_map/pallas_call | solution.py:131
  130.7 8.9 %collective-permute-done.13.refs_3_ = bf16[4,3,256,256]{3,2,1,0:T(8,128)(2,1)} collective-permute-done((bf16[4,3,256,256]{3,2,1,0:T(8,128)(2,1)}, bf16[4,3,256,256]{3,2,1,0:T(8,128)(2,1)}, u32[]{:S(2)}, u32[]{:S(2)}) %collective-permute-start.13) | collective-permute-done | bytes 1572896 | tf_op jit(solution)/shard_map/ppermute | solution.py:416
  139.7 5.2 %collective-permute-done.14.refs_4_ = bf16[4,3,256,256]{3,2,1,0:T(8,128)(2,1)} collective-permute-done((bf16[4,3,256,256]{3,2,1,0:T(8,128)(2,1)}, bf16[4,3,256,256]{3,2,1,0:T(8,128)(2,1)}, u32[]{:S(2)}, u32[]{:S(2)}) %collective-permute-start.14) | collective-permute-done | bytes 1572896 | tf_op jit(solution)/shard_map/ppermute | solution.py:416
  144.9 6.1 %collective-permute-done.10.act_ref = bf16[272,4096]{1,0:T(8,128)(2,1)S(1)} collective-permute-done((bf16[272,4096]{1,0:T(8,128)(2,1)}, bf16[272,4096]{1,0:T(8,128)(2,1)S(1)}, u32[]{:S(2)}, u32[]{:S(2)}) %collective-permute-start.10) | collective-permute-done | bytes 2228256 | tf_op jit(solution)/shard_map/ppermute | solution.py:38
  151.0 5.0 %collective-permute-start.16 = (bf16[4,3,256,256]{3,2,1,0:T(8,128)(2,1)}, bf16[4,3,256,256]{3,2,1,0:T(8,128)(2,1)}, u32[]{:S(2)}, u32[]{:S(2)}) collective-permute-start(bf16[4,3,256,256]{3,2,1,0:T(8,128)(2,1)} %collective-permute-done.13.refs_3_), channel_id=1, source_target_pairs={{0,4},{4,8},{8,12},{1,5},{5,9},{9,13},{2,6},{6,10},{10,14},{3,7},{... | collective-permute-start | bytes 4718600 | tf_op jit(solution)/shard_map/ppermute | solution.py:416
  156.0 1.5 collective-permute-start.17
  157.4 1.6 collective-permute-start.18
  159.0 1.5 collective-permute-start.19
  160.5 4.8 %shard_map.192 = (bf16[3,2,4,256,4096]{4,3,2,1,0:T(8,128)(2,1)}, bf16[2,4,256,128]{3,2,1,0:T(8,128)(2,1)S(1)}) custom-call(s32[3]{0:T(128)S(1)} %pad_add_fusion.where_ref, bf16[272,4096]{1,0:T(8,128)(2,1)S(1)} %collective-permute-done.10.act_ref, f32[8,4096]{1,0:T(8,128)S(1)} %get-tuple-element.74.coeff_ref, ...), custom_call_target="tpu_custom_call", output_to_operand_aliasing={{0}: (4, {}), {1}: (5, {})} | custom-call | flops 1024 | bytes 1024 | tf_op jit(solution)/shard_map/pallas_call | solution.py:131
  165.3 5.0 %shard_map.193 = (bf16[3,2,4,256,4096]{4,3,2,1,0:T(8,128)(2,1)}, bf16[2,4,256,128]{3,2,1,0:T(8,128)(2,1)S(1)}) custom-call(s32[3]{0:T(128)S(1)} %pad_add_fusion.where_ref, bf16[272,4096]{1,0:T(8,128)(2,1)S(1)} %collective-permute-done.15.act_ref, f32[8,4096]{1,0:T(8,128)S(1)} %get-tuple-element.74.coeff_ref, ...), custom_call_target="tpu_custom_call", output_to_operand_aliasing={{0}: (4, {}), {1}: (5, {})} | custom-call | flops 1024 | bytes 1024 | tf_op jit(solution)/shard_map/pallas_call | solution.py:131
  170.3 25.4 %shard_map.194.part_ref = f32[3,2,4,256,256]{4,3,2,1,0:T(8,128)} custom-call(s32[3]{0:T(128)} %copy-done.7, bf16[3,2,4,256,4096]{4,3,2,1,0:T(8,128)(2,1)} %get-tuple-element.113.act_ref, bf16[4,3,256,256]{3,2,1,0:T(8,128)(2,1)} %pad_maximum_fusion.2.refs_0_, bf16[4,3,256,256]{3,2,1,0:T(8,128)(2,1)} %collective-permute-done.8.refs_1_, ...), custom_call_target="tpu_custom_call" | custom-call | flops 1024 | bytes 1024 | tf_op jit(solution)/shard_map/pallas_call | solution.py:203
  195.7 1.4 collective-permute-start.20
  200.3 12.2 %shard_map.195.proj_ref = bf16[3,2,4,256,256]{4,3,2,1,0:T(8,128)(2,1)} custom-call(s32[3]{0:T(128)} %copy-done.7, bf16[3,2,4,256,4096]{4,3,2,1,0:T(8,128)(2,1)} %get-tuple-element.113.act_ref, f32[3,2,4,256,256]{4,3,2,1,0:T(8,128)} %shard_map.194.part_ref, bf16[4,3,256,256]{3,2,1,0:T(8,128)(2,1)} %collective-permute-done.16.below_ref, ...), custom_call_target="tpu_custom_call" | custom-call | flops 1024 | bytes 1024 | tf_op jit(solution)/shard_map/pallas_call | solution.py:230
  212.6 1.9 copy-done.2
  214.5 12.4 %shard_map.196 = (bf16[4,256,256]{2,1,0:T(8,128)(2,1)S(1)}, f32[4,64,256]{2,1,0:T(8,128)S(1)}) custom-call(s32[2]{0:T(128)S(1)} %copy-done.11, s32[3]{0:T(128)S(1)} %copy-done.8, bf16[3,2,4,256,256]{4,3,2,1,0:T(8,128)(2,1)S(1)} %copy-done.2, bf16[2,4,256,128]{3,2,1,0:T(8,128)(2,1)S(1)} %get-tuple-element.117.lora_ref, ...), custom_call_target="tpu_custom_call" | custom-call | flops 1024 | bytes 1024 | tf_op jit(solution)/shard_map/pallas_call | solution.py:343
  226.9 24.8 %collective-permute-done.19.refs_2_ = bf16[2,2,1024,256]{3,2,1,0:T(8,128)(2,1)} collective-permute-done((bf16[2,2,1024,256]{3,2,1,0:T(8,128)(2,1)}, bf16[2,2,1024,256]{3,2,1,0:T(8,128)(2,1)}, u32[]{:S(2)}, u32[]{:S(2)}) %collective-permute-start.19) | collective-permute-done | bytes 2097184 | tf_op jit(solution)/shard_map/ppermute | solution.py:38
  252.5 1.5 collective-permute-start.22
  254.0 2.0 collective-permute-start.23
  256.0 1.9 copy-done.3
  257.9 12.4 %shard_map.197 = (bf16[4,256,256]{2,1,0:T(8,128)(2,1)S(1)}, f32[4,64,256]{2,1,0:T(8,128)S(1)}) custom-call(s32[2]{0:T(128)S(1)} %copy-done.11, s32[3]{0:T(128)S(1)} %copy-done.8, bf16[3,2,4,256,256]{4,3,2,1,0:T(8,128)(2,1)S(1)} %copy-done.3, bf16[2,4,256,128]{3,2,1,0:T(8,128)(2,1)S(1)} %get-tuple-element.117.lora_ref, ...), custom_call_target="tpu_custom_call" | custom-call | flops 1024 | bytes 1024 | tf_op jit(solution)/shard_map/pallas_call | solution.py:343
  274.3 1.5 collective-permute-start.26
  275.8 2.0 collective-permute-start.27
  279.5 6.4 %shard_map.198.refs_4_ = bf16[2,256,2048]{2,1,0:T(8,128)(2,1)} custom-call(s32[3]{0:T(128)S(1)} %copy-done.8, bf16[512,4096]{1,0:T(8,128)(2,1)} %bitcast.79, bf16[4,256,256]{2,1,0:T(8,128)(2,1)S(1)} %pad_maximum_fusion.5.own_ref, bf16[4,256,256]{2,1,0:T(8,128)(2,1)S(1)} %collective-permute-done.24.far_ref, ...), custom_call_target="tpu_custom_call" | custom-call | flops 1024 | bytes 1024 | tf_op jit(solution)/shard_map/pallas_call | solution.py:397
  293.4 6.4 %shard_map.199 = bf16[2,256,2048]{2,1,0:T(8,128)(2,1)} custom-call(s32[3]{0:T(128)S(1)} %copy-done.8, bf16[512,4096]{1,0:T(8,128)(2,1)} %bitcast.80, bf16[4,256,256]{2,1,0:T(8,128)(2,1)S(1)} %pad_maximum_fusion.6.own_ref, bf16[4,256,256]{2,1,0:T(8,128)(2,1)S(1)} %collective-permute-done.28.far_ref, ...), custom_call_target="tpu_custom_call", output_to_operand_aliasing={{}: (8, {})} | custom-call | flops 1024 | bytes 1024 | tf_op jit(solution)/shard_map/pallas_call | solution.py:397
  (108 shorter events, 22.0 us)
Async XLA Ops:
  7.2 40.0 %copy-start = (bf16[4096,128]{1,0:T(8,128)(2,1)S(1)}, bf16[4096,128]{1,0:T(8,128)(2,1)}, u32[]{:S(2)}) copy-start(bf16[4096,128]{1,0:T(8,128)(2,1)} %param.24) | copy-start | bytes 3145732
  7.2 12.4 %copy-start.14 = (f32[1024,256]{1,0:T(8,128)S(1)}, f32[1024,256]{1,0:T(8,128)}, u32[]{:S(2)}) copy-start(f32[1024,256]{1,0:T(8,128)} %param.23) | copy-start | bytes 3145732
  7.2 74.0 %all-gather.3.cloned.1.call-start = ((), (), s32[]{:S(2)}) async-start(), calls=%async_computation | async-start | bytes 2621440 | tf_op jit(solution)/shard_map/all_gather | solution.py:452
  8.3 14.0 %collective-permute-start = (bf16[16,4096]{1,0:T(8,128)(2,1)S(1)}, bf16[16,4096]{1,0:T(8,128)(2,1)S(1)}, u32[]{:S(2)}, u32[]{:S(2)}) collective-permute-start(bf16[16,4096]{1,0:T(8,128)(2,1)S(1)} %constant_dynamic-slice_fusion), channel_id=1, source_target_pairs={{0,1},{1,2},{2,3},{4,5},{5,6},{6,7},{8,9},{9,10},{10,11},{12,13},{... | collective-permute-start | bytes 393224 | tf_op jit(solution)/shard_map/ppermute | solution.py:416
  16.1 20.9 %collective-permute-start.1 = (bf16[3,256,256]{2,1,0:T(8,128)(2,1)}, bf16[3,256,256]{2,1,0:T(8,128)(2,1)S(1)}, u32[]{:S(2)}, u32[]{:S(2)}) collective-permute-start(bf16[3,256,256]{2,1,0:T(8,128)(2,1)} %get-tuple-element.139), channel_id=1, source_target_pairs={{0,1},{1,0},{2,3},{3,2},{4,5},{5,4},{6,7},{7,6},{8,9},{9,8},{10,11... | collective-permute-start | bytes 1179656 | tf_op jit(solution)/shard_map/ppermute | solution.py:38
  17.6 19.4 %collective-permute-start.2 = (bf16[3,256,256]{2,1,0:T(8,128)(2,1)}, bf16[3,256,256]{2,1,0:T(8,128)(2,1)S(1)}, u32[]{:S(2)}, u32[]{:S(2)}) collective-permute-start(bf16[3,256,256]{2,1,0:T(8,128)(2,1)} %get-tuple-element.141), channel_id=1, source_target_pairs={{0,2},{1,3},{2,0},{3,1},{4,6},{5,7},{6,4},{7,5},{8,10},{9,11},{10,... | collective-permute-start | bytes 1179656 | tf_op jit(solution)/shard_map/ppermute | solution.py:38
  17.6 19.4 %collective-permute-start.3 = (bf16[3,256,256]{2,1,0:T(8,128)(2,1)}, bf16[3,256,256]{2,1,0:T(8,128)(2,1)}, u32[]{:S(2)}, u32[]{:S(2)}) collective-permute-start(bf16[3,256,256]{2,1,0:T(8,128)(2,1)} %get-tuple-element.138), channel_id=1, source_target_pairs={{0,3},{1,2},{2,1},{3,0},{4,7},{5,6},{6,5},{7,4},{8,11},{9,10},{10,... | collective-permute-start | bytes 1179656 | tf_op jit(solution)/shard_map/ppermute | solution.py:38
  20.5 1.8 copy-start.16
  22.3 0.7 copy-start.9
  22.3 0.7 copy-start.10
  37.0 28.7 %collective-permute-start.6 = (bf16[272,4096]{1,0:T(8,128)(2,1)}, bf16[272,4096]{1,0:T(8,128)(2,1)}, u32[]{:S(2)}, u32[]{:S(2)}) collective-permute-start(bf16[272,4096]{1,0:T(8,128)(2,1)} %get-tuple-element.86.act_ref), channel_id=1, source_target_pairs={{0,16},{16,0},{1,17},{17,1},{2,18},{18,2},{3,19},{19,3},{4,20},{20... | collective-permute-start | bytes 6684680 | tf_op jit(solution)/shard_map/ppermute | solution.py:38
  37.1 61.8 %collective-permute-start.4 = (bf16[272,4096]{1,0:T(8,128)(2,1)}, bf16[272,4096]{1,0:T(8,128)(2,1)}, u32[]{:S(2)}, u32[]{:S(2)}) collective-permute-start(bf16[272,4096]{1,0:T(8,128)(2,1)} %get-tuple-element.86.act_ref), channel_id=1, source_target_pairs={{0,1},{1,0},{2,3},{3,2},{4,5},{5,4},{6,7},{7,6},{8,9},{9,8},{10,11... | collective-permute-start | bytes 6684680 | tf_op jit(solution)/shard_map/ppermute | solution.py:38
  38.7 60.3 %collective-permute-start.5 = (bf16[272,4096]{1,0:T(8,128)(2,1)}, bf16[272,4096]{1,0:T(8,128)(2,1)}, u32[]{:S(2)}, u32[]{:S(2)}) collective-permute-start(bf16[272,4096]{1,0:T(8,128)(2,1)} %get-tuple-element.86.act_ref), channel_id=1, source_target_pairs={{0,2},{1,3},{2,0},{3,1},{4,6},{5,7},{6,4},{7,5},{8,10},{9,11},{10,... | collective-permute-start | bytes 6684680 | tf_op jit(solution)/shard_map/ppermute | solution.py:38
  38.8 126.5 %copy-start.7 = (s32[3]{0:T(128)}, s32[3]{0:T(128)S(1)}, u32[]{:S(2)}) copy-start(s32[3]{0:T(128)S(1)} %pad_add_fusion.where_ref) | copy-start | bytes 40
  41.2 55.8 %collective-permute-start.8 = (bf16[4,3,256,256]{3,2,1,0:T(8,128)(2,1)}, bf16[4,3,256,256]{3,2,1,0:T(8,128)(2,1)}, u32[]{:S(2)}, u32[]{:S(2)}) collective-permute-start(bf16[4,3,256,256]{3,2,1,0:T(8,128)(2,1)} %pad_maximum_fusion.2.refs_0_), channel_id=1, source_target_pairs={{0,4},{4,8},{8,12},{1,5},{5,9},{9,13},{2,6},{6,10},{10,14},{3,7},{... | collective-permute-start | bytes 4718600 | tf_op jit(solution)/shard_map/ppermute | solution.py:416
  45.9 53.0 %collective-permute-start.9 = (bf16[4,3,256,256]{3,2,1,0:T(8,128)(2,1)}, bf16[4,3,256,256]{3,2,1,0:T(8,128)(2,1)}, u32[]{:S(2)}, u32[]{:S(2)}) collective-permute-start(bf16[4,3,256,256]{3,2,1,0:T(8,128)(2,1)} %pad_maximum_fusion.2.refs_0_), channel_id=1, source_target_pairs={{4,0},{8,4},{12,8},{5,1},{9,5},{13,9},{6,2},{10,6},{14,10},{7,3},{... | collective-permute-start | bytes 4718600 | tf_op jit(solution)/shard_map/ppermute | solution.py:416
  82.9 2.7 collective-permute-start.7
  98.9 21.8 %collective-permute-start.12 = (bf16[272,4096]{1,0:T(8,128)(2,1)}, bf16[272,4096]{1,0:T(8,128)(2,1)S(1)}, u32[]{:S(2)}, u32[]{:S(2)}) collective-permute-start(bf16[272,4096]{1,0:T(8,128)(2,1)} %collective-permute-done.4.act_ref), channel_id=1, source_target_pairs={{0,16},{16,0},{1,17},{17,1},{2,18},{18,2},{3,19},{19,3},{4,20},{20... | collective-permute-start | bytes 6684680 | tf_op jit(solution)/shard_map/ppermute | solution.py:38
  98.9 26.9 %collective-permute-start.11 = (bf16[272,4096]{1,0:T(8,128)(2,1)}, bf16[272,4096]{1,0:T(8,128)(2,1)S(1)}, u32[]{:S(2)}, u32[]{:S(2)}) collective-permute-start(bf16[272,4096]{1,0:T(8,128)(2,1)} %collective-permute-done.5.act_ref), channel_id=1, source_target_pairs={{0,16},{16,0},{1,17},{17,1},{2,18},{18,2},{3,19},{19,3},{4,20},{20... | collective-permute-start | bytes 6684680 | tf_op jit(solution)/shard_map/ppermute | solution.py:38
  99.5 51.5 %collective-permute-start.10 = (bf16[272,4096]{1,0:T(8,128)(2,1)}, bf16[272,4096]{1,0:T(8,128)(2,1)S(1)}, u32[]{:S(2)}, u32[]{:S(2)}) collective-permute-start(bf16[272,4096]{1,0:T(8,128)(2,1)} %get-tuple-element.86.act_ref), channel_id=1, source_target_pairs={{0,3},{1,2},{2,1},{3,0},{4,7},{5,6},{6,5},{7,4},{8,11},{9,10},{10,... | collective-permute-start | bytes 6684680 | tf_op jit(solution)/shard_map/ppermute | solution.py:38
  101.8 37.8 %collective-permute-start.13 = (bf16[4,3,256,256]{3,2,1,0:T(8,128)(2,1)}, bf16[4,3,256,256]{3,2,1,0:T(8,128)(2,1)}, u32[]{:S(2)}, u32[]{:S(2)}) collective-permute-start(bf16[4,3,256,256]{3,2,1,0:T(8,128)(2,1)} %collective-permute-done.8.refs_1_), channel_id=1, source_target_pairs={{0,4},{4,8},{8,12},{1,5},{5,9},{9,13},{2,6},{6,10},{10,14},{3,7},{... | collective-permute-start | bytes 4718600 | tf_op jit(solution)/shard_map/ppermute | solution.py:416
  106.9 38.0 %collective-permute-start.14 = (bf16[4,3,256,256]{3,2,1,0:T(8,128)(2,1)}, bf16[4,3,256,256]{3,2,1,0:T(8,128)(2,1)}, u32[]{:S(2)}, u32[]{:S(2)}) collective-permute-start(bf16[4,3,256,256]{3,2,1,0:T(8,128)(2,1)} %collective-permute-done.9.refs_2_), channel_id=1, source_target_pairs={{4,0},{8,4},{12,8},{5,1},{9,5},{13,9},{6,2},{10,6},{14,10},{7,3},{... | collective-permute-start | bytes 4718600 | tf_op jit(solution)/shard_map/ppermute | solution.py:416
  151.0 14.3 %collective-permute-start.15 = (bf16[272,4096]{1,0:T(8,128)(2,1)S(1)}, bf16[272,4096]{1,0:T(8,128)(2,1)S(1)}, u32[]{:S(2)}, u32[]{:S(2)}) collective-permute-start(bf16[272,4096]{1,0:T(8,128)(2,1)S(1)} %collective-permute-done.10.act_ref), channel_id=1, source_target_pairs={{0,16},{16,0},{1,17},{17,1},{2,18},{18,2},{3,19},{19,3},{4,20},{20... | collective-permute-start | bytes 6684680 | tf_op jit(solution)/shard_map/ppermute | solution.py:38
  151.0 44.8 %collective-permute-start.16 = (bf16[4,3,256,256]{3,2,1,0:T(8,128)(2,1)}, bf16[4,3,256,256]{3,2,1,0:T(8,128)(2,1)}, u32[]{:S(2)}, u32[]{:S(2)}) collective-permute-start(bf16[4,3,256,256]{3,2,1,0:T(8,128)(2,1)} %collective-permute-done.13.refs_3_), channel_id=1, source_target_pairs={{0,4},{4,8},{8,12},{1,5},{5,9},{9,13},{2,6},{6,10},{10,14},{3,7},{... | collective-permute-start | bytes 4718600 | tf_op jit(solution)/shard_map/ppermute | solution.py:416
  156.0 39.8 %collective-permute-start.17 = (bf16[4,3,256,256]{3,2,1,0:T(8,128)(2,1)}, bf16[4,3,256,256]{3,2,1,0:T(8,128)(2,1)}, u32[]{:S(2)}, u32[]{:S(2)}) collective-permute-start(bf16[4,3,256,256]{3,2,1,0:T(8,128)(2,1)} %collective-permute-done.14.refs_4_), channel_id=1, source_target_pairs={{4,0},{8,4},{12,8},{5,1},{9,5},{13,9},{6,2},{10,6},{14,10},{7,3},{... | collective-permute-start | bytes 4718600 | tf_op jit(solution)/shard_map/ppermute | solution.py:416
  157.4 69.5 %collective-permute-start.18 = (bf16[2,2,1024,256]{3,2,1,0:T(8,128)(2,1)}, bf16[2,2,1024,256]{3,2,1,0:T(8,128)(2,1)}, u32[]{:S(2)}, u32[]{:S(2)}) collective-permute-start(bf16[2,2,1024,256]{3,2,1,0:T(8,128)(2,1)} %pad_maximum_fusion.1.refs_0_), channel_id=1, source_target_pairs={{0,1},{1,0},{2,3},{3,2},{4,5},{5,4},{6,7},{7,6},{8,9},{9,8},{10,11... | collective-permute-start | bytes 6291464 | tf_op jit(solution)/shard_map/ppermute | solution.py:38
  159.0 92.7 %collective-permute-start.19 = (bf16[2,2,1024,256]{3,2,1,0:T(8,128)(2,1)}, bf16[2,2,1024,256]{3,2,1,0:T(8,128)(2,1)}, u32[]{:S(2)}, u32[]{:S(2)}) collective-permute-start(bf16[2,2,1024,256]{3,2,1,0:T(8,128)(2,1)} %pad_maximum_fusion.1.refs_0_), channel_id=1, source_target_pairs={{0,2},{1,3},{2,0},{3,1},{4,6},{5,7},{6,4},{7,5},{8,10},{9,11},{10,... | collective-permute-start | bytes 6291464 | tf_op jit(solution)/shard_map/ppermute | solution.py:38
  195.7 74.6 %collective-permute-start.20 = (bf16[2,2,1024,256]{3,2,1,0:T(8,128)(2,1)}, bf16[2,2,1024,256]{3,2,1,0:T(8,128)(2,1)S(1)}, u32[]{:S(2)}, u32[]{:S(2)}) collective-permute-start(bf16[2,2,1024,256]{3,2,1,0:T(8,128)(2,1)} %pad_maximum_fusion.1.refs_0_), channel_id=1, source_target_pairs={{0,3},{1,2},{2,1},{3,0},{4,7},{5,6},{6,5},{7,4},{8,11},{9,10},{10,... | collective-permute-start | bytes 6291464 | tf_op jit(solution)/shard_map/ppermute | solution.py:38
  200.3 12.3 %copy-start.4 = (bf16[520,128]{1,0:T(8,128)(2,1)S(1)}, bf16[520,128]{1,0:T(8,128)(2,1)}, u32[]{:S(2)}) copy-start(bf16[520,128]{1,0:T(8,128)(2,1)} %constant.78.clone.sums_ref) | copy-start | bytes 399364
  200.3 12.3 %copy-start.5 = (bf16[256,256]{1,0:T(8,128)(2,1)S(1)}, bf16[256,256]{1,0:T(8,128)(2,1)}, u32[]{:S(2)}) copy-start(bf16[256,256]{1,0:T(8,128)(2,1)} %constant.80.clone.same_ref) | copy-start | bytes 393220
  200.3 12.3 %copy-start.6 = (f32[64,256]{1,0:T(8,128)S(1)}, f32[64,256]{1,0:T(8,128)}, u32[]{:S(2)}) copy-start(f32[64,256]{1,0:T(8,128)} %constant.79.clone.level_ref) | copy-start | bytes 196612
  200.3 12.3 %copy-start.8 = (s32[3]{0:T(128)S(1)}, s32[3]{0:T(128)}, u32[]{:S(2)}) copy-start(s32[3]{0:T(128)} %copy-done.7) | copy-start | bytes 40
  200.3 12.3 %copy-start.11 = (s32[2]{0:T(128)S(1)}, s32[2]{0:T(128)}, u32[]{:S(2)}) copy-start(s32[2]{0:T(128)} %extent_ref.3) | copy-start | bytes 28
  212.6 1.9 copy-start.2
  252.5 17.8 %collective-permute-start.21 = (bf16[320,256]{1,0:T(8,128)(2,1)}, bf16[320,256]{1,0:T(8,128)(2,1)}, u32[]{:S(2)}, u32[]{:S(2)}) collective-permute-start(bf16[320,256]{1,0:T(8,128)(2,1)} %get-tuple-element.150), channel_id=1, source_target_pairs={{0,1},{1,0},{2,3},{3,2},{4,5},{5,4},{6,7},{7,6},{8,9},{9,8},{10,11... | collective-permute-start | bytes 491528 | tf_op jit(solution)/shard_map/ppermute | solution.py:38
  252.5 17.8 %collective-permute-start.22 = (bf16[320,256]{1,0:T(8,128)(2,1)}, bf16[320,256]{1,0:T(8,128)(2,1)}, u32[]{:S(2)}, u32[]{:S(2)}) collective-permute-start(bf16[320,256]{1,0:T(8,128)(2,1)} %get-tuple-element.149), channel_id=1, source_target_pairs={{0,2},{1,3},{2,0},{3,1},{4,6},{5,7},{6,4},{7,5},{8,10},{9,11},{10,... | collective-permute-start | bytes 491528 | tf_op jit(solution)/shard_map/ppermute | solution.py:38
  254.0 16.3 %collective-permute-start.23 = (bf16[320,256]{1,0:T(8,128)(2,1)S(1)}, bf16[320,256]{1,0:T(8,128)(2,1)}, u32[]{:S(2)}, u32[]{:S(2)}) collective-permute-start(bf16[320,256]{1,0:T(8,128)(2,1)S(1)} %get-tuple-element.148), channel_id=1, source_target_pairs={{0,3},{1,2},{2,1},{3,0},{4,7},{5,6},{6,5},{7,4},{8,11},{9,10},{10,... | collective-permute-start | bytes 491528 | tf_op jit(solution)/shard_map/ppermute | solution.py:38
  256.0 1.9 copy-start.3
  270.4 8.3 %copy-start.12 = (bf16[2,2,1024,256]{3,2,1,0:T(8,128)(2,1)}, bf16[2,2,1024,256]{3,2,1,0:T(8,128)(2,1)S(1)}, u32[]{:S(2)}) copy-start(bf16[2,2,1024,256]{3,2,1,0:T(8,128)(2,1)S(1)} %collective-permute-done.20.refs_3_) | copy-start | bytes 6291460
  273.3 6.2 %collective-permute-start.24 = (bf16[4,256,256]{2,1,0:T(8,128)(2,1)S(1)}, bf16[4,256,256]{2,1,0:T(8,128)(2,1)S(1)}, u32[]{:S(2)}, u32[]{:S(2)}) collective-permute-start(bf16[4,256,256]{2,1,0:T(8,128)(2,1)S(1)} %pad_maximum_fusion.5.own_ref), channel_id=1, source_target_pairs={{0,16},{16,0},{1,17},{17,1},{2,18},{18,2},{3,19},{19,3},{4,20},{20... | collective-permute-start | bytes 1572872 | tf_op jit(solution)/shard_map/ppermute | solution.py:38
  274.2 11.6 %collective-permute-start.25 = (bf16[320,256]{1,0:T(8,128)(2,1)}, bf16[320,256]{1,0:T(8,128)(2,1)}, u32[]{:S(2)}, u32[]{:S(2)}) collective-permute-start(bf16[320,256]{1,0:T(8,128)(2,1)} %get-tuple-element.146), channel_id=1, source_target_pairs={{0,1},{1,0},{2,3},{3,2},{4,5},{5,4},{6,7},{7,6},{8,9},{9,8},{10,11... | collective-permute-start | bytes 491528 | tf_op jit(solution)/shard_map/ppermute | solution.py:38
  274.3 11.6 %collective-permute-start.26 = (bf16[320,256]{1,0:T(8,128)(2,1)}, bf16[320,256]{1,0:T(8,128)(2,1)}, u32[]{:S(2)}, u32[]{:S(2)}) collective-permute-start(bf16[320,256]{1,0:T(8,128)(2,1)} %get-tuple-element.145), channel_id=1, source_target_pairs={{0,2},{1,3},{2,0},{3,1},{4,6},{5,7},{6,4},{7,5},{8,10},{9,11},{10,... | collective-permute-start | bytes 491528 | tf_op jit(solution)/shard_map/ppermute | solution.py:38
  275.8 10.1 %collective-permute-start.27 = (bf16[320,256]{1,0:T(8,128)(2,1)}, bf16[320,256]{1,0:T(8,128)(2,1)}, u32[]{:S(2)}, u32[]{:S(2)}) collective-permute-start(bf16[320,256]{1,0:T(8,128)(2,1)} %get-tuple-element.144), channel_id=1, source_target_pairs={{0,3},{1,2},{2,1},{3,0},{4,7},{5,6},{6,5},{7,4},{8,11},{9,10},{10,... | collective-permute-start | bytes 491528 | tf_op jit(solution)/shard_map/ppermute | solution.py:38
  279.5 11.5 %copy-start.15 = (bf16[320,256]{1,0:T(8,128)(2,1)S(1)}, bf16[320,256]{1,0:T(8,128)(2,1)}, u32[]{:S(2)}) copy-start(bf16[320,256]{1,0:T(8,128)(2,1)} %get-tuple-element.133) | copy-start | bytes 491524
  285.9 5.5 %copy-start.13 = (bf16[2,2,2,64,4,64]{5,4,3,2,1,0:T(4,128)(2,1)S(1)}, bf16[2,2,2,64,4,64]{5,4,3,2,1,0:T(4,128)(2,1)}, u32[]{:S(2)}) copy-start(bf16[2,2,2,64,4,64]{5,4,3,2,1,0:T(4,128)(2,1)} %constant_dynamic-update-slice_fusion.1) | copy-start | bytes 786436
  291.3 2.1 collective-permute-start.28
  293.4 6.4 %copy-start.1 = (bf16[4096,128]{1,0:T(8,128)(2,1)S(1)}, bf16[4096,128]{1,0:T(8,128)(2,1)}, u32[]{:S(2)}) copy-start(bf16[4096,128]{1,0:T(8,128)(2,1)} %param.24) | copy-start | bytes 3145732
Sparse Core Ops, SparseCore 0:
  20.6 60.5 all-gather.2

commit v5 on v4

--- a/solution.py
+++ b/solution.py
@@ -184,19 +184,6 @@
     out_ref[0, 0] = dot(act, lines_ref[...]).reshape(out_ref.shape[2:])
 
 
-def last_kernel(where_ref, act_ref, part_ref, below_ref, above_ref, out_ref, lines_ref):
-    stretches, _, depth, _ = below_ref.shape
-
-    @pl.when(pl.program_id(1) == 0)
-    def _():
-        for d in range(stretches):
-            at = (where_ref[0] ^ d) * depth
-            lines_ref[pl.ds(pl.multiple_of(at, depth), depth), :] = below_ref[d, 0] + above_ref[d, 0]
-
-    act = act_ref[0, 0].reshape(-1, act_ref.shape[-1])
-    out_ref[0, 0] = (part_ref[0, 0] + dot(act, lines_ref[...]).reshape(out_ref.shape[2:])).astype(bf16)
-
-
 def projected(where, mixed, hops):
     stretches, kinds, depth, cols = hops[0].shape
     _, sides, _, span, width = mixed.shape
@@ -216,32 +203,6 @@
     )(where, mixed, *hops)
 
 
-def completed(where, mixed, part, below, above):
-    stretches, kinds, depth, cols = below.shape
-    _, sides, _, span, width = mixed.shape
-    share = stretches * depth
-    last = width // share - 1
-
-    def act_block(j, m, w):
-        return (j, m, 0, 0, jnp.where(w[2] == last, 0, last))
-
-    block = pl.BlockSpec((1, 1, stretches, span, cols), lambda j, m, w: (j, m, 0, 0, 0))
-    line_block = pl.BlockSpec((stretches, 1, depth, cols), lambda j, m, w: (0, j, 0, 0))
-    return pl.pallas_call(
-        last_kernel,
-        grid_spec=pltpu.PrefetchScalarGridSpec(
-            num_scalar_prefetch=1,
-            grid=(kinds, sides),
-            in_specs=[pl.BlockSpec((1, 1, stretches, span, share), act_block), block, line_block, line_block],
-            out_specs=block,
-            scratch_shapes=[pltpu.VMEM((share, cols), bf16)],
-        ),
-        out_shape=jax.ShapeDtypeStruct((kinds, sides, stretches, span, cols), bf16),
-        compiler_params=vmem(60),
-        cost_estimate=SMALL,
-    )(where, mixed, part, below, above)
-
-
 def projected_whole(where, mixed, lines):
     _, stretches, kinds, depth, cols = lines.shape
     lines = lines[:, jnp.arange(stretches) ^ where[0]]
@@ -271,10 +232,11 @@
     return np.tile(np.where(of > by, level, -1.0).astype(np.float32), (1, heads))
 
 
-def wkv_kernel(
-    extent_ref, where_ref, proj_ref, lora_ref, right_ref, speed_ref, reward_ref, scale_ref, sums_ref, level_ref,
-    same_ref, normed_ref, state_ref, memory_ref, *, prompt,
-):
+def wkv_kernel(extent_ref, where_ref, *refs, prompt, parted):
+    if parted:
+        act_ref, below_ref, above_ref, *refs, lines_ref = refs
+    proj_ref, lora_ref, right_ref, speed_ref, reward_ref, scale_ref, sums_ref, level_ref, same_ref, *refs = refs
+    normed_ref, state_ref, memory_ref = refs
     step = pl.program_id(0)
     tokens, cols = proj_ref.shape[3:]
     heads = cols // ATTEND_DIM
@@ -285,12 +247,23 @@
     @pl.when(step == 0)
     def _():
         memory_ref[...] = jnp.zeros_like(memory_ref)
+        if parted:
+            stretches, kinds, depth, _ = below_ref.shape
+            for d in range(stretches):
+                at = pl.ds(pl.multiple_of((where_ref[0] ^ d) * depth, depth), depth)
+                for j in range(kinds):
+                    lines_ref[j, at, :] = below_ref[d, j] + above_ref[d, j]
+
+    def projection(j):
+        if not parted:
+            return proj_ref[j, 0, 0]
+        return (proj_ref[j, 0, 0] + dot(act_ref[j, 0, 0], lines_ref[j])).astype(bf16)
 
     at = step * tokens + lax.broadcasted_iota(jnp.int32, (tokens, cols), 0)
     valid = jnp.where(at < extent_ref[prompt], 1.0, 0.0)
-    r = proj_ref[0, 0, 0]
-    k = proj_ref[1, 0, 0] * valid.astype(bf16)
-    v = proj_ref[2, 0, 0]
+    r = projection(0)
+    k = projection(1) * valid.astype(bf16)
+    v = projection(2)
     decay = -speed_ref[...] * jnp.exp(dot(lora_ref[0, 0], right_ref[...])) * valid
     high = decay.astype(bf16)
     low = (decay - high.astype(f32)).astype(bf16)
@@ -327,8 +300,9 @@
     normed_ref[0] = (centred * lax.rsqrt(spread + eps) * scale_ref[...] * valid).astype(bf16)
 
 
-def recurrence(prompt, extents, where, proj, lora, right, speed, reward, scale):
-    _, _, stretches, span, cols = proj.shape
+def recurrence(prompt, extents, where, mixed, proj, ends, lora, right, speed, reward, scale):
+    kinds, _, stretches, span, cols = proj.shape
+    width = mixed.shape[-1]
     inner = lora.shape[-1]
     heads = cols // ATTEND_DIM
     sums = jnp.asarray(decay_sums(), bf16)
@@ -340,13 +314,27 @@
         return pl.BlockSpec(array.shape, lambda c, e, w: (0,) * array.ndim)
 
     tables = (right, speed, reward, scale, sums, level, same)
+    first, first_specs, scratch = (), [], [pltpu.VMEM((cols, cols), f32)]
+    if ends:
+        share = stretches * ends[0].shape[2]
+        last = width // share - 1
+        first = (mixed, *ends)
+        first_specs = [
+            pl.BlockSpec(
+                (kinds, 1, 1, span, share),
+                lambda c, e, w: (0, w[1] ^ prompt, c, 0, jnp.where(w[2] == last, 0, last)),
+            ),
+            *map(fixed, ends),
+        ]
+        scratch.append(pltpu.VMEM((kinds, share, cols), bf16))
     return pl.pallas_call(
-        functools.partial(wkv_kernel, prompt=prompt),
+        functools.partial(wkv_kernel, prompt=prompt, parted=bool(ends)),
         grid_spec=pltpu.PrefetchScalarGridSpec(
             num_scalar_prefetch=2,
             grid=(stretches,),
-            in_specs=[
-                pl.BlockSpec((3, 1, 1, span, cols), lambda c, e, w: (0, w[1] ^ prompt, c, 0, 0)),
+            in_specs=first_specs
+            + [
+                pl.BlockSpec((kinds, 1, 1, span, cols), lambda c, e, w: (0, w[1] ^ prompt, c, 0, 0)),
                 pl.BlockSpec((1, 1, span, inner), lambda c, e, w: (w[1] ^ prompt, c, 0, 0)),
             ]
             + [fixed(a) for a in tables],
@@ -354,58 +342,61 @@
                 pl.BlockSpec((1, span, cols), lambda c, e, w: (c, 0, 0)),
                 pl.BlockSpec((1, ATTEND_DIM, cols), lambda c, e, w: (c, 0, 0)),
             ],
-            scratch_shapes=[pltpu.VMEM((cols, cols), f32)],
+            scratch_shapes=scratch,
         ),
         out_shape=[
             jax.ShapeDtypeStruct((stretches, span, cols), bf16),
             jax.ShapeDtypeStruct((stretches, ATTEND_DIM, cols), f32),
         ],
-        compiler_params=vmem(40),
+        compiler_params=vmem(56),
         cost_estimate=SMALL,
-    )(extents, where, proj, lora, *tables)
+    )(extents, where, *first, proj, lora, *tables)
 
 
 def finish_kernel(where_ref, x_ref, own_ref, far_ref, *refs):
-    weights, out_ref = refs[:4], refs[-1]
+    weights, out_ref = refs[:5], refs[-1]
     stretches, rows, cols = own_ref.shape
     chunk = weights[0].shape[-1]
     for e in range(stretches):
         places = pl.ds(pl.multiple_of((where_ref[0] ^ e) * chunk, chunk), chunk)
         total = x_ref[:, places].astype(f32)
         for side, lines_ref in enumerate((own_ref, far_ref)):
+            w_ref = weights[e].at[side, 0] if e < 3 else weights[e + side].at[0, 0]
             for d in range(stretches):
                 at = pl.ds(pl.multiple_of((where_ref[0] ^ d) * cols, cols), cols)
-                total += dot(lines_ref[d], weights[e][side, 0, at, :])
+                total += dot(lines_ref[d], w_ref[at, :])
         out_ref[0, :, places] = total.astype(bf16)
 
 
 def finished(prompt, prompts, where, x, own, far, weights, earlier):
-    stretches, rows, cols = own.shape
+    stretches, _, cols = own.shape
+    rows = x.shape[0] // prompts
     _, groups, depth, chunk = weights[0].shape
     share = groups * stretches * chunk
     if chunk % 128:
         order = jnp.arange(stretches) ^ where[0]
         total = lax.dynamic_slice(x, (prompt * rows, where[1] * share), (rows, share)).astype(f32)
+        weights = [*weights[:3], jnp.concatenate(weights[3:])]
         for side, lines in enumerate((own, far)):
             w = jnp.stack([w[side] for w in weights])[order]
             w = jnp.transpose(w, (2, 1, 0, 3)).reshape(depth, share)
-            lines = jnp.transpose(lines[order], (1, 0, 2)).reshape(rows, depth)
+            lines = jnp.transpose(lines[order, :rows], (1, 0, 2)).reshape(rows, depth)
             total += dot(lines, w)
         return jnp.concatenate([*earlier, total.astype(bf16)[None]], axis=0)
     block = stretches * chunk
-    whole = pl.BlockSpec((stretches, rows, cols), lambda g, w: (0, 0, 0))
+    lines_spec = pl.BlockSpec((stretches, rows, cols), lambda g, w: (0, 0, 0))
     return pl.pallas_call(
         finish_kernel,
         grid_spec=pltpu.PrefetchScalarGridSpec(
             num_scalar_prefetch=1,
             grid=(groups,),
-            in_specs=[pl.BlockSpec((rows, block), lambda g, w: (prompt, w[1] * groups + g)), whole, whole]
-            + [pl.BlockSpec((2, 1, depth, chunk), lambda g, w: (0, g, 0, 0))] * len(weights)
+            in_specs=[pl.BlockSpec((rows, block), lambda g, w: (prompt, w[1] * groups + g)), lines_spec, lines_spec]
+            + [pl.BlockSpec((a.shape[0], 1, depth, chunk), lambda g, w: (0, g, 0, 0)) for a in weights]
             + [pl.BlockSpec(memory_space=pl.ANY)] * len(earlier),
             out_specs=pl.BlockSpec((1, rows, block), lambda g, w: (prompt, 0, g)),
         ),
         out_shape=jax.ShapeDtypeStruct((prompts, rows, share), bf16),
-        input_output_aliases={8: 0} if earlier else {},
+        input_output_aliases={9: 0} if earlier else {},
         compiler_params=vmem(48),
         cost_estimate=SMALL,
     )(where, x, own, far, *weights, *earlier)
@@ -480,18 +471,19 @@
     kept = lax.dynamic_slice_in_dim(out_lines, t * share, share, 0)
     given = lax.dynamic_slice_in_dim(out_lines, (1 - t) * share, share, 0)
     out_lines = jnp.stack([kept, swapped(given, "tensor", 1)])
-    near, other, out_lines, act, *rest = tied(near, other, out_lines, act, *results, *hops)
+    near, other, out_lines, *rest = tied(near, other, out_lines, *results, *hops)
     results, hops = tuple(rest[:2]), rest[2:]
 
-    across = swapped(act, "seq", 3)
+    cut = (span + PAST) // 32 * 16
+    across = [swapped(near[:cut], "seq", 2), swapped(other[cut:], "seq", 1)]
     if chained:
         hops += [moved(hops[0], "req", 1), moved(hops[1], "req", -1)]
     results = mixed_in(near, 0, 1, results)
     results = mixed_in(other, 0, 2, results)
     results = mixed_in(swapped(near, "tensor", 1), 1, 1, results)
     results = mixed_in(swapped(other, "tensor", 1), 1, 2, results)
-    across, out_lines, *rest = tied(across, out_lines, *results, *hops)
-    results, hops = tuple(rest[:2]), rest[2:]
+    out_lines, *rest = tied(out_lines, *results, *hops, *across)
+    results, hops, across = tuple(rest[:2]), rest[2:-2], jnp.concatenate(rest[-2:], axis=0)
 
     near, other = swapped(out_lines, "seq", 1), swapped(out_lines, "seq", 2)
     ends = [moved(hops[2], "req", 1), moved(hops[3], "req", -1)] if chained else []
@@ -502,10 +494,7 @@
         proj = projected(where, mixed, [lines, *hops])
     else:
         proj = projected_whole(where, mixed, *hops)
-    mixed, proj, out_lines, *ends = tied(mixed, proj, out_lines, *ends)
-    across = swapped(out_lines, "seq", 3)
-    if chained:
-        proj = completed(where, mixed, proj, *ends)
+    mixed, proj, *ends = tied(mixed, proj, *ends)
 
     def mine(array):
         return lax.dynamic_slice_in_dim(array, s * cols, cols, array.ndim - 1).reshape(-1, cols)
@@ -513,7 +502,7 @@
     tables = [mine(a) for a in (fading_right_matrix, feature_fading_speed, self_reward, cluster_scaling_vector)]
 
     def one_prompt(prompt, proj):
-        normed, states = recurrence(prompt, prompt_extents, where, proj, lora, *tables)
+        normed, states = recurrence(prompt, prompt_extents, where, mixed, proj, ends, lora, *tables)
         return jnp.concatenate([normed, states.astype(bf16)], axis=1)
 
     def exchanged(block):
@@ -521,20 +510,22 @@
         return parts[:1] + [swapped(parts[d], "seq", d) for d in range(1, stretches)]
 
     def output(prompt, blocks, earlier):
-        own_lines = jnp.stack([block[:span] for block in blocks])
-        far_lines = swapped(own_lines, "tensor", 1)
-        return finished(prompt, reqs, where, x, own_lines, far_lines, out_weights, earlier)
+        far_blocks = swapped(blocks, "tensor", 1)
+        return finished(prompt, reqs, where, x, blocks, far_blocks, out_weights, earlier)
 
     block = one_prompt(0, proj)
     block, near, other, proj = tied(block, near, other, proj)
     first = exchanged(block)
-    block, across, *first = tied(one_prompt(1, proj), across, *first)
-    out_weights = [out_lines, near, other, across]
+    across = [swapped(near[:1], "seq", 2), swapped(other[1:], "seq", 1)]
+    block, *first = tied(one_prompt(1, proj), *first)
     second = exchanged(block)
+    first, *across = tied(jnp.stack(first), *across)
+    out_weights = [out_lines, near, other, *across]
     hidden_out = output(0, first, ())
     hidden_out, *second = tied(hidden_out, *second)
+    second = jnp.stack(second)
     hidden_out = output(1, second, (hidden_out,))
-    stretch_blocks = [jnp.stack([block[span:] for block in blocks]) for blocks in (first, second)]
+    stretch_blocks = [blocks[:, span:] for blocks in (first, second)]
 
     heads = cols // ATTEND_DIM
     states = jnp.stack(stretch_blocks).reshape(reqs, 2, 2, ATTEND_DIM, heads, ATTEND_DIM)

time: 311 us -> 286 us (0.920)
  waiting for transfers between devices: 68.7 us -> 42.6 us
  other arithmetic: 5.62 us -> 13 us
  Pallas kernels: 134 us -> 130 us
    ppermute x22 -> x24, waiting for transfers between devices: 33.6 us -> 13.7 us  [swapped(): return lax.ppermute(value, axis, [(i, i ^ by) for i in range(peers)])]
    another operation x12 -> x0, local copies, waits for them, and re-layouts: 8.69 us -> none  [the longest x6 4.8 us: output(): own_lines = jnp.stack([block[:span] for block in blocks])]
    slice x0 -> x6, local copies, waits for them, and re-layouts: none -> 7.22 us  [the longest x2 4.52 us: local(): across = [swapped(near[:1], 'seq', 2), swapped(other[1:], 'seq', 1)]]
    ppermute x7, waiting for transfers between devices: 26 us -> 19.7 us  [moved(): lax.ppermute(value, axis, [(i, i + by) for i in range(peers) if 0 <= i +...]
    pallas_call x3 -> x2, Pallas kernels: 37 us -> 33.5 us  [recurrence(): pl.pallas_call(functools.partial(wkv_kernel, prompt=prompt, parted=bool(e...]
    reshape x2, local copies, waits for them, and re-layouts: 1.49 us -> 4.89 us  [local(): states.reshape(reqs, 1, stretches * heads, ATTEND_DIM * ATTEND_DIM)]
    ppermute x22 -> x24, starting transfers between devices: 19.8 us -> 20.2 us  [swapped(): return lax.ppermute(value, axis, [(i, i ^ by) for i in range(peers)])]
  transfers between devices with their start and end apart: 30 -> 32, of which waited for: 8 -> 11; matrix products, arithmetic and copies ran while one was open for 10% -> 17% of each run, Pallas kernels for 42% -> 44%
where the time goes in v5:
time: 286 us; the launch traced here: 285 us
  Pallas kernels  130 us (45%)
  waiting for transfers between devices  42.6 us (15%)
  local copies, waits for them, and re-layouts  42.4 us (15%)
  starting transfers between devices  41.9 us (15%)
  between operations  14.4 us (5%)
  other arithmetic  13 us (5%)
    pallas_call x8, Pallas kernels, shifted(): pl.pallas_call(mix_kernel, grid_spec=pltpu.PrefetchScalarGridSpec(num_sca...  45.2 us
    pallas_call x2, Pallas kernels, recurrence(): pl.pallas_call(functools.partial(wkv_kernel, prompt=prompt, parted=bool(e...  33.5 us
    pallas_call x1, Pallas kernels, projected(): pl.pallas_call(project_kernel, grid_spec=pltpu.PrefetchScalarGridSpec(num...  25.4 us
    ppermute x7, starting transfers between devices, moved(): lax.ppermute(value, axis, [(i, i + by) for i in range(peers) if 0 <= i +...  21.7 us
    ppermute x24, starting transfers between devices, swapped(): return lax.ppermute(value, axis, [(i, i ^ by) for i in range(peers)])  20.2 us
    ppermute x7, waiting for transfers between devices, moved(): lax.ppermute(value, axis, [(i, i + by) for i in range(peers) if 0 <= i +...  19.7 us
    pallas_call x1, Pallas kernels, ordered(): pl.pallas_call(order_kernel, grid=(width // block,), in_specs=[pl.BlockSp...  14 us
    ppermute x24, waiting for transfers between devices, swapped(): return lax.ppermute(value, axis, [(i, i ^ by) for i in range(peers)])  13.7 us
  transfers between devices with their start and end apart: 32, of which 11 were waited for; matrix products, arithmetic and copies ran while one was open for 17% of the time, Pallas kernels for 44%

profile of v5, /device:TPU:0, one launch (start us, length us, event | category | flops | bytes accessed | tf_op | source)
XLA Modules:
  0.0 284.7 jit_solution(13295939606848404136)
XLA Ops:
  7.2 1.7 constant_dynamic-slice_fusion
  8.9 4.8 %collective-permute-start = (bf16[16,4096]{1,0:T(8,128)(2,1)}, bf16[16,4096]{1,0:T(8,128)(2,1)S(1)}, u32[]{:S(2)}, u32[]{:S(2)}) collective-permute-start(bf16[16,4096]{1,0:T(8,128)(2,1)} %constant_dynamic-slice_fusion), channel_id=1, source_target_pairs={{0,1},{1,2},{2,3},{4,5},{5,6},{6,7},{8,9},{9,10},{10,11},{12,13},{... | collective-permute-start | bytes 393224 | tf_op jit(solution)/shard_map/ppermute | solution.py:407
  13.8 2.9 %dynamic-slice_convert_fusion = (bf16[3,256,256]{2,1,0:T(8,128)(2,1)}, bf16[3,256,256]{2,1,0:T(8,128)(2,1)}, bf16[3,256,256]{2,1,0:T(8,128)(2,1)S(1)}, bf16[3,256,256]{2,1,0:T(8,128)(2,1)}) fusion(f32[3,256,1024]{2,1,0:T(8,128)} %param.22, s32[]{:T(128)S(6)} %select_n.74, s32[]{:T(128)S(6)} %select_n.72, s32[]{:T(128)S(6)} %select_n.71, s32[]{:T(128)S(6)} %select_n.73), kind=kLoop, calls=%fused_computation.8 | loop fusion | bytes 3145744 | tf_op jit(solution)/shard_map/convert_element_type | solution.py:439
  16.7 1.5 collective-permute-start.1
  18.3 2.0 collective-permute-start.3
  21.1 1.8 constant_dynamic-slice_fusion.3
  23.7 14.0 %shard_map.185 = (bf16[272,4096]{1,0:T(8,128)(2,1)}, f32[8,4096]{1,0:T(8,128)S(1)}) custom-call(bf16[272,4096]{1,0:T(8,128)(2,1)S(1)} %pad_maximum_fusion.x_ref, f32[1,4096]{1,0:T(1,128)S(1)} %bitcast.46, f32[8,4096]{1,0:T(8,128)S(1)} %pad.4.coeff_ref, s32[1,4096]{1,0:T(1,128)S(1)} %bitcast.45), custom_call_target="tpu_custom_call" | custom-call | flops 1024 | bytes 1024 | tf_op jit(solution)/shard_map/pallas_call | solution.py:76
  37.7 1.6 collective-permute-start.4
  39.5 2.3 pad_maximum_fusion.2.refs_0_
  41.8 4.7 %collective-permute-start.8 = (bf16[4,3,256,256]{3,2,1,0:T(8,128)(2,1)}, bf16[4,3,256,256]{3,2,1,0:T(8,128)(2,1)}, u32[]{:S(2)}, u32[]{:S(2)}) collective-permute-start(bf16[4,3,256,256]{3,2,1,0:T(8,128)(2,1)} %pad_maximum_fusion.2.refs_0_), channel_id=1, source_target_pairs={{0,4},{4,8},{8,12},{1,5},{5,9},{9,13},{2,6},{6,10},{10,14},{3,7},{... | collective-permute-start | bytes 4718600 | tf_op jit(solution)/shard_map/ppermute | solution.py:407
  47.8 12.1 %gather_fusion = bf16[4096,128]{1,0:T(8,128)(2,1)S(1)} fusion(bf16[4096,128]{1,0:T(8,128)(2,1)S(1)} %copy-done, s32[4096]{0:T(1024)S(1)} %fusion), kind=kCustom, calls=%fused_computation | custom fusion | bytes 2113536 | tf_op jit(solution)/shard_map/gather | solution.py:464
  60.0 6.4 %shard_map.186 = (bf16[3,2,4,256,4096]{4,3,2,1,0:T(8,128)(2,1)}, bf16[2,4,256,128]{3,2,1,0:T(8,128)(2,1)S(1)}) custom-call(s32[3]{0:T(128)S(1)} %pad_add_fusion.where_ref, bf16[272,4096]{1,0:T(8,128)(2,1)} %get-tuple-element.74.act_ref, f32[8,4096]{1,0:T(8,128)S(1)} %get-tuple-element.75.coeff_ref, bf16[4096,128]{1,0:T(8,128)(2,1)S(1)} %gather_fusion), custom_call_target="tpu_custom_call" | custom-call | flops 1024 | bytes 1024 | tf_op jit(solution)/shard_map/pallas_call | solution.py:131
  66.4 6.3 %shard_map.187 = (bf16[3,2,4,256,4096]{4,3,2,1,0:T(8,128)(2,1)}, bf16[2,4,256,128]{3,2,1,0:T(8,128)(2,1)S(1)}) custom-call(s32[3]{0:T(128)S(1)} %pad_add_fusion.where_ref, bf16[272,4096]{1,0:T(8,128)(2,1)} %collective-permute-done.6.act_ref, f32[8,4096]{1,0:T(8,128)S(1)} %get-tuple-element.75.coeff_ref, ...), custom_call_target="tpu_custom_call", output_to_operand_aliasing={{0}: (4, {}), {1}: (5, {})} | custom-call | flops 1024 | bytes 1024 | tf_op jit(solution)/shard_map/pallas_call | solution.py:131
  72.7 9.2 %all-gather.3.cloned.1.call-done = bf16[4096,256]{1,0:T(8,128)(2,1)} async-done(((bf16[1024,256]{1,0:T(8,128)(2,1)}), bf16[4096,256]{1,0:T(8,128)(2,1)}) %all-gather.3.cloned.1.call-update) | async-done | bytes 2097168 | tf_op jit(solution)/shard_map/all_gather | solution.py:443
  81.8 1.7 dynamic-slice_bitcast_fusion
  83.6 2.6 collective-permute-done.7
  86.2 1.5 pad_maximum_fusion.1.refs_0_
  87.8 9.8 %collective-permute-done.8.refs_1_ = bf16[4,3,256,256]{3,2,1,0:T(8,128)(2,1)} collective-permute-done((bf16[4,3,256,256]{3,2,1,0:T(8,128)(2,1)}, bf16[4,3,256,256]{3,2,1,0:T(8,128)(2,1)}, u32[]{:S(2)}, u32[]{:S(2)}) %collective-permute-start.8) | collective-permute-done | bytes 1572896 | tf_op jit(solution)/shard_map/ppermute | solution.py:407
  97.6 2.0 collective-permute-done.9.refs_2_
  100.1 4.9 %collective-permute-start.12 = (bf16[4,3,256,256]{3,2,1,0:T(8,128)(2,1)}, bf16[4,3,256,256]{3,2,1,0:T(8,128)(2,1)}, u32[]{:S(2)}, u32[]{:S(2)}) collective-permute-start(bf16[4,3,256,256]{3,2,1,0:T(8,128)(2,1)} %collective-permute-done.8.refs_1_), channel_id=1, source_target_pairs={{0,4},{4,8},{8,12},{1,5},{5,9},{9,13},{2,6},{6,10},{10,14},{3,7},{... | collective-permute-start | bytes 4718600 | tf_op jit(solution)/shard_map/ppermute | solution.py:407
  107.7 1.6 collective-permute-start.15
  110.5 1.6 collective-permute-start.14
  112.2 6.3 %shard_map.188 = (bf16[3,2,4,256,4096]{4,3,2,1,0:T(8,128)(2,1)}, bf16[2,4,256,128]{3,2,1,0:T(8,128)(2,1)S(1)}) custom-call(s32[3]{0:T(128)S(1)} %pad_add_fusion.where_ref, bf16[272,4096]{1,0:T(8,128)(2,1)} %collective-permute-done.4.act_ref, f32[8,4096]{1,0:T(8,128)S(1)} %get-tuple-element.75.coeff_ref, ...), custom_call_target="tpu_custom_call", output_to_operand_aliasing={{0}: (4, {}), {1}: (5, {})} | custom-call | flops 1024 | bytes 1024 | tf_op jit(solution)/shard_map/pallas_call | solution.py:131
  118.5 6.3 %shard_map.189 = (bf16[3,2,4,256,4096]{4,3,2,1,0:T(8,128)(2,1)}, bf16[2,4,256,128]{3,2,1,0:T(8,128)(2,1)S(1)}) custom-call(s32[3]{0:T(128)S(1)} %pad_add_fusion.where_ref, bf16[272,4096]{1,0:T(8,128)(2,1)} %collective-permute-done.5.act_ref, f32[8,4096]{1,0:T(8,128)S(1)} %get-tuple-element.75.coeff_ref, ...), custom_call_target="tpu_custom_call", output_to_operand_aliasing={{0}: (4, {}), {1}: (5, {})} | custom-call | flops 1024 | bytes 1024 | tf_op jit(solution)/shard_map/pallas_call | solution.py:131
  124.8 5.1 %shard_map.190 = (bf16[3,2,4,256,4096]{4,3,2,1,0:T(8,128)(2,1)}, bf16[2,4,256,128]{3,2,1,0:T(8,128)(2,1)S(1)}) custom-call(s32[3]{0:T(128)S(1)} %pad_add_fusion.where_ref, bf16[272,4096]{1,0:T(8,128)(2,1)S(1)} %collective-permute-done.11.act_ref, f32[8,4096]{1,0:T(8,128)S(1)} %get-tuple-element.75.coeff_ref, ...), custom_call_target="tpu_custom_call", output_to_operand_aliasing={{0}: (4, {}), {1}: (5, {})} | custom-call | flops 1024 | bytes 1024 | tf_op jit(solution)/shard_map/pallas_call | solution.py:131
  129.9 4.9 %shard_map.191 = (bf16[3,2,4,256,4096]{4,3,2,1,0:T(8,128)(2,1)}, bf16[2,4,256,128]{3,2,1,0:T(8,128)(2,1)S(1)}) custom-call(s32[3]{0:T(128)S(1)} %pad_add_fusion.where_ref, bf16[272,4096]{1,0:T(8,128)(2,1)S(1)} %collective-permute-done.10.act_ref, f32[8,4096]{1,0:T(8,128)S(1)} %get-tuple-element.75.coeff_ref, ...), custom_call_target="tpu_custom_call", output_to_operand_aliasing={{0}: (4, {}), {1}: (5, {})} | custom-call | flops 1024 | bytes 1024 | tf_op jit(solution)/shard_map/pallas_call | solution.py:131
  135.4 2.7 collective-permute-done.12.refs_3_
  138.1 5.2 %collective-permute-done.13.refs_4_ = bf16[4,3,256,256]{3,2,1,0:T(8,128)(2,1)} collective-permute-done((bf16[4,3,256,256]{3,2,1,0:T(8,128)(2,1)}, bf16[4,3,256,256]{3,2,1,0:T(8,128)(2,1)}, u32[]{:S(2)}, u32[]{:S(2)}) %collective-permute-start.13) | collective-permute-done | bytes 1572896 | tf_op jit(solution)/shard_map/ppermute | solution.py:407
  143.6 1.6 collective-permute-start.19
  145.1 1.6 collective-permute-start.20
  146.7 3.2 %collective-permute-start.17 = (bf16[4,3,256,256]{3,2,1,0:T(8,128)(2,1)}, bf16[4,3,256,256]{3,2,1,0:T(8,128)(2,1)}, u32[]{:S(2)}, u32[]{:S(2)}) collective-permute-start(bf16[4,3,256,256]{3,2,1,0:T(8,128)(2,1)} %collective-permute-done.12.refs_3_), channel_id=1, source_target_pairs={{0,4},{4,8},{8,12},{1,5},{5,9},{9,13},{2,6},{6,10},{10,14},{3,7},{... | collective-permute-start | bytes 4718600 | tf_op jit(solution)/shard_map/ppermute | solution.py:407
  156.8 4.8 %shard_map.192 = (bf16[3,2,4,256,4096]{4,3,2,1,0:T(8,128)(2,1)}, bf16[2,4,256,128]{3,2,1,0:T(8,128)(2,1)S(1)}) custom-call(s32[3]{0:T(128)S(1)} %pad_add_fusion.where_ref, bf16[272,4096]{1,0:T(8,128)(2,1)S(1)} %constant_dynamic-update-slice_fusion.act_ref, f32[8,4096]{1,0:T(8,128)S(1)} %get-tuple-element.75.coeff_ref, ...), custom_call_target="tpu_custom_call", output_to_operand_aliasing={{0}: (4, {}), {1}: (5, {})} | custom-call | flops 1024 | bytes 1024 | tf_op jit(solution)/shard_map/pallas_call | solution.py:131
  161.6 5.1 %shard_map.193 = (bf16[3,2,4,256,4096]{4,3,2,1,0:T(8,128)(2,1)}, bf16[2,4,256,128]{3,2,1,0:T(8,128)(2,1)S(1)}) custom-call(s32[3]{0:T(128)S(1)} %pad_add_fusion.where_ref, bf16[272,4096]{1,0:T(8,128)(2,1)S(1)} %collective-permute-done.16.act_ref, f32[8,4096]{1,0:T(8,128)S(1)} %get-tuple-element.75.coeff_ref, ...), custom_call_target="tpu_custom_call", output_to_operand_aliasing={{0}: (4, {}), {1}: (5, {})} | custom-call | flops 1024 | bytes 1024 | tf_op jit(solution)/shard_map/pallas_call | solution.py:131
  166.7 25.4 %shard_map.194.refs_3_ = f32[3,2,4,256,256]{4,3,2,1,0:T(8,128)} custom-call(s32[3]{0:T(128)} %copy-done.5, bf16[3,2,4,256,4096]{4,3,2,1,0:T(8,128)(2,1)} %get-tuple-element.113.act_ref.refs_0_, bf16[4,3,256,256]{3,2,1,0:T(8,128)(2,1)} %pad_maximum_fusion.2.refs_0_, bf16[4,3,256,256]{3,2,1,0:T(8,128)(2,1)} %collective-permute-done.8.refs_1_, ...), custom_call_target="tpu_custom_call" | custom-call | flops 1024 | bytes 1024 | tf_op jit(solution)/shard_map/pallas_call | solution.py:190
  192.1 16.7 %shard_map.195 = (bf16[4,256,256]{2,1,0:T(8,128)(2,1)}, f32[4,64,256]{2,1,0:T(8,128)}) custom-call(s32[2]{0:T(128)} %extent_ref.3, s32[3]{0:T(128)} %copy-done.5, bf16[3,2,4,256,4096]{4,3,2,1,0:T(8,128)(2,1)} %get-tuple-element.113.act_ref.refs_0_, bf16[4,3,256,256]{3,2,1,0:T(8,128)(2,1)} %collective-permute-done.17.refs_1_, ...), custom_call_target="tpu_custom_call" | custom-call | flops 1024 | bytes 1024 | tf_op jit(solution)/shard_map/pallas_call | solution.py:330
  210.9 2.3 slice.24
  213.6 2.3 slice.25
  216.3 1.7 collective-permute-start.21
  218.0 1.6 collective-permute-start.22
  219.9 16.7 %shard_map.196 = (bf16[4,256,256]{2,1,0:T(8,128)(2,1)}, f32[4,64,256]{2,1,0:T(8,128)}) custom-call(s32[2]{0:T(128)} %extent_ref.3, s32[3]{0:T(128)} %copy-done.5, bf16[3,2,4,256,4096]{4,3,2,1,0:T(8,128)(2,1)} %get-tuple-element.113.act_ref.refs_0_, bf16[4,3,256,256]{3,2,1,0:T(8,128)(2,1)} %collective-permute-done.17.refs_1_, ...), custom_call_target="tpu_custom_call" | custom-call | flops 1024 | bytes 1024 | tf_op jit(solution)/shard_map/pallas_call | solution.py:330
  238.7 7.0 %collective-permute-done.21 = bf16[320,256]{1,0:T(8,128)(2,1)S(1)} collective-permute-done((bf16[320,256]{1,0:T(8,128)(2,1)S(1)}, bf16[320,256]{1,0:T(8,128)(2,1)S(1)}, u32[]{:S(2)}, u32[]{:S(2)}) %collective-permute-start.21) | collective-permute-done | bytes 163872 | tf_op jit(solution)/shard_map/ppermute | solution.py:38
  245.7 2.8 collective-permute-done.23
  250.3 2.7 collective-permute-start.29
  253.2 6.1 %shard_map.197.refs_5_ = bf16[2,256,2048]{2,1,0:T(8,128)(2,1)} custom-call(s32[3]{0:T(128)S(1)} %copy-done.6, bf16[512,4096]{1,0:T(8,128)(2,1)} %bitcast.49, bf16[4,320,256]{2,1,0:T(8,128)(2,1)S(1)} %pad_maximum_fusion.5.own_ref, bf16[4,320,256]{2,1,0:T(8,128)(2,1)} %collective-permute-done.26.far_ref, bf16[2,2,1024,256]{3,2,1,0:T(8,128)(2,1)} %pad_maximum_fusion.1.refs_0_, ...), custom_call_target="tpu_custom_call" | custom-call | flops 1024 | bytes 1024 | tf_op jit(solution)/shard_map/pallas_call | solution.py:388
  263.0 1.5 reverse_select_fusion.1
  265.7 2.5 copy.35
  268.3 2.4 reshape.42
  271.7 6.1 %shard_map.198 = bf16[2,256,2048]{2,1,0:T(8,128)(2,1)} custom-call(s32[3]{0:T(128)S(1)} %copy-done.6, bf16[512,4096]{1,0:T(8,128)(2,1)} %bitcast.50, bf16[4,320,256]{2,1,0:T(8,128)(2,1)S(1)} %copy-done.4, bf16[4,320,256]{2,1,0:T(8,128)(2,1)} %collective-permute-done.30.far_ref, ...), custom_call_target="tpu_custom_call", output_to_operand_aliasing={{}: (9, {})} | custom-call | flops 1024 | bytes 1024 | tf_op jit(solution)/shard_map/pallas_call | solution.py:388
  (93 shorter events, 28.7 us)
Async XLA Ops:
  7.2 40.7 %copy-start = (bf16[4096,128]{1,0:T(8,128)(2,1)S(1)}, bf16[4096,128]{1,0:T(8,128)(2,1)}, u32[]{:S(2)}) copy-start(bf16[4096,128]{1,0:T(8,128)(2,1)} %param.24) | copy-start | bytes 3145732
  7.2 13.1 %copy-start.9 = (f32[1024,256]{1,0:T(8,128)S(1)}, f32[1024,256]{1,0:T(8,128)}, u32[]{:S(2)}) copy-start(f32[1024,256]{1,0:T(8,128)} %param.23) | copy-start | bytes 3145732
  7.2 74.6 %all-gather.3.cloned.1.call-start = ((), (), s32[]{:S(2)}) async-start(), calls=%async_computation | async-start | bytes 2621440 | tf_op jit(solution)/shard_map/all_gather | solution.py:443
  8.9 14.0 %collective-permute-start = (bf16[16,4096]{1,0:T(8,128)(2,1)}, bf16[16,4096]{1,0:T(8,128)(2,1)S(1)}, u32[]{:S(2)}, u32[]{:S(2)}) collective-permute-start(bf16[16,4096]{1,0:T(8,128)(2,1)} %constant_dynamic-slice_fusion), channel_id=1, source_target_pairs={{0,1},{1,2},{2,3},{4,5},{5,6},{6,7},{8,9},{9,10},{10,11},{12,13},{... | collective-permute-start | bytes 393224 | tf_op jit(solution)/shard_map/ppermute | solution.py:407
  16.7 20.9 %collective-permute-start.1 = (bf16[3,256,256]{2,1,0:T(8,128)(2,1)}, bf16[3,256,256]{2,1,0:T(8,128)(2,1)S(1)}, u32[]{:S(2)}, u32[]{:S(2)}) collective-permute-start(bf16[3,256,256]{2,1,0:T(8,128)(2,1)} %get-tuple-element.141), channel_id=1, source_target_pairs={{0,1},{1,0},{2,3},{3,2},{4,5},{5,4},{6,7},{7,6},{8,9},{9,8},{10,11... | collective-permute-start | bytes 1179656 | tf_op jit(solution)/shard_map/ppermute | solution.py:38
  18.2 19.4 %collective-permute-start.2 = (bf16[3,256,256]{2,1,0:T(8,128)(2,1)}, bf16[3,256,256]{2,1,0:T(8,128)(2,1)S(1)}, u32[]{:S(2)}, u32[]{:S(2)}) collective-permute-start(bf16[3,256,256]{2,1,0:T(8,128)(2,1)} %get-tuple-element.143), channel_id=1, source_target_pairs={{0,2},{1,3},{2,0},{3,1},{4,6},{5,7},{6,4},{7,5},{8,10},{9,11},{10,... | collective-permute-start | bytes 1179656 | tf_op jit(solution)/shard_map/ppermute | solution.py:38
  18.3 19.4 %collective-permute-start.3 = (bf16[3,256,256]{2,1,0:T(8,128)(2,1)}, bf16[3,256,256]{2,1,0:T(8,128)(2,1)}, u32[]{:S(2)}, u32[]{:S(2)}) collective-permute-start(bf16[3,256,256]{2,1,0:T(8,128)(2,1)} %get-tuple-element.140), channel_id=1, source_target_pairs={{0,3},{1,2},{2,1},{3,0},{4,7},{5,6},{6,5},{7,4},{8,11},{9,10},{10,... | collective-permute-start | bytes 1179656 | tf_op jit(solution)/shard_map/ppermute | solution.py:38
  21.1 1.8 copy-start.10
  22.9 0.7 copy-start.7
  22.9 0.7 copy-start.8
  37.7 28.7 %collective-permute-start.6 = (bf16[272,4096]{1,0:T(8,128)(2,1)}, bf16[272,4096]{1,0:T(8,128)(2,1)}, u32[]{:S(2)}, u32[]{:S(2)}) collective-permute-start(bf16[272,4096]{1,0:T(8,128)(2,1)} %get-tuple-element.74.act_ref), channel_id=1, source_target_pairs={{0,16},{16,0},{1,17},{17,1},{2,18},{18,2},{3,19},{19,3},{4,20},{20... | collective-permute-start | bytes 6684680 | tf_op jit(solution)/shard_map/ppermute | solution.py:38
  37.7 61.8 %collective-permute-start.4 = (bf16[272,4096]{1,0:T(8,128)(2,1)}, bf16[272,4096]{1,0:T(8,128)(2,1)}, u32[]{:S(2)}, u32[]{:S(2)}) collective-permute-start(bf16[272,4096]{1,0:T(8,128)(2,1)} %get-tuple-element.74.act_ref), channel_id=1, source_target_pairs={{0,1},{1,0},{2,3},{3,2},{4,5},{5,4},{6,7},{7,6},{8,9},{9,8},{10,11... | collective-permute-start | bytes 6684680 | tf_op jit(solution)/shard_map/ppermute | solution.py:38
  39.3 60.3 %collective-permute-start.5 = (bf16[272,4096]{1,0:T(8,128)(2,1)}, bf16[272,4096]{1,0:T(8,128)(2,1)}, u32[]{:S(2)}, u32[]{:S(2)}) collective-permute-start(bf16[272,4096]{1,0:T(8,128)(2,1)} %get-tuple-element.74.act_ref), channel_id=1, source_target_pairs={{0,2},{1,3},{2,0},{3,1},{4,6},{5,7},{6,4},{7,5},{8,10},{9,11},{10,... | collective-permute-start | bytes 6684680 | tf_op jit(solution)/shard_map/ppermute | solution.py:38
  39.5 122.2 %copy-start.5 = (s32[3]{0:T(128)}, s32[3]{0:T(128)S(1)}, u32[]{:S(2)}) copy-start(s32[3]{0:T(128)S(1)} %pad_add_fusion.where_ref) | copy-start | bytes 40
  41.8 55.8 %collective-permute-start.8 = (bf16[4,3,256,256]{3,2,1,0:T(8,128)(2,1)}, bf16[4,3,256,256]{3,2,1,0:T(8,128)(2,1)}, u32[]{:S(2)}, u32[]{:S(2)}) collective-permute-start(bf16[4,3,256,256]{3,2,1,0:T(8,128)(2,1)} %pad_maximum_fusion.2.refs_0_), channel_id=1, source_target_pairs={{0,4},{4,8},{8,12},{1,5},{5,9},{9,13},{2,6},{6,10},{10,14},{3,7},{... | collective-permute-start | bytes 4718600 | tf_op jit(solution)/shard_map/ppermute | solution.py:407
  46.5 53.0 %collective-permute-start.9 = (bf16[4,3,256,256]{3,2,1,0:T(8,128)(2,1)}, bf16[4,3,256,256]{3,2,1,0:T(8,128)(2,1)}, u32[]{:S(2)}, u32[]{:S(2)}) collective-permute-start(bf16[4,3,256,256]{3,2,1,0:T(8,128)(2,1)} %pad_maximum_fusion.2.refs_0_), channel_id=1, source_target_pairs={{4,0},{8,4},{12,8},{5,1},{9,5},{13,9},{6,2},{10,6},{14,10},{7,3},{... | collective-permute-start | bytes 4718600 | tf_op jit(solution)/shard_map/ppermute | solution.py:407
  83.5 2.7 collective-permute-start.7
  99.6 11.0 %collective-permute-start.11 = (bf16[272,4096]{1,0:T(8,128)(2,1)}, bf16[272,4096]{1,0:T(8,128)(2,1)S(1)}, u32[]{:S(2)}, u32[]{:S(2)}) collective-permute-start(bf16[272,4096]{1,0:T(8,128)(2,1)} %collective-permute-done.4.act_ref), channel_id=1, source_target_pairs={{0,16},{16,0},{1,17},{17,1},{2,18},{18,2},{3,19},{19,3},{4,20},{20... | collective-permute-start | bytes 6684680 | tf_op jit(solution)/shard_map/ppermute | solution.py:38
  99.6 30.3 %collective-permute-start.10 = (bf16[272,4096]{1,0:T(8,128)(2,1)}, bf16[272,4096]{1,0:T(8,128)(2,1)S(1)}, u32[]{:S(2)}, u32[]{:S(2)}) collective-permute-start(bf16[272,4096]{1,0:T(8,128)(2,1)} %collective-permute-done.5.act_ref), channel_id=1, source_target_pairs={{0,16},{16,0},{1,17},{17,1},{2,18},{18,2},{3,19},{19,3},{4,20},{20... | collective-permute-start | bytes 6684680 | tf_op jit(solution)/shard_map/ppermute | solution.py:38
  100.1 38.0 %collective-permute-start.12 = (bf16[4,3,256,256]{3,2,1,0:T(8,128)(2,1)}, bf16[4,3,256,256]{3,2,1,0:T(8,128)(2,1)}, u32[]{:S(2)}, u32[]{:S(2)}) collective-permute-start(bf16[4,3,256,256]{3,2,1,0:T(8,128)(2,1)} %collective-permute-done.8.refs_1_), channel_id=1, source_target_pairs={{0,4},{4,8},{8,12},{1,5},{5,9},{9,13},{2,6},{6,10},{10,14},{3,7},{... | collective-permute-start | bytes 4718600 | tf_op jit(solution)/shard_map/ppermute | solution.py:407
  105.0 38.3 %collective-permute-start.13 = (bf16[4,3,256,256]{3,2,1,0:T(8,128)(2,1)}, bf16[4,3,256,256]{3,2,1,0:T(8,128)(2,1)}, u32[]{:S(2)}, u32[]{:S(2)}) collective-permute-start(bf16[4,3,256,256]{3,2,1,0:T(8,128)(2,1)} %collective-permute-done.9.refs_2_), channel_id=1, source_target_pairs={{4,0},{8,4},{12,8},{5,1},{9,5},{13,9},{6,2},{10,6},{14,10},{7,3},{... | collective-permute-start | bytes 4718600 | tf_op jit(solution)/shard_map/ppermute | solution.py:407
  107.7 27.7 %collective-permute-start.15 = (bf16[144,4096]{1,0:T(8,128)(2,1)S(1)}, bf16[144,4096]{1,0:T(8,128)(2,1)S(1)}, u32[]{:S(2)}, u32[]{:S(2)}) collective-permute-start(bf16[144,4096]{1,0:T(8,128)(2,1)S(1)} %slice.23), channel_id=1, source_target_pairs={{0,1},{1,0},{2,3},{3,2},{4,5},{5,4},{6,7},{7,6},{8,9},{9,8},{10,11... | collective-permute-start | bytes 3538952 | tf_op jit(solution)/shard_map/ppermute | solution.py:38
  110.5 24.6 %collective-permute-start.14 = (bf16[128,4096]{1,0:T(8,128)(2,1)S(1)}, bf16[128,4096]{1,0:T(8,128)(2,1)S(1)}, u32[]{:S(2)}, u32[]{:S(2)}) collective-permute-start(bf16[128,4096]{1,0:T(8,128)(2,1)S(1)} %slice.22), channel_id=1, source_target_pairs={{0,2},{1,3},{2,0},{3,1},{4,6},{5,7},{6,4},{7,5},{8,10},{9,11},{10,... | collective-permute-start | bytes 3145736 | tf_op jit(solution)/shard_map/ppermute | solution.py:38
  143.5 18.1 %collective-permute-start.16 = (bf16[272,4096]{1,0:T(8,128)(2,1)S(1)}, bf16[272,4096]{1,0:T(8,128)(2,1)S(1)}, u32[]{:S(2)}, u32[]{:S(2)}) collective-permute-start(bf16[272,4096]{1,0:T(8,128)(2,1)S(1)} %constant_dynamic-update-slice_fusion.act_ref), channel_id=1, source_target_pairs={{0,16},{16,0},{1,17},{17,1},{2,18},{18,2},{3,19},{19,3},{4,20},{20... | collective-permute-start | bytes 6684680 | tf_op jit(solution)/shard_map/ppermute | solution.py:38
  143.6 67.4 %collective-permute-start.19 = (bf16[2,2,1024,256]{3,2,1,0:T(8,128)(2,1)}, bf16[2,2,1024,256]{3,2,1,0:T(8,128)(2,1)}, u32[]{:S(2)}, u32[]{:S(2)}) collective-permute-start(bf16[2,2,1024,256]{3,2,1,0:T(8,128)(2,1)} %pad_maximum_fusion.1.refs_0_), channel_id=1, source_target_pairs={{0,1},{1,0},{2,3},{3,2},{4,5},{5,4},{6,7},{7,6},{8,9},{9,8},{10,11... | collective-permute-start | bytes 6291464 | tf_op jit(solution)/shard_map/ppermute | solution.py:38
  145.1 65.8 %collective-permute-start.20 = (bf16[2,2,1024,256]{3,2,1,0:T(8,128)(2,1)}, bf16[2,2,1024,256]{3,2,1,0:T(8,128)(2,1)}, u32[]{:S(2)}, u32[]{:S(2)}) collective-permute-start(bf16[2,2,1024,256]{3,2,1,0:T(8,128)(2,1)} %pad_maximum_fusion.1.refs_0_), channel_id=1, source_target_pairs={{0,2},{1,3},{2,0},{3,1},{4,6},{5,7},{6,4},{7,5},{8,10},{9,11},{10,... | collective-permute-start | bytes 6291464 | tf_op jit(solution)/shard_map/ppermute | solution.py:38
  146.7 45.4 %collective-permute-start.17 = (bf16[4,3,256,256]{3,2,1,0:T(8,128)(2,1)}, bf16[4,3,256,256]{3,2,1,0:T(8,128)(2,1)}, u32[]{:S(2)}, u32[]{:S(2)}) collective-permute-start(bf16[4,3,256,256]{3,2,1,0:T(8,128)(2,1)} %collective-permute-done.12.refs_3_), channel_id=1, source_target_pairs={{0,4},{4,8},{8,12},{1,5},{5,9},{9,13},{2,6},{6,10},{10,14},{3,7},{... | collective-permute-start | bytes 4718600 | tf_op jit(solution)/shard_map/ppermute | solution.py:407
  149.9 42.2 %collective-permute-start.18 = (bf16[4,3,256,256]{3,2,1,0:T(8,128)(2,1)}, bf16[4,3,256,256]{3,2,1,0:T(8,128)(2,1)}, u32[]{:S(2)}, u32[]{:S(2)}) collective-permute-start(bf16[4,3,256,256]{3,2,1,0:T(8,128)(2,1)} %collective-permute-done.13.refs_4_), channel_id=1, source_target_pairs={{4,0},{8,4},{12,8},{5,1},{9,5},{13,9},{6,2},{10,6},{14,10},{7,3},{... | collective-permute-start | bytes 4718600 | tf_op jit(solution)/shard_map/ppermute | solution.py:407
  166.7 25.4 %copy-start.2 = (bf16[2,4,256,128]{3,2,1,0:T(8,128)(2,1)}, bf16[2,4,256,128]{3,2,1,0:T(8,128)(2,1)S(1)}, u32[]{:S(2)}) copy-start(bf16[2,4,256,128]{3,2,1,0:T(8,128)(2,1)S(1)} %get-tuple-element.117.refs_4_) | copy-start | bytes 1572868
  213.2 35.4 %collective-permute-start.24 = (bf16[1,2,1024,256]{3,2,1,0:T(8,128)(2,1)}, bf16[1,2,1024,256]{3,2,1,0:T(8,128)(2,1)S(1)}, u32[]{:S(2)}, u32[]{:S(2)}) collective-permute-start(bf16[1,2,1024,256]{3,2,1,0:T(8,128)(2,1)} %slice.24), channel_id=1, source_target_pairs={{0,2},{1,3},{2,0},{3,1},{4,6},{5,7},{6,4},{7,5},{8,10},{9,11},{10,... | collective-permute-start | bytes 3145736 | tf_op jit(solution)/shard_map/ppermute | solution.py:38
  215.9 32.8 %collective-permute-start.25 = (bf16[1,2,1024,256]{3,2,1,0:T(8,128)(2,1)}, bf16[1,2,1024,256]{3,2,1,0:T(8,128)(2,1)S(1)}, u32[]{:S(2)}, u32[]{:S(2)}) collective-permute-start(bf16[1,2,1024,256]{3,2,1,0:T(8,128)(2,1)} %slice.25), channel_id=1, source_target_pairs={{0,1},{1,0},{2,3},{3,2},{4,5},{5,4},{6,7},{7,6},{8,9},{9,8},{10,11... | collective-permute-start | bytes 3145736 | tf_op jit(solution)/shard_map/ppermute | solution.py:38
  216.3 29.4 %collective-permute-start.21 = (bf16[320,256]{1,0:T(8,128)(2,1)S(1)}, bf16[320,256]{1,0:T(8,128)(2,1)S(1)}, u32[]{:S(2)}, u32[]{:S(2)}) collective-permute-start(bf16[320,256]{1,0:T(8,128)(2,1)S(1)} %get-tuple-element.152), channel_id=1, source_target_pairs={{0,1},{1,0},{2,3},{3,2},{4,5},{5,4},{6,7},{7,6},{8,9},{9,8},{10,11... | collective-permute-start | bytes 491528 | tf_op jit(solution)/shard_map/ppermute | solution.py:38
  218.0 27.7 %collective-permute-start.22 = (bf16[320,256]{1,0:T(8,128)(2,1)S(1)}, bf16[320,256]{1,0:T(8,128)(2,1)S(1)}, u32[]{:S(2)}, u32[]{:S(2)}) collective-permute-start(bf16[320,256]{1,0:T(8,128)(2,1)S(1)} %get-tuple-element.151), channel_id=1, source_target_pairs={{0,2},{1,3},{2,0},{3,1},{4,6},{5,7},{6,4},{7,5},{8,10},{9,11},{10,... | collective-permute-start | bytes 491528 | tf_op jit(solution)/shard_map/ppermute | solution.py:38
  219.6 28.9 %collective-permute-start.23 = (bf16[320,256]{1,0:T(8,128)(2,1)S(1)}, bf16[320,256]{1,0:T(8,128)(2,1)S(1)}, u32[]{:S(2)}, u32[]{:S(2)}) collective-permute-start(bf16[320,256]{1,0:T(8,128)(2,1)S(1)} %get-tuple-element.150), channel_id=1, source_target_pairs={{0,3},{1,2},{2,1},{3,0},{4,7},{5,6},{6,5},{7,4},{8,11},{9,10},{10,... | collective-permute-start | bytes 491528 | tf_op jit(solution)/shard_map/ppermute | solution.py:38
  237.6 15.6 %copy-start.6 = (s32[3]{0:T(128)S(1)}, s32[3]{0:T(128)}, u32[]{:S(2)}) copy-start(s32[3]{0:T(128)} %copy-done.5) | copy-start | bytes 40
  248.7 4.5 %collective-permute-start.26 = (bf16[4,320,256]{2,1,0:T(8,128)(2,1)S(1)}, bf16[4,320,256]{2,1,0:T(8,128)(2,1)}, u32[]{:S(2)}, u32[]{:S(2)}) collective-permute-start(bf16[4,320,256]{2,1,0:T(8,128)(2,1)S(1)} %pad_maximum_fusion.5.own_ref), channel_id=1, source_target_pairs={{0,16},{16,0},{1,17},{17,1},{2,18},{18,2},{3,19},{19,3},{4,20},{20... | collective-permute-start | bytes 1966088 | tf_op jit(solution)/shard_map/ppermute | solution.py:38
  249.5 9.8 %collective-permute-start.27 = (bf16[320,256]{1,0:T(8,128)(2,1)}, bf16[320,256]{1,0:T(8,128)(2,1)}, u32[]{:S(2)}, u32[]{:S(2)}) collective-permute-start(bf16[320,256]{1,0:T(8,128)(2,1)} %get-tuple-element.148), channel_id=1, source_target_pairs={{0,1},{1,0},{2,3},{3,2},{4,5},{5,4},{6,7},{7,6},{8,9},{9,8},{10,11... | collective-permute-start | bytes 491528 | tf_op jit(solution)/shard_map/ppermute | solution.py:38
  249.8 10.1 %collective-permute-start.28 = (bf16[320,256]{1,0:T(8,128)(2,1)}, bf16[320,256]{1,0:T(8,128)(2,1)}, u32[]{:S(2)}, u32[]{:S(2)}) collective-permute-start(bf16[320,256]{1,0:T(8,128)(2,1)} %get-tuple-element.147), channel_id=1, source_target_pairs={{0,2},{1,3},{2,0},{3,1},{4,6},{5,7},{6,4},{7,5},{8,10},{9,11},{10,... | collective-permute-start | bytes 491528 | tf_op jit(solution)/shard_map/ppermute | solution.py:38
  250.3 9.6 %collective-permute-start.29 = (bf16[320,256]{1,0:T(8,128)(2,1)S(1)}, bf16[320,256]{1,0:T(8,128)(2,1)}, u32[]{:S(2)}, u32[]{:S(2)}) collective-permute-start(bf16[320,256]{1,0:T(8,128)(2,1)S(1)} %get-tuple-element.146), channel_id=1, source_target_pairs={{0,3},{1,2},{2,1},{3,0},{4,7},{5,6},{6,5},{7,4},{8,11},{9,10},{10,... | collective-permute-start | bytes 491528 | tf_op jit(solution)/shard_map/ppermute | solution.py:38
  261.1 4.6 %copy-start.3 = (bf16[4,320,256]{2,1,0:T(8,128)(2,1)}, bf16[4,320,256]{2,1,0:T(8,128)(2,1)S(1)}, u32[]{:S(2)}) copy-start(bf16[4,320,256]{2,1,0:T(8,128)(2,1)S(1)} %pad_maximum_fusion.6.own_ref) | copy-start | bytes 1966084
  261.1 9.5 %collective-permute-start.30 = (bf16[4,320,256]{2,1,0:T(8,128)(2,1)S(1)}, bf16[4,320,256]{2,1,0:T(8,128)(2,1)}, u32[]{:S(2)}, u32[]{:S(2)}) collective-permute-start(bf16[4,320,256]{2,1,0:T(8,128)(2,1)S(1)} %pad_maximum_fusion.6.own_ref), channel_id=1, source_target_pairs={{0,16},{16,0},{1,17},{17,1},{2,18},{18,2},{3,19},{19,3},{4,20},{20... | collective-permute-start | bytes 1966088 | tf_op jit(solution)/shard_map/ppermute | solution.py:38
  270.6 1.1 copy-start.4
  271.7 6.1 %copy-start.1 = (bf16[4096,128]{1,0:T(8,128)(2,1)S(1)}, bf16[4096,128]{1,0:T(8,128)(2,1)}, u32[]{:S(2)}) copy-start(bf16[4096,128]{1,0:T(8,128)(2,1)} %param.24) | copy-start | bytes 3145732
Sparse Core Ops, SparseCore 0:
  21.2 60.5 all-gather.2

commit v6 on v5

--- a/solution.py
+++ b/solution.py
@@ -191,10 +191,10 @@
         project_kernel,
         grid_spec=pltpu.PrefetchScalarGridSpec(
             num_scalar_prefetch=1,
-            grid=(kinds, sides),
-            in_specs=[pl.BlockSpec((1, 1, stretches, span, width), lambda j, m, w: (j, m, 0, 0, 0))]
+            grid=(kinds, 2 * sides),
+            in_specs=[pl.BlockSpec((1, 1, stretches // 2, span, width), lambda j, m, w: (j, m // 2, m % 2, 0, 0))]
             + [pl.BlockSpec((stretches, 1, depth, cols), lambda j, m, w: (0, j, 0, 0))] * len(hops),
-            out_specs=pl.BlockSpec((1, 1, stretches, span, cols), lambda j, m, w: (j, m, 0, 0, 0)),
+            out_specs=pl.BlockSpec((1, 1, stretches // 2, span, cols), lambda j, m, w: (j, m // 2, m % 2, 0, 0)),
             scratch_shapes=[pltpu.VMEM((width, cols), bf16)],
         ),
         out_shape=jax.ShapeDtypeStruct((kinds, sides, stretches, span, cols), f32),
@@ -236,7 +236,7 @@
     if parted:
         act_ref, below_ref, above_ref, *refs, lines_ref = refs
     proj_ref, lora_ref, right_ref, speed_ref, reward_ref, scale_ref, sums_ref, level_ref, same_ref, *refs = refs
-    normed_ref, state_ref, memory_ref = refs
+    out_ref, memory_ref = refs
     step = pl.program_id(0)
     tokens, cols = proj_ref.shape[3:]
     heads = cols // ATTEND_DIM
@@ -290,14 +290,14 @@
     folded = memory[:ATTEND_DIM]
     for h in range(1, heads):
         folded += memory[h * ATTEND_DIM : (h + 1) * ATTEND_DIM]
-    state_ref[0] = folded
+    out_ref[0, tokens:] = folded.astype(bf16)
 
     y = jnp.concatenate(rows, axis=0) + own
     y_high = y.astype(bf16)
     y_low = (y - y_high.astype(f32)).astype(bf16)
     centred = y - (dot(y_high, same) + dot(y_low, same)) * (1.0 / ATTEND_DIM)
     spread = dot((centred * centred).astype(bf16), same) * (1.0 / ATTEND_DIM)
-    normed_ref[0] = (centred * lax.rsqrt(spread + eps) * scale_ref[...] * valid).astype(bf16)
+    out_ref[0, :tokens] = (centred * lax.rsqrt(spread + eps) * scale_ref[...] * valid).astype(bf16)
 
 
 def recurrence(prompt, extents, where, mixed, proj, ends, lora, right, speed, reward, scale):
@@ -338,16 +338,10 @@
                 pl.BlockSpec((1, 1, span, inner), lambda c, e, w: (w[1] ^ prompt, c, 0, 0)),
             ]
             + [fixed(a) for a in tables],
-            out_specs=[
-                pl.BlockSpec((1, span, cols), lambda c, e, w: (c, 0, 0)),
-                pl.BlockSpec((1, ATTEND_DIM, cols), lambda c, e, w: (c, 0, 0)),
-            ],
+            out_specs=pl.BlockSpec((1, span + ATTEND_DIM, cols), lambda c, e, w: (c, 0, 0)),
             scratch_shapes=scratch,
         ),
-        out_shape=[
-            jax.ShapeDtypeStruct((stretches, span, cols), bf16),
-            jax.ShapeDtypeStruct((stretches, ATTEND_DIM, cols), f32),
-        ],
+        out_shape=jax.ShapeDtypeStruct((stretches, span + ATTEND_DIM, cols), bf16),
         compiler_params=vmem(56),
         cost_estimate=SMALL,
     )(extents, where, *first, proj, lora, *tables)
@@ -402,6 +396,46 @@
     )(where, x, own, far, *weights, *earlier)
 
 
+def states_kernel(where_ref, blocks_ref, pick_ref, *refs):
+    out_ref = refs[-1]
+    stretches, _, cols = blocks_ref.shape
+    heads = cols // ATTEND_DIM
+    half = ATTEND_DIM // 2
+    for b in range(stretches):
+        lines = dot_nt(pick_ref[...], blocks_ref[where_ref[0] ^ b])
+        for h in range(heads):
+            at = 2 * h * half
+            pairs = jnp.concatenate([lines[at : at + half], lines[at + half : at + 2 * half]], axis=1)
+            head = b * heads + h
+            for i in range(half):
+                out_ref[0, 0, head : head + 1, 2 * i * ATTEND_DIM : 2 * (i + 1) * ATTEND_DIM] = pairs[i : i + 1]
+
+
+def states_laid(prompt, prompts, where, blocks, earlier):
+    stretches, lines, cols = blocks.shape
+    heads = cols // ATTEND_DIM
+    order = np.arange(cols).reshape(heads, ATTEND_DIM // 2, 2).transpose(0, 2, 1).reshape(-1)
+    pick = jnp.asarray(order[:, None] == np.arange(cols)[None, :], bf16)
+    shape = (1, 1, stretches * heads, ATTEND_DIM * ATTEND_DIM)
+    return pl.pallas_call(
+        states_kernel,
+        grid_spec=pltpu.PrefetchScalarGridSpec(
+            num_scalar_prefetch=1,
+            grid=(1,),
+            in_specs=[
+                pl.BlockSpec((stretches, ATTEND_DIM, cols), lambda n, w: (0, lines // ATTEND_DIM - 1, 0)),
+                pl.BlockSpec((cols, cols), lambda n, w: (0, 0)),
+            ]
+            + [pl.BlockSpec(memory_space=pl.ANY)] * len(earlier),
+            out_specs=pl.BlockSpec(shape, lambda n, w: (prompt, 0, 0, 0)),
+        ),
+        out_shape=jax.ShapeDtypeStruct((prompts, *shape[1:]), f32),
+        input_output_aliases={3: 0} if earlier else {},
+        compiler_params=vmem(32),
+        cost_estimate=SMALL,
+    )(where, blocks, pick, *earlier)
+
+
 def moved(value, axis, by):
     peers = lax.axis_size(axis)
     return lax.ppermute(value, axis, [(i, i + by) for i in range(peers) if 0 <= i + by < peers])
@@ -467,7 +501,12 @@
     results = mixed_in(act, 0, 0, ())
     results = mixed_in(swapped(act, "tensor", 1), 1, 0, results)
     share = groups // cores
-    out_lines, *results = tied(out_lines, *results)
+    def mine(array):
+        return lax.dynamic_slice_in_dim(array, s * cols, cols, array.ndim - 1).reshape(-1, cols)
+
+    tables = [mine(a) for a in (fading_right_matrix, feature_fading_speed, self_reward, cluster_scaling_vector)]
+    out_lines, *rest = tied(out_lines, *results, *tables)
+    results, tables = rest[:2], rest[2:]
     kept = lax.dynamic_slice_in_dim(out_lines, t * share, share, 0)
     given = lax.dynamic_slice_in_dim(out_lines, (1 - t) * share, share, 0)
     out_lines = jnp.stack([kept, swapped(given, "tensor", 1)])
@@ -494,16 +533,11 @@
         proj = projected(where, mixed, [lines, *hops])
     else:
         proj = projected_whole(where, mixed, *hops)
-    mixed, proj, *ends = tied(mixed, proj, *ends)
-
-    def mine(array):
-        return lax.dynamic_slice_in_dim(array, s * cols, cols, array.ndim - 1).reshape(-1, cols)
-
-    tables = [mine(a) for a in (fading_right_matrix, feature_fading_speed, self_reward, cluster_scaling_vector)]
+    mixed, proj, near, other, *ends = tied(mixed, proj, near, other, *ends)
+    across = [swapped(near[:1], "seq", 2), swapped(other[1:], "seq", 1)]
 
     def one_prompt(prompt, proj):
-        normed, states = recurrence(prompt, prompt_extents, where, mixed, proj, ends, lora, *tables)
-        return jnp.concatenate([normed, states.astype(bf16)], axis=1)
+        return recurrence(prompt, prompt_extents, where, mixed, proj, ends, lora, *tables)
 
     def exchanged(block):
         parts = [lax.dynamic_index_in_dim(block, s ^ d, 0, keepdims=False) for d in range(stretches)]
@@ -513,26 +547,19 @@
         far_blocks = swapped(blocks, "tensor", 1)
         return finished(prompt, reqs, where, x, blocks, far_blocks, out_weights, earlier)
 
-    block = one_prompt(0, proj)
-    block, near, other, proj = tied(block, near, other, proj)
+    block, proj = tied(one_prompt(0, proj), proj)
     first = exchanged(block)
-    across = [swapped(near[:1], "seq", 2), swapped(other[1:], "seq", 1)]
-    block, *first = tied(one_prompt(1, proj), *first)
+    block, *rest = tied(one_prompt(1, proj), *first, *across)
+    first, across = rest[:-2], rest[-2:]
     second = exchanged(block)
-    first, *across = tied(jnp.stack(first), *across)
+    first = jnp.stack(first)
     out_weights = [out_lines, near, other, *across]
     hidden_out = output(0, first, ())
-    hidden_out, *second = tied(hidden_out, *second)
+    stretch_states = states_laid(0, reqs, where, first, ())
+    hidden_out, stretch_states, *second = tied(hidden_out, stretch_states, *second)
     second = jnp.stack(second)
     hidden_out = output(1, second, (hidden_out,))
-    stretch_blocks = [blocks[:, span:] for blocks in (first, second)]
-
-    heads = cols // ATTEND_DIM
-    states = jnp.stack(stretch_blocks).reshape(reqs, 2, 2, ATTEND_DIM, heads, ATTEND_DIM)
-    states = jnp.where(s % 2 == 1, states[:, :, ::-1], states)
-    states = jnp.where(s // 2 == 1, states[:, ::-1], states)
-    states = jnp.transpose(states, (0, 1, 2, 4, 5, 3)).astype(f32)
-    stretch_states = states.reshape(reqs, 1, stretches * heads, ATTEND_DIM * ATTEND_DIM)
+    stretch_states = states_laid(1, reqs, where, second, (stretch_states,))
     return (hidden_out, stretch_states)
 
 

time: 286 us -> 267 us (0.934)
  waiting for transfers between devices: 42.6 us -> 31.8 us
  other arithmetic: 13 us -> 5.06 us
  local copies, waits for them, and re-layouts: 42.4 us -> 35.4 us
  Pallas kernels: 130 us -> 135 us
    all_gather x1, waiting for transfers between devices: 9.17 us -> 0.01 us  [local(): out_lines = lax.all_gather(out_half, 'req', axis=0, tiled=False)]
    ppermute x24, waiting for transfers between devices: 13.7 us -> 8.25 us  [swapped(): return lax.ppermute(value, axis, [(i, i ^ by) for i in range(peers)])]
    reshape x2 -> x0, local copies, waits for them, and re-layouts: 4.89 us -> none  [local(): states.reshape(reqs, 1, stretches * heads, ATTEND_DIM * ATTEND_DIM)]
    ppermute x7, waiting for transfers between devices: 19.7 us -> 23.5 us  [moved(): lax.ppermute(value, axis, [(i, i + by) for i in range(peers) if 0 <= i +...]
    pallas_call x0 -> x2, Pallas kernels: none -> 3.24 us  [states_laid(): pl.pallas_call(states_kernel, grid_spec=pltpu.PrefetchScalarGridSpec(num_...]
  transfers between devices with their start and end apart: 32 -> 32, of which waited for: 11 -> 11; matrix products, arithmetic and copies ran while one was open for 17% -> 14% of each run, Pallas kernels for 44% -> 49%
where the time goes in v6:
time: 267 us; the launch traced here: 265 us
  Pallas kernels  135 us (51%)
  starting transfers between devices  43.2 us (16%)
  local copies, waits for them, and re-layouts  35.4 us (13%)
  waiting for transfers between devices  31.8 us (12%)
  between operations  14.4 us (5%)
  other arithmetic  5.06 us (2%)
    pallas_call x8, Pallas kernels, shifted(): pl.pallas_call(mix_kernel, grid_spec=pltpu.PrefetchScalarGridSpec(num_sca...  44.6 us
    pallas_call x2, Pallas kernels, recurrence(): pl.pallas_call(functools.partial(wkv_kernel, prompt=prompt, parted=bool(e...  33.5 us
    pallas_call x1, Pallas kernels, projected(): pl.pallas_call(project_kernel, grid_spec=pltpu.PrefetchScalarGridSpec(num...  28.1 us
    ppermute x7, waiting for transfers between devices, moved(): lax.ppermute(value, axis, [(i, i + by) for i in range(peers) if 0 <= i +...  23.5 us
    ppermute x7, starting transfers between devices, moved(): lax.ppermute(value, axis, [(i, i + by) for i in range(peers) if 0 <= i +...  21.7 us
    ppermute x24, starting transfers between devices, swapped(): return lax.ppermute(value, axis, [(i, i ^ by) for i in range(peers)])  21.5 us
    pallas_call x1, Pallas kernels, ordered(): pl.pallas_call(order_kernel, grid=(width // block,), in_specs=[pl.BlockSp...  14 us
    gather x1, local copies, waits for them, and re-layouts, local(): left = fading_left_matrix[perm]  12.1 us
  transfers between devices with their start and end apart: 32, of which 11 were waited for; matrix products, arithmetic and copies ran while one was open for 14% of the time, Pallas kernels for 49%

profile of v6, /device:TPU:0, one launch (start us, length us, event | category | flops | bytes accessed | tf_op | source)
XLA Modules:
  0.0 265.4 jit_solution(17304763514817818932)
XLA Ops:
  8.3 4.8 %collective-permute-start = (bf16[16,4096]{1,0:T(8,128)(2,1)S(1)}, bf16[16,4096]{1,0:T(8,128)(2,1)S(1)}, u32[]{:S(2)}, u32[]{:S(2)}) collective-permute-start(bf16[16,4096]{1,0:T(8,128)(2,1)S(1)} %constant_dynamic-slice_fusion), channel_id=1, source_target_pairs={{0,1},{1,2},{2,3},{4,5},{5,6},{6,7},{8,9},{9,10},{10,11},{12,13},{... | collective-permute-start | bytes 393224 | tf_op jit(solution)/shard_map/ppermute | solution.py:441
  13.2 2.9 %dynamic-slice_convert_fusion = (bf16[3,256,256]{2,1,0:T(8,128)(2,1)}, bf16[3,256,256]{2,1,0:T(8,128)(2,1)}, bf16[3,256,256]{2,1,0:T(8,128)(2,1)S(1)}, bf16[3,256,256]{2,1,0:T(8,128)(2,1)}) fusion(f32[3,256,1024]{2,1,0:T(8,128)} %param.24, s32[]{:T(128)S(6)} %select_n.49, s32[]{:T(128)S(6)} %select_n.47, s32[]{:T(128)S(6)} %select_n.46, s32[]{:T(128)S(6)} %select_n.48), kind=kLoop, calls=%fused_computation.5 | loop fusion | bytes 3145744 | tf_op jit(solution)/shard_map/convert_element_type | solution.py:473
  16.1 1.5 collective-permute-start.1
  17.6 2.0 collective-permute-start.3
  20.5 1.8 constant_dynamic-slice_fusion.3
  23.0 14.0 %shard_map.203 = (bf16[272,4096]{1,0:T(8,128)(2,1)}, f32[8,4096]{1,0:T(8,128)S(1)}) custom-call(bf16[272,4096]{1,0:T(8,128)(2,1)S(1)} %pad_maximum_fusion.x_ref, f32[1,4096]{1,0:T(1,128)S(1)} %bitcast.42, f32[8,4096]{1,0:T(8,128)S(1)} %pad.4.coeff_ref, s32[1,4096]{1,0:T(1,128)S(1)} %bitcast.41), custom_call_target="tpu_custom_call" | custom-call | flops 1024 | bytes 1024 | tf_op jit(solution)/shard_map/pallas_call | solution.py:76
  37.1 1.6 collective-permute-start.4
  42.9 1.5 constant_dynamic-slice_fusion.2.refs_5_
  44.3 2.3 pad_maximum_fusion.2.refs_0_
  46.6 4.7 %collective-permute-start.8 = (bf16[4,3,256,256]{3,2,1,0:T(8,128)(2,1)}, bf16[4,3,256,256]{3,2,1,0:T(8,128)(2,1)}, u32[]{:S(2)}, u32[]{:S(2)}) collective-permute-start(bf16[4,3,256,256]{3,2,1,0:T(8,128)(2,1)} %pad_maximum_fusion.2.refs_0_), channel_id=1, source_target_pairs={{0,4},{4,8},{8,12},{1,5},{5,9},{9,13},{2,6},{6,10},{10,14},{3,7},{... | collective-permute-start | bytes 4718600 | tf_op jit(solution)/shard_map/ppermute | solution.py:441
  52.7 12.1 %gather_fusion = bf16[4096,128]{1,0:T(8,128)(2,1)S(1)} fusion(bf16[4096,128]{1,0:T(8,128)(2,1)S(1)} %copy-done, s32[4096]{0:T(1024)S(1)} %fusion), kind=kCustom, calls=%fused_computation | custom fusion | bytes 2113536 | tf_op jit(solution)/shard_map/gather | solution.py:498
  64.8 6.3 %shard_map.204 = (bf16[3,2,4,256,4096]{4,3,2,1,0:T(8,128)(2,1)}, bf16[2,4,256,128]{3,2,1,0:T(8,128)(2,1)S(1)}) custom-call(s32[3]{0:T(128)S(1)} %pad_add_fusion.where_ref, bf16[272,4096]{1,0:T(8,128)(2,1)} %get-tuple-element.74.act_ref, f32[8,4096]{1,0:T(8,128)S(1)} %get-tuple-element.75.coeff_ref, bf16[4096,128]{1,0:T(8,128)(2,1)S(1)} %gather_fusion), custom_call_target="tpu_custom_call" | custom-call | flops 1024 | bytes 1024 | tf_op jit(solution)/shard_map/pallas_call | solution.py:131
  71.1 6.3 %shard_map.205 = (bf16[3,2,4,256,4096]{4,3,2,1,0:T(8,128)(2,1)}, bf16[2,4,256,128]{3,2,1,0:T(8,128)(2,1)S(1)}) custom-call(s32[3]{0:T(128)S(1)} %pad_add_fusion.where_ref, bf16[272,4096]{1,0:T(8,128)(2,1)} %collective-permute-done.6.act_ref, f32[8,4096]{1,0:T(8,128)S(1)} %get-tuple-element.75.coeff_ref, ...), custom_call_target="tpu_custom_call", output_to_operand_aliasing={{0}: (4, {}), {1}: (5, {})} | custom-call | flops 1024 | bytes 1024 | tf_op jit(solution)/shard_map/pallas_call | solution.py:131
  77.4 1.7 dynamic-slice_bitcast_fusion
  79.2 2.6 collective-permute-done.7
  81.8 1.5 pad_maximum_fusion.1.refs_0_
  83.3 13.8 %collective-permute-done.8.refs_1_ = bf16[4,3,256,256]{3,2,1,0:T(8,128)(2,1)} collective-permute-done((bf16[4,3,256,256]{3,2,1,0:T(8,128)(2,1)}, bf16[4,3,256,256]{3,2,1,0:T(8,128)(2,1)}, u32[]{:S(2)}, u32[]{:S(2)}) %collective-permute-start.8) | collective-permute-done | bytes 1572896 | tf_op jit(solution)/shard_map/ppermute | solution.py:441
  97.1 1.9 collective-permute-done.9.refs_2_
  99.5 4.9 %collective-permute-start.12 = (bf16[4,3,256,256]{3,2,1,0:T(8,128)(2,1)}, bf16[4,3,256,256]{3,2,1,0:T(8,128)(2,1)}, u32[]{:S(2)}, u32[]{:S(2)}) collective-permute-start(bf16[4,3,256,256]{3,2,1,0:T(8,128)(2,1)} %collective-permute-done.8.refs_1_), channel_id=1, source_target_pairs={{0,4},{4,8},{8,12},{1,5},{5,9},{9,13},{2,6},{6,10},{10,14},{3,7},{... | collective-permute-start | bytes 4718600 | tf_op jit(solution)/shard_map/ppermute | solution.py:441
  107.1 1.6 collective-permute-start.15
  110.0 1.7 collective-permute-start.14
  111.6 6.3 %shard_map.206 = (bf16[3,2,4,256,4096]{4,3,2,1,0:T(8,128)(2,1)}, bf16[2,4,256,128]{3,2,1,0:T(8,128)(2,1)S(1)}) custom-call(s32[3]{0:T(128)S(1)} %pad_add_fusion.where_ref, bf16[272,4096]{1,0:T(8,128)(2,1)} %collective-permute-done.4.act_ref, f32[8,4096]{1,0:T(8,128)S(1)} %get-tuple-element.75.coeff_ref, ...), custom_call_target="tpu_custom_call", output_to_operand_aliasing={{0}: (4, {}), {1}: (5, {})} | custom-call | flops 1024 | bytes 1024 | tf_op jit(solution)/shard_map/pallas_call | solution.py:131
  118.0 6.3 %shard_map.207 = (bf16[3,2,4,256,4096]{4,3,2,1,0:T(8,128)(2,1)}, bf16[2,4,256,128]{3,2,1,0:T(8,128)(2,1)S(1)}) custom-call(s32[3]{0:T(128)S(1)} %pad_add_fusion.where_ref, bf16[272,4096]{1,0:T(8,128)(2,1)} %collective-permute-done.5.act_ref, f32[8,4096]{1,0:T(8,128)S(1)} %get-tuple-element.75.coeff_ref, ...), custom_call_target="tpu_custom_call", output_to_operand_aliasing={{0}: (4, {}), {1}: (5, {})} | custom-call | flops 1024 | bytes 1024 | tf_op jit(solution)/shard_map/pallas_call | solution.py:131
  124.2 4.8 %shard_map.208 = (bf16[3,2,4,256,4096]{4,3,2,1,0:T(8,128)(2,1)}, bf16[2,4,256,128]{3,2,1,0:T(8,128)(2,1)S(1)}) custom-call(s32[3]{0:T(128)S(1)} %pad_add_fusion.where_ref, bf16[272,4096]{1,0:T(8,128)(2,1)S(1)} %collective-permute-done.11.act_ref, f32[8,4096]{1,0:T(8,128)S(1)} %get-tuple-element.75.coeff_ref, ...), custom_call_target="tpu_custom_call", output_to_operand_aliasing={{0}: (4, {}), {1}: (5, {})} | custom-call | flops 1024 | bytes 1024 | tf_op jit(solution)/shard_map/pallas_call | solution.py:131
  129.1 4.8 %shard_map.209 = (bf16[3,2,4,256,4096]{4,3,2,1,0:T(8,128)(2,1)}, bf16[2,4,256,128]{3,2,1,0:T(8,128)(2,1)S(1)}) custom-call(s32[3]{0:T(128)S(1)} %pad_add_fusion.where_ref, bf16[272,4096]{1,0:T(8,128)(2,1)S(1)} %collective-permute-done.10.act_ref, f32[8,4096]{1,0:T(8,128)S(1)} %get-tuple-element.75.coeff_ref, ...), custom_call_target="tpu_custom_call", output_to_operand_aliasing={{0}: (4, {}), {1}: (5, {})} | custom-call | flops 1024 | bytes 1024 | tf_op jit(solution)/shard_map/pallas_call | solution.py:131
  134.8 2.7 %collective-permute-done.12.refs_3_ = bf16[4,3,256,256]{3,2,1,0:T(8,128)(2,1)} collective-permute-done((bf16[4,3,256,256]{3,2,1,0:T(8,128)(2,1)}, bf16[4,3,256,256]{3,2,1,0:T(8,128)(2,1)}, u32[]{:S(2)}, u32[]{:S(2)}) %collective-permute-start.12) | collective-permute-done | bytes 1572896 | tf_op jit(solution)/shard_map/ppermute | solution.py:441
  137.5 5.2 %collective-permute-done.13.refs_4_ = bf16[4,3,256,256]{3,2,1,0:T(8,128)(2,1)} collective-permute-done((bf16[4,3,256,256]{3,2,1,0:T(8,128)(2,1)}, bf16[4,3,256,256]{3,2,1,0:T(8,128)(2,1)}, u32[]{:S(2)}, u32[]{:S(2)}) %collective-permute-start.13) | collective-permute-done | bytes 1572896 | tf_op jit(solution)/shard_map/ppermute | solution.py:441
  143.0 1.6 collective-permute-start.17
  144.5 1.6 collective-permute-start.18
  146.2 3.2 %collective-permute-start.19 = (bf16[4,3,256,256]{3,2,1,0:T(8,128)(2,1)}, bf16[4,3,256,256]{3,2,1,0:T(8,128)(2,1)}, u32[]{:S(2)}, u32[]{:S(2)}) collective-permute-start(bf16[4,3,256,256]{3,2,1,0:T(8,128)(2,1)} %collective-permute-done.12.refs_3_), channel_id=1, source_target_pairs={{0,4},{4,8},{8,12},{1,5},{5,9},{9,13},{2,6},{6,10},{10,14},{3,7},{... | collective-permute-start | bytes 4718600 | tf_op jit(solution)/shard_map/ppermute | solution.py:441
  149.4 1.5 collective-permute-start.20
  150.8 5.0 %shard_map.210 = (bf16[3,2,4,256,4096]{4,3,2,1,0:T(8,128)(2,1)}, bf16[2,4,256,128]{3,2,1,0:T(8,128)(2,1)S(1)}) custom-call(s32[3]{0:T(128)S(1)} %pad_add_fusion.where_ref, bf16[272,4096]{1,0:T(8,128)(2,1)S(1)} %constant_dynamic-update-slice_fusion.act_ref, f32[8,4096]{1,0:T(8,128)S(1)} %get-tuple-element.75.coeff_ref, ...), custom_call_target="tpu_custom_call", output_to_operand_aliasing={{0}: (4, {}), {1}: (5, {})} | custom-call | flops 1024 | bytes 1024 | tf_op jit(solution)/shard_map/pallas_call | solution.py:131
  155.8 4.9 %shard_map.211 = (bf16[3,2,4,256,4096]{4,3,2,1,0:T(8,128)(2,1)}, bf16[2,4,256,128]{3,2,1,0:T(8,128)(2,1)S(1)}) custom-call(s32[3]{0:T(128)S(1)} %pad_add_fusion.where_ref, bf16[272,4096]{1,0:T(8,128)(2,1)S(1)} %collective-permute-done.16.act_ref, f32[8,4096]{1,0:T(8,128)S(1)} %get-tuple-element.75.coeff_ref, ...), custom_call_target="tpu_custom_call", output_to_operand_aliasing={{0}: (4, {}), {1}: (5, {})} | custom-call | flops 1024 | bytes 1024 | tf_op jit(solution)/shard_map/pallas_call | solution.py:131
  160.7 28.1 %shard_map.212.refs_3_ = f32[3,2,4,256,256]{4,3,2,1,0:T(8,128)} custom-call(s32[3]{0:T(128)} %copy-done.4, bf16[3,2,4,256,4096]{4,3,2,1,0:T(8,128)(2,1)} %get-tuple-element.114.act_ref.refs_0_, bf16[4,3,256,256]{3,2,1,0:T(8,128)(2,1)} %pad_maximum_fusion.2.refs_0_, bf16[4,3,256,256]{3,2,1,0:T(8,128)(2,1)} %collective-permute-done.8.refs_1_, ...), custom_call_target="tpu_custom_call" | custom-call | flops 1024 | bytes 1024 | tf_op jit(solution)/shard_map/pallas_call | solution.py:190
  188.8 2.5 collective-permute-done.17.refs_1_
  192.6 2.3 slice.18
  194.8 1.6 collective-permute-start.24
  196.4 2.3 slice.19
  199.1 16.7 %shard_map.213 = bf16[4,320,256]{2,1,0:T(8,128)(2,1)} custom-call(s32[2]{0:T(128)} %extent_ref.3, s32[3]{0:T(128)} %copy-done.4, bf16[3,2,4,256,4096]{4,3,2,1,0:T(8,128)(2,1)} %get-tuple-element.114.act_ref.refs_0_, bf16[4,3,256,256]{3,2,1,0:T(8,128)(2,1)} %collective-permute-done.19.refs_1_, bf16[4,3,256,256]{3,2,1,0:T(8,128)(2,1)} %collective-permute-done.20.refs_2_, ...), custom_call_target="tpu_custom_call" | custom-call | flops 1024 | bytes 1024 | tf_op jit(solution)/shard_map/pallas_call | solution.py:330
  217.0 1.7 collective-permute-start.21
  219.1 1.4 collective-permute-start.23
  220.5 16.7 %shard_map.214 = bf16[4,320,256]{2,1,0:T(8,128)(2,1)} custom-call(s32[2]{0:T(128)} %extent_ref.3, s32[3]{0:T(128)} %copy-done.4, bf16[3,2,4,256,4096]{4,3,2,1,0:T(8,128)(2,1)} %get-tuple-element.114.act_ref.refs_0_, bf16[4,3,256,256]{3,2,1,0:T(8,128)(2,1)} %collective-permute-done.19.refs_1_, bf16[4,3,256,256]{3,2,1,0:T(8,128)(2,1)} %collective-permute-done.20.refs_2_, ...), custom_call_target="tpu_custom_call" | custom-call | flops 1024 | bytes 1024 | tf_op jit(solution)/shard_map/pallas_call | solution.py:330
  238.7 1.7 collective-permute-start.27
  240.9 1.4 collective-permute-start.29
  242.3 1.6 shard_map.216.refs_0_
  243.9 6.0 %shard_map.215.refs_5_ = bf16[2,256,2048]{2,1,0:T(8,128)(2,1)} custom-call(s32[3]{0:T(128)S(1)} %copy-done.5, bf16[512,4096]{1,0:T(8,128)(2,1)} %bitcast.45, bf16[4,320,256]{2,1,0:T(8,128)(2,1)S(1)} %pad_maximum_fusion.3.own_ref.blocks_ref, bf16[4,320,256]{2,1,0:T(8,128)(2,1)S(1)} %collective-permute-done.26.far_ref, ...), custom_call_target="tpu_custom_call" | custom-call | flops 1024 | bytes 1024 | tf_op jit(solution)/shard_map/pallas_call | solution.py:382
  250.5 1.6 shard_map.218
  252.6 6.0 %shard_map.217 = bf16[2,256,2048]{2,1,0:T(8,128)(2,1)} custom-call(s32[3]{0:T(128)S(1)} %copy-done.5, bf16[512,4096]{1,0:T(8,128)(2,1)} %bitcast.46, bf16[4,320,256]{2,1,0:T(8,128)(2,1)S(1)} %pad_maximum_fusion.4.own_ref.blocks_ref, bf16[4,320,256]{2,1,0:T(8,128)(2,1)S(1)} %collective-permute-done.30.far_ref, ...), custom_call_target="tpu_custom_call", output_to_operand_aliasing={{}: (9, {})} | custom-call | flops 1024 | bytes 1024 | tf_op jit(solution)/shard_map/pallas_call | solution.py:382
  (79 shorter events, 20.0 us)
Async XLA Ops:
  7.2 45.5 %copy-start = (bf16[4096,128]{1,0:T(8,128)(2,1)S(1)}, bf16[4096,128]{1,0:T(8,128)(2,1)}, u32[]{:S(2)}) copy-start(bf16[4096,128]{1,0:T(8,128)(2,1)} %param.26) | copy-start | bytes 3145732
  7.2 12.4 %copy-start.8 = (f32[1024,256]{1,0:T(8,128)S(1)}, f32[1024,256]{1,0:T(8,128)}, u32[]{:S(2)}) copy-start(f32[1024,256]{1,0:T(8,128)} %param.25) | copy-start | bytes 3145732
  7.2 70.2 %all-gather.3.cloned.1.call-start = ((), (), s32[]{:S(2)}) async-start(), calls=%async_computation | async-start | bytes 2621440 | tf_op jit(solution)/shard_map/all_gather | solution.py:477
  8.3 14.0 %collective-permute-start = (bf16[16,4096]{1,0:T(8,128)(2,1)S(1)}, bf16[16,4096]{1,0:T(8,128)(2,1)S(1)}, u32[]{:S(2)}, u32[]{:S(2)}) collective-permute-start(bf16[16,4096]{1,0:T(8,128)(2,1)S(1)} %constant_dynamic-slice_fusion), channel_id=1, source_target_pairs={{0,1},{1,2},{2,3},{4,5},{5,6},{6,7},{8,9},{9,10},{10,11},{12,13},{... | collective-permute-start | bytes 393224 | tf_op jit(solution)/shard_map/ppermute | solution.py:441
  16.1 20.9 %collective-permute-start.1 = (bf16[3,256,256]{2,1,0:T(8,128)(2,1)}, bf16[3,256,256]{2,1,0:T(8,128)(2,1)S(1)}, u32[]{:S(2)}, u32[]{:S(2)}) collective-permute-start(bf16[3,256,256]{2,1,0:T(8,128)(2,1)} %get-tuple-element.141), channel_id=1, source_target_pairs={{0,1},{1,0},{2,3},{3,2},{4,5},{5,4},{6,7},{7,6},{8,9},{9,8},{10,11... | collective-permute-start | bytes 1179656 | tf_op jit(solution)/shard_map/ppermute | solution.py:38
  17.6 19.4 %collective-permute-start.2 = (bf16[3,256,256]{2,1,0:T(8,128)(2,1)}, bf16[3,256,256]{2,1,0:T(8,128)(2,1)S(1)}, u32[]{:S(2)}, u32[]{:S(2)}) collective-permute-start(bf16[3,256,256]{2,1,0:T(8,128)(2,1)} %get-tuple-element.143), channel_id=1, source_target_pairs={{0,2},{1,3},{2,0},{3,1},{4,6},{5,7},{6,4},{7,5},{8,10},{9,11},{10,... | collective-permute-start | bytes 1179656 | tf_op jit(solution)/shard_map/ppermute | solution.py:38
  17.6 19.4 %collective-permute-start.3 = (bf16[3,256,256]{2,1,0:T(8,128)(2,1)}, bf16[3,256,256]{2,1,0:T(8,128)(2,1)}, u32[]{:S(2)}, u32[]{:S(2)}) collective-permute-start(bf16[3,256,256]{2,1,0:T(8,128)(2,1)} %get-tuple-element.140), channel_id=1, source_target_pairs={{0,3},{1,2},{2,1},{3,0},{4,7},{5,6},{6,5},{7,4},{8,11},{9,10},{10,... | collective-permute-start | bytes 1179656 | tf_op jit(solution)/shard_map/ppermute | solution.py:38
  20.5 1.8 copy-start.9
  22.3 0.7 copy-start.6
  22.3 0.7 copy-start.7
  37.1 34.1 %collective-permute-start.6 = (bf16[272,4096]{1,0:T(8,128)(2,1)}, bf16[272,4096]{1,0:T(8,128)(2,1)}, u32[]{:S(2)}, u32[]{:S(2)}) collective-permute-start(bf16[272,4096]{1,0:T(8,128)(2,1)} %get-tuple-element.74.act_ref), channel_id=1, source_target_pairs={{0,16},{16,0},{1,17},{17,1},{2,18},{18,2},{3,19},{19,3},{4,20},{20... | collective-permute-start | bytes 6684680 | tf_op jit(solution)/shard_map/ppermute | solution.py:38
  37.1 61.8 %collective-permute-start.4 = (bf16[272,4096]{1,0:T(8,128)(2,1)}, bf16[272,4096]{1,0:T(8,128)(2,1)}, u32[]{:S(2)}, u32[]{:S(2)}) collective-permute-start(bf16[272,4096]{1,0:T(8,128)(2,1)} %get-tuple-element.74.act_ref), channel_id=1, source_target_pairs={{0,1},{1,0},{2,3},{3,2},{4,5},{5,4},{6,7},{7,6},{8,9},{9,8},{10,11... | collective-permute-start | bytes 6684680 | tf_op jit(solution)/shard_map/ppermute | solution.py:38
  38.7 60.3 %collective-permute-start.5 = (bf16[272,4096]{1,0:T(8,128)(2,1)}, bf16[272,4096]{1,0:T(8,128)(2,1)}, u32[]{:S(2)}, u32[]{:S(2)}) collective-permute-start(bf16[272,4096]{1,0:T(8,128)(2,1)} %get-tuple-element.74.act_ref), channel_id=1, source_target_pairs={{0,2},{1,3},{2,0},{3,1},{4,6},{5,7},{6,4},{7,5},{8,10},{9,11},{10,... | collective-permute-start | bytes 6684680 | tf_op jit(solution)/shard_map/ppermute | solution.py:38
  42.9 113.0 %copy-start.4 = (s32[3]{0:T(128)}, s32[3]{0:T(128)S(1)}, u32[]{:S(2)}) copy-start(s32[3]{0:T(128)S(1)} %pad_add_fusion.where_ref) | copy-start | bytes 40
  46.6 50.4 %collective-permute-start.8 = (bf16[4,3,256,256]{3,2,1,0:T(8,128)(2,1)}, bf16[4,3,256,256]{3,2,1,0:T(8,128)(2,1)}, u32[]{:S(2)}, u32[]{:S(2)}) collective-permute-start(bf16[4,3,256,256]{3,2,1,0:T(8,128)(2,1)} %pad_maximum_fusion.2.refs_0_), channel_id=1, source_target_pairs={{0,4},{4,8},{8,12},{1,5},{5,9},{9,13},{2,6},{6,10},{10,14},{3,7},{... | collective-permute-start | bytes 4718600 | tf_op jit(solution)/shard_map/ppermute | solution.py:441
  51.3 47.6 %collective-permute-start.9 = (bf16[4,3,256,256]{3,2,1,0:T(8,128)(2,1)}, bf16[4,3,256,256]{3,2,1,0:T(8,128)(2,1)}, u32[]{:S(2)}, u32[]{:S(2)}) collective-permute-start(bf16[4,3,256,256]{3,2,1,0:T(8,128)(2,1)} %pad_maximum_fusion.2.refs_0_), channel_id=1, source_target_pairs={{4,0},{8,4},{12,8},{5,1},{9,5},{13,9},{6,2},{10,6},{14,10},{7,3},{... | collective-permute-start | bytes 4718600 | tf_op jit(solution)/shard_map/ppermute | solution.py:441
  79.1 2.7 %collective-permute-start.7 = (bf16[2,1024,256]{2,1,0:T(8,128)(2,1)S(1)}, bf16[2,1024,256]{2,1,0:T(8,128)(2,1)S(1)}, u32[]{:S(2)}, u32[]{:S(2)}) collective-permute-start(bf16[2,1024,256]{2,1,0:T(8,128)(2,1)S(1)} %get-tuple-element.145), channel_id=1, source_target_pairs={{0,16},{16,0},{1,17},{17,1},{2,18},{18,2},{3,19},{19,3},{4,20},{20... | collective-permute-start | bytes 3145736 | tf_op jit(solution)/shard_map/ppermute | solution.py:38
  99.0 11.0 %collective-permute-start.11 = (bf16[272,4096]{1,0:T(8,128)(2,1)}, bf16[272,4096]{1,0:T(8,128)(2,1)S(1)}, u32[]{:S(2)}, u32[]{:S(2)}) collective-permute-start(bf16[272,4096]{1,0:T(8,128)(2,1)} %collective-permute-done.4.act_ref), channel_id=1, source_target_pairs={{0,16},{16,0},{1,17},{17,1},{2,18},{18,2},{3,19},{19,3},{4,20},{20... | collective-permute-start | bytes 6684680 | tf_op jit(solution)/shard_map/ppermute | solution.py:38
  99.0 30.1 %collective-permute-start.10 = (bf16[272,4096]{1,0:T(8,128)(2,1)}, bf16[272,4096]{1,0:T(8,128)(2,1)S(1)}, u32[]{:S(2)}, u32[]{:S(2)}) collective-permute-start(bf16[272,4096]{1,0:T(8,128)(2,1)} %collective-permute-done.5.act_ref), channel_id=1, source_target_pairs={{0,16},{16,0},{1,17},{17,1},{2,18},{18,2},{3,19},{19,3},{4,20},{20... | collective-permute-start | bytes 6684680 | tf_op jit(solution)/shard_map/ppermute | solution.py:38
  99.5 38.0 %collective-permute-start.12 = (bf16[4,3,256,256]{3,2,1,0:T(8,128)(2,1)}, bf16[4,3,256,256]{3,2,1,0:T(8,128)(2,1)}, u32[]{:S(2)}, u32[]{:S(2)}) collective-permute-start(bf16[4,3,256,256]{3,2,1,0:T(8,128)(2,1)} %collective-permute-done.8.refs_1_), channel_id=1, source_target_pairs={{0,4},{4,8},{8,12},{1,5},{5,9},{9,13},{2,6},{6,10},{10,14},{3,7},{... | collective-permute-start | bytes 4718600 | tf_op jit(solution)/shard_map/ppermute | solution.py:441
  104.4 38.3 %collective-permute-start.13 = (bf16[4,3,256,256]{3,2,1,0:T(8,128)(2,1)}, bf16[4,3,256,256]{3,2,1,0:T(8,128)(2,1)}, u32[]{:S(2)}, u32[]{:S(2)}) collective-permute-start(bf16[4,3,256,256]{3,2,1,0:T(8,128)(2,1)} %collective-permute-done.9.refs_2_), channel_id=1, source_target_pairs={{4,0},{8,4},{12,8},{5,1},{9,5},{13,9},{6,2},{10,6},{14,10},{7,3},{... | collective-permute-start | bytes 4718600 | tf_op jit(solution)/shard_map/ppermute | solution.py:441
  107.1 27.7 %collective-permute-start.15 = (bf16[144,4096]{1,0:T(8,128)(2,1)S(1)}, bf16[144,4096]{1,0:T(8,128)(2,1)S(1)}, u32[]{:S(2)}, u32[]{:S(2)}) collective-permute-start(bf16[144,4096]{1,0:T(8,128)(2,1)S(1)} %slice.17), channel_id=1, source_target_pairs={{0,1},{1,0},{2,3},{3,2},{4,5},{5,4},{6,7},{7,6},{8,9},{9,8},{10,11... | collective-permute-start | bytes 3538952 | tf_op jit(solution)/shard_map/ppermute | solution.py:38
  110.0 24.6 %collective-permute-start.14 = (bf16[128,4096]{1,0:T(8,128)(2,1)S(1)}, bf16[128,4096]{1,0:T(8,128)(2,1)S(1)}, u32[]{:S(2)}, u32[]{:S(2)}) collective-permute-start(bf16[128,4096]{1,0:T(8,128)(2,1)S(1)} %slice.16), channel_id=1, source_target_pairs={{0,2},{1,3},{2,0},{3,1},{4,6},{5,7},{6,4},{7,5},{8,10},{9,11},{10,... | collective-permute-start | bytes 3145736 | tf_op jit(solution)/shard_map/ppermute | solution.py:38
  142.9 12.9 %collective-permute-start.16 = (bf16[272,4096]{1,0:T(8,128)(2,1)S(1)}, bf16[272,4096]{1,0:T(8,128)(2,1)S(1)}, u32[]{:S(2)}, u32[]{:S(2)}) collective-permute-start(bf16[272,4096]{1,0:T(8,128)(2,1)S(1)} %constant_dynamic-update-slice_fusion.act_ref), channel_id=1, source_target_pairs={{0,16},{16,0},{1,17},{17,1},{2,18},{18,2},{3,19},{19,3},{4,20},{20... | collective-permute-start | bytes 6684680 | tf_op jit(solution)/shard_map/ppermute | solution.py:38
  143.0 48.4 %collective-permute-start.17 = (bf16[2,2,1024,256]{3,2,1,0:T(8,128)(2,1)}, bf16[2,2,1024,256]{3,2,1,0:T(8,128)(2,1)}, u32[]{:S(2)}, u32[]{:S(2)}) collective-permute-start(bf16[2,2,1024,256]{3,2,1,0:T(8,128)(2,1)} %pad_maximum_fusion.1.refs_0_), channel_id=1, source_target_pairs={{0,1},{1,0},{2,3},{3,2},{4,5},{5,4},{6,7},{7,6},{8,9},{9,8},{10,11... | collective-permute-start | bytes 6291464 | tf_op jit(solution)/shard_map/ppermute | solution.py:38
  144.5 48.0 %collective-permute-start.18 = (bf16[2,2,1024,256]{3,2,1,0:T(8,128)(2,1)}, bf16[2,2,1024,256]{3,2,1,0:T(8,128)(2,1)}, u32[]{:S(2)}, u32[]{:S(2)}) collective-permute-start(bf16[2,2,1024,256]{3,2,1,0:T(8,128)(2,1)} %pad_maximum_fusion.1.refs_0_), channel_id=1, source_target_pairs={{0,2},{1,3},{2,0},{3,1},{4,6},{5,7},{6,4},{7,5},{8,10},{9,11},{10,... | collective-permute-start | bytes 6291464 | tf_op jit(solution)/shard_map/ppermute | solution.py:38
  146.2 42.7 %collective-permute-start.19 = (bf16[4,3,256,256]{3,2,1,0:T(8,128)(2,1)}, bf16[4,3,256,256]{3,2,1,0:T(8,128)(2,1)}, u32[]{:S(2)}, u32[]{:S(2)}) collective-permute-start(bf16[4,3,256,256]{3,2,1,0:T(8,128)(2,1)} %collective-permute-done.12.refs_3_), channel_id=1, source_target_pairs={{0,4},{4,8},{8,12},{1,5},{5,9},{9,13},{2,6},{6,10},{10,14},{3,7},{... | collective-permute-start | bytes 4718600 | tf_op jit(solution)/shard_map/ppermute | solution.py:441
  149.4 39.5 %collective-permute-start.20 = (bf16[4,3,256,256]{3,2,1,0:T(8,128)(2,1)}, bf16[4,3,256,256]{3,2,1,0:T(8,128)(2,1)}, u32[]{:S(2)}, u32[]{:S(2)}) collective-permute-start(bf16[4,3,256,256]{3,2,1,0:T(8,128)(2,1)} %collective-permute-done.13.refs_4_), channel_id=1, source_target_pairs={{4,0},{8,4},{12,8},{5,1},{9,5},{13,9},{6,2},{10,6},{14,10},{7,3},{... | collective-permute-start | bytes 4718600 | tf_op jit(solution)/shard_map/ppermute | solution.py:441
  160.7 28.1 %copy-start.2 = (bf16[2,4,256,128]{3,2,1,0:T(8,128)(2,1)}, bf16[2,4,256,128]{3,2,1,0:T(8,128)(2,1)S(1)}, u32[]{:S(2)}) copy-start(bf16[2,4,256,128]{3,2,1,0:T(8,128)(2,1)S(1)} %get-tuple-element.118.refs_4_) | copy-start | bytes 1572868
  194.8 42.5 %collective-permute-start.24 = (bf16[1,2,1024,256]{3,2,1,0:T(8,128)(2,1)}, bf16[1,2,1024,256]{3,2,1,0:T(8,128)(2,1)S(1)}, u32[]{:S(2)}, u32[]{:S(2)}) collective-permute-start(bf16[1,2,1024,256]{3,2,1,0:T(8,128)(2,1)} %slice.18), channel_id=1, source_target_pairs={{0,2},{1,3},{2,0},{3,1},{4,6},{5,7},{6,4},{7,5},{8,10},{9,11},{10,... | collective-permute-start | bytes 3145736 | tf_op jit(solution)/shard_map/ppermute | solution.py:38
  198.7 38.6 %collective-permute-start.25 = (bf16[1,2,1024,256]{3,2,1,0:T(8,128)(2,1)}, bf16[1,2,1024,256]{3,2,1,0:T(8,128)(2,1)S(1)}, u32[]{:S(2)}, u32[]{:S(2)}) collective-permute-start(bf16[1,2,1024,256]{3,2,1,0:T(8,128)(2,1)} %slice.19), channel_id=1, source_target_pairs={{0,1},{1,0},{2,3},{3,2},{4,5},{5,4},{6,7},{7,6},{8,9},{9,8},{10,11... | collective-permute-start | bytes 3145736 | tf_op jit(solution)/shard_map/ppermute | solution.py:38
  217.0 20.3 %collective-permute-start.21 = (bf16[320,256]{1,0:T(8,128)(2,1)S(1)}, bf16[320,256]{1,0:T(8,128)(2,1)S(1)}, u32[]{:S(2)}, u32[]{:S(2)}) collective-permute-start(bf16[320,256]{1,0:T(8,128)(2,1)S(1)} %get-tuple-element.152), channel_id=1, source_target_pairs={{0,1},{1,0},{2,3},{3,2},{4,5},{5,4},{6,7},{7,6},{8,9},{9,8},{10,11... | collective-permute-start | bytes 491528 | tf_op jit(solution)/shard_map/ppermute | solution.py:38
  218.7 18.6 %collective-permute-start.22 = (bf16[320,256]{1,0:T(8,128)(2,1)S(1)}, bf16[320,256]{1,0:T(8,128)(2,1)S(1)}, u32[]{:S(2)}, u32[]{:S(2)}) collective-permute-start(bf16[320,256]{1,0:T(8,128)(2,1)S(1)} %get-tuple-element.151), channel_id=1, source_target_pairs={{0,2},{1,3},{2,0},{3,1},{4,6},{5,7},{6,4},{7,5},{8,10},{9,11},{10,... | collective-permute-start | bytes 491528 | tf_op jit(solution)/shard_map/ppermute | solution.py:38
  219.1 18.2 %collective-permute-start.23 = (bf16[320,256]{1,0:T(8,128)(2,1)S(1)}, bf16[320,256]{1,0:T(8,128)(2,1)S(1)}, u32[]{:S(2)}, u32[]{:S(2)}) collective-permute-start(bf16[320,256]{1,0:T(8,128)(2,1)S(1)} %get-tuple-element.150), channel_id=1, source_target_pairs={{0,3},{1,2},{2,1},{3,0},{4,7},{5,6},{6,5},{7,4},{8,11},{9,10},{10,... | collective-permute-start | bytes 491528 | tf_op jit(solution)/shard_map/ppermute | solution.py:38
  237.3 5.0 %copy-start.3 = (bf16[256,256]{1,0:T(8,128)(2,1)S(1)}, bf16[256,256]{1,0:T(8,128)(2,1)}, u32[]{:S(2)}) copy-start(bf16[256,256]{1,0:T(8,128)(2,1)} %constant.63.clone.pick_ref) | copy-start | bytes 393220
  237.3 5.0 %copy-start.5 = (s32[3]{0:T(128)S(1)}, s32[3]{0:T(128)}, u32[]{:S(2)}) copy-start(s32[3]{0:T(128)} %copy-done.4) | copy-start | bytes 40
  237.4 6.5 %collective-permute-start.26 = (bf16[4,320,256]{2,1,0:T(8,128)(2,1)S(1)}, bf16[4,320,256]{2,1,0:T(8,128)(2,1)S(1)}, u32[]{:S(2)}, u32[]{:S(2)}) collective-permute-start(bf16[4,320,256]{2,1,0:T(8,128)(2,1)S(1)} %pad_maximum_fusion.3.own_ref.blocks_ref), channel_id=1, source_target_pairs={{0,16},{16,0},{1,17},{17,1},{2,18},{18,2},{3,19},{19,3},{4,20},{20... | collective-permute-start | bytes 1966088 | tf_op jit(solution)/shard_map/ppermute | solution.py:38
  238.7 11.2 %collective-permute-start.27 = (bf16[320,256]{1,0:T(8,128)(2,1)S(1)}, bf16[320,256]{1,0:T(8,128)(2,1)S(1)}, u32[]{:S(2)}, u32[]{:S(2)}) collective-permute-start(bf16[320,256]{1,0:T(8,128)(2,1)S(1)} %get-tuple-element.148), channel_id=1, source_target_pairs={{0,1},{1,0},{2,3},{3,2},{4,5},{5,4},{6,7},{7,6},{8,9},{9,8},{10,11... | collective-permute-start | bytes 491528 | tf_op jit(solution)/shard_map/ppermute | solution.py:38
  240.5 9.8 %collective-permute-start.28 = (bf16[320,256]{1,0:T(8,128)(2,1)S(1)}, bf16[320,256]{1,0:T(8,128)(2,1)S(1)}, u32[]{:S(2)}, u32[]{:S(2)}) collective-permute-start(bf16[320,256]{1,0:T(8,128)(2,1)S(1)} %get-tuple-element.147), channel_id=1, source_target_pairs={{0,2},{1,3},{2,0},{3,1},{4,6},{5,7},{6,4},{7,5},{8,10},{9,11},{10,... | collective-permute-start | bytes 491528 | tf_op jit(solution)/shard_map/ppermute | solution.py:38
  240.9 9.4 %collective-permute-start.29 = (bf16[320,256]{1,0:T(8,128)(2,1)S(1)}, bf16[320,256]{1,0:T(8,128)(2,1)S(1)}, u32[]{:S(2)}, u32[]{:S(2)}) collective-permute-start(bf16[320,256]{1,0:T(8,128)(2,1)S(1)} %get-tuple-element.146), channel_id=1, source_target_pairs={{0,3},{1,2},{2,1},{3,0},{4,7},{5,6},{6,5},{7,4},{8,11},{9,10},{10,... | collective-permute-start | bytes 491528 | tf_op jit(solution)/shard_map/ppermute | solution.py:38
  250.4 2.2 collective-permute-start.30
  252.6 6.0 %copy-start.1 = (bf16[4096,128]{1,0:T(8,128)(2,1)S(1)}, bf16[4096,128]{1,0:T(8,128)(2,1)}, u32[]{:S(2)}) copy-start(bf16[4096,128]{1,0:T(8,128)(2,1)} %param.26) | copy-start | bytes 3145732
Sparse Core Ops, SparseCore 0:
  20.6 55.2 all-gather.2

commit v7 on v6

--- a/solution.py
+++ b/solution.py
@@ -181,7 +181,9 @@
                         place(r, lambda d: hops[ref][d, 0])
 
     act = act_ref[0, 0].reshape(-1, act_ref.shape[-1])
-    out_ref[0, 0] = dot(act, lines_ref[...]).reshape(out_ref.shape[2:])
+    half = act.shape[1] // 2
+    total = dot(act[:, :half], lines_ref[:half, :]) + dot(act[:, half:], lines_ref[half:, :])
+    out_ref[0, 0] = total.reshape(out_ref.shape[2:])
 
 
 def projected(where, mixed, hops):
@@ -191,10 +193,10 @@
         project_kernel,
         grid_spec=pltpu.PrefetchScalarGridSpec(
             num_scalar_prefetch=1,
-            grid=(kinds, 2 * sides),
-            in_specs=[pl.BlockSpec((1, 1, stretches // 2, span, width), lambda j, m, w: (j, m // 2, m % 2, 0, 0))]
+            grid=(kinds, sides),
+            in_specs=[pl.BlockSpec((1, 1, stretches, span, width), lambda j, m, w: (j, m, 0, 0, 0))]
             + [pl.BlockSpec((stretches, 1, depth, cols), lambda j, m, w: (0, j, 0, 0))] * len(hops),
-            out_specs=pl.BlockSpec((1, 1, stretches // 2, span, cols), lambda j, m, w: (j, m // 2, m % 2, 0, 0)),
+            out_specs=pl.BlockSpec((1, 1, stretches, span, cols), lambda j, m, w: (j, m, 0, 0, 0)),
             scratch_shapes=[pltpu.VMEM((width, cols), bf16)],
         ),
         out_shape=jax.ShapeDtypeStruct((kinds, sides, stretches, span, cols), f32),
@@ -436,6 +438,10 @@
     )(where, blocks, pick, *earlier)
 
 
+def tied(*values):
+    return lax.optimization_barrier(values)
+
+
 def moved(value, axis, by):
     peers = lax.axis_size(axis)
     return lax.ppermute(value, axis, [(i, i + by) for i in range(peers) if 0 <= i + by < peers])
@@ -469,18 +475,15 @@
     x = incoming_activations.reshape(rows, width)
     own_x = lax.dynamic_slice_in_dim(x, t * span, span, 0)
     past = moved(own_x[span - PAST :], "seq", 1)
+    out_half, shards = tied(learner_projection_slices.astype(bf16), learner_acceptor_lookup_slices)
+    out_lines = lax.all_gather(out_half, "req", axis=0, tiled=False)
     pieces = [
-        lax.dynamic_slice_in_dim(learner_acceptor_lookup_slices, (s ^ d) * cols, cols, 2).astype(bf16)
+        lax.dynamic_slice_in_dim(shards, (s ^ d) * cols, cols, 2).astype(bf16)
         for d in range(stretches)
     ]
-    out_half = learner_projection_slices.astype(bf16)
-    out_lines = lax.all_gather(out_half, "req", axis=0, tiled=False)
     got = [swapped(pieces[d], "seq", d) for d in range(1, stretches)]
 
-    def tied(*values):
-        return lax.optimization_barrier(values)
-
-    own_x, past, *_ = tied(own_x, past, out_half, *pieces)
+    own_x, past, *_ = tied(own_x, past, *pieces)
     coeffs = jnp.pad(lagged_blending_weights, ((0, PREFIX - 4), (0, 0)))
     act, coeffs = ordered(
         jnp.concatenate([past, own_x], axis=0),
@@ -504,14 +507,14 @@
     def mine(array):
         return lax.dynamic_slice_in_dim(array, s * cols, cols, array.ndim - 1).reshape(-1, cols)
 
-    tables = [mine(a) for a in (fading_right_matrix, feature_fading_speed, self_reward, cluster_scaling_vector)]
+    tables = (fading_right_matrix, feature_fading_speed, self_reward, cluster_scaling_vector)
     out_lines, *rest = tied(out_lines, *results, *tables)
-    results, tables = rest[:2], rest[2:]
+    results, tables = rest[:2], [mine(a) for a in rest[2:]]
     kept = lax.dynamic_slice_in_dim(out_lines, t * share, share, 0)
     given = lax.dynamic_slice_in_dim(out_lines, (1 - t) * share, share, 0)
     out_lines = jnp.stack([kept, swapped(given, "tensor", 1)])
-    near, other, out_lines, *rest = tied(near, other, out_lines, *results, *hops)
-    results, hops = tuple(rest[:2]), rest[2:]
+    near, other, out_lines, *rest = tied(near, other, out_lines, *results, *tables, *hops)
+    results, tables, hops = tuple(rest[:2]), rest[2:6], rest[6:]
 
     cut = (span + PAST) // 32 * 16
     across = [swapped(near[:cut], "seq", 2), swapped(other[cut:], "seq", 1)]
@@ -521,10 +524,12 @@
     results = mixed_in(other, 0, 2, results)
     results = mixed_in(swapped(near, "tensor", 1), 1, 1, results)
     results = mixed_in(swapped(other, "tensor", 1), 1, 2, results)
-    out_lines, *rest = tied(out_lines, *results, *hops, *across)
-    results, hops, across = tuple(rest[:2]), rest[2:-2], jnp.concatenate(rest[-2:], axis=0)
-
+    out_lines, *rest = tied(out_lines, *results, *across)
+    results, across = tuple(rest[:2]), rest[2:]
     near, other = swapped(out_lines, "seq", 1), swapped(out_lines, "seq", 2)
+    across = jnp.concatenate(across, axis=0)
+    across, *hops = tied(across, *hops)
+
     ends = [moved(hops[2], "req", 1), moved(hops[3], "req", -1)] if chained else []
     last = swapped(across, "tensor", 1)
     results = mixed_in(across, 0, 3, results)

time: 267 us -> 270 us (1.011)
  waiting for transfers between devices: 31.8 us -> 37.5 us
    all_gather x1, waiting for transfers between devices: 0.01 us -> 9.96 us  [local(): out_lines = lax.all_gather(out_half, 'req', axis=0, tiled=False)]
    ppermute x7, waiting for transfers between devices: 23.5 us -> 20.6 us  [moved(): lax.ppermute(value, axis, [(i, i + by) for i in range(peers) if 0 <= i +...]
  transfers between devices with their start and end apart: 32 -> 32, of which waited for: 11 -> 11; matrix products, arithmetic and copies ran while one was open for 14% -> 14% of each run, Pallas kernels for 49% -> 47%
where the time goes in v7:
time: 270 us; the launch traced here: 269 us
  Pallas kernels  133 us (49%)
  starting transfers between devices  43.2 us (16%)
  waiting for transfers between devices  37.5 us (14%)
  local copies, waits for them, and re-layouts  35.1 us (13%)
  between operations  14.4 us (5%)
  other arithmetic  5.54 us (2%)
    pallas_call x8, Pallas kernels, shifted(): pl.pallas_call(mix_kernel, grid_spec=pltpu.PrefetchScalarGridSpec(num_sca...  44.8 us
    pallas_call x2, Pallas kernels, recurrence(): pl.pallas_call(functools.partial(wkv_kernel, prompt=prompt, parted=bool(e...  33.5 us
    pallas_call x1, Pallas kernels, projected(): pl.pallas_call(project_kernel, grid_spec=pltpu.PrefetchScalarGridSpec(num...  25.5 us
    ppermute x24, starting transfers between devices, swapped(): return lax.ppermute(value, axis, [(i, i ^ by) for i in range(peers)])  21.6 us
    ppermute x7, starting transfers between devices, moved(): lax.ppermute(value, axis, [(i, i + by) for i in range(peers) if 0 <= i +...  21.6 us
    ppermute x7, waiting for transfers between devices, moved(): lax.ppermute(value, axis, [(i, i + by) for i in range(peers) if 0 <= i +...  20.6 us
    pallas_call x1, Pallas kernels, ordered(): pl.pallas_call(order_kernel, grid=(width // block,), in_specs=[pl.BlockSp...  14 us
    gather x1, local copies, waits for them, and re-layouts, local(): left = fading_left_matrix[perm]  12.1 us
  transfers between devices with their start and end apart: 32, of which 11 were waited for; matrix products, arithmetic and copies ran while one was open for 14% of the time, Pallas kernels for 47%

profile of v7, /device:TPU:0, one launch (start us, length us, event | category | flops | bytes accessed | tf_op | source)
XLA Modules:
  0.0 268.6 jit_solution(3218660878071209297)
XLA Ops:
  8.2 4.8 %collective-permute-start = (bf16[16,4096]{1,0:T(8,128)(2,1)S(1)}, bf16[16,4096]{1,0:T(8,128)(2,1)S(1)}, u32[]{:S(2)}, u32[]{:S(2)}) collective-permute-start(bf16[16,4096]{1,0:T(8,128)(2,1)S(1)} %constant_dynamic-slice_fusion), channel_id=1, source_target_pairs={{0,1},{1,2},{2,3},{4,5},{5,6},{6,7},{8,9},{9,10},{10,11},{12,13},{... | collective-permute-start | bytes 393224 | tf_op jit(solution)/shard_map/ppermute | solution.py:447
  13.1 2.1 convert_element_type.17
  15.2 2.9 %dynamic-slice_convert_fusion = (bf16[3,256,256]{2,1,0:T(8,128)(2,1)S(1)}, bf16[3,256,256]{2,1,0:T(8,128)(2,1)}, bf16[3,256,256]{2,1,0:T(8,128)(2,1)}, bf16[3,256,256]{2,1,0:T(8,128)(2,1)S(1)}) fusion(f32[3,256,1024]{2,1,0:T(8,128)} %param.24, s32[]{:T(128)S(6)} %select_n.49, s32[]{:T(128)S(6)} %select_n.48, s32[]{:T(128)S(6)} %select_n.47, s32[]{:T(128)S(6)} %select_n.46), kind=kLoop, calls=%fused_computation.6 | loop fusion | bytes 3145744 | tf_op jit(solution)/shard_map/convert_element_type | solution.py:481
  18.1 1.5 collective-permute-start.1
  19.6 2.0 collective-permute-start.3
  21.6 1.8 constant_dynamic-slice_fusion.3
  24.2 14.0 %shard_map.203 = (bf16[272,4096]{1,0:T(8,128)(2,1)}, f32[8,4096]{1,0:T(8,128)S(1)}) custom-call(bf16[272,4096]{1,0:T(8,128)(2,1)S(1)} %pad_maximum_fusion.x_ref, f32[1,4096]{1,0:T(1,128)S(1)} %bitcast.42, f32[8,4096]{1,0:T(8,128)S(1)} %pad.4.coeff_ref, s32[1,4096]{1,0:T(1,128)S(1)} %bitcast.41), custom_call_target="tpu_custom_call" | custom-call | flops 1024 | bytes 1024 | tf_op jit(solution)/shard_map/pallas_call | solution.py:76
  40.6 1.3 pad_maximum_fusion.3.refs_0_
  42.0 4.7 %collective-permute-start.8 = (bf16[4,3,256,256]{3,2,1,0:T(8,128)(2,1)}, bf16[4,3,256,256]{3,2,1,0:T(8,128)(2,1)}, u32[]{:S(2)}, u32[]{:S(2)}) collective-permute-start(bf16[4,3,256,256]{3,2,1,0:T(8,128)(2,1)} %pad_maximum_fusion.3.refs_0_), channel_id=1, source_target_pairs={{0,4},{4,8},{8,12},{1,5},{5,9},{9,13},{2,6},{6,10},{10,14},{3,7},{... | collective-permute-start | bytes 4718600 | tf_op jit(solution)/shard_map/ppermute | solution.py:447
  48.0 12.1 %gather_fusion = bf16[4096,128]{1,0:T(8,128)(2,1)S(1)} fusion(bf16[4096,128]{1,0:T(8,128)(2,1)S(1)} %copy-done, s32[4096]{0:T(1024)S(1)} %fusion), kind=kCustom, calls=%fused_computation | custom fusion | bytes 2113536 | tf_op jit(solution)/shard_map/gather | solution.py:501
  60.1 6.4 %shard_map.204 = (bf16[3,2,4,256,4096]{4,3,2,1,0:T(8,128)(2,1)}, bf16[2,4,256,128]{3,2,1,0:T(8,128)(2,1)S(1)}) custom-call(s32[3]{0:T(128)S(1)} %pad_add_fusion.where_ref, bf16[272,4096]{1,0:T(8,128)(2,1)} %get-tuple-element.82.act_ref, f32[8,4096]{1,0:T(8,128)S(1)} %get-tuple-element.84.coeff_ref, bf16[4096,128]{1,0:T(8,128)(2,1)S(1)} %gather_fusion), custom_call_target="tpu_custom_call" | custom-call | flops 1024 | bytes 1024 | tf_op jit(solution)/shard_map/pallas_call | solution.py:131
  66.5 6.3 %shard_map.205 = (bf16[3,2,4,256,4096]{4,3,2,1,0:T(8,128)(2,1)}, bf16[2,4,256,128]{3,2,1,0:T(8,128)(2,1)S(1)}) custom-call(s32[3]{0:T(128)S(1)} %pad_add_fusion.where_ref, bf16[272,4096]{1,0:T(8,128)(2,1)} %collective-permute-done.6.act_ref, f32[8,4096]{1,0:T(8,128)S(1)} %get-tuple-element.84.coeff_ref, ...), custom_call_target="tpu_custom_call", output_to_operand_aliasing={{0}: (4, {}), {1}: (5, {})} | custom-call | flops 1024 | bytes 1024 | tf_op jit(solution)/shard_map/pallas_call | solution.py:131
  72.8 10.0 %all-gather.3.cloned.1.call-done = bf16[4096,256]{1,0:T(8,128)(2,1)} async-done(((bf16[1024,256]{1,0:T(8,128)(2,1)}), bf16[4096,256]{1,0:T(8,128)(2,1)}) %all-gather.3.cloned.1.call-update) | async-done | bytes 2097168 | tf_op jit(solution)/shard_map/all_gather | solution.py:479
  82.7 1.7 dynamic-slice_bitcast_fusion
  88.4 1.5 constant_dynamic-slice_fusion.1.refs_5_
  89.9 1.5 pad_maximum_fusion.2.refs_0_
  91.4 6.7 %collective-permute-done.8.refs_1_ = bf16[4,3,256,256]{3,2,1,0:T(8,128)(2,1)} collective-permute-done((bf16[4,3,256,256]{3,2,1,0:T(8,128)(2,1)}, bf16[4,3,256,256]{3,2,1,0:T(8,128)(2,1)}, u32[]{:S(2)}, u32[]{:S(2)}) %collective-permute-start.8) | collective-permute-done | bytes 1572896 | tf_op jit(solution)/shard_map/ppermute | solution.py:447
  98.1 2.0 collective-permute-done.9.refs_2_
  100.6 1.4 slice.17
  102.0 1.5 collective-permute-start.13
  103.5 4.9 %collective-permute-start.14 = (bf16[4,3,256,256]{3,2,1,0:T(8,128)(2,1)}, bf16[4,3,256,256]{3,2,1,0:T(8,128)(2,1)}, u32[]{:S(2)}, u32[]{:S(2)}) collective-permute-start(bf16[4,3,256,256]{3,2,1,0:T(8,128)(2,1)} %collective-permute-done.8.refs_1_), channel_id=1, source_target_pairs={{0,4},{4,8},{8,12},{1,5},{5,9},{9,13},{2,6},{6,10},{10,14},{3,7},{... | collective-permute-start | bytes 4718600 | tf_op jit(solution)/shard_map/ppermute | solution.py:447
  111.0 1.6 collective-permute-start.12
  112.7 6.3 %shard_map.206 = (bf16[3,2,4,256,4096]{4,3,2,1,0:T(8,128)(2,1)}, bf16[2,4,256,128]{3,2,1,0:T(8,128)(2,1)S(1)}) custom-call(s32[3]{0:T(128)S(1)} %pad_add_fusion.where_ref, bf16[272,4096]{1,0:T(8,128)(2,1)} %collective-permute-done.4.act_ref, f32[8,4096]{1,0:T(8,128)S(1)} %get-tuple-element.84.coeff_ref, ...), custom_call_target="tpu_custom_call", output_to_operand_aliasing={{0}: (4, {}), {1}: (5, {})} | custom-call | flops 1024 | bytes 1024 | tf_op jit(solution)/shard_map/pallas_call | solution.py:131
  119.0 6.3 %shard_map.207 = (bf16[3,2,4,256,4096]{4,3,2,1,0:T(8,128)(2,1)}, bf16[2,4,256,128]{3,2,1,0:T(8,128)(2,1)S(1)}) custom-call(s32[3]{0:T(128)S(1)} %pad_add_fusion.where_ref, bf16[272,4096]{1,0:T(8,128)(2,1)} %collective-permute-done.5.act_ref, f32[8,4096]{1,0:T(8,128)S(1)} %get-tuple-element.84.coeff_ref, ...), custom_call_target="tpu_custom_call", output_to_operand_aliasing={{0}: (4, {}), {1}: (5, {})} | custom-call | flops 1024 | bytes 1024 | tf_op jit(solution)/shard_map/pallas_call | solution.py:131
  125.3 4.9 %shard_map.208 = (bf16[3,2,4,256,4096]{4,3,2,1,0:T(8,128)(2,1)}, bf16[2,4,256,128]{3,2,1,0:T(8,128)(2,1)S(1)}) custom-call(s32[3]{0:T(128)S(1)} %pad_add_fusion.where_ref, bf16[272,4096]{1,0:T(8,128)(2,1)S(1)} %collective-permute-done.11.act_ref, f32[8,4096]{1,0:T(8,128)S(1)} %get-tuple-element.84.coeff_ref, ...), custom_call_target="tpu_custom_call", output_to_operand_aliasing={{0}: (4, {}), {1}: (5, {})} | custom-call | flops 1024 | bytes 1024 | tf_op jit(solution)/shard_map/pallas_call | solution.py:131
  130.1 4.8 %shard_map.209 = (bf16[3,2,4,256,4096]{4,3,2,1,0:T(8,128)(2,1)}, bf16[2,4,256,128]{3,2,1,0:T(8,128)(2,1)S(1)}) custom-call(s32[3]{0:T(128)S(1)} %pad_add_fusion.where_ref, bf16[272,4096]{1,0:T(8,128)(2,1)S(1)} %collective-permute-done.10.act_ref, f32[8,4096]{1,0:T(8,128)S(1)} %get-tuple-element.84.coeff_ref, ...), custom_call_target="tpu_custom_call", output_to_operand_aliasing={{0}: (4, {}), {1}: (5, {})} | custom-call | flops 1024 | bytes 1024 | tf_op jit(solution)/shard_map/pallas_call | solution.py:131
  135.9 5.3 %collective-permute-done.14.refs_3_ = bf16[4,3,256,256]{3,2,1,0:T(8,128)(2,1)} collective-permute-done((bf16[4,3,256,256]{3,2,1,0:T(8,128)(2,1)}, bf16[4,3,256,256]{3,2,1,0:T(8,128)(2,1)}, u32[]{:S(2)}, u32[]{:S(2)}) %collective-permute-start.14) | collective-permute-done | bytes 1572896 | tf_op jit(solution)/shard_map/ppermute | solution.py:447
  141.2 5.2 %collective-permute-done.15.refs_4_ = bf16[4,3,256,256]{3,2,1,0:T(8,128)(2,1)} collective-permute-done((bf16[4,3,256,256]{3,2,1,0:T(8,128)(2,1)}, bf16[4,3,256,256]{3,2,1,0:T(8,128)(2,1)}, u32[]{:S(2)}, u32[]{:S(2)}) %collective-permute-start.15) | collective-permute-done | bytes 1572896 | tf_op jit(solution)/shard_map/ppermute | solution.py:447
  147.0 1.4 collective-permute-start.18
  148.4 3.1 %collective-permute-start.19 = (bf16[4,3,256,256]{3,2,1,0:T(8,128)(2,1)}, bf16[4,3,256,256]{3,2,1,0:T(8,128)(2,1)}, u32[]{:S(2)}, u32[]{:S(2)}) collective-permute-start(bf16[4,3,256,256]{3,2,1,0:T(8,128)(2,1)} %collective-permute-done.14.refs_3_), channel_id=1, source_target_pairs={{0,4},{4,8},{8,12},{1,5},{5,9},{9,13},{2,6},{6,10},{10,14},{3,7},{... | collective-permute-start | bytes 4718600 | tf_op jit(solution)/shard_map/ppermute | solution.py:447
  151.5 1.5 collective-permute-start.20
  153.0 5.0 %shard_map.210 = (bf16[3,2,4,256,4096]{4,3,2,1,0:T(8,128)(2,1)}, bf16[2,4,256,128]{3,2,1,0:T(8,128)(2,1)S(1)}) custom-call(s32[3]{0:T(128)S(1)} %pad_add_fusion.where_ref, bf16[272,4096]{1,0:T(8,128)(2,1)S(1)} %pad_maximum_fusion.1.act_ref, f32[8,4096]{1,0:T(8,128)S(1)} %get-tuple-element.84.coeff_ref, ...), custom_call_target="tpu_custom_call", output_to_operand_aliasing={{0}: (4, {}), {1}: (5, {})} | custom-call | flops 1024 | bytes 1024 | tf_op jit(solution)/shard_map/pallas_call | solution.py:131
  158.0 4.9 %shard_map.211 = (bf16[3,2,4,256,4096]{4,3,2,1,0:T(8,128)(2,1)}, bf16[2,4,256,128]{3,2,1,0:T(8,128)(2,1)S(1)}) custom-call(s32[3]{0:T(128)S(1)} %pad_add_fusion.where_ref, bf16[272,4096]{1,0:T(8,128)(2,1)S(1)} %collective-permute-done.16.act_ref, f32[8,4096]{1,0:T(8,128)S(1)} %get-tuple-element.84.coeff_ref, ...), custom_call_target="tpu_custom_call", output_to_operand_aliasing={{0}: (4, {}), {1}: (5, {})} | custom-call | flops 1024 | bytes 1024 | tf_op jit(solution)/shard_map/pallas_call | solution.py:131
  162.8 25.5 %shard_map.212.refs_3_ = f32[3,2,4,256,256]{4,3,2,1,0:T(8,128)} custom-call(s32[3]{0:T(128)} %copy-done.4, bf16[3,2,4,256,4096]{4,3,2,1,0:T(8,128)(2,1)} %get-tuple-element.128.act_ref.refs_0_, bf16[4,3,256,256]{3,2,1,0:T(8,128)(2,1)} %pad_maximum_fusion.3.refs_0_, bf16[4,3,256,256]{3,2,1,0:T(8,128)(2,1)} %collective-permute-done.8.refs_1_, ...), custom_call_target="tpu_custom_call" | custom-call | flops 1024 | bytes 1024 | tf_op jit(solution)/shard_map/pallas_call | solution.py:192
  188.3 1.4 collective-permute-done.20.refs_2_
  189.7 5.1 %collective-permute-done.17.refs_1_ = bf16[2,2,1024,256]{3,2,1,0:T(8,128)(2,1)} collective-permute-done((bf16[2,2,1024,256]{3,2,1,0:T(8,128)(2,1)}, bf16[2,2,1024,256]{3,2,1,0:T(8,128)(2,1)}, u32[]{:S(2)}, u32[]{:S(2)}) %collective-permute-start.17) | collective-permute-done | bytes 2097184 | tf_op jit(solution)/shard_map/ppermute | solution.py:38
  195.0 2.3 slice.18
  197.3 1.4 collective-permute-start.24
  198.7 2.3 slice.19
  201.0 1.6 collective-permute-start.25
  202.7 16.7 %shard_map.213 = bf16[4,320,256]{2,1,0:T(8,128)(2,1)} custom-call(s32[2]{0:T(128)} %extent_ref.3, s32[3]{0:T(128)} %copy-done.4, bf16[3,2,4,256,4096]{4,3,2,1,0:T(8,128)(2,1)} %get-tuple-element.128.act_ref.refs_0_, bf16[4,3,256,256]{3,2,1,0:T(8,128)(2,1)} %collective-permute-done.19.refs_1_, bf16[4,3,256,256]{3,2,1,0:T(8,128)(2,1)} %collective-permute-done.20.refs_2_, ...), custom_call_target="tpu_custom_call" | custom-call | flops 1024 | bytes 1024 | tf_op jit(solution)/shard_map/pallas_call | solution.py:332
  221.7 2.5 collective-permute-start.23
  224.2 16.7 %shard_map.214 = bf16[4,320,256]{2,1,0:T(8,128)(2,1)} custom-call(s32[2]{0:T(128)} %extent_ref.3, s32[3]{0:T(128)} %copy-done.4, bf16[3,2,4,256,4096]{4,3,2,1,0:T(8,128)(2,1)} %get-tuple-element.128.act_ref.refs_0_, bf16[4,3,256,256]{3,2,1,0:T(8,128)(2,1)} %collective-permute-done.19.refs_1_, bf16[4,3,256,256]{3,2,1,0:T(8,128)(2,1)} %collective-permute-done.20.refs_2_, ...), custom_call_target="tpu_custom_call" | custom-call | flops 1024 | bytes 1024 | tf_op jit(solution)/shard_map/pallas_call | solution.py:332
  243.4 2.5 collective-permute-start.29
  245.9 1.6 shard_map.216.refs_0_
  247.5 6.0 %shard_map.215.refs_5_ = bf16[2,256,2048]{2,1,0:T(8,128)(2,1)} custom-call(s32[3]{0:T(128)S(1)} %copy-done.5, bf16[512,4096]{1,0:T(8,128)(2,1)} %bitcast.45, bf16[4,320,256]{2,1,0:T(8,128)(2,1)S(1)} %pad_maximum_fusion.4.own_ref.blocks_ref, bf16[4,320,256]{2,1,0:T(8,128)(2,1)S(1)} %collective-permute-done.26.far_ref, ...), custom_call_target="tpu_custom_call" | custom-call | flops 1024 | bytes 1024 | tf_op jit(solution)/shard_map/pallas_call | solution.py:384
  253.7 1.6 shard_map.218
  255.8 6.0 %shard_map.217 = bf16[2,256,2048]{2,1,0:T(8,128)(2,1)} custom-call(s32[3]{0:T(128)S(1)} %copy-done.5, bf16[512,4096]{1,0:T(8,128)(2,1)} %bitcast.46, bf16[4,320,256]{2,1,0:T(8,128)(2,1)S(1)} %pad_maximum_fusion.5.own_ref.blocks_ref, bf16[4,320,256]{2,1,0:T(8,128)(2,1)S(1)} %collective-permute-done.30.far_ref, ...), custom_call_target="tpu_custom_call", output_to_operand_aliasing={{}: (9, {})} | custom-call | flops 1024 | bytes 1024 | tf_op jit(solution)/shard_map/pallas_call | solution.py:384
  (76 shorter events, 19.8 us)
Async XLA Ops:
  7.2 40.8 %copy-start = (bf16[4096,128]{1,0:T(8,128)(2,1)S(1)}, bf16[4096,128]{1,0:T(8,128)(2,1)}, u32[]{:S(2)}) copy-start(bf16[4096,128]{1,0:T(8,128)(2,1)} %param.26) | copy-start | bytes 3145732
  7.2 75.6 %all-gather.3.cloned.1.call-start = ((), (), s32[]{:S(2)}) async-start(), calls=%async_computation | async-start | bytes 2621440 | tf_op jit(solution)/shard_map/all_gather | solution.py:479
  8.2 15.2 %collective-permute-start = (bf16[16,4096]{1,0:T(8,128)(2,1)S(1)}, bf16[16,4096]{1,0:T(8,128)(2,1)S(1)}, u32[]{:S(2)}, u32[]{:S(2)}) collective-permute-start(bf16[16,4096]{1,0:T(8,128)(2,1)S(1)} %constant_dynamic-slice_fusion), channel_id=1, source_target_pairs={{0,1},{1,2},{2,3},{4,5},{5,6},{6,7},{8,9},{9,10},{10,11},{12,13},{... | collective-permute-start | bytes 393224 | tf_op jit(solution)/shard_map/ppermute | solution.py:447
  18.1 20.1 %collective-permute-start.1 = (bf16[3,256,256]{2,1,0:T(8,128)(2,1)}, bf16[3,256,256]{2,1,0:T(8,128)(2,1)S(1)}, u32[]{:S(2)}, u32[]{:S(2)}) collective-permute-start(bf16[3,256,256]{2,1,0:T(8,128)(2,1)} %get-tuple-element.156), channel_id=1, source_target_pairs={{0,1},{1,0},{2,3},{3,2},{4,5},{5,4},{6,7},{7,6},{8,9},{9,8},{10,11... | collective-permute-start | bytes 1179656 | tf_op jit(solution)/shard_map/ppermute | solution.py:38
  19.6 18.9 %collective-permute-start.2 = (bf16[3,256,256]{2,1,0:T(8,128)(2,1)}, bf16[3,256,256]{2,1,0:T(8,128)(2,1)S(1)}, u32[]{:S(2)}, u32[]{:S(2)}) collective-permute-start(bf16[3,256,256]{2,1,0:T(8,128)(2,1)} %get-tuple-element.155), channel_id=1, source_target_pairs={{0,2},{1,3},{2,0},{3,1},{4,6},{5,7},{6,4},{7,5},{8,10},{9,11},{10,... | collective-permute-start | bytes 1179656 | tf_op jit(solution)/shard_map/ppermute | solution.py:38
  19.6 18.9 %collective-permute-start.3 = (bf16[3,256,256]{2,1,0:T(8,128)(2,1)S(1)}, bf16[3,256,256]{2,1,0:T(8,128)(2,1)S(1)}, u32[]{:S(2)}, u32[]{:S(2)}) collective-permute-start(bf16[3,256,256]{2,1,0:T(8,128)(2,1)S(1)} %get-tuple-element.154), channel_id=1, source_target_pairs={{0,3},{1,2},{2,1},{3,0},{4,7},{5,6},{6,5},{7,4},{8,11},{9,10},{10,... | collective-permute-start | bytes 1179656 | tf_op jit(solution)/shard_map/ppermute | solution.py:38
  21.6 1.8 copy-start.8
  23.4 0.7 copy-start.6
  23.4 0.7 copy-start.7
  38.5 28.0 %collective-permute-start.6 = (bf16[272,4096]{1,0:T(8,128)(2,1)}, bf16[272,4096]{1,0:T(8,128)(2,1)}, u32[]{:S(2)}, u32[]{:S(2)}) collective-permute-start(bf16[272,4096]{1,0:T(8,128)(2,1)} %get-tuple-element.82.act_ref), channel_id=1, source_target_pairs={{0,16},{16,0},{1,17},{17,1},{2,18},{18,2},{3,19},{19,3},{4,20},{20... | collective-permute-start | bytes 6684680 | tf_op jit(solution)/shard_map/ppermute | solution.py:38
  38.5 61.5 %collective-permute-start.4 = (bf16[272,4096]{1,0:T(8,128)(2,1)}, bf16[272,4096]{1,0:T(8,128)(2,1)}, u32[]{:S(2)}, u32[]{:S(2)}) collective-permute-start(bf16[272,4096]{1,0:T(8,128)(2,1)} %get-tuple-element.82.act_ref), channel_id=1, source_target_pairs={{0,1},{1,0},{2,3},{3,2},{4,5},{5,4},{6,7},{7,6},{8,9},{9,8},{10,11... | collective-permute-start | bytes 6684680 | tf_op jit(solution)/shard_map/ppermute | solution.py:38
  39.8 60.3 %collective-permute-start.5 = (bf16[272,4096]{1,0:T(8,128)(2,1)}, bf16[272,4096]{1,0:T(8,128)(2,1)}, u32[]{:S(2)}, u32[]{:S(2)}) collective-permute-start(bf16[272,4096]{1,0:T(8,128)(2,1)} %get-tuple-element.82.act_ref), channel_id=1, source_target_pairs={{0,2},{1,3},{2,0},{3,1},{4,6},{5,7},{6,4},{7,5},{8,10},{9,11},{10,... | collective-permute-start | bytes 6684680 | tf_op jit(solution)/shard_map/ppermute | solution.py:38
  40.6 117.3 %copy-start.4 = (s32[3]{0:T(128)}, s32[3]{0:T(128)S(1)}, u32[]{:S(2)}) copy-start(s32[3]{0:T(128)S(1)} %pad_add_fusion.where_ref) | copy-start | bytes 40
  42.0 56.1 %collective-permute-start.8 = (bf16[4,3,256,256]{3,2,1,0:T(8,128)(2,1)}, bf16[4,3,256,256]{3,2,1,0:T(8,128)(2,1)}, u32[]{:S(2)}, u32[]{:S(2)}) collective-permute-start(bf16[4,3,256,256]{3,2,1,0:T(8,128)(2,1)} %pad_maximum_fusion.3.refs_0_), channel_id=1, source_target_pairs={{0,4},{4,8},{8,12},{1,5},{5,9},{9,13},{2,6},{6,10},{10,14},{3,7},{... | collective-permute-start | bytes 4718600 | tf_op jit(solution)/shard_map/ppermute | solution.py:447
  46.7 53.4 %collective-permute-start.9 = (bf16[4,3,256,256]{3,2,1,0:T(8,128)(2,1)}, bf16[4,3,256,256]{3,2,1,0:T(8,128)(2,1)}, u32[]{:S(2)}, u32[]{:S(2)}) collective-permute-start(bf16[4,3,256,256]{3,2,1,0:T(8,128)(2,1)} %pad_maximum_fusion.3.refs_0_), channel_id=1, source_target_pairs={{4,0},{8,4},{12,8},{5,1},{9,5},{13,9},{6,2},{10,6},{14,10},{7,3},{... | collective-permute-start | bytes 4718600 | tf_op jit(solution)/shard_map/ppermute | solution.py:447
  84.4 5.5 %collective-permute-start.7 = (bf16[2,1024,256]{2,1,0:T(8,128)(2,1)S(1)}, bf16[2,1024,256]{2,1,0:T(8,128)(2,1)S(1)}, u32[]{:S(2)}, u32[]{:S(2)}) collective-permute-start(bf16[2,1024,256]{2,1,0:T(8,128)(2,1)S(1)} %get-tuple-element.159), channel_id=1, source_target_pairs={{0,16},{16,0},{1,17},{17,1},{2,18},{18,2},{3,19},{19,3},{4,20},{20... | collective-permute-start | bytes 3145736 | tf_op jit(solution)/shard_map/ppermute | solution.py:38
  100.1 11.0 %collective-permute-start.11 = (bf16[272,4096]{1,0:T(8,128)(2,1)}, bf16[272,4096]{1,0:T(8,128)(2,1)S(1)}, u32[]{:S(2)}, u32[]{:S(2)}) collective-permute-start(bf16[272,4096]{1,0:T(8,128)(2,1)} %collective-permute-done.4.act_ref), channel_id=1, source_target_pairs={{0,16},{16,0},{1,17},{17,1},{2,18},{18,2},{3,19},{19,3},{4,20},{20... | collective-permute-start | bytes 6684680 | tf_op jit(solution)/shard_map/ppermute | solution.py:38
  100.1 30.1 %collective-permute-start.10 = (bf16[272,4096]{1,0:T(8,128)(2,1)}, bf16[272,4096]{1,0:T(8,128)(2,1)S(1)}, u32[]{:S(2)}, u32[]{:S(2)}) collective-permute-start(bf16[272,4096]{1,0:T(8,128)(2,1)} %collective-permute-done.5.act_ref), channel_id=1, source_target_pairs={{0,16},{16,0},{1,17},{17,1},{2,18},{18,2},{3,19},{19,3},{4,20},{20... | collective-permute-start | bytes 6684680 | tf_op jit(solution)/shard_map/ppermute | solution.py:38
  102.0 33.7 %collective-permute-start.13 = (bf16[144,4096]{1,0:T(8,128)(2,1)S(1)}, bf16[144,4096]{1,0:T(8,128)(2,1)S(1)}, u32[]{:S(2)}, u32[]{:S(2)}) collective-permute-start(bf16[144,4096]{1,0:T(8,128)(2,1)S(1)} %slice.17), channel_id=1, source_target_pairs={{0,1},{1,0},{2,3},{3,2},{4,5},{5,4},{6,7},{7,6},{8,9},{9,8},{10,11... | collective-permute-start | bytes 3538952 | tf_op jit(solution)/shard_map/ppermute | solution.py:38
  103.5 37.7 %collective-permute-start.14 = (bf16[4,3,256,256]{3,2,1,0:T(8,128)(2,1)}, bf16[4,3,256,256]{3,2,1,0:T(8,128)(2,1)}, u32[]{:S(2)}, u32[]{:S(2)}) collective-permute-start(bf16[4,3,256,256]{3,2,1,0:T(8,128)(2,1)} %collective-permute-done.8.refs_1_), channel_id=1, source_target_pairs={{0,4},{4,8},{8,12},{1,5},{5,9},{9,13},{2,6},{6,10},{10,14},{3,7},{... | collective-permute-start | bytes 4718600 | tf_op jit(solution)/shard_map/ppermute | solution.py:447
  108.4 38.0 %collective-permute-start.15 = (bf16[4,3,256,256]{3,2,1,0:T(8,128)(2,1)}, bf16[4,3,256,256]{3,2,1,0:T(8,128)(2,1)}, u32[]{:S(2)}, u32[]{:S(2)}) collective-permute-start(bf16[4,3,256,256]{3,2,1,0:T(8,128)(2,1)} %collective-permute-done.9.refs_2_), channel_id=1, source_target_pairs={{4,0},{8,4},{12,8},{5,1},{9,5},{13,9},{6,2},{10,6},{14,10},{7,3},{... | collective-permute-start | bytes 4718600 | tf_op jit(solution)/shard_map/ppermute | solution.py:447
  111.0 24.6 %collective-permute-start.12 = (bf16[128,4096]{1,0:T(8,128)(2,1)S(1)}, bf16[128,4096]{1,0:T(8,128)(2,1)S(1)}, u32[]{:S(2)}, u32[]{:S(2)}) collective-permute-start(bf16[128,4096]{1,0:T(8,128)(2,1)S(1)} %slice.16), channel_id=1, source_target_pairs={{0,2},{1,3},{2,0},{3,1},{4,6},{5,7},{6,4},{7,5},{8,10},{9,11},{10,... | collective-permute-start | bytes 3145736 | tf_op jit(solution)/shard_map/ppermute | solution.py:38
  146.4 11.5 %collective-permute-start.16 = (bf16[272,4096]{1,0:T(8,128)(2,1)S(1)}, bf16[272,4096]{1,0:T(8,128)(2,1)S(1)}, u32[]{:S(2)}, u32[]{:S(2)}) collective-permute-start(bf16[272,4096]{1,0:T(8,128)(2,1)S(1)} %pad_maximum_fusion.1.act_ref), channel_id=1, source_target_pairs={{0,16},{16,0},{1,17},{17,1},{2,18},{18,2},{3,19},{19,3},{4,20},{20... | collective-permute-start | bytes 6684680 | tf_op jit(solution)/shard_map/ppermute | solution.py:38
  146.4 48.4 %collective-permute-start.17 = (bf16[2,2,1024,256]{3,2,1,0:T(8,128)(2,1)}, bf16[2,2,1024,256]{3,2,1,0:T(8,128)(2,1)}, u32[]{:S(2)}, u32[]{:S(2)}) collective-permute-start(bf16[2,2,1024,256]{3,2,1,0:T(8,128)(2,1)} %pad_maximum_fusion.2.refs_0_), channel_id=1, source_target_pairs={{0,1},{1,0},{2,3},{3,2},{4,5},{5,4},{6,7},{7,6},{8,9},{9,8},{10,11... | collective-permute-start | bytes 6291464 | tf_op jit(solution)/shard_map/ppermute | solution.py:38
  147.0 48.1 %collective-permute-start.18 = (bf16[2,2,1024,256]{3,2,1,0:T(8,128)(2,1)}, bf16[2,2,1024,256]{3,2,1,0:T(8,128)(2,1)}, u32[]{:S(2)}, u32[]{:S(2)}) collective-permute-start(bf16[2,2,1024,256]{3,2,1,0:T(8,128)(2,1)} %pad_maximum_fusion.2.refs_0_), channel_id=1, source_target_pairs={{0,2},{1,3},{2,0},{3,1},{4,6},{5,7},{6,4},{7,5},{8,10},{9,11},{10,... | collective-permute-start | bytes 6291464 | tf_op jit(solution)/shard_map/ppermute | solution.py:38
  148.4 39.9 %collective-permute-start.19 = (bf16[4,3,256,256]{3,2,1,0:T(8,128)(2,1)}, bf16[4,3,256,256]{3,2,1,0:T(8,128)(2,1)}, u32[]{:S(2)}, u32[]{:S(2)}) collective-permute-start(bf16[4,3,256,256]{3,2,1,0:T(8,128)(2,1)} %collective-permute-done.14.refs_3_), channel_id=1, source_target_pairs={{0,4},{4,8},{8,12},{1,5},{5,9},{9,13},{2,6},{6,10},{10,14},{3,7},{... | collective-permute-start | bytes 4718600 | tf_op jit(solution)/shard_map/ppermute | solution.py:447
  151.5 38.2 %collective-permute-start.20 = (bf16[4,3,256,256]{3,2,1,0:T(8,128)(2,1)}, bf16[4,3,256,256]{3,2,1,0:T(8,128)(2,1)}, u32[]{:S(2)}, u32[]{:S(2)}) collective-permute-start(bf16[4,3,256,256]{3,2,1,0:T(8,128)(2,1)} %collective-permute-done.15.refs_4_), channel_id=1, source_target_pairs={{4,0},{8,4},{12,8},{5,1},{9,5},{13,9},{6,2},{10,6},{14,10},{7,3},{... | collective-permute-start | bytes 4718600 | tf_op jit(solution)/shard_map/ppermute | solution.py:447
  162.8 25.5 %copy-start.2 = (bf16[2,4,256,128]{3,2,1,0:T(8,128)(2,1)}, bf16[2,4,256,128]{3,2,1,0:T(8,128)(2,1)S(1)}, u32[]{:S(2)}) copy-start(bf16[2,4,256,128]{3,2,1,0:T(8,128)(2,1)S(1)} %get-tuple-element.132.refs_4_) | copy-start | bytes 1572868
  197.3 43.6 %collective-permute-start.24 = (bf16[1,2,1024,256]{3,2,1,0:T(8,128)(2,1)}, bf16[1,2,1024,256]{3,2,1,0:T(8,128)(2,1)S(1)}, u32[]{:S(2)}, u32[]{:S(2)}) collective-permute-start(bf16[1,2,1024,256]{3,2,1,0:T(8,128)(2,1)} %slice.18), channel_id=1, source_target_pairs={{0,2},{1,3},{2,0},{3,1},{4,6},{5,7},{6,4},{7,5},{8,10},{9,11},{10,... | collective-permute-start | bytes 3145736 | tf_op jit(solution)/shard_map/ppermute | solution.py:38
  201.0 39.9 %collective-permute-start.25 = (bf16[1,2,1024,256]{3,2,1,0:T(8,128)(2,1)}, bf16[1,2,1024,256]{3,2,1,0:T(8,128)(2,1)S(1)}, u32[]{:S(2)}, u32[]{:S(2)}) collective-permute-start(bf16[1,2,1024,256]{3,2,1,0:T(8,128)(2,1)} %slice.19), channel_id=1, source_target_pairs={{0,1},{1,0},{2,3},{3,2},{4,5},{5,4},{6,7},{7,6},{8,9},{9,8},{10,11... | collective-permute-start | bytes 3145736 | tf_op jit(solution)/shard_map/ppermute | solution.py:38
  220.6 20.3 %collective-permute-start.21 = (bf16[320,256]{1,0:T(8,128)(2,1)S(1)}, bf16[320,256]{1,0:T(8,128)(2,1)S(1)}, u32[]{:S(2)}, u32[]{:S(2)}) collective-permute-start(bf16[320,256]{1,0:T(8,128)(2,1)S(1)} %get-tuple-element.166), channel_id=1, source_target_pairs={{0,1},{1,0},{2,3},{3,2},{4,5},{5,4},{6,7},{7,6},{8,9},{9,8},{10,11... | collective-permute-start | bytes 491528 | tf_op jit(solution)/shard_map/ppermute | solution.py:38
  221.1 19.8 %collective-permute-start.22 = (bf16[320,256]{1,0:T(8,128)(2,1)S(1)}, bf16[320,256]{1,0:T(8,128)(2,1)S(1)}, u32[]{:S(2)}, u32[]{:S(2)}) collective-permute-start(bf16[320,256]{1,0:T(8,128)(2,1)S(1)} %get-tuple-element.165), channel_id=1, source_target_pairs={{0,2},{1,3},{2,0},{3,1},{4,6},{5,7},{6,4},{7,5},{8,10},{9,11},{10,... | collective-permute-start | bytes 491528 | tf_op jit(solution)/shard_map/ppermute | solution.py:38
  221.7 19.3 %collective-permute-start.23 = (bf16[320,256]{1,0:T(8,128)(2,1)S(1)}, bf16[320,256]{1,0:T(8,128)(2,1)S(1)}, u32[]{:S(2)}, u32[]{:S(2)}) collective-permute-start(bf16[320,256]{1,0:T(8,128)(2,1)S(1)} %get-tuple-element.164), channel_id=1, source_target_pairs={{0,3},{1,2},{2,1},{3,0},{4,7},{5,6},{6,5},{7,4},{8,11},{9,10},{10,... | collective-permute-start | bytes 491528 | tf_op jit(solution)/shard_map/ppermute | solution.py:38
  240.9 5.0 %copy-start.3 = (bf16[256,256]{1,0:T(8,128)(2,1)S(1)}, bf16[256,256]{1,0:T(8,128)(2,1)}, u32[]{:S(2)}) copy-start(bf16[256,256]{1,0:T(8,128)(2,1)} %constant.63.clone.pick_ref) | copy-start | bytes 393220
  240.9 5.0 %copy-start.5 = (s32[3]{0:T(128)S(1)}, s32[3]{0:T(128)}, u32[]{:S(2)}) copy-start(s32[3]{0:T(128)} %copy-done.4) | copy-start | bytes 40
  241.0 6.5 %collective-permute-start.26 = (bf16[4,320,256]{2,1,0:T(8,128)(2,1)S(1)}, bf16[4,320,256]{2,1,0:T(8,128)(2,1)S(1)}, u32[]{:S(2)}, u32[]{:S(2)}) collective-permute-start(bf16[4,320,256]{2,1,0:T(8,128)(2,1)S(1)} %pad_maximum_fusion.4.own_ref.blocks_ref), channel_id=1, source_target_pairs={{0,16},{16,0},{1,17},{17,1},{2,18},{18,2},{3,19},{19,3},{4,20},{20... | collective-permute-start | bytes 1966088 | tf_op jit(solution)/shard_map/ppermute | solution.py:38
  242.3 11.2 %collective-permute-start.27 = (bf16[320,256]{1,0:T(8,128)(2,1)S(1)}, bf16[320,256]{1,0:T(8,128)(2,1)S(1)}, u32[]{:S(2)}, u32[]{:S(2)}) collective-permute-start(bf16[320,256]{1,0:T(8,128)(2,1)S(1)} %get-tuple-element.162), channel_id=1, source_target_pairs={{0,1},{1,0},{2,3},{3,2},{4,5},{5,4},{6,7},{7,6},{8,9},{9,8},{10,11... | collective-permute-start | bytes 491528 | tf_op jit(solution)/shard_map/ppermute | solution.py:38
  242.8 10.7 %collective-permute-start.28 = (bf16[320,256]{1,0:T(8,128)(2,1)S(1)}, bf16[320,256]{1,0:T(8,128)(2,1)S(1)}, u32[]{:S(2)}, u32[]{:S(2)}) collective-permute-start(bf16[320,256]{1,0:T(8,128)(2,1)S(1)} %get-tuple-element.161), channel_id=1, source_target_pairs={{0,2},{1,3},{2,0},{3,1},{4,6},{5,7},{6,4},{7,5},{8,10},{9,11},{10,... | collective-permute-start | bytes 491528 | tf_op jit(solution)/shard_map/ppermute | solution.py:38
  243.4 10.1 %collective-permute-start.29 = (bf16[320,256]{1,0:T(8,128)(2,1)S(1)}, bf16[320,256]{1,0:T(8,128)(2,1)S(1)}, u32[]{:S(2)}, u32[]{:S(2)}) collective-permute-start(bf16[320,256]{1,0:T(8,128)(2,1)S(1)} %get-tuple-element.160), channel_id=1, source_target_pairs={{0,3},{1,2},{2,1},{3,0},{4,7},{5,6},{6,5},{7,4},{8,11},{9,10},{10,... | collective-permute-start | bytes 491528 | tf_op jit(solution)/shard_map/ppermute | solution.py:38
  253.6 2.2 collective-permute-start.30
  255.8 6.0 %copy-start.1 = (bf16[4096,128]{1,0:T(8,128)(2,1)S(1)}, bf16[4096,128]{1,0:T(8,128)(2,1)}, u32[]{:S(2)}) copy-start(bf16[4096,128]{1,0:T(8,128)(2,1)} %param.26) | copy-start | bytes 3145732
Sparse Core Ops, SparseCore 0:
  21.7 60.9 all-gather.2

commit v8 on v7

--- a/solution.py
+++ b/solution.py
@@ -42,14 +42,14 @@
     return pltpu.CompilerParams(vmem_limit_bytes=mib * 2**20)
 
 
-def order_kernel(x_ref, gain_ref, coeff_ref, perm_ref, out_ref, coeff_out_ref, cur_ref):
-    rows, width = x_ref.shape
-    block = out_ref.shape[1]
+def order_kernel(where_ref, past_ref, x_ref, gain_ref, coeff_ref, perm_ref, out_ref, coeff_out_ref, cur_ref):
+    rows, block = out_ref.shape
+    width = x_ref.shape[1]
     depth = 256
 
     @pl.when(pl.program_id(0) == 0)
     def _():
-        x = x_ref[...].astype(f32)
+        x = jnp.concatenate([past_ref[...], x_ref[...]], axis=0).astype(f32)
         mean = jnp.mean(x, axis=-1, keepdims=True)
         centred = x - mean
         spread = jnp.mean(centred * centred, axis=-1, keepdims=True)
@@ -70,30 +70,35 @@
     coeff_out_ref[...] = total[rows : rows + PREFIX] + total[rows + PREFIX :]
 
 
-def ordered(x, gain, coeffs, perm):
-    rows, width = x.shape
+def ordered(where, past, x, gain, coeffs, perm):
+    span, width = x.shape[0] // 2, x.shape[1]
+    rows = span + PAST
     block = 512
     return pl.pallas_call(
         order_kernel,
-        grid=(width // block,),
-        in_specs=[
-            pl.BlockSpec((rows, width), lambda n: (0, 0)),
-            pl.BlockSpec((1, width), lambda n: (0, 0)),
-            pl.BlockSpec((PREFIX, width), lambda n: (0, 0)),
-            pl.BlockSpec((1, block), lambda n: (0, n)),
-        ],
-        out_specs=[
-            pl.BlockSpec((rows, block), lambda n: (0, n)),
-            pl.BlockSpec((PREFIX, block), lambda n: (0, n)),
-        ],
+        grid_spec=pltpu.PrefetchScalarGridSpec(
+            num_scalar_prefetch=1,
+            grid=(width // block,),
+            in_specs=[
+                pl.BlockSpec((PAST, width), lambda n, w: (0, 0)),
+                pl.BlockSpec((span, width), lambda n, w: (w[1], 0)),
+                pl.BlockSpec((1, width), lambda n, w: (0, 0)),
+                pl.BlockSpec((PREFIX, width), lambda n, w: (0, 0)),
+                pl.BlockSpec((1, block), lambda n, w: (0, n)),
+            ],
+            out_specs=[
+                pl.BlockSpec((rows, block), lambda n, w: (0, n)),
+                pl.BlockSpec((PREFIX, block), lambda n, w: (0, n)),
+            ],
+            scratch_shapes=[pltpu.VMEM((rows + 2 * PREFIX, width), bf16)],
+        ),
         out_shape=[
             jax.ShapeDtypeStruct((rows, width), bf16),
             jax.ShapeDtypeStruct((PREFIX, width), f32),
         ],
-        scratch_shapes=[pltpu.VMEM((rows + 2 * PREFIX, width), bf16)],
         compiler_params=vmem(40),
         cost_estimate=SMALL,
-    )(x, gain, coeffs, perm)
+    )(where, past, x, gain, coeffs, perm)
 
 
 def mix_kernel(where_ref, act_ref, coeff_ref, left_ref, *refs):
@@ -124,9 +129,12 @@
 
 
 def shifted(where, act, coeffs, left, side, apart, stretches, earlier):
-    span, width = act.shape[0] - PAST, act.shape[1]
+    span, width = act.shape[-2] - PAST, act.shape[-1]
     inner = left.shape[1]
     block = 1024
+    act_spec = pl.BlockSpec((span + PAST, block), lambda n, w: (0, n))
+    if act.ndim == 3:
+        act_spec = pl.BlockSpec((None, span + PAST, block), lambda n, w: (1 - w[1], 0, n))
     kept = pl.BlockSpec(memory_space=pl.ANY)
     return pl.pallas_call(
         mix_kernel,
@@ -134,7 +142,7 @@
             num_scalar_prefetch=1,
             grid=(width // block,),
             in_specs=[
-                pl.BlockSpec((span + PAST, block), lambda n, w: (0, n)),
+                act_spec,
                 pl.BlockSpec((PREFIX, block), lambda n, w: (0, n)),
                 pl.BlockSpec((block, inner), lambda n, w: (n, 0)),
             ]
@@ -155,54 +163,59 @@
     )(where, act, coeffs, left, *earlier)
 
 
-def project_kernel(where_ref, act_ref, *refs):
-    *hops, out_ref, lines_ref = refs
+def project_kernel(where_ref, *refs):
+    *refs, out_ref, lines_ref = refs
+    parts = where_ref[2] // 2
+    acts, hops = refs[:3], refs[3:]
     stretches, _, depth, _ = hops[0].shape
-    reqs = lines_ref.shape[0] // (stretches * depth)
-    reach = len(hops) // 2
-
-    def place(r, values):
-        for d in range(stretches):
-            at = (r * stretches + (where_ref[0] ^ d)) * depth
-            lines_ref[pl.ds(pl.multiple_of(at, depth), depth), :] = values(d)
+    share = stretches * depth
+
+    def place(r, ref):
+        slot = r - parts
+
+        @pl.when((slot >= 0) & (slot < len(acts)))
+        def _():
+            for d in range(stretches):
+                at = slot * share + (where_ref[0] ^ d) * depth
+                lines_ref[pl.ds(pl.multiple_of(at, depth), depth), :] = ref[d, 0]
 
     @pl.when(pl.program_id(1) == 0)
     def _():
-        me = where_ref[2]
-        place(me, lambda d: hops[0][d, 0])
-        for hop in range(1, reqs):
-            for r, ref in ((me - hop, 2 * hop - 1), (me + hop, 2 * hop)):
-
-                @pl.when((r >= 0) & (r < reqs))
-                def _():
-                    if hop > reach:
-                        place(r, lambda d: jnp.zeros_like(hops[0][d, 0]))
-                    else:
-                        place(r, lambda d: hops[ref][d, 0])
-
-    act = act_ref[0, 0].reshape(-1, act_ref.shape[-1])
-    half = act.shape[1] // 2
-    total = dot(act[:, :half], lines_ref[:half, :]) + dot(act[:, half:], lines_ref[half:, :])
+        place(where_ref[2], hops[0])
+        for hop in range(1, len(hops) // 2 + 1):
+            place(where_ref[2] - hop, hops[2 * hop - 1])
+            place(where_ref[2] + hop, hops[2 * hop])
+
+    total = None
+    for i, act_ref in enumerate(acts):
+        found = dot(act_ref[0, 0].reshape(-1, share), lines_ref[i * share : (i + 1) * share, :])
+        total = found if total is None else total + found
     out_ref[0, 0] = total.reshape(out_ref.shape[2:])
 
 
 def projected(where, mixed, hops):
     stretches, kinds, depth, cols = hops[0].shape
     _, sides, _, span, width = mixed.shape
+    share = stretches * depth
+    parts = width // share - 1
+
+    def act_spec(i):
+        return pl.BlockSpec((1, 1, stretches, span, share), lambda j, m, w: (j, m, 0, 0, w[2] // 2 + i))
+
     return pl.pallas_call(
         project_kernel,
         grid_spec=pltpu.PrefetchScalarGridSpec(
             num_scalar_prefetch=1,
             grid=(kinds, sides),
-            in_specs=[pl.BlockSpec((1, 1, stretches, span, width), lambda j, m, w: (j, m, 0, 0, 0))]
+            in_specs=[act_spec(i) for i in range(parts)]
             + [pl.BlockSpec((stretches, 1, depth, cols), lambda j, m, w: (0, j, 0, 0))] * len(hops),
             out_specs=pl.BlockSpec((1, 1, stretches, span, cols), lambda j, m, w: (j, m, 0, 0, 0)),
-            scratch_shapes=[pltpu.VMEM((width, cols), bf16)],
+            scratch_shapes=[pltpu.VMEM((parts * share, cols), bf16)],
         ),
         out_shape=jax.ShapeDtypeStruct((kinds, sides, stretches, span, cols), f32),
         compiler_params=vmem(60),
         cost_estimate=SMALL,
-    )(where, mixed, *hops)
+    )(where, *[mixed] * parts, *hops)
 
 
 def projected_whole(where, mixed, lines):
@@ -236,7 +249,8 @@
 
 def wkv_kernel(extent_ref, where_ref, *refs, prompt, parted):
     if parted:
-        act_ref, below_ref, above_ref, *refs, lines_ref = refs
+        act_ref, *last_refs = refs[:5]
+        *refs, lines_ref = refs[5:]
     proj_ref, lora_ref, right_ref, speed_ref, reward_ref, scale_ref, sums_ref, level_ref, same_ref, *refs = refs
     out_ref, memory_ref = refs
     step = pl.program_id(0)
@@ -250,11 +264,15 @@
     def _():
         memory_ref[...] = jnp.zeros_like(memory_ref)
         if parted:
-            stretches, kinds, depth, _ = below_ref.shape
-            for d in range(stretches):
-                at = pl.ds(pl.multiple_of((where_ref[0] ^ d) * depth, depth), depth)
-                for j in range(kinds):
-                    lines_ref[j, at, :] = below_ref[d, j] + above_ref[d, j]
+            for r, last_ref in enumerate(last_refs):
+
+                @pl.when(where_ref[2] == r)
+                def _():
+                    stretches, kinds, depth, _ = last_ref.shape
+                    for d in range(stretches):
+                        at = pl.ds(pl.multiple_of((where_ref[0] ^ d) * depth, depth), depth)
+                        for j in range(kinds):
+                            lines_ref[j, at, :] = last_ref[d, j]
 
     def projection(j):
         if not parted:
@@ -324,7 +342,7 @@
         first_specs = [
             pl.BlockSpec(
                 (kinds, 1, 1, span, share),
-                lambda c, e, w: (0, w[1] ^ prompt, c, 0, jnp.where(w[2] == last, 0, last)),
+                lambda c, e, w: (0, w[1] ^ prompt, c, 0, jnp.where(w[2] < 2, last, 0)),
             ),
             *map(fixed, ends),
         ]
@@ -473,8 +491,7 @@
     where = jnp.stack([s, t, lax.axis_index("req")]).astype(jnp.int32)
 
     x = incoming_activations.reshape(rows, width)
-    own_x = lax.dynamic_slice_in_dim(x, t * span, span, 0)
-    past = moved(own_x[span - PAST :], "seq", 1)
+    past = moved(lax.dynamic_slice_in_dim(x, t * span + span - PAST, PAST, 0), "seq", 1)
     out_half, shards = tied(learner_projection_slices.astype(bf16), learner_acceptor_lookup_slices)
     out_lines = lax.all_gather(out_half, "req", axis=0, tiled=False)
     pieces = [
@@ -483,10 +500,12 @@
     ]
     got = [swapped(pieces[d], "seq", d) for d in range(1, stretches)]
 
-    own_x, past, *_ = tied(own_x, past, *pieces)
+    past, *_ = tied(past, *pieces)
     coeffs = jnp.pad(lagged_blending_weights, ((0, PREFIX - 4), (0, 0)))
     act, coeffs = ordered(
-        jnp.concatenate([past, own_x], axis=0),
+        where,
+        past,
+        x,
         standardize_scaling.reshape(1, width),
         coeffs,
         learner_line_permutation.reshape(1, width),
@@ -523,23 +542,26 @@
     results = mixed_in(near, 0, 1, results)
     results = mixed_in(other, 0, 2, results)
     results = mixed_in(swapped(near, "tensor", 1), 1, 1, results)
-    results = mixed_in(swapped(other, "tensor", 1), 1, 2, results)
+    results = mixed_in(lax.all_gather(other, "tensor", axis=0), 1, 2, results)
     out_lines, *rest = tied(out_lines, *results, *across)
     results, across = tuple(rest[:2]), rest[2:]
     near, other = swapped(out_lines, "seq", 1), swapped(out_lines, "seq", 2)
     across = jnp.concatenate(across, axis=0)
-    across, *hops = tied(across, *hops)
-
-    ends = [moved(hops[2], "req", 1), moved(hops[3], "req", -1)] if chained else []
     last = swapped(across, "tensor", 1)
     results = mixed_in(across, 0, 3, results)
+    *results, = tied(*results, *hops)
+    results, hops = tuple(results[:2]), results[2:]
+
+    ends = [moved(hops[2], "req", 1), moved(hops[3], "req", -1)] if chained else []
     mixed, lora = mixed_in(last, 1, 3, results)
     if chained:
         proj = projected(where, mixed, [lines, *hops])
     else:
         proj = projected_whole(where, mixed, *hops)
-    mixed, proj, near, other, *ends = tied(mixed, proj, near, other, *ends)
+    proj, near, other = tied(proj, near, other)
     across = [swapped(near[:1], "seq", 2), swapped(other[1:], "seq", 1)]
+    if chained:
+        ends = [ends[1], hops[3], hops[2], ends[0]]
 
     def one_prompt(prompt, proj):
         return recurrence(prompt, prompt_extents, where, mixed, proj, ends, lora, *tables)

time: 270 us -> 269 us (level)
  waiting for transfers between devices: 37.5 us -> 31.8 us
  local copies, waits for them, and re-layouts: 35.1 us -> 40.6 us
    all_gather x1, waiting for transfers between devices: 9.96 us -> 0.01 us  [local(): out_lines = lax.all_gather(out_half, 'req', axis=0, tiled=False)]
    unnamed x18 -> x27, local copies, waits for them, and re-layouts: 0.6 us -> 6.77 us
    ppermute x24 -> x23, waiting for transfers between devices: 6.93 us -> 11.3 us  [swapped(): return lax.ppermute(value, axis, [(i, i ^ by) for i in range(peers)])]
    pallas_call x1, Pallas kernels: 25.5 us -> 21.6 us  [projected(): pl.pallas_call(project_kernel, grid_spec=pltpu.PrefetchScalarGridSpec(num...]
    ppermute x24 -> x23, starting transfers between devices: 21.6 us -> 20.9 us  [swapped(): return lax.ppermute(value, axis, [(i, i ^ by) for i in range(peers)])]
  transfers between devices with their start and end apart: 32 -> 32, of which waited for: 11 -> 8; matrix products, arithmetic and copies ran while one was open for 14% -> 14% of each run, Pallas kernels for 47% -> 47%
where the time goes in v8:
time: 269 us; the launch traced here: 268 us
  Pallas kernels  132 us (49%)
  starting transfers between devices  43.9 us (16%)
  local copies, waits for them, and re-layouts  40.6 us (15%)
  waiting for transfers between devices  31.8 us (12%)
  between operations  14.3 us (5%)
  other arithmetic  5.22 us (2%)
    pallas_call x8, Pallas kernels, shifted(): pl.pallas_call(mix_kernel, grid_spec=pltpu.PrefetchScalarGridSpec(num_sca...  45.1 us
    pallas_call x2, Pallas kernels, recurrence(): pl.pallas_call(functools.partial(wkv_kernel, prompt=prompt, parted=bool(e...  35.3 us
    ppermute x7, starting transfers between devices, moved(): lax.ppermute(value, axis, [(i, i + by) for i in range(peers) if 0 <= i +...  22.9 us
    pallas_call x1, Pallas kernels, projected(): pl.pallas_call(project_kernel, grid_spec=pltpu.PrefetchScalarGridSpec(num...  21.6 us
    ppermute x23, starting transfers between devices, swapped(): return lax.ppermute(value, axis, [(i, i ^ by) for i in range(peers)])  20.9 us
    ppermute x7, waiting for transfers between devices, moved(): lax.ppermute(value, axis, [(i, i + by) for i in range(peers) if 0 <= i +...  20.4 us
    pallas_call x1, Pallas kernels, ordered(): pl.pallas_call(order_kernel, grid_spec=pltpu.PrefetchScalarGridSpec(num_s...  14.6 us
    gather x1, local copies, waits for them, and re-layouts, local(): left = fading_left_matrix[perm]  12.1 us
  transfers between devices with their start and end apart: 32, of which 8 were waited for; matrix products, arithmetic and copies ran while one was open for 14% of the time, Pallas kernels for 47%

profile of v8, /device:TPU:0, one launch (start us, length us, event | category | flops | bytes accessed | tf_op | source)
XLA Modules:
  0.0 267.5 jit_solution(434165381883737837)
XLA Ops:
  7.2 2.1 convert_element_type.17
  9.5 2.9 %dynamic-slice_convert_fusion = (bf16[3,256,256]{2,1,0:T(8,128)(2,1)}, bf16[3,256,256]{2,1,0:T(8,128)(2,1)}, bf16[3,256,256]{2,1,0:T(8,128)(2,1)}, bf16[3,256,256]{2,1,0:T(8,128)(2,1)S(1)}) fusion(f32[3,256,1024]{2,1,0:T(8,128)} %param.24, s32[]{:T(128)S(6)} %select_n.49, s32[]{:T(128)S(6)} %select_n.48, s32[]{:T(128)S(6)} %select_n.47, s32[]{:T(128)S(6)} %select_n.46), kind=kLoop, calls=%fused_computation.4 | loop fusion | bytes 3145744 | tf_op jit(solution)/shard_map/convert_element_type | solution.py:498
  12.4 2.9 %collective-permute-start.1 = (bf16[3,256,256]{2,1,0:T(8,128)(2,1)}, bf16[3,256,256]{2,1,0:T(8,128)(2,1)S(1)}, u32[]{:S(2)}, u32[]{:S(2)}) collective-permute-start(bf16[3,256,256]{2,1,0:T(8,128)(2,1)} %get-tuple-element.150), channel_id=1, source_target_pairs={{0,1},{1,0},{2,3},{3,2},{4,5},{5,4},{6,7},{7,6},{8,9},{9,8},{10,11... | collective-permute-start | bytes 1179656 | tf_op jit(solution)/shard_map/ppermute | solution.py:38
  15.4 1.5 collective-permute-start.2
  17.8 3.9 %collective-permute-start = (bf16[16,4096]{1,0:T(8,128)(2,1)S(1)}, bf16[16,4096]{1,0:T(8,128)(2,1)S(1)}, u32[]{:S(2)}, u32[]{:S(2)}) collective-permute-start(bf16[16,4096]{1,0:T(8,128)(2,1)S(1)} %constant_dynamic-slice_fusion.2), channel_id=1, source_target_pairs={{0,1},{1,2},{2,3},{4,5},{5,6},{6,7},{8,9},{9,10},{10,11},{12,13},{... | collective-permute-start | bytes 393224 | tf_op jit(solution)/shard_map/ppermute | solution.py:465
  21.8 13.4 %collective-permute-done.past_ref = bf16[16,4096]{1,0:T(8,128)(2,1)S(1)} collective-permute-done((bf16[16,4096]{1,0:T(8,128)(2,1)S(1)}, bf16[16,4096]{1,0:T(8,128)(2,1)S(1)}, u32[]{:S(2)}, u32[]{:S(2)}) %collective-permute-start) | collective-permute-done | bytes 131104 | tf_op jit(solution)/shard_map/ppermute | solution.py:465
  35.2 2.2 copy-done.3
  37.4 14.6 %shard_map.203 = (bf16[272,4096]{1,0:T(8,128)(2,1)}, f32[8,4096]{1,0:T(8,128)S(1)}) custom-call(s32[3]{0:T(128)S(1)} %pad_add_fusion.where_ref, bf16[16,4096]{1,0:T(8,128)(2,1)S(1)} %collective-permute-done.past_ref, bf16[512,4096]{1,0:T(8,128)(2,1)S(1)} %bitcast.45, f32[1,4096]{1,0:T(1,128)S(1)} %bitcast.48, f32[8,4096]{1,0:T(8,128)S(1)} %pad.4.coeff_ref, ...), custom_call_target="tpu_custom_call" | custom-call | flops 1024 | bytes 1024 | tf_op jit(solution)/shard_map/pallas_call | solution.py:77
  52.1 2.6 collective-permute-start.4
  54.7 1.5 collective-permute-start.5
  57.5 4.6 %collective-permute-start.8 = (bf16[4,3,256,256]{3,2,1,0:T(8,128)(2,1)}, bf16[4,3,256,256]{3,2,1,0:T(8,128)(2,1)}, u32[]{:S(2)}, u32[]{:S(2)}) collective-permute-start(bf16[4,3,256,256]{3,2,1,0:T(8,128)(2,1)} %pad_maximum_fusion.1.refs_3_), channel_id=1, source_target_pairs={{0,4},{4,8},{8,12},{1,5},{5,9},{9,13},{2,6},{6,10},{10,14},{3,7},{... | collective-permute-start | bytes 4718600 | tf_op jit(solution)/shard_map/ppermute | solution.py:465
  63.4 12.1 %gather_fusion = bf16[4096,128]{1,0:T(8,128)(2,1)S(1)} fusion(bf16[4096,128]{1,0:T(8,128)(2,1)S(1)} %copy-done, s32[4096]{0:T(1024)S(1)} %fusion), kind=kCustom, calls=%fused_computation | custom fusion | bytes 2113536 | tf_op jit(solution)/shard_map/gather | solution.py:520
  75.5 6.3 %shard_map.204 = (bf16[3,2,4,256,4096]{4,3,2,1,0:T(8,128)(2,1)}, bf16[2,4,256,128]{3,2,1,0:T(8,128)(2,1)S(1)}) custom-call(s32[3]{0:T(128)S(1)} %pad_add_fusion.where_ref, bf16[272,4096]{1,0:T(8,128)(2,1)} %get-tuple-element.78.act_ref, f32[8,4096]{1,0:T(8,128)S(1)} %get-tuple-element.80.coeff_ref, bf16[4096,128]{1,0:T(8,128)(2,1)S(1)} %gather_fusion), custom_call_target="tpu_custom_call" | custom-call | flops 1024 | bytes 1024 | tf_op jit(solution)/shard_map/pallas_call | solution.py:139
  81.9 6.4 %shard_map.205 = (bf16[3,2,4,256,4096]{4,3,2,1,0:T(8,128)(2,1)}, bf16[2,4,256,128]{3,2,1,0:T(8,128)(2,1)S(1)}) custom-call(s32[3]{0:T(128)S(1)} %pad_add_fusion.where_ref, bf16[272,4096]{1,0:T(8,128)(2,1)} %collective-permute-done.6.act_ref, f32[8,4096]{1,0:T(8,128)S(1)} %get-tuple-element.80.coeff_ref, ...), custom_call_target="tpu_custom_call", output_to_operand_aliasing={{0}: (4, {}), {1}: (5, {})} | custom-call | flops 1024 | bytes 1024 | tf_op jit(solution)/shard_map/pallas_call | solution.py:139
  88.3 1.7 dynamic-slice_bitcast_fusion
  93.9 1.5 constant_dynamic-slice_fusion.refs_7_
  95.3 1.5 pad_maximum_fusion.refs_0_
  96.8 3.3 %collective-permute-done.9.refs_5_ = bf16[4,3,256,256]{3,2,1,0:T(8,128)(2,1)} collective-permute-done((bf16[4,3,256,256]{3,2,1,0:T(8,128)(2,1)}, bf16[4,3,256,256]{3,2,1,0:T(8,128)(2,1)}, u32[]{:S(2)}, u32[]{:S(2)}) %collective-permute-start.9) | collective-permute-done | bytes 1572896 | tf_op jit(solution)/shard_map/ppermute | solution.py:465
  100.2 3.8 %collective-permute-done.4.act_ref = bf16[272,4096]{1,0:T(8,128)(2,1)} collective-permute-done((bf16[272,4096]{1,0:T(8,128)(2,1)}, bf16[272,4096]{1,0:T(8,128)(2,1)}, u32[]{:S(2)}, u32[]{:S(2)}) %collective-permute-start.4) | collective-permute-done | bytes 2228256 | tf_op jit(solution)/shard_map/ppermute | solution.py:38
  104.0 1.5 collective-permute-done.5.act_ref
  105.6 2.4 slice.13
  108.3 2.3 slice.12
  110.5 1.5 collective-permute-start.11
  112.1 4.9 %collective-permute-start.14 = (bf16[4,3,256,256]{3,2,1,0:T(8,128)(2,1)}, bf16[4,3,256,256]{3,2,1,0:T(8,128)(2,1)}, u32[]{:S(2)}, u32[]{:S(2)}) collective-permute-start(bf16[4,3,256,256]{3,2,1,0:T(8,128)(2,1)} %collective-permute-done.8.refs_4_), channel_id=1, source_target_pairs={{0,4},{4,8},{8,12},{1,5},{5,9},{9,13},{2,6},{6,10},{10,14},{3,7},{... | collective-permute-start | bytes 4718600 | tf_op jit(solution)/shard_map/ppermute | solution.py:465
  118.2 6.3 %shard_map.206 = (bf16[3,2,4,256,4096]{4,3,2,1,0:T(8,128)(2,1)}, bf16[2,4,256,128]{3,2,1,0:T(8,128)(2,1)S(1)}) custom-call(s32[3]{0:T(128)S(1)} %pad_add_fusion.where_ref, bf16[272,4096]{1,0:T(8,128)(2,1)} %collective-permute-done.4.act_ref, f32[8,4096]{1,0:T(8,128)S(1)} %get-tuple-element.80.coeff_ref, ...), custom_call_target="tpu_custom_call", output_to_operand_aliasing={{0}: (4, {}), {1}: (5, {})} | custom-call | flops 1024 | bytes 1024 | tf_op jit(solution)/shard_map/pallas_call | solution.py:139
  124.5 6.4 %shard_map.207 = (bf16[3,2,4,256,4096]{4,3,2,1,0:T(8,128)(2,1)}, bf16[2,4,256,128]{3,2,1,0:T(8,128)(2,1)S(1)}) custom-call(s32[3]{0:T(128)S(1)} %pad_add_fusion.where_ref, bf16[272,4096]{1,0:T(8,128)(2,1)} %collective-permute-done.5.act_ref, f32[8,4096]{1,0:T(8,128)S(1)} %get-tuple-element.80.coeff_ref, ...), custom_call_target="tpu_custom_call", output_to_operand_aliasing={{0}: (4, {}), {1}: (5, {})} | custom-call | flops 1024 | bytes 1024 | tf_op jit(solution)/shard_map/pallas_call | solution.py:139
  130.9 4.9 %shard_map.208 = (bf16[3,2,4,256,4096]{4,3,2,1,0:T(8,128)(2,1)}, bf16[2,4,256,128]{3,2,1,0:T(8,128)(2,1)S(1)}) custom-call(s32[3]{0:T(128)S(1)} %pad_add_fusion.where_ref, bf16[272,4096]{1,0:T(8,128)(2,1)S(1)} %collective-permute-done.10.act_ref, f32[8,4096]{1,0:T(8,128)S(1)} %get-tuple-element.80.coeff_ref, ...), custom_call_target="tpu_custom_call", output_to_operand_aliasing={{0}: (4, {}), {1}: (5, {})} | custom-call | flops 1024 | bytes 1024 | tf_op jit(solution)/shard_map/pallas_call | solution.py:139
  135.8 2.3 copy-done.4
  138.0 4.8 %shard_map.209 = (bf16[3,2,4,256,4096]{4,3,2,1,0:T(8,128)(2,1)}, bf16[2,4,256,128]{3,2,1,0:T(8,128)(2,1)S(1)}) custom-call(s32[3]{0:T(128)S(1)} %pad_add_fusion.where_ref, bf16[2,272,4096]{2,1,0:T(8,128)(2,1)S(1)} %bitcast.46, f32[8,4096]{1,0:T(8,128)S(1)} %get-tuple-element.80.coeff_ref, ...), custom_call_target="tpu_custom_call", output_to_operand_aliasing={{0}: (4, {}), {1}: (5, {})} | custom-call | flops 1024 | bytes 1024 | tf_op jit(solution)/shard_map/pallas_call | solution.py:139
  144.3 1.7 collective-permute-start.18
  146.4 5.0 %shard_map.210 = (bf16[3,2,4,256,4096]{4,3,2,1,0:T(8,128)(2,1)}, bf16[2,4,256,128]{3,2,1,0:T(8,128)(2,1)S(1)}) custom-call(s32[3]{0:T(128)S(1)} %pad_add_fusion.where_ref, bf16[272,4096]{1,0:T(8,128)(2,1)S(1)} %constant_dynamic-update-slice_fusion.act_ref, f32[8,4096]{1,0:T(8,128)S(1)} %get-tuple-element.80.coeff_ref, ...), custom_call_target="tpu_custom_call", output_to_operand_aliasing={{0}: (4, {}), {1}: (5, {})} | custom-call | flops 1024 | bytes 1024 | tf_op jit(solution)/shard_map/pallas_call | solution.py:139
  151.4 3.6 %collective-permute-done.15.refs_7_.refs_2_ = bf16[4,3,256,256]{3,2,1,0:T(8,128)(2,1)} collective-permute-done((bf16[4,3,256,256]{3,2,1,0:T(8,128)(2,1)}, bf16[4,3,256,256]{3,2,1,0:T(8,128)(2,1)}, u32[]{:S(2)}, u32[]{:S(2)}) %collective-permute-start.15) | collective-permute-done | bytes 1572896 | tf_op jit(solution)/shard_map/ppermute | solution.py:465
  156.4 5.7 %collective-permute-start.17 = (bf16[4,3,256,256]{3,2,1,0:T(8,128)(2,1)}, bf16[4,3,256,256]{3,2,1,0:T(8,128)(2,1)}, u32[]{:S(2)}, u32[]{:S(2)}) collective-permute-start(bf16[4,3,256,256]{3,2,1,0:T(8,128)(2,1)} %collective-permute-done.14.refs_6_.refs_3_), channel_id=1, source_target_pairs={{0,4},{4,8},{8,12},{1,5},{5,9},{9,13},{2,6},{6,10},{10,14},{3,7},{... | collective-permute-start | bytes 4718600 | tf_op jit(solution)/shard_map/ppermute | solution.py:465
  162.1 4.9 %shard_map.211 = (bf16[3,2,4,256,4096]{4,3,2,1,0:T(8,128)(2,1)}, bf16[2,4,256,128]{3,2,1,0:T(8,128)(2,1)S(1)}) custom-call(s32[3]{0:T(128)S(1)} %pad_add_fusion.where_ref, bf16[272,4096]{1,0:T(8,128)(2,1)S(1)} %collective-permute-done.13.act_ref, f32[8,4096]{1,0:T(8,128)S(1)} %get-tuple-element.80.coeff_ref, ...), custom_call_target="tpu_custom_call", output_to_operand_aliasing={{0}: (4, {}), {1}: (5, {})} | custom-call | flops 1024 | bytes 1024 | tf_op jit(solution)/shard_map/pallas_call | solution.py:139
  167.0 21.6 %shard_map.212.refs_5_ = f32[3,2,4,256,256]{4,3,2,1,0:T(8,128)} custom-call(s32[3]{0:T(128)} %copy-done.8, bf16[3,2,4,256,4096]{4,3,2,1,0:T(8,128)(2,1)} %get-tuple-element.119.refs_0_.refs_1_.refs_2_, bf16[3,2,4,256,4096]{4,3,2,1,0:T(8,128)(2,1)} %get-tuple-element.119.refs_0_.refs_1_.refs_2_, ...), custom_call_target="tpu_custom_call" | custom-call | flops 1024 | bytes 1024 | tf_op jit(solution)/shard_map/pallas_call | solution.py:205
  188.6 4.1 %collective-permute-done.18.refs_1_ = bf16[2,2,1024,256]{3,2,1,0:T(8,128)(2,1)} collective-permute-done((bf16[2,2,1024,256]{3,2,1,0:T(8,128)(2,1)}, bf16[2,2,1024,256]{3,2,1,0:T(8,128)(2,1)}, u32[]{:S(2)}, u32[]{:S(2)}) %collective-permute-start.18) | collective-permute-done | bytes 2097184 | tf_op jit(solution)/shard_map/ppermute | solution.py:38
  192.7 1.4 collective-permute-done.19.refs_2_
  195.8 2.3 slice.15
  198.6 17.6 %shard_map.213 = bf16[4,320,256]{2,1,0:T(8,128)(2,1)} custom-call(s32[2]{0:T(128)} %extent_ref.3, s32[3]{0:T(128)} %copy-done.8, bf16[3,2,4,256,4096]{4,3,2,1,0:T(8,128)(2,1)} %get-tuple-element.119.refs_0_.refs_1_.refs_2_, bf16[4,3,256,256]{3,2,1,0:T(8,128)(2,1)} %collective-permute-done.16.refs_1_, ...), custom_call_target="tpu_custom_call" | custom-call | flops 1024 | bytes 1024 | tf_op jit(solution)/shard_map/pallas_call | solution.py:350
  217.5 1.5 collective-permute-start.20
  219.0 1.7 collective-permute-start.21
  221.0 17.6 %shard_map.214 = bf16[4,320,256]{2,1,0:T(8,128)(2,1)} custom-call(s32[2]{0:T(128)} %extent_ref.3, s32[3]{0:T(128)} %copy-done.8, bf16[3,2,4,256,4096]{4,3,2,1,0:T(8,128)(2,1)} %get-tuple-element.119.refs_0_.refs_1_.refs_2_, bf16[4,3,256,256]{3,2,1,0:T(8,128)(2,1)} %collective-permute-done.16.refs_1_, ...), custom_call_target="tpu_custom_call" | custom-call | flops 1024 | bytes 1024 | tf_op jit(solution)/shard_map/pallas_call | solution.py:350
  241.2 1.5 collective-permute-start.26
  242.7 1.7 collective-permute-start.27
  244.8 1.6 shard_map.216.refs_0_
  246.4 6.0 %shard_map.215.refs_5_ = bf16[2,256,2048]{2,1,0:T(8,128)(2,1)} custom-call(s32[3]{0:T(128)S(1)} %copy-done.9, bf16[512,4096]{1,0:T(8,128)(2,1)} %bitcast.43, bf16[4,320,256]{2,1,0:T(8,128)(2,1)S(1)} %pad_maximum_fusion.2.own_ref.blocks_ref, bf16[4,320,256]{2,1,0:T(8,128)(2,1)S(1)} %collective-permute-done.25.far_ref, ...), custom_call_target="tpu_custom_call" | custom-call | flops 1024 | bytes 1024 | tf_op jit(solution)/shard_map/pallas_call | solution.py:402
  252.6 1.6 shard_map.218
  254.7 6.0 %shard_map.217 = bf16[2,256,2048]{2,1,0:T(8,128)(2,1)} custom-call(s32[3]{0:T(128)S(1)} %copy-done.9, bf16[512,4096]{1,0:T(8,128)(2,1)} %bitcast.44, bf16[4,320,256]{2,1,0:T(8,128)(2,1)S(1)} %pad_maximum_fusion.3.own_ref.blocks_ref, bf16[4,320,256]{2,1,0:T(8,128)(2,1)S(1)} %collective-permute-done.29.far_ref, ...), custom_call_target="tpu_custom_call", output_to_operand_aliasing={{}: (9, {})} | custom-call | flops 1024 | bytes 1024 | tf_op jit(solution)/shard_map/pallas_call | solution.py:402
  (84 shorter events, 19.7 us)
Async XLA Ops:
  7.2 56.2 %copy-start = (bf16[4096,128]{1,0:T(8,128)(2,1)S(1)}, bf16[4096,128]{1,0:T(8,128)(2,1)}, u32[]{:S(2)}) copy-start(bf16[4096,128]{1,0:T(8,128)(2,1)} %param.26) | copy-start | bytes 3145732
  7.2 81.1 %all-gather.5.cloned.1.call-start = ((), (), s32[]{:S(2)}) async-start(), calls=%async_computation | async-start | bytes 2621440 | tf_op jit(solution)/shard_map/all_gather | solution.py:496
  9.4 12.3 %copy-start.12 = (f32[4,4096]{1,0:T(4,128)S(1)}, f32[4,4096]{1,0:T(4,128)}, u32[]{:S(2)}) copy-start(f32[4,4096]{1,0:T(4,128)} %param.22) | copy-start | bytes 196612
  9.4 25.8 %copy-start.10 = (s32[4096]{0:T(1024)S(1)}, s32[4096]{0:T(1024)}, u32[]{:S(2)}) copy-start(s32[4096]{0:T(1024)} %param.23) | copy-start | bytes 49156
  9.4 25.8 %copy-start.11 = (f32[4096]{0:T(1024)S(1)}, f32[4096]{0:T(1024)}, u32[]{:S(2)}) copy-start(f32[4096]{0:T(1024)} %param.21) | copy-start | bytes 49156
  9.4 126.4 %all-gather.7.cloned.1.call-start = ((), (), s32[]{:S(2)}) async-start(), calls=%async_computation.1 | async-start | bytes 6684672 | tf_op jit(solution)/shard_map/all_gather | solution.py:545
  12.4 39.6 %collective-permute-start.1 = (bf16[3,256,256]{2,1,0:T(8,128)(2,1)}, bf16[3,256,256]{2,1,0:T(8,128)(2,1)S(1)}, u32[]{:S(2)}, u32[]{:S(2)}) collective-permute-start(bf16[3,256,256]{2,1,0:T(8,128)(2,1)} %get-tuple-element.150), channel_id=1, source_target_pairs={{0,1},{1,0},{2,3},{3,2},{4,5},{5,4},{6,7},{7,6},{8,9},{9,8},{10,11... | collective-permute-start | bytes 1179656 | tf_op jit(solution)/shard_map/ppermute | solution.py:38
  15.4 36.6 %collective-permute-start.2 = (bf16[3,256,256]{2,1,0:T(8,128)(2,1)}, bf16[3,256,256]{2,1,0:T(8,128)(2,1)S(1)}, u32[]{:S(2)}, u32[]{:S(2)}) collective-permute-start(bf16[3,256,256]{2,1,0:T(8,128)(2,1)} %get-tuple-element.149), channel_id=1, source_target_pairs={{0,2},{1,3},{2,0},{3,1},{4,6},{5,7},{6,4},{7,5},{8,10},{9,11},{10,... | collective-permute-start | bytes 1179656 | tf_op jit(solution)/shard_map/ppermute | solution.py:38
  16.9 35.1 %collective-permute-start.3 = (bf16[3,256,256]{2,1,0:T(8,128)(2,1)}, bf16[3,256,256]{2,1,0:T(8,128)(2,1)S(1)}, u32[]{:S(2)}, u32[]{:S(2)}) collective-permute-start(bf16[3,256,256]{2,1,0:T(8,128)(2,1)} %get-tuple-element.148), channel_id=1, source_target_pairs={{0,3},{1,2},{2,1},{3,0},{4,7},{5,6},{6,5},{7,4},{8,11},{9,10},{10,... | collective-permute-start | bytes 1179656 | tf_op jit(solution)/shard_map/ppermute | solution.py:38
  17.8 17.4 %collective-permute-start = (bf16[16,4096]{1,0:T(8,128)(2,1)S(1)}, bf16[16,4096]{1,0:T(8,128)(2,1)S(1)}, u32[]{:S(2)}, u32[]{:S(2)}) collective-permute-start(bf16[16,4096]{1,0:T(8,128)(2,1)S(1)} %constant_dynamic-slice_fusion.2), channel_id=1, source_target_pairs={{0,1},{1,2},{2,3},{4,5},{5,6},{6,7},{8,9},{9,10},{10,11},{12,13},{... | collective-permute-start | bytes 393224 | tf_op jit(solution)/shard_map/ppermute | solution.py:465
  21.8 140.3 %copy-start.8 = (s32[3]{0:T(128)}, s32[3]{0:T(128)S(1)}, u32[]{:S(2)}) copy-start(s32[3]{0:T(128)S(1)} %pad_add_fusion.where_ref) | copy-start | bytes 40
  35.2 2.2 copy-start.3
  52.0 29.9 %collective-permute-start.6 = (bf16[272,4096]{1,0:T(8,128)(2,1)}, bf16[272,4096]{1,0:T(8,128)(2,1)}, u32[]{:S(2)}, u32[]{:S(2)}) collective-permute-start(bf16[272,4096]{1,0:T(8,128)(2,1)} %get-tuple-element.78.act_ref), channel_id=1, source_target_pairs={{0,16},{16,0},{1,17},{17,1},{2,18},{18,2},{3,19},{19,3},{4,20},{20... | collective-permute-start | bytes 6684680 | tf_op jit(solution)/shard_map/ppermute | solution.py:38
  52.1 51.9 %collective-permute-start.4 = (bf16[272,4096]{1,0:T(8,128)(2,1)}, bf16[272,4096]{1,0:T(8,128)(2,1)}, u32[]{:S(2)}, u32[]{:S(2)}) collective-permute-start(bf16[272,4096]{1,0:T(8,128)(2,1)} %get-tuple-element.78.act_ref), channel_id=1, source_target_pairs={{0,1},{1,0},{2,3},{3,2},{4,5},{5,4},{6,7},{7,6},{8,9},{9,8},{10,11... | collective-permute-start | bytes 6684680 | tf_op jit(solution)/shard_map/ppermute | solution.py:38
  54.7 50.8 %collective-permute-start.5 = (bf16[272,4096]{1,0:T(8,128)(2,1)}, bf16[272,4096]{1,0:T(8,128)(2,1)}, u32[]{:S(2)}, u32[]{:S(2)}) collective-permute-start(bf16[272,4096]{1,0:T(8,128)(2,1)} %get-tuple-element.78.act_ref), channel_id=1, source_target_pairs={{0,2},{1,3},{2,0},{3,1},{4,6},{5,7},{6,4},{7,5},{8,10},{9,11},{10,... | collective-permute-start | bytes 6684680 | tf_op jit(solution)/shard_map/ppermute | solution.py:38
  57.5 39.4 %collective-permute-start.8 = (bf16[4,3,256,256]{3,2,1,0:T(8,128)(2,1)}, bf16[4,3,256,256]{3,2,1,0:T(8,128)(2,1)}, u32[]{:S(2)}, u32[]{:S(2)}) collective-permute-start(bf16[4,3,256,256]{3,2,1,0:T(8,128)(2,1)} %pad_maximum_fusion.1.refs_3_), channel_id=1, source_target_pairs={{0,4},{4,8},{8,12},{1,5},{5,9},{9,13},{2,6},{6,10},{10,14},{3,7},{... | collective-permute-start | bytes 4718600 | tf_op jit(solution)/shard_map/ppermute | solution.py:465
  62.1 38.1 %collective-permute-start.9 = (bf16[4,3,256,256]{3,2,1,0:T(8,128)(2,1)}, bf16[4,3,256,256]{3,2,1,0:T(8,128)(2,1)}, u32[]{:S(2)}, u32[]{:S(2)}) collective-permute-start(bf16[4,3,256,256]{3,2,1,0:T(8,128)(2,1)} %pad_maximum_fusion.1.refs_3_), channel_id=1, source_target_pairs={{4,0},{8,4},{12,8},{5,1},{9,5},{13,9},{6,2},{10,6},{14,10},{7,3},{... | collective-permute-start | bytes 4718600 | tf_op jit(solution)/shard_map/ppermute | solution.py:465
  89.9 5.4 %collective-permute-start.7 = (bf16[2,1024,256]{2,1,0:T(8,128)(2,1)S(1)}, bf16[2,1024,256]{2,1,0:T(8,128)(2,1)S(1)}, u32[]{:S(2)}, u32[]{:S(2)}) collective-permute-start(bf16[2,1024,256]{2,1,0:T(8,128)(2,1)S(1)} %get-tuple-element.153), channel_id=1, source_target_pairs={{0,16},{16,0},{1,17},{17,1},{2,18},{18,2},{3,19},{19,3},{4,20},{20... | collective-permute-start | bytes 3145736 | tf_op jit(solution)/shard_map/ppermute | solution.py:38
  105.5 25.4 %collective-permute-start.10 = (bf16[272,4096]{1,0:T(8,128)(2,1)}, bf16[272,4096]{1,0:T(8,128)(2,1)S(1)}, u32[]{:S(2)}, u32[]{:S(2)}) collective-permute-start(bf16[272,4096]{1,0:T(8,128)(2,1)} %collective-permute-done.4.act_ref), channel_id=1, source_target_pairs={{0,16},{16,0},{1,17},{17,1},{2,18},{18,2},{3,19},{19,3},{4,20},{20... | collective-permute-start | bytes 6684680 | tf_op jit(solution)/shard_map/ppermute | solution.py:38
  108.0 34.9 %collective-permute-start.12 = (bf16[144,4096]{1,0:T(8,128)(2,1)}, bf16[144,4096]{1,0:T(8,128)(2,1)S(1)}, u32[]{:S(2)}, u32[]{:S(2)}) collective-permute-start(bf16[144,4096]{1,0:T(8,128)(2,1)} %slice.13), channel_id=1, source_target_pairs={{0,1},{1,0},{2,3},{3,2},{4,5},{5,4},{6,7},{7,6},{8,9},{9,8},{10,11... | collective-permute-start | bytes 3538952 | tf_op jit(solution)/shard_map/ppermute | solution.py:38
  110.5 32.3 %collective-permute-start.11 = (bf16[128,4096]{1,0:T(8,128)(2,1)}, bf16[128,4096]{1,0:T(8,128)(2,1)}, u32[]{:S(2)}, u32[]{:S(2)}) collective-permute-start(bf16[128,4096]{1,0:T(8,128)(2,1)} %slice.12), channel_id=1, source_target_pairs={{0,2},{1,3},{2,0},{3,1},{4,6},{5,7},{6,4},{7,5},{8,10},{9,11},{10,... | collective-permute-start | bytes 3145736 | tf_op jit(solution)/shard_map/ppermute | solution.py:38
  112.1 39.4 %collective-permute-start.14 = (bf16[4,3,256,256]{3,2,1,0:T(8,128)(2,1)}, bf16[4,3,256,256]{3,2,1,0:T(8,128)(2,1)}, u32[]{:S(2)}, u32[]{:S(2)}) collective-permute-start(bf16[4,3,256,256]{3,2,1,0:T(8,128)(2,1)} %collective-permute-done.8.refs_4_), channel_id=1, source_target_pairs={{0,4},{4,8},{8,12},{1,5},{5,9},{9,13},{2,6},{6,10},{10,14},{3,7},{... | collective-permute-start | bytes 4718600 | tf_op jit(solution)/shard_map/ppermute | solution.py:465
  116.9 38.2 %collective-permute-start.15 = (bf16[4,3,256,256]{3,2,1,0:T(8,128)(2,1)}, bf16[4,3,256,256]{3,2,1,0:T(8,128)(2,1)}, u32[]{:S(2)}, u32[]{:S(2)}) collective-permute-start(bf16[4,3,256,256]{3,2,1,0:T(8,128)(2,1)} %collective-permute-done.9.refs_5_), channel_id=1, source_target_pairs={{4,0},{8,4},{12,8},{5,1},{9,5},{13,9},{6,2},{10,6},{14,10},{7,3},{... | collective-permute-start | bytes 4718600 | tf_op jit(solution)/shard_map/ppermute | solution.py:465
  135.8 2.3 copy-start.4
  144.3 17.8 %collective-permute-start.13 = (bf16[272,4096]{1,0:T(8,128)(2,1)S(1)}, bf16[272,4096]{1,0:T(8,128)(2,1)S(1)}, u32[]{:S(2)}, u32[]{:S(2)}) collective-permute-start(bf16[272,4096]{1,0:T(8,128)(2,1)S(1)} %constant_dynamic-update-slice_fusion.act_ref), channel_id=1, source_target_pairs={{0,16},{16,0},{1,17},{17,1},{2,18},{18,2},{3,19},{19,3},{4,20},{20... | collective-permute-start | bytes 6684680 | tf_op jit(solution)/shard_map/ppermute | solution.py:38
  144.3 48.4 %collective-permute-start.18 = (bf16[2,2,1024,256]{3,2,1,0:T(8,128)(2,1)}, bf16[2,2,1024,256]{3,2,1,0:T(8,128)(2,1)}, u32[]{:S(2)}, u32[]{:S(2)}) collective-permute-start(bf16[2,2,1024,256]{3,2,1,0:T(8,128)(2,1)} %pad_maximum_fusion.refs_0_), channel_id=1, source_target_pairs={{0,1},{1,0},{2,3},{3,2},{4,5},{5,4},{6,7},{7,6},{8,9},{9,8},{10,11... | collective-permute-start | bytes 6291464 | tf_op jit(solution)/shard_map/ppermute | solution.py:38
  146.1 48.0 %collective-permute-start.19 = (bf16[2,2,1024,256]{3,2,1,0:T(8,128)(2,1)}, bf16[2,2,1024,256]{3,2,1,0:T(8,128)(2,1)}, u32[]{:S(2)}, u32[]{:S(2)}) collective-permute-start(bf16[2,2,1024,256]{3,2,1,0:T(8,128)(2,1)} %pad_maximum_fusion.refs_0_), channel_id=1, source_target_pairs={{0,2},{1,3},{2,0},{3,1},{4,6},{5,7},{6,4},{7,5},{8,10},{9,11},{10,... | collective-permute-start | bytes 6291464 | tf_op jit(solution)/shard_map/ppermute | solution.py:38
  155.1 43.6 %collective-permute-start.16 = (bf16[4,3,256,256]{3,2,1,0:T(8,128)(2,1)}, bf16[4,3,256,256]{3,2,1,0:T(8,128)(2,1)}, u32[]{:S(2)}, u32[]{:S(2)}) collective-permute-start(bf16[4,3,256,256]{3,2,1,0:T(8,128)(2,1)} %collective-permute-done.15.refs_7_.refs_2_), channel_id=1, source_target_pairs={{4,0},{8,4},{12,8},{5,1},{9,5},{13,9},{6,2},{10,6},{14,10},{7,3},{... | collective-permute-start | bytes 4718600 | tf_op jit(solution)/shard_map/ppermute | solution.py:465
  156.4 42.3 %collective-permute-start.17 = (bf16[4,3,256,256]{3,2,1,0:T(8,128)(2,1)}, bf16[4,3,256,256]{3,2,1,0:T(8,128)(2,1)}, u32[]{:S(2)}, u32[]{:S(2)}) collective-permute-start(bf16[4,3,256,256]{3,2,1,0:T(8,128)(2,1)} %collective-permute-done.14.refs_6_.refs_3_), channel_id=1, source_target_pairs={{0,4},{4,8},{8,12},{1,5},{5,9},{9,13},{2,6},{6,10},{10,14},{3,7},{... | collective-permute-start | bytes 4718600 | tf_op jit(solution)/shard_map/ppermute | solution.py:465
  167.0 21.6 %copy-start.2 = (bf16[2,4,256,128]{3,2,1,0:T(8,128)(2,1)}, bf16[2,4,256,128]{3,2,1,0:T(8,128)(2,1)S(1)}, u32[]{:S(2)}) copy-start(bf16[2,4,256,128]{3,2,1,0:T(8,128)(2,1)S(1)} %get-tuple-element.126.refs_6_) | copy-start | bytes 1572868
  195.4 43.3 %collective-permute-start.23 = (bf16[1,2,1024,256]{3,2,1,0:T(8,128)(2,1)S(1)}, bf16[1,2,1024,256]{3,2,1,0:T(8,128)(2,1)S(1)}, u32[]{:S(2)}, u32[]{:S(2)}) collective-permute-start(bf16[1,2,1024,256]{3,2,1,0:T(8,128)(2,1)S(1)} %slice.14), channel_id=1, source_target_pairs={{0,2},{1,3},{2,0},{3,1},{4,6},{5,7},{6,4},{7,5},{8,10},{9,11},{10,... | collective-permute-start | bytes 3145736 | tf_op jit(solution)/shard_map/ppermute | solution.py:38
  198.0 40.7 %collective-permute-start.24 = (bf16[1,2,1024,256]{3,2,1,0:T(8,128)(2,1)}, bf16[1,2,1024,256]{3,2,1,0:T(8,128)(2,1)S(1)}, u32[]{:S(2)}, u32[]{:S(2)}) collective-permute-start(bf16[1,2,1024,256]{3,2,1,0:T(8,128)(2,1)} %slice.15), channel_id=1, source_target_pairs={{0,1},{1,0},{2,3},{3,2},{4,5},{5,4},{6,7},{7,6},{8,9},{9,8},{10,11... | collective-permute-start | bytes 3145736 | tf_op jit(solution)/shard_map/ppermute | solution.py:38
  217.5 21.2 %collective-permute-start.20 = (bf16[320,256]{1,0:T(8,128)(2,1)S(1)}, bf16[320,256]{1,0:T(8,128)(2,1)S(1)}, u32[]{:S(2)}, u32[]{:S(2)}) collective-permute-start(bf16[320,256]{1,0:T(8,128)(2,1)S(1)} %get-tuple-element.160), channel_id=1, source_target_pairs={{0,1},{1,0},{2,3},{3,2},{4,5},{5,4},{6,7},{7,6},{8,9},{9,8},{10,11... | collective-permute-start | bytes 491528 | tf_op jit(solution)/shard_map/ppermute | solution.py:38
  219.0 19.7 %collective-permute-start.21 = (bf16[320,256]{1,0:T(8,128)(2,1)S(1)}, bf16[320,256]{1,0:T(8,128)(2,1)S(1)}, u32[]{:S(2)}, u32[]{:S(2)}) collective-permute-start(bf16[320,256]{1,0:T(8,128)(2,1)S(1)} %get-tuple-element.159), channel_id=1, source_target_pairs={{0,2},{1,3},{2,0},{3,1},{4,6},{5,7},{6,4},{7,5},{8,10},{9,11},{10,... | collective-permute-start | bytes 491528 | tf_op jit(solution)/shard_map/ppermute | solution.py:38
  220.7 18.0 %collective-permute-start.22 = (bf16[320,256]{1,0:T(8,128)(2,1)S(1)}, bf16[320,256]{1,0:T(8,128)(2,1)S(1)}, u32[]{:S(2)}, u32[]{:S(2)}) collective-permute-start(bf16[320,256]{1,0:T(8,128)(2,1)S(1)} %get-tuple-element.158), channel_id=1, source_target_pairs={{0,3},{1,2},{2,1},{3,0},{4,7},{5,6},{6,5},{7,4},{8,11},{9,10},{10,... | collective-permute-start | bytes 491528 | tf_op jit(solution)/shard_map/ppermute | solution.py:38
  238.7 6.1 %copy-start.7 = (bf16[256,256]{1,0:T(8,128)(2,1)S(1)}, bf16[256,256]{1,0:T(8,128)(2,1)}, u32[]{:S(2)}) copy-start(bf16[256,256]{1,0:T(8,128)(2,1)} %constant.68.clone.pick_ref) | copy-start | bytes 393220
  238.7 6.1 %copy-start.9 = (s32[3]{0:T(128)S(1)}, s32[3]{0:T(128)}, u32[]{:S(2)}) copy-start(s32[3]{0:T(128)} %copy-done.8) | copy-start | bytes 40
  238.7 1.0 copy-start.5
  239.7 6.7 %copy-start.6 = (bf16[1,2,1024,256]{3,2,1,0:T(8,128)(2,1)S(1)}, bf16[1,2,1024,256]{3,2,1,0:T(8,128)(2,1)}, u32[]{:S(2)}) copy-start(bf16[1,2,1024,256]{3,2,1,0:T(8,128)(2,1)} %copy-done.5) | copy-start | bytes 3145732
  239.8 6.6 %collective-permute-start.25 = (bf16[4,320,256]{2,1,0:T(8,128)(2,1)S(1)}, bf16[4,320,256]{2,1,0:T(8,128)(2,1)S(1)}, u32[]{:S(2)}, u32[]{:S(2)}) collective-permute-start(bf16[4,320,256]{2,1,0:T(8,128)(2,1)S(1)} %pad_maximum_fusion.2.own_ref.blocks_ref), channel_id=1, source_target_pairs={{0,16},{16,0},{1,17},{17,1},{2,18},{18,2},{3,19},{19,3},{4,20},{20... | collective-permute-start | bytes 1966088 | tf_op jit(solution)/shard_map/ppermute | solution.py:38
  241.2 11.2 %collective-permute-start.26 = (bf16[320,256]{1,0:T(8,128)(2,1)S(1)}, bf16[320,256]{1,0:T(8,128)(2,1)S(1)}, u32[]{:S(2)}, u32[]{:S(2)}) collective-permute-start(bf16[320,256]{1,0:T(8,128)(2,1)S(1)} %get-tuple-element.156), channel_id=1, source_target_pairs={{0,1},{1,0},{2,3},{3,2},{4,5},{5,4},{6,7},{7,6},{8,9},{9,8},{10,11... | collective-permute-start | bytes 491528 | tf_op jit(solution)/shard_map/ppermute | solution.py:38
  242.7 9.7 %collective-permute-start.27 = (bf16[320,256]{1,0:T(8,128)(2,1)S(1)}, bf16[320,256]{1,0:T(8,128)(2,1)S(1)}, u32[]{:S(2)}, u32[]{:S(2)}) collective-permute-start(bf16[320,256]{1,0:T(8,128)(2,1)S(1)} %get-tuple-element.155), channel_id=1, source_target_pairs={{0,2},{1,3},{2,0},{3,1},{4,6},{5,7},{6,4},{7,5},{8,10},{9,11},{10,... | collective-permute-start | bytes 491528 | tf_op jit(solution)/shard_map/ppermute | solution.py:38
  244.4 8.0 %collective-permute-start.28 = (bf16[320,256]{1,0:T(8,128)(2,1)S(1)}, bf16[320,256]{1,0:T(8,128)(2,1)S(1)}, u32[]{:S(2)}, u32[]{:S(2)}) collective-permute-start(bf16[320,256]{1,0:T(8,128)(2,1)S(1)} %get-tuple-element.154), channel_id=1, source_target_pairs={{0,3},{1,2},{2,1},{3,0},{4,7},{5,6},{6,5},{7,4},{8,11},{9,10},{10,... | collective-permute-start | bytes 491528 | tf_op jit(solution)/shard_map/ppermute | solution.py:38
  252.5 2.2 collective-permute-start.29
  254.7 6.0 %copy-start.1 = (bf16[4096,128]{1,0:T(8,128)(2,1)S(1)}, bf16[4096,128]{1,0:T(8,128)(2,1)}, u32[]{:S(2)}) copy-start(bf16[4096,128]{1,0:T(8,128)(2,1)} %param.26) | copy-start | bytes 3145732
Sparse Core Ops, SparseCore 0:
  10.2 48.6 all-gather.4
  105.6 14.3 all-gather.6

commit v9 on v8

--- a/solution.py
+++ b/solution.py
@@ -42,14 +42,14 @@
     return pltpu.CompilerParams(vmem_limit_bytes=mib * 2**20)
 
 
-def order_kernel(where_ref, past_ref, x_ref, gain_ref, coeff_ref, perm_ref, out_ref, coeff_out_ref, cur_ref):
-    rows, block = out_ref.shape
-    width = x_ref.shape[1]
+def order_kernel(x_ref, gain_ref, coeff_ref, perm_ref, out_ref, coeff_out_ref, cur_ref):
+    rows, width = x_ref.shape
+    block = out_ref.shape[1]
     depth = 256
 
     @pl.when(pl.program_id(0) == 0)
     def _():
-        x = jnp.concatenate([past_ref[...], x_ref[...]], axis=0).astype(f32)
+        x = x_ref[...].astype(f32)
         mean = jnp.mean(x, axis=-1, keepdims=True)
         centred = x - mean
         spread = jnp.mean(centred * centred, axis=-1, keepdims=True)
@@ -70,35 +70,30 @@
     coeff_out_ref[...] = total[rows : rows + PREFIX] + total[rows + PREFIX :]
 
 
-def ordered(where, past, x, gain, coeffs, perm):
-    span, width = x.shape[0] // 2, x.shape[1]
-    rows = span + PAST
+def ordered(x, gain, coeffs, perm):
+    rows, width = x.shape
     block = 512
     return pl.pallas_call(
         order_kernel,
-        grid_spec=pltpu.PrefetchScalarGridSpec(
-            num_scalar_prefetch=1,
-            grid=(width // block,),
-            in_specs=[
-                pl.BlockSpec((PAST, width), lambda n, w: (0, 0)),
-                pl.BlockSpec((span, width), lambda n, w: (w[1], 0)),
-                pl.BlockSpec((1, width), lambda n, w: (0, 0)),
-                pl.BlockSpec((PREFIX, width), lambda n, w: (0, 0)),
-                pl.BlockSpec((1, block), lambda n, w: (0, n)),
-            ],
-            out_specs=[
-                pl.BlockSpec((rows, block), lambda n, w: (0, n)),
-                pl.BlockSpec((PREFIX, block), lambda n, w: (0, n)),
-            ],
-            scratch_shapes=[pltpu.VMEM((rows + 2 * PREFIX, width), bf16)],
-        ),
+        grid=(width // block,),
+        in_specs=[
+            pl.BlockSpec((rows, width), lambda n: (0, 0)),
+            pl.BlockSpec((1, width), lambda n: (0, 0)),
+            pl.BlockSpec((PREFIX, width), lambda n: (0, 0)),
+            pl.BlockSpec((1, block), lambda n: (0, n)),
+        ],
+        out_specs=[
+            pl.BlockSpec((rows, block), lambda n: (0, n)),
+            pl.BlockSpec((PREFIX, block), lambda n: (0, n)),
+        ],
         out_shape=[
             jax.ShapeDtypeStruct((rows, width), bf16),
             jax.ShapeDtypeStruct((PREFIX, width), f32),
         ],
+        scratch_shapes=[pltpu.VMEM((rows + 2 * PREFIX, width), bf16)],
         compiler_params=vmem(40),
         cost_estimate=SMALL,
-    )(where, past, x, gain, coeffs, perm)
+    )(x, gain, coeffs, perm)
 
 
 def mix_kernel(where_ref, act_ref, coeff_ref, left_ref, *refs):
@@ -491,7 +486,8 @@
     where = jnp.stack([s, t, lax.axis_index("req")]).astype(jnp.int32)
 
     x = incoming_activations.reshape(rows, width)
-    past = moved(lax.dynamic_slice_in_dim(x, t * span + span - PAST, PAST, 0), "seq", 1)
+    own_x = lax.dynamic_slice_in_dim(x, t * span, span, 0)
+    past = moved(own_x[span - PAST :], "seq", 1)
     out_half, shards = tied(learner_projection_slices.astype(bf16), learner_acceptor_lookup_slices)
     out_lines = lax.all_gather(out_half, "req", axis=0, tiled=False)
     pieces = [
@@ -500,12 +496,10 @@
     ]
     got = [swapped(pieces[d], "seq", d) for d in range(1, stretches)]
 
-    past, *_ = tied(past, *pieces)
+    own_x, past, *_ = tied(own_x, past, *pieces)
     coeffs = jnp.pad(lagged_blending_weights, ((0, PREFIX - 4), (0, 0)))
     act, coeffs = ordered(
-        where,
-        past,
-        x,
+        jnp.concatenate([past, own_x], axis=0),
         standardize_scaling.reshape(1, width),
         coeffs,
         learner_line_permutation.reshape(1, width),
@@ -542,10 +536,11 @@
     results = mixed_in(near, 0, 1, results)
     results = mixed_in(other, 0, 2, results)
     results = mixed_in(swapped(near, "tensor", 1), 1, 1, results)
-    results = mixed_in(lax.all_gather(other, "tensor", axis=0), 1, 2, results)
+    both = lax.all_gather(other, "tensor", axis=0)
     out_lines, *rest = tied(out_lines, *results, *across)
     results, across = tuple(rest[:2]), rest[2:]
     near, other = swapped(out_lines, "seq", 1), swapped(out_lines, "seq", 2)
+    results = mixed_in(both, 1, 2, results)
     across = jnp.concatenate(across, axis=0)
     last = swapped(across, "tensor", 1)
     results = mixed_in(across, 0, 3, results)

time: 269 us -> 261 us (0.970)
  waiting for transfers between devices: 31.8 us -> 19.9 us
  Pallas kernels: 132 us -> 136 us
    ppermute x7, waiting for transfers between devices: 20.4 us -> 9.05 us  [moved(): lax.ppermute(value, axis, [(i, i + by) for i in range(peers) if 0 <= i +...]
    ppermute x23, waiting for transfers between devices: 11.3 us -> 0.89 us  [swapped(): return lax.ppermute(value, axis, [(i, i ^ by) for i in range(peers)])]
    all_gather x1, waiting for transfers between devices: 0.01 us -> 9.94 us  [local(): out_lines = lax.all_gather(out_half, 'req', axis=0, tiled=False)]
    pallas_call x8, Pallas kernels: 45.1 us -> 49.6 us  [shifted(): pl.pallas_call(mix_kernel, grid_spec=pltpu.PrefetchScalarGridSpec(num_sca...]
    unnamed x27 -> x21, local copies, waits for them, and re-layouts: 6.77 us -> 3.96 us
  transfers between devices with their start and end apart: 32 -> 32, of which waited for: 8 -> 6; matrix products, arithmetic and copies ran while one was open for 14% -> 16% of each run, Pallas kernels for 47% -> 50%
where the time goes in v9:
time: 261 us; the launch traced here: 259 us
  Pallas kernels  136 us (52%)
  starting transfers between devices  44.3 us (17%)
  local copies, waits for them, and re-layouts  39.7 us (15%)
  waiting for transfers between devices  19.9 us (8%)
  between operations  14.4 us (6%)
  other arithmetic  5.31 us (2%)
    pallas_call x8, Pallas kernels, shifted(): pl.pallas_call(mix_kernel, grid_spec=pltpu.PrefetchScalarGridSpec(num_sca...  49.6 us
    pallas_call x2, Pallas kernels, recurrence(): pl.pallas_call(functools.partial(wkv_kernel, prompt=prompt, parted=bool(e...  35.3 us
    ppermute x7, starting transfers between devices, moved(): lax.ppermute(value, axis, [(i, i + by) for i in range(peers) if 0 <= i +...  24.1 us
    pallas_call x1, Pallas kernels, projected(): pl.pallas_call(project_kernel, grid_spec=pltpu.PrefetchScalarGridSpec(num...  21.6 us
    ppermute x23, starting transfers between devices, swapped(): return lax.ppermute(value, axis, [(i, i ^ by) for i in range(peers)])  20.1 us
    pallas_call x1, Pallas kernels, ordered(): pl.pallas_call(order_kernel, grid=(width // block,), in_specs=[pl.BlockSp...  13.9 us
    gather x1, local copies, waits for them, and re-layouts, local(): left = fading_left_matrix[perm]  12.1 us
    pallas_call x2, Pallas kernels, finished(): pl.pallas_call(finish_kernel, grid_spec=pltpu.PrefetchScalarGridSpec(num_...  12 us
  transfers between devices with their start and end apart: 32, of which 6 were waited for; matrix products, arithmetic and copies ran while one was open for 16% of the time, Pallas kernels for 50%

profile of v9, /device:TPU:0, one launch (start us, length us, event | category | flops | bytes accessed | tf_op | source)
XLA Modules:
  0.0 259.2 jit_solution(610064084188581027)
XLA Ops:
  8.2 4.8 %collective-permute-start = (bf16[16,4096]{1,0:T(8,128)(2,1)S(1)}, bf16[16,4096]{1,0:T(8,128)(2,1)S(1)}, u32[]{:S(2)}, u32[]{:S(2)}) collective-permute-start(bf16[16,4096]{1,0:T(8,128)(2,1)S(1)} %constant_dynamic-slice_fusion), channel_id=1, source_target_pairs={{0,1},{1,2},{2,3},{4,5},{5,6},{6,7},{8,9},{9,10},{10,11},{12,13},{... | collective-permute-start | bytes 393224 | tf_op jit(solution)/shard_map/ppermute | solution.py:460
  13.1 2.1 convert_element_type.17
  15.2 2.9 %dynamic-slice_convert_fusion = (bf16[3,256,256]{2,1,0:T(8,128)(2,1)S(1)}, bf16[3,256,256]{2,1,0:T(8,128)(2,1)}, bf16[3,256,256]{2,1,0:T(8,128)(2,1)}, bf16[3,256,256]{2,1,0:T(8,128)(2,1)S(1)}) fusion(f32[3,256,1024]{2,1,0:T(8,128)} %param.24, s32[]{:T(128)S(6)} %select_n.49, s32[]{:T(128)S(6)} %select_n.48, s32[]{:T(128)S(6)} %select_n.47, s32[]{:T(128)S(6)} %select_n.46), kind=kLoop, calls=%fused_computation.5 | loop fusion | bytes 3145744 | tf_op jit(solution)/shard_map/convert_element_type | solution.py:494
  18.1 1.5 collective-permute-start.1
  19.6 2.0 collective-permute-start.3
  21.7 1.7 constant_dynamic-slice_fusion.3
  24.2 13.9 %shard_map.203 = (bf16[272,4096]{1,0:T(8,128)(2,1)}, f32[8,4096]{1,0:T(8,128)S(1)}) custom-call(bf16[272,4096]{1,0:T(8,128)(2,1)S(1)} %pad_maximum_fusion.x_ref, f32[1,4096]{1,0:T(1,128)S(1)} %bitcast.44, f32[8,4096]{1,0:T(8,128)S(1)} %pad.4.coeff_ref, s32[1,4096]{1,0:T(1,128)S(1)} %bitcast.43), custom_call_target="tpu_custom_call" | custom-call | flops 1024 | bytes 1024 | tf_op jit(solution)/shard_map/pallas_call | solution.py:76
  40.6 1.3 pad_maximum_fusion.2.refs_3_
  42.0 4.6 %collective-permute-start.8 = (bf16[4,3,256,256]{3,2,1,0:T(8,128)(2,1)}, bf16[4,3,256,256]{3,2,1,0:T(8,128)(2,1)}, u32[]{:S(2)}, u32[]{:S(2)}) collective-permute-start(bf16[4,3,256,256]{3,2,1,0:T(8,128)(2,1)} %pad_maximum_fusion.2.refs_3_), channel_id=1, source_target_pairs={{0,4},{4,8},{8,12},{1,5},{5,9},{9,13},{2,6},{6,10},{10,14},{3,7},{... | collective-permute-start | bytes 4718600 | tf_op jit(solution)/shard_map/ppermute | solution.py:460
  46.6 1.3 collective-permute-start.9
  47.9 12.1 %gather_fusion = bf16[4096,128]{1,0:T(8,128)(2,1)S(1)} fusion(bf16[4096,128]{1,0:T(8,128)(2,1)S(1)} %copy-done, s32[4096]{0:T(1024)S(1)} %fusion), kind=kCustom, calls=%fused_computation | custom fusion | bytes 2113536 | tf_op jit(solution)/shard_map/gather | solution.py:514
  60.1 6.4 %shard_map.204 = (bf16[3,2,4,256,4096]{4,3,2,1,0:T(8,128)(2,1)}, bf16[2,4,256,128]{3,2,1,0:T(8,128)(2,1)S(1)}) custom-call(s32[3]{0:T(128)S(1)} %pad_add_fusion.where_ref, bf16[272,4096]{1,0:T(8,128)(2,1)} %get-tuple-element.80.act_ref, f32[8,4096]{1,0:T(8,128)S(1)} %get-tuple-element.82.coeff_ref, bf16[4096,128]{1,0:T(8,128)(2,1)S(1)} %gather_fusion), custom_call_target="tpu_custom_call" | custom-call | flops 1024 | bytes 1024 | tf_op jit(solution)/shard_map/pallas_call | solution.py:134
  66.4 6.4 %shard_map.205 = (bf16[3,2,4,256,4096]{4,3,2,1,0:T(8,128)(2,1)}, bf16[2,4,256,128]{3,2,1,0:T(8,128)(2,1)S(1)}) custom-call(s32[3]{0:T(128)S(1)} %pad_add_fusion.where_ref, bf16[272,4096]{1,0:T(8,128)(2,1)} %collective-permute-done.6.act_ref, f32[8,4096]{1,0:T(8,128)S(1)} %get-tuple-element.82.coeff_ref, ...), custom_call_target="tpu_custom_call", output_to_operand_aliasing={{0}: (4, {}), {1}: (5, {})} | custom-call | flops 1024 | bytes 1024 | tf_op jit(solution)/shard_map/pallas_call | solution.py:134
  72.8 9.9 %all-gather.5.cloned.1.call-done = bf16[4096,256]{1,0:T(8,128)(2,1)} async-done(((bf16[1024,256]{1,0:T(8,128)(2,1)}), bf16[4096,256]{1,0:T(8,128)(2,1)}) %all-gather.5.cloned.1.call-update) | async-done | bytes 2097168 | tf_op jit(solution)/shard_map/all_gather | solution.py:492
  82.8 1.7 dynamic-slice_bitcast_fusion
  84.5 1.3 dynamic_slice.67
  85.9 1.3 dynamic_slice.68
  87.2 1.3 dynamic_slice.66
  88.5 1.5 constant_dynamic-slice_fusion.1.refs_7_
  90.0 1.5 pad_maximum_fusion.1.refs_0_
  91.5 6.6 %collective-permute-done.8.refs_4_ = bf16[4,3,256,256]{3,2,1,0:T(8,128)(2,1)} collective-permute-done((bf16[4,3,256,256]{3,2,1,0:T(8,128)(2,1)}, bf16[4,3,256,256]{3,2,1,0:T(8,128)(2,1)}, u32[]{:S(2)}, u32[]{:S(2)}) %collective-permute-start.8) | collective-permute-done | bytes 1572896 | tf_op jit(solution)/shard_map/ppermute | solution.py:460
  98.1 2.0 collective-permute-done.9.refs_5_
  100.1 1.4 slice.17
  101.5 1.5 collective-permute-start.12
  103.0 1.3 slice.16
  104.3 1.5 collective-permute-start.11
  105.9 5.1 %collective-permute-start.14 = (bf16[4,3,256,256]{3,2,1,0:T(8,128)(2,1)}, bf16[4,3,256,256]{3,2,1,0:T(8,128)(2,1)}, u32[]{:S(2)}, u32[]{:S(2)}) collective-permute-start(bf16[4,3,256,256]{3,2,1,0:T(8,128)(2,1)} %collective-permute-done.8.refs_4_), channel_id=1, source_target_pairs={{0,4},{4,8},{8,12},{1,5},{5,9},{9,13},{2,6},{6,10},{10,14},{3,7},{... | collective-permute-start | bytes 4718600 | tf_op jit(solution)/shard_map/ppermute | solution.py:460
  112.3 6.3 %shard_map.206 = (bf16[3,2,4,256,4096]{4,3,2,1,0:T(8,128)(2,1)}, bf16[2,4,256,128]{3,2,1,0:T(8,128)(2,1)S(1)}) custom-call(s32[3]{0:T(128)S(1)} %pad_add_fusion.where_ref, bf16[272,4096]{1,0:T(8,128)(2,1)} %collective-permute-done.4.act_ref, f32[8,4096]{1,0:T(8,128)S(1)} %get-tuple-element.82.coeff_ref, ...), custom_call_target="tpu_custom_call", output_to_operand_aliasing={{0}: (4, {}), {1}: (5, {})} | custom-call | flops 1024 | bytes 1024 | tf_op jit(solution)/shard_map/pallas_call | solution.py:134
  118.6 6.4 %shard_map.207 = (bf16[3,2,4,256,4096]{4,3,2,1,0:T(8,128)(2,1)}, bf16[2,4,256,128]{3,2,1,0:T(8,128)(2,1)S(1)}) custom-call(s32[3]{0:T(128)S(1)} %pad_add_fusion.where_ref, bf16[272,4096]{1,0:T(8,128)(2,1)} %collective-permute-done.5.act_ref, f32[8,4096]{1,0:T(8,128)S(1)} %get-tuple-element.82.coeff_ref, ...), custom_call_target="tpu_custom_call", output_to_operand_aliasing={{0}: (4, {}), {1}: (5, {})} | custom-call | flops 1024 | bytes 1024 | tf_op jit(solution)/shard_map/pallas_call | solution.py:134
  124.9 6.3 %shard_map.208 = (bf16[3,2,4,256,4096]{4,3,2,1,0:T(8,128)(2,1)}, bf16[2,4,256,128]{3,2,1,0:T(8,128)(2,1)S(1)}) custom-call(s32[3]{0:T(128)S(1)} %pad_add_fusion.where_ref, bf16[272,4096]{1,0:T(8,128)(2,1)} %collective-permute-done.10.act_ref, f32[8,4096]{1,0:T(8,128)S(1)} %get-tuple-element.82.coeff_ref, ...), custom_call_target="tpu_custom_call", output_to_operand_aliasing={{0}: (4, {}), {1}: (5, {})} | custom-call | flops 1024 | bytes 1024 | tf_op jit(solution)/shard_map/pallas_call | solution.py:134
  135.1 2.3 copy-done.3
  137.4 4.8 %shard_map.209 = (bf16[3,2,4,256,4096]{4,3,2,1,0:T(8,128)(2,1)}, bf16[2,4,256,128]{3,2,1,0:T(8,128)(2,1)S(1)}) custom-call(s32[3]{0:T(128)S(1)} %pad_add_fusion.where_ref, bf16[2,272,4096]{2,1,0:T(8,128)(2,1)S(1)} %bitcast.42, f32[8,4096]{1,0:T(8,128)S(1)} %get-tuple-element.82.coeff_ref, ...), custom_call_target="tpu_custom_call", output_to_operand_aliasing={{0}: (4, {}), {1}: (5, {})} | custom-call | flops 1024 | bytes 1024 | tf_op jit(solution)/shard_map/pallas_call | solution.py:134
  142.2 6.4 %shard_map.210 = (bf16[3,2,4,256,4096]{4,3,2,1,0:T(8,128)(2,1)}, bf16[2,4,256,128]{3,2,1,0:T(8,128)(2,1)S(1)}) custom-call(s32[3]{0:T(128)S(1)} %pad_add_fusion.where_ref, bf16[272,4096]{1,0:T(8,128)(2,1)} %constant_dynamic-update-slice_fusion.act_ref, f32[8,4096]{1,0:T(8,128)S(1)} %get-tuple-element.82.coeff_ref, ...), custom_call_target="tpu_custom_call", output_to_operand_aliasing={{0}: (4, {}), {1}: (5, {})} | custom-call | flops 1024 | bytes 1024 | tf_op jit(solution)/shard_map/pallas_call | solution.py:134
  149.1 1.3 collective-permute-start.16
  150.4 5.7 %collective-permute-start.17 = (bf16[4,3,256,256]{3,2,1,0:T(8,128)(2,1)}, bf16[4,3,256,256]{3,2,1,0:T(8,128)(2,1)}, u32[]{:S(2)}, u32[]{:S(2)}) collective-permute-start(bf16[4,3,256,256]{3,2,1,0:T(8,128)(2,1)} %collective-permute-done.14.refs_6_.refs_3_), channel_id=1, source_target_pairs={{0,4},{4,8},{8,12},{1,5},{5,9},{9,13},{2,6},{6,10},{10,14},{3,7},{... | collective-permute-start | bytes 4718600 | tf_op jit(solution)/shard_map/ppermute | solution.py:460
  156.1 6.5 %shard_map.211 = (bf16[3,2,4,256,4096]{4,3,2,1,0:T(8,128)(2,1)}, bf16[2,4,256,128]{3,2,1,0:T(8,128)(2,1)S(1)}) custom-call(s32[3]{0:T(128)S(1)} %pad_add_fusion.where_ref, bf16[272,4096]{1,0:T(8,128)(2,1)} %collective-permute-done.13.act_ref, f32[8,4096]{1,0:T(8,128)S(1)} %get-tuple-element.82.coeff_ref, ...), custom_call_target="tpu_custom_call", output_to_operand_aliasing={{0}: (4, {}), {1}: (5, {})} | custom-call | flops 1024 | bytes 1024 | tf_op jit(solution)/shard_map/pallas_call | solution.py:134
  162.7 21.6 %shard_map.212.refs_5_ = f32[3,2,4,256,256]{4,3,2,1,0:T(8,128)} custom-call(s32[3]{0:T(128)} %copy-done.5, bf16[3,2,4,256,4096]{4,3,2,1,0:T(8,128)(2,1)} %get-tuple-element.121.refs_0_.refs_1_.refs_2_, bf16[3,2,4,256,4096]{4,3,2,1,0:T(8,128)(2,1)} %get-tuple-element.121.refs_0_.refs_1_.refs_2_, ...), custom_call_target="tpu_custom_call" | custom-call | flops 1024 | bytes 1024 | tf_op jit(solution)/shard_map/pallas_call | solution.py:200
  184.3 2.3 slice.18
  187.6 2.3 slice.19
  189.9 1.5 collective-permute-start.24
  191.4 17.6 %shard_map.213 = bf16[4,320,256]{2,1,0:T(8,128)(2,1)} custom-call(s32[2]{0:T(128)} %extent_ref.3, s32[3]{0:T(128)} %copy-done.5, bf16[3,2,4,256,4096]{4,3,2,1,0:T(8,128)(2,1)} %get-tuple-element.121.refs_0_.refs_1_.refs_2_, bf16[4,3,256,256]{3,2,1,0:T(8,128)(2,1)} %collective-permute-done.16.refs_1_, ...), custom_call_target="tpu_custom_call" | custom-call | flops 1024 | bytes 1024 | tf_op jit(solution)/shard_map/pallas_call | solution.py:345
  211.8 2.0 collective-permute-start.22
  213.8 17.6 %shard_map.214 = bf16[4,320,256]{2,1,0:T(8,128)(2,1)} custom-call(s32[2]{0:T(128)} %extent_ref.3, s32[3]{0:T(128)} %copy-done.5, bf16[3,2,4,256,4096]{4,3,2,1,0:T(8,128)(2,1)} %get-tuple-element.121.refs_0_.refs_1_.refs_2_, bf16[4,3,256,256]{3,2,1,0:T(8,128)(2,1)} %collective-permute-done.16.refs_1_, ...), custom_call_target="tpu_custom_call" | custom-call | flops 1024 | bytes 1024 | tf_op jit(solution)/shard_map/pallas_call | solution.py:345
  234.5 2.0 collective-permute-start.28
  236.4 1.6 shard_map.216.refs_0_
  238.1 6.0 %shard_map.215.refs_5_ = bf16[2,256,2048]{2,1,0:T(8,128)(2,1)} custom-call(s32[3]{0:T(128)S(1)} %copy-done.6, bf16[512,4096]{1,0:T(8,128)(2,1)} %bitcast.47, bf16[4,320,256]{2,1,0:T(8,128)(2,1)S(1)} %pad_maximum_fusion.3.own_ref.blocks_ref, bf16[4,320,256]{2,1,0:T(8,128)(2,1)S(1)} %collective-permute-done.25.far_ref, ...), custom_call_target="tpu_custom_call" | custom-call | flops 1024 | bytes 1024 | tf_op jit(solution)/shard_map/pallas_call | solution.py:397
  244.2 1.6 shard_map.218
  246.3 6.0 %shard_map.217 = bf16[2,256,2048]{2,1,0:T(8,128)(2,1)} custom-call(s32[3]{0:T(128)S(1)} %copy-done.6, bf16[512,4096]{1,0:T(8,128)(2,1)} %bitcast.48, bf16[4,320,256]{2,1,0:T(8,128)(2,1)S(1)} %pad_maximum_fusion.4.own_ref.blocks_ref, bf16[4,320,256]{2,1,0:T(8,128)(2,1)S(1)} %collective-permute-done.29.far_ref, ...), custom_call_target="tpu_custom_call", output_to_operand_aliasing={{}: (9, {})} | custom-call | flops 1024 | bytes 1024 | tf_op jit(solution)/shard_map/pallas_call | solution.py:397
  (80 shorter events, 17.5 us)
Async XLA Ops:
  7.2 40.8 %copy-start = (bf16[4096,128]{1,0:T(8,128)(2,1)S(1)}, bf16[4096,128]{1,0:T(8,128)(2,1)}, u32[]{:S(2)}) copy-start(bf16[4096,128]{1,0:T(8,128)(2,1)} %param.26) | copy-start | bytes 3145732
  7.2 75.6 %all-gather.5.cloned.1.call-start = ((), (), s32[]{:S(2)}) async-start(), calls=%async_computation | async-start | bytes 2621440 | tf_op jit(solution)/shard_map/all_gather | solution.py:492
  8.2 15.2 %collective-permute-start = (bf16[16,4096]{1,0:T(8,128)(2,1)S(1)}, bf16[16,4096]{1,0:T(8,128)(2,1)S(1)}, u32[]{:S(2)}, u32[]{:S(2)}) collective-permute-start(bf16[16,4096]{1,0:T(8,128)(2,1)S(1)} %constant_dynamic-slice_fusion), channel_id=1, source_target_pairs={{0,1},{1,2},{2,3},{4,5},{5,6},{6,7},{8,9},{9,10},{10,11},{12,13},{... | collective-permute-start | bytes 393224 | tf_op jit(solution)/shard_map/ppermute | solution.py:460
  18.1 20.0 %collective-permute-start.1 = (bf16[3,256,256]{2,1,0:T(8,128)(2,1)}, bf16[3,256,256]{2,1,0:T(8,128)(2,1)S(1)}, u32[]{:S(2)}, u32[]{:S(2)}) collective-permute-start(bf16[3,256,256]{2,1,0:T(8,128)(2,1)} %get-tuple-element.152), channel_id=1, source_target_pairs={{0,1},{1,0},{2,3},{3,2},{4,5},{5,4},{6,7},{7,6},{8,9},{9,8},{10,11... | collective-permute-start | bytes 1179656 | tf_op jit(solution)/shard_map/ppermute | solution.py:38
  19.6 18.9 %collective-permute-start.2 = (bf16[3,256,256]{2,1,0:T(8,128)(2,1)}, bf16[3,256,256]{2,1,0:T(8,128)(2,1)S(1)}, u32[]{:S(2)}, u32[]{:S(2)}) collective-permute-start(bf16[3,256,256]{2,1,0:T(8,128)(2,1)} %get-tuple-element.151), channel_id=1, source_target_pairs={{0,2},{1,3},{2,0},{3,1},{4,6},{5,7},{6,4},{7,5},{8,10},{9,11},{10,... | collective-permute-start | bytes 1179656 | tf_op jit(solution)/shard_map/ppermute | solution.py:38
  19.6 18.9 %collective-permute-start.3 = (bf16[3,256,256]{2,1,0:T(8,128)(2,1)S(1)}, bf16[3,256,256]{2,1,0:T(8,128)(2,1)S(1)}, u32[]{:S(2)}, u32[]{:S(2)}) collective-permute-start(bf16[3,256,256]{2,1,0:T(8,128)(2,1)S(1)} %get-tuple-element.150), channel_id=1, source_target_pairs={{0,3},{1,2},{2,1},{3,0},{4,7},{5,6},{6,5},{7,4},{8,11},{9,10},{10,... | collective-permute-start | bytes 1179656 | tf_op jit(solution)/shard_map/ppermute | solution.py:38
  21.6 1.8 copy-start.9
  21.6 113.5 %all-gather.7.cloned.1.call-start = ((), (), s32[]{:S(2)}) async-start(), calls=%async_computation.1 | async-start | bytes 6684672 | tf_op jit(solution)/shard_map/all_gather | solution.py:539
  23.4 0.7 copy-start.7
  23.5 0.7 copy-start.8
  38.5 27.9 %collective-permute-start.6 = (bf16[272,4096]{1,0:T(8,128)(2,1)}, bf16[272,4096]{1,0:T(8,128)(2,1)}, u32[]{:S(2)}, u32[]{:S(2)}) collective-permute-start(bf16[272,4096]{1,0:T(8,128)(2,1)} %get-tuple-element.80.act_ref), channel_id=1, source_target_pairs={{0,16},{16,0},{1,17},{17,1},{2,18},{18,2},{3,19},{19,3},{4,20},{20... | collective-permute-start | bytes 6684680 | tf_op jit(solution)/shard_map/ppermute | solution.py:38
  38.5 61.6 %collective-permute-start.4 = (bf16[272,4096]{1,0:T(8,128)(2,1)}, bf16[272,4096]{1,0:T(8,128)(2,1)}, u32[]{:S(2)}, u32[]{:S(2)}) collective-permute-start(bf16[272,4096]{1,0:T(8,128)(2,1)} %get-tuple-element.80.act_ref), channel_id=1, source_target_pairs={{0,1},{1,0},{2,3},{3,2},{4,5},{5,4},{6,7},{7,6},{8,9},{9,8},{10,11... | collective-permute-start | bytes 6684680 | tf_op jit(solution)/shard_map/ppermute | solution.py:38
  39.8 60.3 %collective-permute-start.5 = (bf16[272,4096]{1,0:T(8,128)(2,1)}, bf16[272,4096]{1,0:T(8,128)(2,1)}, u32[]{:S(2)}, u32[]{:S(2)}) collective-permute-start(bf16[272,4096]{1,0:T(8,128)(2,1)} %get-tuple-element.80.act_ref), channel_id=1, source_target_pairs={{0,2},{1,3},{2,0},{3,1},{4,6},{5,7},{6,4},{7,5},{8,10},{9,11},{10,... | collective-permute-start | bytes 6684680 | tf_op jit(solution)/shard_map/ppermute | solution.py:38
  40.6 115.5 %copy-start.5 = (s32[3]{0:T(128)}, s32[3]{0:T(128)S(1)}, u32[]{:S(2)}) copy-start(s32[3]{0:T(128)S(1)} %pad_add_fusion.where_ref) | copy-start | bytes 40
  42.0 56.1 %collective-permute-start.8 = (bf16[4,3,256,256]{3,2,1,0:T(8,128)(2,1)}, bf16[4,3,256,256]{3,2,1,0:T(8,128)(2,1)}, u32[]{:S(2)}, u32[]{:S(2)}) collective-permute-start(bf16[4,3,256,256]{3,2,1,0:T(8,128)(2,1)} %pad_maximum_fusion.2.refs_3_), channel_id=1, source_target_pairs={{0,4},{4,8},{8,12},{1,5},{5,9},{9,13},{2,6},{6,10},{10,14},{3,7},{... | collective-permute-start | bytes 4718600 | tf_op jit(solution)/shard_map/ppermute | solution.py:460
  46.6 53.5 %collective-permute-start.9 = (bf16[4,3,256,256]{3,2,1,0:T(8,128)(2,1)}, bf16[4,3,256,256]{3,2,1,0:T(8,128)(2,1)}, u32[]{:S(2)}, u32[]{:S(2)}) collective-permute-start(bf16[4,3,256,256]{3,2,1,0:T(8,128)(2,1)} %pad_maximum_fusion.2.refs_3_), channel_id=1, source_target_pairs={{4,0},{8,4},{12,8},{5,1},{9,5},{13,9},{6,2},{10,6},{14,10},{7,3},{... | collective-permute-start | bytes 4718600 | tf_op jit(solution)/shard_map/ppermute | solution.py:460
  84.5 5.5 %collective-permute-start.7 = (bf16[2,1024,256]{2,1,0:T(8,128)(2,1)S(1)}, bf16[2,1024,256]{2,1,0:T(8,128)(2,1)S(1)}, u32[]{:S(2)}, u32[]{:S(2)}) collective-permute-start(bf16[2,1024,256]{2,1,0:T(8,128)(2,1)S(1)} %get-tuple-element.155), channel_id=1, source_target_pairs={{0,16},{16,0},{1,17},{17,1},{2,18},{18,2},{3,19},{19,3},{4,20},{20... | collective-permute-start | bytes 3145736 | tf_op jit(solution)/shard_map/ppermute | solution.py:38
  100.1 24.9 %collective-permute-start.10 = (bf16[272,4096]{1,0:T(8,128)(2,1)}, bf16[272,4096]{1,0:T(8,128)(2,1)}, u32[]{:S(2)}, u32[]{:S(2)}) collective-permute-start(bf16[272,4096]{1,0:T(8,128)(2,1)} %collective-permute-done.4.act_ref), channel_id=1, source_target_pairs={{0,16},{16,0},{1,17},{17,1},{2,18},{18,2},{3,19},{19,3},{4,20},{20... | collective-permute-start | bytes 6684680 | tf_op jit(solution)/shard_map/ppermute | solution.py:38
  101.5 29.8 %collective-permute-start.12 = (bf16[144,4096]{1,0:T(8,128)(2,1)S(1)}, bf16[144,4096]{1,0:T(8,128)(2,1)S(1)}, u32[]{:S(2)}, u32[]{:S(2)}) collective-permute-start(bf16[144,4096]{1,0:T(8,128)(2,1)S(1)} %slice.17), channel_id=1, source_target_pairs={{0,1},{1,0},{2,3},{3,2},{4,5},{5,4},{6,7},{7,6},{8,9},{9,8},{10,11... | collective-permute-start | bytes 3538952 | tf_op jit(solution)/shard_map/ppermute | solution.py:38
  104.3 26.9 %collective-permute-start.11 = (bf16[128,4096]{1,0:T(8,128)(2,1)S(1)}, bf16[128,4096]{1,0:T(8,128)(2,1)S(1)}, u32[]{:S(2)}, u32[]{:S(2)}) collective-permute-start(bf16[128,4096]{1,0:T(8,128)(2,1)S(1)} %slice.16), channel_id=1, source_target_pairs={{0,2},{1,3},{2,0},{3,1},{4,6},{5,7},{6,4},{7,5},{8,10},{9,11},{10,... | collective-permute-start | bytes 3145736 | tf_op jit(solution)/shard_map/ppermute | solution.py:38
  105.9 42.8 %collective-permute-start.14 = (bf16[4,3,256,256]{3,2,1,0:T(8,128)(2,1)}, bf16[4,3,256,256]{3,2,1,0:T(8,128)(2,1)}, u32[]{:S(2)}, u32[]{:S(2)}) collective-permute-start(bf16[4,3,256,256]{3,2,1,0:T(8,128)(2,1)} %collective-permute-done.8.refs_4_), channel_id=1, source_target_pairs={{0,4},{4,8},{8,12},{1,5},{5,9},{9,13},{2,6},{6,10},{10,14},{3,7},{... | collective-permute-start | bytes 4718600 | tf_op jit(solution)/shard_map/ppermute | solution.py:460
  111.0 38.2 %collective-permute-start.15 = (bf16[4,3,256,256]{3,2,1,0:T(8,128)(2,1)}, bf16[4,3,256,256]{3,2,1,0:T(8,128)(2,1)}, u32[]{:S(2)}, u32[]{:S(2)}) collective-permute-start(bf16[4,3,256,256]{3,2,1,0:T(8,128)(2,1)} %collective-permute-done.9.refs_5_), channel_id=1, source_target_pairs={{4,0},{8,4},{12,8},{5,1},{9,5},{13,9},{6,2},{10,6},{14,10},{7,3},{... | collective-permute-start | bytes 4718600 | tf_op jit(solution)/shard_map/ppermute | solution.py:460
  133.5 22.6 %collective-permute-start.13 = (bf16[272,4096]{1,0:T(8,128)(2,1)}, bf16[272,4096]{1,0:T(8,128)(2,1)}, u32[]{:S(2)}, u32[]{:S(2)}) collective-permute-start(bf16[272,4096]{1,0:T(8,128)(2,1)} %constant_dynamic-update-slice_fusion.act_ref), channel_id=1, source_target_pairs={{0,16},{16,0},{1,17},{17,1},{2,18},{18,2},{3,19},{19,3},{4,20},{20... | collective-permute-start | bytes 6684680 | tf_op jit(solution)/shard_map/ppermute | solution.py:38
  133.5 50.8 %collective-permute-start.18 = (bf16[2,2,1024,256]{3,2,1,0:T(8,128)(2,1)}, bf16[2,2,1024,256]{3,2,1,0:T(8,128)(2,1)}, u32[]{:S(2)}, u32[]{:S(2)}) collective-permute-start(bf16[2,2,1024,256]{3,2,1,0:T(8,128)(2,1)} %pad_maximum_fusion.1.refs_0_), channel_id=1, source_target_pairs={{0,1},{1,0},{2,3},{3,2},{4,5},{5,4},{6,7},{7,6},{8,9},{9,8},{10,11... | collective-permute-start | bytes 6291464 | tf_op jit(solution)/shard_map/ppermute | solution.py:38
  134.3 50.0 %collective-permute-start.19 = (bf16[2,2,1024,256]{3,2,1,0:T(8,128)(2,1)}, bf16[2,2,1024,256]{3,2,1,0:T(8,128)(2,1)}, u32[]{:S(2)}, u32[]{:S(2)}) collective-permute-start(bf16[2,2,1024,256]{3,2,1,0:T(8,128)(2,1)} %pad_maximum_fusion.1.refs_0_), channel_id=1, source_target_pairs={{0,2},{1,3},{2,0},{3,1},{4,6},{5,7},{6,4},{7,5},{8,10},{9,11},{10,... | collective-permute-start | bytes 6291464 | tf_op jit(solution)/shard_map/ppermute | solution.py:38
  135.1 2.3 copy-start.3
  149.1 42.3 %collective-permute-start.16 = (bf16[4,3,256,256]{3,2,1,0:T(8,128)(2,1)}, bf16[4,3,256,256]{3,2,1,0:T(8,128)(2,1)}, u32[]{:S(2)}, u32[]{:S(2)}) collective-permute-start(bf16[4,3,256,256]{3,2,1,0:T(8,128)(2,1)} %collective-permute-done.15.refs_7_.refs_2_), channel_id=1, source_target_pairs={{4,0},{8,4},{12,8},{5,1},{9,5},{13,9},{6,2},{10,6},{14,10},{7,3},{... | collective-permute-start | bytes 4718600 | tf_op jit(solution)/shard_map/ppermute | solution.py:460
  150.4 41.0 %collective-permute-start.17 = (bf16[4,3,256,256]{3,2,1,0:T(8,128)(2,1)}, bf16[4,3,256,256]{3,2,1,0:T(8,128)(2,1)}, u32[]{:S(2)}, u32[]{:S(2)}) collective-permute-start(bf16[4,3,256,256]{3,2,1,0:T(8,128)(2,1)} %collective-permute-done.14.refs_6_.refs_3_), channel_id=1, source_target_pairs={{0,4},{4,8},{8,12},{1,5},{5,9},{9,13},{2,6},{6,10},{10,14},{3,7},{... | collective-permute-start | bytes 4718600 | tf_op jit(solution)/shard_map/ppermute | solution.py:460
  162.7 21.6 %copy-start.2 = (bf16[2,4,256,128]{3,2,1,0:T(8,128)(2,1)}, bf16[2,4,256,128]{3,2,1,0:T(8,128)(2,1)S(1)}, u32[]{:S(2)}) copy-start(bf16[2,4,256,128]{3,2,1,0:T(8,128)(2,1)S(1)} %get-tuple-element.128.refs_6_) | copy-start | bytes 1572868
  186.6 44.9 %collective-permute-start.23 = (bf16[1,2,1024,256]{3,2,1,0:T(8,128)(2,1)}, bf16[1,2,1024,256]{3,2,1,0:T(8,128)(2,1)S(1)}, u32[]{:S(2)}, u32[]{:S(2)}) collective-permute-start(bf16[1,2,1024,256]{3,2,1,0:T(8,128)(2,1)} %slice.18), channel_id=1, source_target_pairs={{0,2},{1,3},{2,0},{3,1},{4,6},{5,7},{6,4},{7,5},{8,10},{9,11},{10,... | collective-permute-start | bytes 3145736 | tf_op jit(solution)/shard_map/ppermute | solution.py:38
  189.9 41.6 %collective-permute-start.24 = (bf16[1,2,1024,256]{3,2,1,0:T(8,128)(2,1)}, bf16[1,2,1024,256]{3,2,1,0:T(8,128)(2,1)S(1)}, u32[]{:S(2)}, u32[]{:S(2)}) collective-permute-start(bf16[1,2,1024,256]{3,2,1,0:T(8,128)(2,1)} %slice.19), channel_id=1, source_target_pairs={{0,1},{1,0},{2,3},{3,2},{4,5},{5,4},{6,7},{7,6},{8,9},{9,8},{10,11... | collective-permute-start | bytes 3145736 | tf_op jit(solution)/shard_map/ppermute | solution.py:38
  210.2 21.2 %collective-permute-start.20 = (bf16[320,256]{1,0:T(8,128)(2,1)S(1)}, bf16[320,256]{1,0:T(8,128)(2,1)S(1)}, u32[]{:S(2)}, u32[]{:S(2)}) collective-permute-start(bf16[320,256]{1,0:T(8,128)(2,1)S(1)} %get-tuple-element.162), channel_id=1, source_target_pairs={{0,1},{1,0},{2,3},{3,2},{4,5},{5,4},{6,7},{7,6},{8,9},{9,8},{10,11... | collective-permute-start | bytes 491528 | tf_op jit(solution)/shard_map/ppermute | solution.py:38
  210.8 20.7 %collective-permute-start.21 = (bf16[320,256]{1,0:T(8,128)(2,1)S(1)}, bf16[320,256]{1,0:T(8,128)(2,1)S(1)}, u32[]{:S(2)}, u32[]{:S(2)}) collective-permute-start(bf16[320,256]{1,0:T(8,128)(2,1)S(1)} %get-tuple-element.161), channel_id=1, source_target_pairs={{0,2},{1,3},{2,0},{3,1},{4,6},{5,7},{6,4},{7,5},{8,10},{9,11},{10,... | collective-permute-start | bytes 491528 | tf_op jit(solution)/shard_map/ppermute | solution.py:38
  211.8 19.7 %collective-permute-start.22 = (bf16[320,256]{1,0:T(8,128)(2,1)S(1)}, bf16[320,256]{1,0:T(8,128)(2,1)S(1)}, u32[]{:S(2)}, u32[]{:S(2)}) collective-permute-start(bf16[320,256]{1,0:T(8,128)(2,1)S(1)} %get-tuple-element.160), channel_id=1, source_target_pairs={{0,3},{1,2},{2,1},{3,0},{4,7},{5,6},{6,5},{7,4},{8,11},{9,10},{10,... | collective-permute-start | bytes 491528 | tf_op jit(solution)/shard_map/ppermute | solution.py:38
  231.4 5.0 %copy-start.4 = (bf16[256,256]{1,0:T(8,128)(2,1)S(1)}, bf16[256,256]{1,0:T(8,128)(2,1)}, u32[]{:S(2)}) copy-start(bf16[256,256]{1,0:T(8,128)(2,1)} %constant.63.clone.pick_ref) | copy-start | bytes 393220
  231.4 5.0 %copy-start.6 = (s32[3]{0:T(128)S(1)}, s32[3]{0:T(128)}, u32[]{:S(2)}) copy-start(s32[3]{0:T(128)} %copy-done.5) | copy-start | bytes 40
  231.6 6.5 %collective-permute-start.25 = (bf16[4,320,256]{2,1,0:T(8,128)(2,1)S(1)}, bf16[4,320,256]{2,1,0:T(8,128)(2,1)S(1)}, u32[]{:S(2)}, u32[]{:S(2)}) collective-permute-start(bf16[4,320,256]{2,1,0:T(8,128)(2,1)S(1)} %pad_maximum_fusion.3.own_ref.blocks_ref), channel_id=1, source_target_pairs={{0,16},{16,0},{1,17},{17,1},{2,18},{18,2},{3,19},{19,3},{4,20},{20... | collective-permute-start | bytes 1966088 | tf_op jit(solution)/shard_map/ppermute | solution.py:38
  232.9 11.2 %collective-permute-start.26 = (bf16[320,256]{1,0:T(8,128)(2,1)S(1)}, bf16[320,256]{1,0:T(8,128)(2,1)S(1)}, u32[]{:S(2)}, u32[]{:S(2)}) collective-permute-start(bf16[320,256]{1,0:T(8,128)(2,1)S(1)} %get-tuple-element.158), channel_id=1, source_target_pairs={{0,1},{1,0},{2,3},{3,2},{4,5},{5,4},{6,7},{7,6},{8,9},{9,8},{10,11... | collective-permute-start | bytes 491528 | tf_op jit(solution)/shard_map/ppermute | solution.py:38
  233.5 10.6 %collective-permute-start.27 = (bf16[320,256]{1,0:T(8,128)(2,1)S(1)}, bf16[320,256]{1,0:T(8,128)(2,1)S(1)}, u32[]{:S(2)}, u32[]{:S(2)}) collective-permute-start(bf16[320,256]{1,0:T(8,128)(2,1)S(1)} %get-tuple-element.157), channel_id=1, source_target_pairs={{0,2},{1,3},{2,0},{3,1},{4,6},{5,7},{6,4},{7,5},{8,10},{9,11},{10,... | collective-permute-start | bytes 491528 | tf_op jit(solution)/shard_map/ppermute | solution.py:38
  234.5 9.6 %collective-permute-start.28 = (bf16[320,256]{1,0:T(8,128)(2,1)S(1)}, bf16[320,256]{1,0:T(8,128)(2,1)S(1)}, u32[]{:S(2)}, u32[]{:S(2)}) collective-permute-start(bf16[320,256]{1,0:T(8,128)(2,1)S(1)} %get-tuple-element.156), channel_id=1, source_target_pairs={{0,3},{1,2},{2,1},{3,0},{4,7},{5,6},{6,5},{7,4},{8,11},{9,10},{10,... | collective-permute-start | bytes 491528 | tf_op jit(solution)/shard_map/ppermute | solution.py:38
  244.2 2.2 collective-permute-start.29
  246.3 6.0 %copy-start.1 = (bf16[4096,128]{1,0:T(8,128)(2,1)S(1)}, bf16[4096,128]{1,0:T(8,128)(2,1)}, u32[]{:S(2)}) copy-start(bf16[4096,128]{1,0:T(8,128)(2,1)} %param.26) | copy-start | bytes 3145732
Sparse Core Ops, SparseCore 0:
  21.7 61.0 all-gather.4
  100.2 14.4 all-gather.6

commit v10 on v9

--- a/solution.py
+++ b/solution.py
@@ -224,7 +224,7 @@
     place = np.arange(CHUNK)
     of, by = place[:, None], place[None, :]
     parts = []
-    for level in range(LEVELS):
+    for level in range(1, LEVELS):
         half = 1 << level
         middle = (of // (2 * half)) * 2 * half + half - 1
         later = (of % (2 * half)) >= half
@@ -284,21 +284,27 @@
     low = (decay - high.astype(f32)).astype(bf16)
     own = dot((r.astype(f32) * reward_ref[...] * k.astype(f32)).astype(bf16), same) * v.astype(f32)
 
+    subs = [slice(at, at + CHUNK) for at in range(0, tokens, CHUNK)]
+    both = jnp.concatenate([jnp.concatenate([part[lines] for lines in subs], axis=1) for part in (high, low)], axis=0)
+    all_kept = jnp.exp(dot(sums_ref[...], both))
     memory = memory_ref[...]
     rows = []
-    for sub in range(tokens // CHUNK):
-        lines = slice(sub * CHUNK, (sub + 1) * CHUNK)
+    for sub, lines in enumerate(subs):
         r_sub, k_sub, v_sub = r[lines], k[lines], v[lines]
-        kept = jnp.exp(dot(sums_ref[...], jnp.concatenate([high[lines], low[lines]], axis=0)))
+        kept = all_kept[:, sub * cols : (sub + 1) * cols]
         scores = jnp.zeros((CHUNK, heads * CHUNK), f32)
         for bit in range(LEVELS):
-            part = kept[bit * CHUNK : (bit + 1) * CHUNK].astype(bf16)
-            lookup = jnp.concatenate([k_sub * part] * heads, axis=0) * same
-            scores = jnp.where(level == bit, dot_nt(r_sub * part, lookup), scores)
+            query, lookup = r_sub, k_sub
+            if bit:
+                part = kept[(bit - 1) * CHUNK : bit * CHUNK].astype(bf16)
+                query, lookup = query * part, lookup * part
+            lookup = jnp.concatenate([lookup] * heads, axis=0) * same
+            scores = jnp.where(level == bit, dot_nt(query, lookup), scores)
         v_heads = jnp.concatenate([v_sub] * heads, axis=0) * same
-        from_start = r_sub * kept[LEVELS * CHUNK : (LEVELS + 1) * CHUNK].astype(bf16)
-        to_end = k_sub * kept[(LEVELS + 1) * CHUNK : (LEVELS + 2) * CHUNK].astype(bf16)
-        whole = kept[(LEVELS + 2) * CHUNK : (LEVELS + 2) * CHUNK + 1]
+        after = (LEVELS - 1) * CHUNK
+        from_start = r_sub * kept[after : after + CHUNK].astype(bf16)
+        to_end = k_sub * kept[after + CHUNK : after + 2 * CHUNK].astype(bf16)
+        whole = kept[after + 2 * CHUNK : after + 2 * CHUNK + 1]
         rows.append(dot_nt(from_start, memory.astype(bf16)) + dot(scores.astype(bf16), v_heads))
         memory = memory * whole + same_f32 * dot_tn(v_sub, to_end)
     memory_ref[...] = memory

time: 261 us -> 259 us (level)
  no operation moved by 1% of the time
where the time goes in v10:
time: 259 us; the launch traced here: 257 us
  Pallas kernels  134 us (52%)
  starting transfers between devices  44.3 us (17%)
  local copies, waits for them, and re-layouts  39.7 us (15%)
  waiting for transfers between devices  19.9 us (8%)
  between operations  14.4 us (6%)
  other arithmetic  5.31 us (2%)
    pallas_call x8, Pallas kernels, shifted(): pl.pallas_call(mix_kernel, grid_spec=pltpu.PrefetchScalarGridSpec(num_sca...  49.4 us
    pallas_call x2, Pallas kernels, recurrence(): pl.pallas_call(functools.partial(wkv_kernel, prompt=prompt, parted=bool(e...  33.7 us
    ppermute x7, starting transfers between devices, moved(): lax.ppermute(value, axis, [(i, i + by) for i in range(peers) if 0 <= i +...  24.1 us
    pallas_call x1, Pallas kernels, projected(): pl.pallas_call(project_kernel, grid_spec=pltpu.PrefetchScalarGridSpec(num...  21.6 us
    ppermute x23, starting transfers between devices, swapped(): return lax.ppermute(value, axis, [(i, i ^ by) for i in range(peers)])  20.1 us
    pallas_call x1, Pallas kernels, ordered(): pl.pallas_call(order_kernel, grid=(width // block,), in_specs=[pl.BlockSp...  13.9 us
    gather x1, local copies, waits for them, and re-layouts, local(): left = fading_left_matrix[perm]  12.1 us
    pallas_call x2, Pallas kernels, finished(): pl.pallas_call(finish_kernel, grid_spec=pltpu.PrefetchScalarGridSpec(num_...  12 us
  transfers between devices with their start and end apart: 32, of which 6 were waited for; matrix products, arithmetic and copies ran while one was open for 16% of the time, Pallas kernels for 50%

profile of v10, /device:TPU:0, one launch (start us, length us, event | category | flops | bytes accessed | tf_op | source)
XLA Modules:
  0.0 257.4 jit_solution(2367621633235218574)
XLA Ops:
  8.2 4.8 %collective-permute-start = (bf16[16,4096]{1,0:T(8,128)(2,1)S(1)}, bf16[16,4096]{1,0:T(8,128)(2,1)S(1)}, u32[]{:S(2)}, u32[]{:S(2)}) collective-permute-start(bf16[16,4096]{1,0:T(8,128)(2,1)S(1)} %constant_dynamic-slice_fusion), channel_id=1, source_target_pairs={{0,1},{1,2},{2,3},{4,5},{5,6},{6,7},{8,9},{9,10},{10,11},{12,13},{... | collective-permute-start | bytes 393224 | tf_op jit(solution)/shard_map/ppermute | solution.py:466
  13.1 2.1 convert_element_type.17
  15.2 2.9 %dynamic-slice_convert_fusion = (bf16[3,256,256]{2,1,0:T(8,128)(2,1)S(1)}, bf16[3,256,256]{2,1,0:T(8,128)(2,1)}, bf16[3,256,256]{2,1,0:T(8,128)(2,1)}, bf16[3,256,256]{2,1,0:T(8,128)(2,1)S(1)}) fusion(f32[3,256,1024]{2,1,0:T(8,128)} %param.24, s32[]{:T(128)S(6)} %select_n.49, s32[]{:T(128)S(6)} %select_n.48, s32[]{:T(128)S(6)} %select_n.47, s32[]{:T(128)S(6)} %select_n.46), kind=kLoop, calls=%fused_computation.5 | loop fusion | bytes 3145744 | tf_op jit(solution)/shard_map/convert_element_type | solution.py:500
  18.1 1.5 collective-permute-start.1
  19.6 2.0 collective-permute-start.3
  21.7 1.7 constant_dynamic-slice_fusion.3
  24.2 13.9 %shard_map.203 = (bf16[272,4096]{1,0:T(8,128)(2,1)}, f32[8,4096]{1,0:T(8,128)S(1)}) custom-call(bf16[272,4096]{1,0:T(8,128)(2,1)S(1)} %pad_maximum_fusion.x_ref, f32[1,4096]{1,0:T(1,128)S(1)} %bitcast.44, f32[8,4096]{1,0:T(8,128)S(1)} %pad.4.coeff_ref, s32[1,4096]{1,0:T(1,128)S(1)} %bitcast.43), custom_call_target="tpu_custom_call" | custom-call | flops 1024 | bytes 1024 | tf_op jit(solution)/shard_map/pallas_call | solution.py:76
  40.6 1.3 pad_maximum_fusion.2.refs_3_
  42.0 4.6 %collective-permute-start.8 = (bf16[4,3,256,256]{3,2,1,0:T(8,128)(2,1)}, bf16[4,3,256,256]{3,2,1,0:T(8,128)(2,1)}, u32[]{:S(2)}, u32[]{:S(2)}) collective-permute-start(bf16[4,3,256,256]{3,2,1,0:T(8,128)(2,1)} %pad_maximum_fusion.2.refs_3_), channel_id=1, source_target_pairs={{0,4},{4,8},{8,12},{1,5},{5,9},{9,13},{2,6},{6,10},{10,14},{3,7},{... | collective-permute-start | bytes 4718600 | tf_op jit(solution)/shard_map/ppermute | solution.py:466
  46.6 1.3 collective-permute-start.9
  47.9 12.1 %gather_fusion = bf16[4096,128]{1,0:T(8,128)(2,1)S(1)} fusion(bf16[4096,128]{1,0:T(8,128)(2,1)S(1)} %copy-done, s32[4096]{0:T(1024)S(1)} %fusion), kind=kCustom, calls=%fused_computation | custom fusion | bytes 2113536 | tf_op jit(solution)/shard_map/gather | solution.py:520
  60.1 6.4 %shard_map.204 = (bf16[3,2,4,256,4096]{4,3,2,1,0:T(8,128)(2,1)}, bf16[2,4,256,128]{3,2,1,0:T(8,128)(2,1)S(1)}) custom-call(s32[3]{0:T(128)S(1)} %pad_add_fusion.where_ref, bf16[272,4096]{1,0:T(8,128)(2,1)} %get-tuple-element.80.act_ref, f32[8,4096]{1,0:T(8,128)S(1)} %get-tuple-element.82.coeff_ref, bf16[4096,128]{1,0:T(8,128)(2,1)S(1)} %gather_fusion), custom_call_target="tpu_custom_call" | custom-call | flops 1024 | bytes 1024 | tf_op jit(solution)/shard_map/pallas_call | solution.py:134
  66.4 6.4 %shard_map.205 = (bf16[3,2,4,256,4096]{4,3,2,1,0:T(8,128)(2,1)}, bf16[2,4,256,128]{3,2,1,0:T(8,128)(2,1)S(1)}) custom-call(s32[3]{0:T(128)S(1)} %pad_add_fusion.where_ref, bf16[272,4096]{1,0:T(8,128)(2,1)} %collective-permute-done.6.act_ref, f32[8,4096]{1,0:T(8,128)S(1)} %get-tuple-element.82.coeff_ref, ...), custom_call_target="tpu_custom_call", output_to_operand_aliasing={{0}: (4, {}), {1}: (5, {})} | custom-call | flops 1024 | bytes 1024 | tf_op jit(solution)/shard_map/pallas_call | solution.py:134
  72.8 9.9 %all-gather.5.cloned.1.call-done = bf16[4096,256]{1,0:T(8,128)(2,1)} async-done(((bf16[1024,256]{1,0:T(8,128)(2,1)}), bf16[4096,256]{1,0:T(8,128)(2,1)}) %all-gather.5.cloned.1.call-update) | async-done | bytes 2097168 | tf_op jit(solution)/shard_map/all_gather | solution.py:498
  82.8 1.7 dynamic-slice_bitcast_fusion
  84.5 1.3 dynamic_slice.67
  85.9 1.3 dynamic_slice.68
  87.2 1.3 dynamic_slice.66
  88.5 1.5 constant_dynamic-slice_fusion.1.refs_7_
  90.0 1.5 pad_maximum_fusion.1.refs_0_
  91.5 6.6 %collective-permute-done.8.refs_4_ = bf16[4,3,256,256]{3,2,1,0:T(8,128)(2,1)} collective-permute-done((bf16[4,3,256,256]{3,2,1,0:T(8,128)(2,1)}, bf16[4,3,256,256]{3,2,1,0:T(8,128)(2,1)}, u32[]{:S(2)}, u32[]{:S(2)}) %collective-permute-start.8) | collective-permute-done | bytes 1572896 | tf_op jit(solution)/shard_map/ppermute | solution.py:466
  98.1 2.0 collective-permute-done.9.refs_5_
  100.1 1.4 slice.17
  101.5 1.5 collective-permute-start.12
  103.0 1.3 slice.16
  104.3 1.5 collective-permute-start.11
  105.9 5.1 %collective-permute-start.14 = (bf16[4,3,256,256]{3,2,1,0:T(8,128)(2,1)}, bf16[4,3,256,256]{3,2,1,0:T(8,128)(2,1)}, u32[]{:S(2)}, u32[]{:S(2)}) collective-permute-start(bf16[4,3,256,256]{3,2,1,0:T(8,128)(2,1)} %collective-permute-done.8.refs_4_), channel_id=1, source_target_pairs={{0,4},{4,8},{8,12},{1,5},{5,9},{9,13},{2,6},{6,10},{10,14},{3,7},{... | collective-permute-start | bytes 4718600 | tf_op jit(solution)/shard_map/ppermute | solution.py:466
  112.3 6.3 %shard_map.206 = (bf16[3,2,4,256,4096]{4,3,2,1,0:T(8,128)(2,1)}, bf16[2,4,256,128]{3,2,1,0:T(8,128)(2,1)S(1)}) custom-call(s32[3]{0:T(128)S(1)} %pad_add_fusion.where_ref, bf16[272,4096]{1,0:T(8,128)(2,1)} %collective-permute-done.4.act_ref, f32[8,4096]{1,0:T(8,128)S(1)} %get-tuple-element.82.coeff_ref, ...), custom_call_target="tpu_custom_call", output_to_operand_aliasing={{0}: (4, {}), {1}: (5, {})} | custom-call | flops 1024 | bytes 1024 | tf_op jit(solution)/shard_map/pallas_call | solution.py:134
  118.6 6.4 %shard_map.207 = (bf16[3,2,4,256,4096]{4,3,2,1,0:T(8,128)(2,1)}, bf16[2,4,256,128]{3,2,1,0:T(8,128)(2,1)S(1)}) custom-call(s32[3]{0:T(128)S(1)} %pad_add_fusion.where_ref, bf16[272,4096]{1,0:T(8,128)(2,1)} %collective-permute-done.5.act_ref, f32[8,4096]{1,0:T(8,128)S(1)} %get-tuple-element.82.coeff_ref, ...), custom_call_target="tpu_custom_call", output_to_operand_aliasing={{0}: (4, {}), {1}: (5, {})} | custom-call | flops 1024 | bytes 1024 | tf_op jit(solution)/shard_map/pallas_call | solution.py:134
  124.9 6.3 %shard_map.208 = (bf16[3,2,4,256,4096]{4,3,2,1,0:T(8,128)(2,1)}, bf16[2,4,256,128]{3,2,1,0:T(8,128)(2,1)S(1)}) custom-call(s32[3]{0:T(128)S(1)} %pad_add_fusion.where_ref, bf16[272,4096]{1,0:T(8,128)(2,1)} %collective-permute-done.10.act_ref, f32[8,4096]{1,0:T(8,128)S(1)} %get-tuple-element.82.coeff_ref, ...), custom_call_target="tpu_custom_call", output_to_operand_aliasing={{0}: (4, {}), {1}: (5, {})} | custom-call | flops 1024 | bytes 1024 | tf_op jit(solution)/shard_map/pallas_call | solution.py:134
  135.1 2.3 copy-done.3
  137.4 4.8 %shard_map.209 = (bf16[3,2,4,256,4096]{4,3,2,1,0:T(8,128)(2,1)}, bf16[2,4,256,128]{3,2,1,0:T(8,128)(2,1)S(1)}) custom-call(s32[3]{0:T(128)S(1)} %pad_add_fusion.where_ref, bf16[2,272,4096]{2,1,0:T(8,128)(2,1)S(1)} %bitcast.42, f32[8,4096]{1,0:T(8,128)S(1)} %get-tuple-element.82.coeff_ref, ...), custom_call_target="tpu_custom_call", output_to_operand_aliasing={{0}: (4, {}), {1}: (5, {})} | custom-call | flops 1024 | bytes 1024 | tf_op jit(solution)/shard_map/pallas_call | solution.py:134
  142.2 6.4 %shard_map.210 = (bf16[3,2,4,256,4096]{4,3,2,1,0:T(8,128)(2,1)}, bf16[2,4,256,128]{3,2,1,0:T(8,128)(2,1)S(1)}) custom-call(s32[3]{0:T(128)S(1)} %pad_add_fusion.where_ref, bf16[272,4096]{1,0:T(8,128)(2,1)} %constant_dynamic-update-slice_fusion.act_ref, f32[8,4096]{1,0:T(8,128)S(1)} %get-tuple-element.82.coeff_ref, ...), custom_call_target="tpu_custom_call", output_to_operand_aliasing={{0}: (4, {}), {1}: (5, {})} | custom-call | flops 1024 | bytes 1024 | tf_op jit(solution)/shard_map/pallas_call | solution.py:134
  149.1 1.3 collective-permute-start.16
  150.4 5.7 %collective-permute-start.17 = (bf16[4,3,256,256]{3,2,1,0:T(8,128)(2,1)}, bf16[4,3,256,256]{3,2,1,0:T(8,128)(2,1)}, u32[]{:S(2)}, u32[]{:S(2)}) collective-permute-start(bf16[4,3,256,256]{3,2,1,0:T(8,128)(2,1)} %collective-permute-done.14.refs_6_.refs_3_), channel_id=1, source_target_pairs={{0,4},{4,8},{8,12},{1,5},{5,9},{9,13},{2,6},{6,10},{10,14},{3,7},{... | collective-permute-start | bytes 4718600 | tf_op jit(solution)/shard_map/ppermute | solution.py:466
  156.1 6.4 %shard_map.211 = (bf16[3,2,4,256,4096]{4,3,2,1,0:T(8,128)(2,1)}, bf16[2,4,256,128]{3,2,1,0:T(8,128)(2,1)S(1)}) custom-call(s32[3]{0:T(128)S(1)} %pad_add_fusion.where_ref, bf16[272,4096]{1,0:T(8,128)(2,1)} %collective-permute-done.13.act_ref, f32[8,4096]{1,0:T(8,128)S(1)} %get-tuple-element.82.coeff_ref, ...), custom_call_target="tpu_custom_call", output_to_operand_aliasing={{0}: (4, {}), {1}: (5, {})} | custom-call | flops 1024 | bytes 1024 | tf_op jit(solution)/shard_map/pallas_call | solution.py:134
  162.5 21.6 %shard_map.212.refs_5_ = f32[3,2,4,256,256]{4,3,2,1,0:T(8,128)} custom-call(s32[3]{0:T(128)} %copy-done.5, bf16[3,2,4,256,4096]{4,3,2,1,0:T(8,128)(2,1)} %get-tuple-element.121.refs_0_.refs_1_.refs_2_, bf16[3,2,4,256,4096]{4,3,2,1,0:T(8,128)(2,1)} %get-tuple-element.121.refs_0_.refs_1_.refs_2_, ...), custom_call_target="tpu_custom_call" | custom-call | flops 1024 | bytes 1024 | tf_op jit(solution)/shard_map/pallas_call | solution.py:200
  184.1 2.3 slice.18
  187.4 2.3 slice.19
  189.7 1.5 collective-permute-start.24
  191.2 16.8 %shard_map.213 = bf16[4,320,256]{2,1,0:T(8,128)(2,1)} custom-call(s32[2]{0:T(128)} %extent_ref.3, s32[3]{0:T(128)} %copy-done.5, bf16[3,2,4,256,4096]{4,3,2,1,0:T(8,128)(2,1)} %get-tuple-element.121.refs_0_.refs_1_.refs_2_, bf16[4,3,256,256]{3,2,1,0:T(8,128)(2,1)} %collective-permute-done.16.refs_1_, ...), custom_call_target="tpu_custom_call" | custom-call | flops 1024 | bytes 1024 | tf_op jit(solution)/shard_map/pallas_call | solution.py:351
  210.8 2.0 collective-permute-start.22
  212.8 16.8 %shard_map.214 = bf16[4,320,256]{2,1,0:T(8,128)(2,1)} custom-call(s32[2]{0:T(128)} %extent_ref.3, s32[3]{0:T(128)} %copy-done.5, bf16[3,2,4,256,4096]{4,3,2,1,0:T(8,128)(2,1)} %get-tuple-element.121.refs_0_.refs_1_.refs_2_, bf16[4,3,256,256]{3,2,1,0:T(8,128)(2,1)} %collective-permute-done.16.refs_1_, ...), custom_call_target="tpu_custom_call" | custom-call | flops 1024 | bytes 1024 | tf_op jit(solution)/shard_map/pallas_call | solution.py:351
  232.7 2.0 collective-permute-start.28
  234.6 1.6 shard_map.216.refs_0_
  236.3 6.0 %shard_map.215.refs_5_ = bf16[2,256,2048]{2,1,0:T(8,128)(2,1)} custom-call(s32[3]{0:T(128)S(1)} %copy-done.6, bf16[512,4096]{1,0:T(8,128)(2,1)} %bitcast.47, bf16[4,320,256]{2,1,0:T(8,128)(2,1)S(1)} %pad_maximum_fusion.3.own_ref.blocks_ref, bf16[4,320,256]{2,1,0:T(8,128)(2,1)S(1)} %collective-permute-done.25.far_ref, ...), custom_call_target="tpu_custom_call" | custom-call | flops 1024 | bytes 1024 | tf_op jit(solution)/shard_map/pallas_call | solution.py:403
  242.4 1.6 shard_map.218
  244.5 6.0 %shard_map.217 = bf16[2,256,2048]{2,1,0:T(8,128)(2,1)} custom-call(s32[3]{0:T(128)S(1)} %copy-done.6, bf16[512,4096]{1,0:T(8,128)(2,1)} %bitcast.48, bf16[4,320,256]{2,1,0:T(8,128)(2,1)S(1)} %pad_maximum_fusion.4.own_ref.blocks_ref, bf16[4,320,256]{2,1,0:T(8,128)(2,1)S(1)} %collective-permute-done.29.far_ref, ...), custom_call_target="tpu_custom_call", output_to_operand_aliasing={{}: (9, {})} | custom-call | flops 1024 | bytes 1024 | tf_op jit(solution)/shard_map/pallas_call | solution.py:403
  (80 shorter events, 17.5 us)
Async XLA Ops:
  7.2 40.8 %copy-start = (bf16[4096,128]{1,0:T(8,128)(2,1)S(1)}, bf16[4096,128]{1,0:T(8,128)(2,1)}, u32[]{:S(2)}) copy-start(bf16[4096,128]{1,0:T(8,128)(2,1)} %param.26) | copy-start | bytes 3145732
  7.2 75.6 %all-gather.5.cloned.1.call-start = ((), (), s32[]{:S(2)}) async-start(), calls=%async_computation | async-start | bytes 2621440 | tf_op jit(solution)/shard_map/all_gather | solution.py:498
  8.2 15.2 %collective-permute-start = (bf16[16,4096]{1,0:T(8,128)(2,1)S(1)}, bf16[16,4096]{1,0:T(8,128)(2,1)S(1)}, u32[]{:S(2)}, u32[]{:S(2)}) collective-permute-start(bf16[16,4096]{1,0:T(8,128)(2,1)S(1)} %constant_dynamic-slice_fusion), channel_id=1, source_target_pairs={{0,1},{1,2},{2,3},{4,5},{5,6},{6,7},{8,9},{9,10},{10,11},{12,13},{... | collective-permute-start | bytes 393224 | tf_op jit(solution)/shard_map/ppermute | solution.py:466
  18.1 20.0 %collective-permute-start.1 = (bf16[3,256,256]{2,1,0:T(8,128)(2,1)}, bf16[3,256,256]{2,1,0:T(8,128)(2,1)S(1)}, u32[]{:S(2)}, u32[]{:S(2)}) collective-permute-start(bf16[3,256,256]{2,1,0:T(8,128)(2,1)} %get-tuple-element.152), channel_id=1, source_target_pairs={{0,1},{1,0},{2,3},{3,2},{4,5},{5,4},{6,7},{7,6},{8,9},{9,8},{10,11... | collective-permute-start | bytes 1179656 | tf_op jit(solution)/shard_map/ppermute | solution.py:38
  19.6 18.9 %collective-permute-start.2 = (bf16[3,256,256]{2,1,0:T(8,128)(2,1)}, bf16[3,256,256]{2,1,0:T(8,128)(2,1)S(1)}, u32[]{:S(2)}, u32[]{:S(2)}) collective-permute-start(bf16[3,256,256]{2,1,0:T(8,128)(2,1)} %get-tuple-element.151), channel_id=1, source_target_pairs={{0,2},{1,3},{2,0},{3,1},{4,6},{5,7},{6,4},{7,5},{8,10},{9,11},{10,... | collective-permute-start | bytes 1179656 | tf_op jit(solution)/shard_map/ppermute | solution.py:38
  19.6 18.9 %collective-permute-start.3 = (bf16[3,256,256]{2,1,0:T(8,128)(2,1)S(1)}, bf16[3,256,256]{2,1,0:T(8,128)(2,1)S(1)}, u32[]{:S(2)}, u32[]{:S(2)}) collective-permute-start(bf16[3,256,256]{2,1,0:T(8,128)(2,1)S(1)} %get-tuple-element.150), channel_id=1, source_target_pairs={{0,3},{1,2},{2,1},{3,0},{4,7},{5,6},{6,5},{7,4},{8,11},{9,10},{10,... | collective-permute-start | bytes 1179656 | tf_op jit(solution)/shard_map/ppermute | solution.py:38
  21.6 1.8 copy-start.9
  21.6 113.5 %all-gather.7.cloned.1.call-start = ((), (), s32[]{:S(2)}) async-start(), calls=%async_computation.1 | async-start | bytes 6684672 | tf_op jit(solution)/shard_map/all_gather | solution.py:545
  23.4 0.7 copy-start.7
  23.5 0.7 copy-start.8
  38.5 27.9 %collective-permute-start.6 = (bf16[272,4096]{1,0:T(8,128)(2,1)}, bf16[272,4096]{1,0:T(8,128)(2,1)}, u32[]{:S(2)}, u32[]{:S(2)}) collective-permute-start(bf16[272,4096]{1,0:T(8,128)(2,1)} %get-tuple-element.80.act_ref), channel_id=1, source_target_pairs={{0,16},{16,0},{1,17},{17,1},{2,18},{18,2},{3,19},{19,3},{4,20},{20... | collective-permute-start | bytes 6684680 | tf_op jit(solution)/shard_map/ppermute | solution.py:38
  38.5 61.6 %collective-permute-start.4 = (bf16[272,4096]{1,0:T(8,128)(2,1)}, bf16[272,4096]{1,0:T(8,128)(2,1)}, u32[]{:S(2)}, u32[]{:S(2)}) collective-permute-start(bf16[272,4096]{1,0:T(8,128)(2,1)} %get-tuple-element.80.act_ref), channel_id=1, source_target_pairs={{0,1},{1,0},{2,3},{3,2},{4,5},{5,4},{6,7},{7,6},{8,9},{9,8},{10,11... | collective-permute-start | bytes 6684680 | tf_op jit(solution)/shard_map/ppermute | solution.py:38
  39.8 60.3 %collective-permute-start.5 = (bf16[272,4096]{1,0:T(8,128)(2,1)}, bf16[272,4096]{1,0:T(8,128)(2,1)}, u32[]{:S(2)}, u32[]{:S(2)}) collective-permute-start(bf16[272,4096]{1,0:T(8,128)(2,1)} %get-tuple-element.80.act_ref), channel_id=1, source_target_pairs={{0,2},{1,3},{2,0},{3,1},{4,6},{5,7},{6,4},{7,5},{8,10},{9,11},{10,... | collective-permute-start | bytes 6684680 | tf_op jit(solution)/shard_map/ppermute | solution.py:38
  40.6 115.5 %copy-start.5 = (s32[3]{0:T(128)}, s32[3]{0:T(128)S(1)}, u32[]{:S(2)}) copy-start(s32[3]{0:T(128)S(1)} %pad_add_fusion.where_ref) | copy-start | bytes 40
  42.0 56.1 %collective-permute-start.8 = (bf16[4,3,256,256]{3,2,1,0:T(8,128)(2,1)}, bf16[4,3,256,256]{3,2,1,0:T(8,128)(2,1)}, u32[]{:S(2)}, u32[]{:S(2)}) collective-permute-start(bf16[4,3,256,256]{3,2,1,0:T(8,128)(2,1)} %pad_maximum_fusion.2.refs_3_), channel_id=1, source_target_pairs={{0,4},{4,8},{8,12},{1,5},{5,9},{9,13},{2,6},{6,10},{10,14},{3,7},{... | collective-permute-start | bytes 4718600 | tf_op jit(solution)/shard_map/ppermute | solution.py:466
  46.6 53.5 %collective-permute-start.9 = (bf16[4,3,256,256]{3,2,1,0:T(8,128)(2,1)}, bf16[4,3,256,256]{3,2,1,0:T(8,128)(2,1)}, u32[]{:S(2)}, u32[]{:S(2)}) collective-permute-start(bf16[4,3,256,256]{3,2,1,0:T(8,128)(2,1)} %pad_maximum_fusion.2.refs_3_), channel_id=1, source_target_pairs={{4,0},{8,4},{12,8},{5,1},{9,5},{13,9},{6,2},{10,6},{14,10},{7,3},{... | collective-permute-start | bytes 4718600 | tf_op jit(solution)/shard_map/ppermute | solution.py:466
  84.5 5.5 %collective-permute-start.7 = (bf16[2,1024,256]{2,1,0:T(8,128)(2,1)S(1)}, bf16[2,1024,256]{2,1,0:T(8,128)(2,1)S(1)}, u32[]{:S(2)}, u32[]{:S(2)}) collective-permute-start(bf16[2,1024,256]{2,1,0:T(8,128)(2,1)S(1)} %get-tuple-element.155), channel_id=1, source_target_pairs={{0,16},{16,0},{1,17},{17,1},{2,18},{18,2},{3,19},{19,3},{4,20},{20... | collective-permute-start | bytes 3145736 | tf_op jit(solution)/shard_map/ppermute | solution.py:38
  100.1 24.9 %collective-permute-start.10 = (bf16[272,4096]{1,0:T(8,128)(2,1)}, bf16[272,4096]{1,0:T(8,128)(2,1)}, u32[]{:S(2)}, u32[]{:S(2)}) collective-permute-start(bf16[272,4096]{1,0:T(8,128)(2,1)} %collective-permute-done.4.act_ref), channel_id=1, source_target_pairs={{0,16},{16,0},{1,17},{17,1},{2,18},{18,2},{3,19},{19,3},{4,20},{20... | collective-permute-start | bytes 6684680 | tf_op jit(solution)/shard_map/ppermute | solution.py:38
  101.5 29.8 %collective-permute-start.12 = (bf16[144,4096]{1,0:T(8,128)(2,1)S(1)}, bf16[144,4096]{1,0:T(8,128)(2,1)S(1)}, u32[]{:S(2)}, u32[]{:S(2)}) collective-permute-start(bf16[144,4096]{1,0:T(8,128)(2,1)S(1)} %slice.17), channel_id=1, source_target_pairs={{0,1},{1,0},{2,3},{3,2},{4,5},{5,4},{6,7},{7,6},{8,9},{9,8},{10,11... | collective-permute-start | bytes 3538952 | tf_op jit(solution)/shard_map/ppermute | solution.py:38
  104.3 26.9 %collective-permute-start.11 = (bf16[128,4096]{1,0:T(8,128)(2,1)S(1)}, bf16[128,4096]{1,0:T(8,128)(2,1)S(1)}, u32[]{:S(2)}, u32[]{:S(2)}) collective-permute-start(bf16[128,4096]{1,0:T(8,128)(2,1)S(1)} %slice.16), channel_id=1, source_target_pairs={{0,2},{1,3},{2,0},{3,1},{4,6},{5,7},{6,4},{7,5},{8,10},{9,11},{10,... | collective-permute-start | bytes 3145736 | tf_op jit(solution)/shard_map/ppermute | solution.py:38
  105.9 42.8 %collective-permute-start.14 = (bf16[4,3,256,256]{3,2,1,0:T(8,128)(2,1)}, bf16[4,3,256,256]{3,2,1,0:T(8,128)(2,1)}, u32[]{:S(2)}, u32[]{:S(2)}) collective-permute-start(bf16[4,3,256,256]{3,2,1,0:T(8,128)(2,1)} %collective-permute-done.8.refs_4_), channel_id=1, source_target_pairs={{0,4},{4,8},{8,12},{1,5},{5,9},{9,13},{2,6},{6,10},{10,14},{3,7},{... | collective-permute-start | bytes 4718600 | tf_op jit(solution)/shard_map/ppermute | solution.py:466
  111.0 38.2 %collective-permute-start.15 = (bf16[4,3,256,256]{3,2,1,0:T(8,128)(2,1)}, bf16[4,3,256,256]{3,2,1,0:T(8,128)(2,1)}, u32[]{:S(2)}, u32[]{:S(2)}) collective-permute-start(bf16[4,3,256,256]{3,2,1,0:T(8,128)(2,1)} %collective-permute-done.9.refs_5_), channel_id=1, source_target_pairs={{4,0},{8,4},{12,8},{5,1},{9,5},{13,9},{6,2},{10,6},{14,10},{7,3},{... | collective-permute-start | bytes 4718600 | tf_op jit(solution)/shard_map/ppermute | solution.py:466
  133.5 22.7 %collective-permute-start.13 = (bf16[272,4096]{1,0:T(8,128)(2,1)}, bf16[272,4096]{1,0:T(8,128)(2,1)}, u32[]{:S(2)}, u32[]{:S(2)}) collective-permute-start(bf16[272,4096]{1,0:T(8,128)(2,1)} %constant_dynamic-update-slice_fusion.act_ref), channel_id=1, source_target_pairs={{0,16},{16,0},{1,17},{17,1},{2,18},{18,2},{3,19},{19,3},{4,20},{20... | collective-permute-start | bytes 6684680 | tf_op jit(solution)/shard_map/ppermute | solution.py:38
  133.5 50.6 %collective-permute-start.18 = (bf16[2,2,1024,256]{3,2,1,0:T(8,128)(2,1)}, bf16[2,2,1024,256]{3,2,1,0:T(8,128)(2,1)}, u32[]{:S(2)}, u32[]{:S(2)}) collective-permute-start(bf16[2,2,1024,256]{3,2,1,0:T(8,128)(2,1)} %pad_maximum_fusion.1.refs_0_), channel_id=1, source_target_pairs={{0,1},{1,0},{2,3},{3,2},{4,5},{5,4},{6,7},{7,6},{8,9},{9,8},{10,11... | collective-permute-start | bytes 6291464 | tf_op jit(solution)/shard_map/ppermute | solution.py:38
  134.3 49.8 %collective-permute-start.19 = (bf16[2,2,1024,256]{3,2,1,0:T(8,128)(2,1)}, bf16[2,2,1024,256]{3,2,1,0:T(8,128)(2,1)}, u32[]{:S(2)}, u32[]{:S(2)}) collective-permute-start(bf16[2,2,1024,256]{3,2,1,0:T(8,128)(2,1)} %pad_maximum_fusion.1.refs_0_), channel_id=1, source_target_pairs={{0,2},{1,3},{2,0},{3,1},{4,6},{5,7},{6,4},{7,5},{8,10},{9,11},{10,... | collective-permute-start | bytes 6291464 | tf_op jit(solution)/shard_map/ppermute | solution.py:38
  135.1 2.3 copy-start.3
  149.1 42.1 %collective-permute-start.16 = (bf16[4,3,256,256]{3,2,1,0:T(8,128)(2,1)}, bf16[4,3,256,256]{3,2,1,0:T(8,128)(2,1)}, u32[]{:S(2)}, u32[]{:S(2)}) collective-permute-start(bf16[4,3,256,256]{3,2,1,0:T(8,128)(2,1)} %collective-permute-done.15.refs_7_.refs_2_), channel_id=1, source_target_pairs={{4,0},{8,4},{12,8},{5,1},{9,5},{13,9},{6,2},{10,6},{14,10},{7,3},{... | collective-permute-start | bytes 4718600 | tf_op jit(solution)/shard_map/ppermute | solution.py:466
  150.4 40.8 %collective-permute-start.17 = (bf16[4,3,256,256]{3,2,1,0:T(8,128)(2,1)}, bf16[4,3,256,256]{3,2,1,0:T(8,128)(2,1)}, u32[]{:S(2)}, u32[]{:S(2)}) collective-permute-start(bf16[4,3,256,256]{3,2,1,0:T(8,128)(2,1)} %collective-permute-done.14.refs_6_.refs_3_), channel_id=1, source_target_pairs={{0,4},{4,8},{8,12},{1,5},{5,9},{9,13},{2,6},{6,10},{10,14},{3,7},{... | collective-permute-start | bytes 4718600 | tf_op jit(solution)/shard_map/ppermute | solution.py:466
  162.5 21.6 %copy-start.2 = (bf16[2,4,256,128]{3,2,1,0:T(8,128)(2,1)}, bf16[2,4,256,128]{3,2,1,0:T(8,128)(2,1)S(1)}, u32[]{:S(2)}) copy-start(bf16[2,4,256,128]{3,2,1,0:T(8,128)(2,1)S(1)} %get-tuple-element.128.refs_6_) | copy-start | bytes 1572868
  186.4 43.3 %collective-permute-start.23 = (bf16[1,2,1024,256]{3,2,1,0:T(8,128)(2,1)}, bf16[1,2,1024,256]{3,2,1,0:T(8,128)(2,1)S(1)}, u32[]{:S(2)}, u32[]{:S(2)}) collective-permute-start(bf16[1,2,1024,256]{3,2,1,0:T(8,128)(2,1)} %slice.18), channel_id=1, source_target_pairs={{0,2},{1,3},{2,0},{3,1},{4,6},{5,7},{6,4},{7,5},{8,10},{9,11},{10,... | collective-permute-start | bytes 3145736 | tf_op jit(solution)/shard_map/ppermute | solution.py:38
  189.7 40.0 %collective-permute-start.24 = (bf16[1,2,1024,256]{3,2,1,0:T(8,128)(2,1)}, bf16[1,2,1024,256]{3,2,1,0:T(8,128)(2,1)S(1)}, u32[]{:S(2)}, u32[]{:S(2)}) collective-permute-start(bf16[1,2,1024,256]{3,2,1,0:T(8,128)(2,1)} %slice.19), channel_id=1, source_target_pairs={{0,1},{1,0},{2,3},{3,2},{4,5},{5,4},{6,7},{7,6},{8,9},{9,8},{10,11... | collective-permute-start | bytes 3145736 | tf_op jit(solution)/shard_map/ppermute | solution.py:38
  209.2 20.4 %collective-permute-start.20 = (bf16[320,256]{1,0:T(8,128)(2,1)S(1)}, bf16[320,256]{1,0:T(8,128)(2,1)S(1)}, u32[]{:S(2)}, u32[]{:S(2)}) collective-permute-start(bf16[320,256]{1,0:T(8,128)(2,1)S(1)} %get-tuple-element.162), channel_id=1, source_target_pairs={{0,1},{1,0},{2,3},{3,2},{4,5},{5,4},{6,7},{7,6},{8,9},{9,8},{10,11... | collective-permute-start | bytes 491528 | tf_op jit(solution)/shard_map/ppermute | solution.py:38
  209.8 19.9 %collective-permute-start.21 = (bf16[320,256]{1,0:T(8,128)(2,1)S(1)}, bf16[320,256]{1,0:T(8,128)(2,1)S(1)}, u32[]{:S(2)}, u32[]{:S(2)}) collective-permute-start(bf16[320,256]{1,0:T(8,128)(2,1)S(1)} %get-tuple-element.161), channel_id=1, source_target_pairs={{0,2},{1,3},{2,0},{3,1},{4,6},{5,7},{6,4},{7,5},{8,10},{9,11},{10,... | collective-permute-start | bytes 491528 | tf_op jit(solution)/shard_map/ppermute | solution.py:38
  210.8 18.9 %collective-permute-start.22 = (bf16[320,256]{1,0:T(8,128)(2,1)S(1)}, bf16[320,256]{1,0:T(8,128)(2,1)S(1)}, u32[]{:S(2)}, u32[]{:S(2)}) collective-permute-start(bf16[320,256]{1,0:T(8,128)(2,1)S(1)} %get-tuple-element.160), channel_id=1, source_target_pairs={{0,3},{1,2},{2,1},{3,0},{4,7},{5,6},{6,5},{7,4},{8,11},{9,10},{10,... | collective-permute-start | bytes 491528 | tf_op jit(solution)/shard_map/ppermute | solution.py:38
  229.6 5.0 %copy-start.4 = (bf16[256,256]{1,0:T(8,128)(2,1)S(1)}, bf16[256,256]{1,0:T(8,128)(2,1)}, u32[]{:S(2)}) copy-start(bf16[256,256]{1,0:T(8,128)(2,1)} %constant.63.clone.pick_ref) | copy-start | bytes 393220
  229.6 5.0 %copy-start.6 = (s32[3]{0:T(128)S(1)}, s32[3]{0:T(128)}, u32[]{:S(2)}) copy-start(s32[3]{0:T(128)} %copy-done.5) | copy-start | bytes 40
  229.8 6.5 %collective-permute-start.25 = (bf16[4,320,256]{2,1,0:T(8,128)(2,1)S(1)}, bf16[4,320,256]{2,1,0:T(8,128)(2,1)S(1)}, u32[]{:S(2)}, u32[]{:S(2)}) collective-permute-start(bf16[4,320,256]{2,1,0:T(8,128)(2,1)S(1)} %pad_maximum_fusion.3.own_ref.blocks_ref), channel_id=1, source_target_pairs={{0,16},{16,0},{1,17},{17,1},{2,18},{18,2},{3,19},{19,3},{4,20},{20... | collective-permute-start | bytes 1966088 | tf_op jit(solution)/shard_map/ppermute | solution.py:38
  231.1 11.2 %collective-permute-start.26 = (bf16[320,256]{1,0:T(8,128)(2,1)S(1)}, bf16[320,256]{1,0:T(8,128)(2,1)S(1)}, u32[]{:S(2)}, u32[]{:S(2)}) collective-permute-start(bf16[320,256]{1,0:T(8,128)(2,1)S(1)} %get-tuple-element.158), channel_id=1, source_target_pairs={{0,1},{1,0},{2,3},{3,2},{4,5},{5,4},{6,7},{7,6},{8,9},{9,8},{10,11... | collective-permute-start | bytes 491528 | tf_op jit(solution)/shard_map/ppermute | solution.py:38
  231.7 10.6 %collective-permute-start.27 = (bf16[320,256]{1,0:T(8,128)(2,1)S(1)}, bf16[320,256]{1,0:T(8,128)(2,1)S(1)}, u32[]{:S(2)}, u32[]{:S(2)}) collective-permute-start(bf16[320,256]{1,0:T(8,128)(2,1)S(1)} %get-tuple-element.157), channel_id=1, source_target_pairs={{0,2},{1,3},{2,0},{3,1},{4,6},{5,7},{6,4},{7,5},{8,10},{9,11},{10,... | collective-permute-start | bytes 491528 | tf_op jit(solution)/shard_map/ppermute | solution.py:38
  232.7 9.6 %collective-permute-start.28 = (bf16[320,256]{1,0:T(8,128)(2,1)S(1)}, bf16[320,256]{1,0:T(8,128)(2,1)S(1)}, u32[]{:S(2)}, u32[]{:S(2)}) collective-permute-start(bf16[320,256]{1,0:T(8,128)(2,1)S(1)} %get-tuple-element.156), channel_id=1, source_target_pairs={{0,3},{1,2},{2,1},{3,0},{4,7},{5,6},{6,5},{7,4},{8,11},{9,10},{10,... | collective-permute-start | bytes 491528 | tf_op jit(solution)/shard_map/ppermute | solution.py:38
  242.4 2.2 collective-permute-start.29
  244.5 6.0 %copy-start.1 = (bf16[4096,128]{1,0:T(8,128)(2,1)S(1)}, bf16[4096,128]{1,0:T(8,128)(2,1)}, u32[]{:S(2)}) copy-start(bf16[4096,128]{1,0:T(8,128)(2,1)} %param.26) | copy-start | bytes 3145732
Sparse Core Ops, SparseCore 0:
  21.7 61.0 all-gather.4
  100.2 14.4 all-gather.6

commit v11 on v10

--- a/solution.py
+++ b/solution.py
@@ -126,7 +126,7 @@
 def shifted(where, act, coeffs, left, side, apart, stretches, earlier):
     span, width = act.shape[-2] - PAST, act.shape[-1]
     inner = left.shape[1]
-    block = 1024
+    block = 512
     act_spec = pl.BlockSpec((span + PAST, block), lambda n, w: (0, n))
     if act.ndim == 3:
         act_spec = pl.BlockSpec((None, span + PAST, block), lambda n, w: (1 - w[1], 0, n))

time: 259 us -> 270 us (1.042)
  Pallas kernels: 134 us -> 149 us
  waiting for transfers between devices: 19.9 us -> 15.7 us
    pallas_call x8, Pallas kernels: 49.4 us -> 64.2 us  [shifted(): pl.pallas_call(mix_kernel, grid_spec=pltpu.PrefetchScalarGridSpec(num_sca...]
    all_gather x1, waiting for transfers between devices: 9.94 us -> 6.18 us  [local(): out_lines = lax.all_gather(out_half, 'req', axis=0, tiled=False)]
  transfers between devices with their start and end apart: 32 -> 32, of which waited for: 6 -> 5; matrix products, arithmetic and copies ran while one was open for 16% -> 15% of each run, Pallas kernels for 50% -> 53%
where the time goes in v11:
time: 270 us; the launch traced here: 268 us
  Pallas kernels  149 us (55%)
  starting transfers between devices  44.7 us (17%)
  local copies, waits for them, and re-layouts  39.7 us (15%)
  waiting for transfers between devices  15.7 us (6%)
  between operations  14.4 us (5%)
  other arithmetic  5.31 us (2%)
    pallas_call x8, Pallas kernels, shifted(): pl.pallas_call(mix_kernel, grid_spec=pltpu.PrefetchScalarGridSpec(num_sca...  64.2 us
    pallas_call x2, Pallas kernels, recurrence(): pl.pallas_call(functools.partial(wkv_kernel, prompt=prompt, parted=bool(e...  33.7 us
    ppermute x7, starting transfers between devices, moved(): lax.ppermute(value, axis, [(i, i + by) for i in range(peers) if 0 <= i +...  24.7 us
    pallas_call x1, Pallas kernels, projected(): pl.pallas_call(project_kernel, grid_spec=pltpu.PrefetchScalarGridSpec(num...  21.6 us
    ppermute x23, starting transfers between devices, swapped(): return lax.ppermute(value, axis, [(i, i ^ by) for i in range(peers)])  19.9 us
    pallas_call x1, Pallas kernels, ordered(): pl.pallas_call(order_kernel, grid=(width // block,), in_specs=[pl.BlockSp...  13.9 us
    gather x1, local copies, waits for them, and re-layouts, local(): left = fading_left_matrix[perm]  12.1 us
    pallas_call x2, Pallas kernels, finished(): pl.pallas_call(finish_kernel, grid_spec=pltpu.PrefetchScalarGridSpec(num_...  12 us
  transfers between devices with their start and end apart: 32, of which 5 were waited for; matrix products, arithmetic and copies ran while one was open for 15% of the time, Pallas kernels for 53%

profile of v11, /device:TPU:0, one launch (start us, length us, event | category | flops | bytes accessed | tf_op | source)
XLA Modules:
  0.0 268.4 jit_solution(16383224395411787749)
XLA Ops:
  8.2 4.8 %collective-permute-start = (bf16[16,4096]{1,0:T(8,128)(2,1)S(1)}, bf16[16,4096]{1,0:T(8,128)(2,1)S(1)}, u32[]{:S(2)}, u32[]{:S(2)}) collective-permute-start(bf16[16,4096]{1,0:T(8,128)(2,1)S(1)} %constant_dynamic-slice_fusion), channel_id=1, source_target_pairs={{0,1},{1,2},{2,3},{4,5},{5,6},{6,7},{8,9},{9,10},{10,11},{12,13},{... | collective-permute-start | bytes 393224 | tf_op jit(solution)/shard_map/ppermute | solution.py:466
  13.1 2.1 convert_element_type.17
  15.2 2.9 %dynamic-slice_convert_fusion = (bf16[3,256,256]{2,1,0:T(8,128)(2,1)S(1)}, bf16[3,256,256]{2,1,0:T(8,128)(2,1)}, bf16[3,256,256]{2,1,0:T(8,128)(2,1)}, bf16[3,256,256]{2,1,0:T(8,128)(2,1)S(1)}) fusion(f32[3,256,1024]{2,1,0:T(8,128)} %param.24, s32[]{:T(128)S(6)} %select_n.49, s32[]{:T(128)S(6)} %select_n.48, s32[]{:T(128)S(6)} %select_n.47, s32[]{:T(128)S(6)} %select_n.46), kind=kLoop, calls=%fused_computation.5 | loop fusion | bytes 3145744 | tf_op jit(solution)/shard_map/convert_element_type | solution.py:500
  18.1 1.5 collective-permute-start.1
  19.6 2.0 collective-permute-start.3
  21.7 1.7 constant_dynamic-slice_fusion.3
  24.2 13.9 %shard_map.203 = (bf16[272,4096]{1,0:T(8,128)(2,1)}, f32[8,4096]{1,0:T(8,128)S(1)}) custom-call(bf16[272,4096]{1,0:T(8,128)(2,1)S(1)} %pad_maximum_fusion.x_ref, f32[1,4096]{1,0:T(1,128)S(1)} %bitcast.44, f32[8,4096]{1,0:T(8,128)S(1)} %pad.4.coeff_ref, s32[1,4096]{1,0:T(1,128)S(1)} %bitcast.43), custom_call_target="tpu_custom_call" | custom-call | flops 1024 | bytes 1024 | tf_op jit(solution)/shard_map/pallas_call | solution.py:76
  40.6 1.3 pad_maximum_fusion.2.refs_3_
  42.0 4.6 %collective-permute-start.8 = (bf16[4,3,256,256]{3,2,1,0:T(8,128)(2,1)}, bf16[4,3,256,256]{3,2,1,0:T(8,128)(2,1)}, u32[]{:S(2)}, u32[]{:S(2)}) collective-permute-start(bf16[4,3,256,256]{3,2,1,0:T(8,128)(2,1)} %pad_maximum_fusion.2.refs_3_), channel_id=1, source_target_pairs={{0,4},{4,8},{8,12},{1,5},{5,9},{9,13},{2,6},{6,10},{10,14},{3,7},{... | collective-permute-start | bytes 4718600 | tf_op jit(solution)/shard_map/ppermute | solution.py:466
  47.9 12.1 %gather_fusion = bf16[4096,128]{1,0:T(8,128)(2,1)S(1)} fusion(bf16[4096,128]{1,0:T(8,128)(2,1)S(1)} %copy-done, s32[4096]{0:T(1024)S(1)} %fusion), kind=kCustom, calls=%fused_computation | custom fusion | bytes 2113536 | tf_op jit(solution)/shard_map/gather | solution.py:520
  60.1 8.2 %shard_map.204 = (bf16[3,2,4,256,4096]{4,3,2,1,0:T(8,128)(2,1)}, bf16[2,4,256,128]{3,2,1,0:T(8,128)(2,1)S(1)}) custom-call(s32[3]{0:T(128)S(1)} %pad_add_fusion.where_ref, bf16[272,4096]{1,0:T(8,128)(2,1)} %get-tuple-element.80.act_ref, f32[8,4096]{1,0:T(8,128)S(1)} %get-tuple-element.82.coeff_ref, bf16[4096,128]{1,0:T(8,128)(2,1)S(1)} %gather_fusion), custom_call_target="tpu_custom_call" | custom-call | flops 1024 | bytes 1024 | tf_op jit(solution)/shard_map/pallas_call | solution.py:134
  68.3 8.3 %shard_map.205 = (bf16[3,2,4,256,4096]{4,3,2,1,0:T(8,128)(2,1)}, bf16[2,4,256,128]{3,2,1,0:T(8,128)(2,1)S(1)}) custom-call(s32[3]{0:T(128)S(1)} %pad_add_fusion.where_ref, bf16[272,4096]{1,0:T(8,128)(2,1)} %collective-permute-done.6.act_ref, f32[8,4096]{1,0:T(8,128)S(1)} %get-tuple-element.82.coeff_ref, ...), custom_call_target="tpu_custom_call", output_to_operand_aliasing={{0}: (4, {}), {1}: (5, {})} | custom-call | flops 1024 | bytes 1024 | tf_op jit(solution)/shard_map/pallas_call | solution.py:134
  76.6 6.2 %all-gather.5.cloned.1.call-done = bf16[4096,256]{1,0:T(8,128)(2,1)} async-done(((bf16[1024,256]{1,0:T(8,128)(2,1)}), bf16[4096,256]{1,0:T(8,128)(2,1)}) %all-gather.5.cloned.1.call-update) | async-done | bytes 2097168 | tf_op jit(solution)/shard_map/all_gather | solution.py:498
  82.8 1.7 dynamic-slice_bitcast_fusion
  84.5 1.3 dynamic_slice.67
  85.9 1.3 dynamic_slice.68
  87.2 1.3 dynamic_slice.66
  88.5 1.5 constant_dynamic-slice_fusion.1.refs_7_
  90.0 1.5 pad_maximum_fusion.1.refs_0_
  91.5 6.6 %collective-permute-done.8.refs_4_ = bf16[4,3,256,256]{3,2,1,0:T(8,128)(2,1)} collective-permute-done((bf16[4,3,256,256]{3,2,1,0:T(8,128)(2,1)}, bf16[4,3,256,256]{3,2,1,0:T(8,128)(2,1)}, u32[]{:S(2)}, u32[]{:S(2)}) %collective-permute-start.8) | collective-permute-done | bytes 1572896 | tf_op jit(solution)/shard_map/ppermute | solution.py:466
  98.1 2.0 collective-permute-done.9.refs_5_
  100.1 1.4 slice.17
  101.5 1.5 collective-permute-start.12
  103.0 1.3 slice.16
  104.3 1.5 collective-permute-start.11
  105.9 5.1 %collective-permute-start.14 = (bf16[4,3,256,256]{3,2,1,0:T(8,128)(2,1)}, bf16[4,3,256,256]{3,2,1,0:T(8,128)(2,1)}, u32[]{:S(2)}, u32[]{:S(2)}) collective-permute-start(bf16[4,3,256,256]{3,2,1,0:T(8,128)(2,1)} %collective-permute-done.8.refs_4_), channel_id=1, source_target_pairs={{0,4},{4,8},{8,12},{1,5},{5,9},{9,13},{2,6},{6,10},{10,14},{3,7},{... | collective-permute-start | bytes 4718600 | tf_op jit(solution)/shard_map/ppermute | solution.py:466
  112.3 8.3 %shard_map.206 = (bf16[3,2,4,256,4096]{4,3,2,1,0:T(8,128)(2,1)}, bf16[2,4,256,128]{3,2,1,0:T(8,128)(2,1)S(1)}) custom-call(s32[3]{0:T(128)S(1)} %pad_add_fusion.where_ref, bf16[272,4096]{1,0:T(8,128)(2,1)} %collective-permute-done.4.act_ref, f32[8,4096]{1,0:T(8,128)S(1)} %get-tuple-element.82.coeff_ref, ...), custom_call_target="tpu_custom_call", output_to_operand_aliasing={{0}: (4, {}), {1}: (5, {})} | custom-call | flops 1024 | bytes 1024 | tf_op jit(solution)/shard_map/pallas_call | solution.py:134
  120.6 8.3 %shard_map.207 = (bf16[3,2,4,256,4096]{4,3,2,1,0:T(8,128)(2,1)}, bf16[2,4,256,128]{3,2,1,0:T(8,128)(2,1)S(1)}) custom-call(s32[3]{0:T(128)S(1)} %pad_add_fusion.where_ref, bf16[272,4096]{1,0:T(8,128)(2,1)} %collective-permute-done.5.act_ref, f32[8,4096]{1,0:T(8,128)S(1)} %get-tuple-element.82.coeff_ref, ...), custom_call_target="tpu_custom_call", output_to_operand_aliasing={{0}: (4, {}), {1}: (5, {})} | custom-call | flops 1024 | bytes 1024 | tf_op jit(solution)/shard_map/pallas_call | solution.py:134
  128.9 8.3 %shard_map.208 = (bf16[3,2,4,256,4096]{4,3,2,1,0:T(8,128)(2,1)}, bf16[2,4,256,128]{3,2,1,0:T(8,128)(2,1)S(1)}) custom-call(s32[3]{0:T(128)S(1)} %pad_add_fusion.where_ref, bf16[272,4096]{1,0:T(8,128)(2,1)} %collective-permute-done.10.act_ref, f32[8,4096]{1,0:T(8,128)S(1)} %get-tuple-element.82.coeff_ref, ...), custom_call_target="tpu_custom_call", output_to_operand_aliasing={{0}: (4, {}), {1}: (5, {})} | custom-call | flops 1024 | bytes 1024 | tf_op jit(solution)/shard_map/pallas_call | solution.py:134
  140.4 2.3 copy-done.3
  142.7 6.1 %shard_map.209 = (bf16[3,2,4,256,4096]{4,3,2,1,0:T(8,128)(2,1)}, bf16[2,4,256,128]{3,2,1,0:T(8,128)(2,1)S(1)}) custom-call(s32[3]{0:T(128)S(1)} %pad_add_fusion.where_ref, bf16[2,272,4096]{2,1,0:T(8,128)(2,1)S(1)} %bitcast.42, f32[8,4096]{1,0:T(8,128)S(1)} %get-tuple-element.82.coeff_ref, ...), custom_call_target="tpu_custom_call", output_to_operand_aliasing={{0}: (4, {}), {1}: (5, {})} | custom-call | flops 1024 | bytes 1024 | tf_op jit(solution)/shard_map/pallas_call | solution.py:134
  148.8 8.3 %shard_map.210 = (bf16[3,2,4,256,4096]{4,3,2,1,0:T(8,128)(2,1)}, bf16[2,4,256,128]{3,2,1,0:T(8,128)(2,1)S(1)}) custom-call(s32[3]{0:T(128)S(1)} %pad_add_fusion.where_ref, bf16[272,4096]{1,0:T(8,128)(2,1)} %constant_dynamic-update-slice_fusion.act_ref, f32[8,4096]{1,0:T(8,128)S(1)} %get-tuple-element.82.coeff_ref, ...), custom_call_target="tpu_custom_call", output_to_operand_aliasing={{0}: (4, {}), {1}: (5, {})} | custom-call | flops 1024 | bytes 1024 | tf_op jit(solution)/shard_map/pallas_call | solution.py:134
  157.1 1.3 collective-permute-start.16
  158.4 6.3 %collective-permute-start.17 = (bf16[4,3,256,256]{3,2,1,0:T(8,128)(2,1)}, bf16[4,3,256,256]{3,2,1,0:T(8,128)(2,1)}, u32[]{:S(2)}, u32[]{:S(2)}) collective-permute-start(bf16[4,3,256,256]{3,2,1,0:T(8,128)(2,1)} %collective-permute-done.14.refs_6_.refs_3_), channel_id=1, source_target_pairs={{0,4},{4,8},{8,12},{1,5},{5,9},{9,13},{2,6},{6,10},{10,14},{3,7},{... | collective-permute-start | bytes 4718600 | tf_op jit(solution)/shard_map/ppermute | solution.py:466
  164.7 8.4 %shard_map.211 = (bf16[3,2,4,256,4096]{4,3,2,1,0:T(8,128)(2,1)}, bf16[2,4,256,128]{3,2,1,0:T(8,128)(2,1)S(1)}) custom-call(s32[3]{0:T(128)S(1)} %pad_add_fusion.where_ref, bf16[272,4096]{1,0:T(8,128)(2,1)} %collective-permute-done.13.act_ref, f32[8,4096]{1,0:T(8,128)S(1)} %get-tuple-element.82.coeff_ref, ...), custom_call_target="tpu_custom_call", output_to_operand_aliasing={{0}: (4, {}), {1}: (5, {})} | custom-call | flops 1024 | bytes 1024 | tf_op jit(solution)/shard_map/pallas_call | solution.py:134
  173.1 21.6 %shard_map.212.refs_5_ = f32[3,2,4,256,256]{4,3,2,1,0:T(8,128)} custom-call(s32[3]{0:T(128)} %copy-done.5, bf16[3,2,4,256,4096]{4,3,2,1,0:T(8,128)(2,1)} %get-tuple-element.121.refs_0_.refs_1_.refs_2_, bf16[3,2,4,256,4096]{4,3,2,1,0:T(8,128)(2,1)} %get-tuple-element.121.refs_0_.refs_1_.refs_2_, ...), custom_call_target="tpu_custom_call" | custom-call | flops 1024 | bytes 1024 | tf_op jit(solution)/shard_map/pallas_call | solution.py:200
  194.7 2.3 slice.18
  196.9 1.3 collective-permute-start.23
  198.2 2.3 slice.19
  200.5 1.7 collective-permute-start.24
  202.2 16.8 %shard_map.213 = bf16[4,320,256]{2,1,0:T(8,128)(2,1)} custom-call(s32[2]{0:T(128)} %extent_ref.3, s32[3]{0:T(128)} %copy-done.5, bf16[3,2,4,256,4096]{4,3,2,1,0:T(8,128)(2,1)} %get-tuple-element.121.refs_0_.refs_1_.refs_2_, bf16[4,3,256,256]{3,2,1,0:T(8,128)(2,1)} %collective-permute-done.16.refs_1_, ...), custom_call_target="tpu_custom_call" | custom-call | flops 1024 | bytes 1024 | tf_op jit(solution)/shard_map/pallas_call | solution.py:351
  221.4 2.4 collective-permute-start.22
  223.8 16.8 %shard_map.214 = bf16[4,320,256]{2,1,0:T(8,128)(2,1)} custom-call(s32[2]{0:T(128)} %extent_ref.3, s32[3]{0:T(128)} %copy-done.5, bf16[3,2,4,256,4096]{4,3,2,1,0:T(8,128)(2,1)} %get-tuple-element.121.refs_0_.refs_1_.refs_2_, bf16[4,3,256,256]{3,2,1,0:T(8,128)(2,1)} %collective-permute-done.16.refs_1_, ...), custom_call_target="tpu_custom_call" | custom-call | flops 1024 | bytes 1024 | tf_op jit(solution)/shard_map/pallas_call | solution.py:351
  243.2 2.4 collective-permute-start.28
  245.6 1.6 shard_map.216.refs_0_
  247.3 6.0 %shard_map.215.refs_5_ = bf16[2,256,2048]{2,1,0:T(8,128)(2,1)} custom-call(s32[3]{0:T(128)S(1)} %copy-done.6, bf16[512,4096]{1,0:T(8,128)(2,1)} %bitcast.47, bf16[4,320,256]{2,1,0:T(8,128)(2,1)S(1)} %pad_maximum_fusion.3.own_ref.blocks_ref, bf16[4,320,256]{2,1,0:T(8,128)(2,1)S(1)} %collective-permute-done.25.far_ref, ...), custom_call_target="tpu_custom_call" | custom-call | flops 1024 | bytes 1024 | tf_op jit(solution)/shard_map/pallas_call | solution.py:403
  253.4 1.6 shard_map.218
  255.5 6.0 %shard_map.217 = bf16[2,256,2048]{2,1,0:T(8,128)(2,1)} custom-call(s32[3]{0:T(128)S(1)} %copy-done.6, bf16[512,4096]{1,0:T(8,128)(2,1)} %bitcast.48, bf16[4,320,256]{2,1,0:T(8,128)(2,1)S(1)} %pad_maximum_fusion.4.own_ref.blocks_ref, bf16[4,320,256]{2,1,0:T(8,128)(2,1)S(1)} %collective-permute-done.29.far_ref, ...), custom_call_target="tpu_custom_call", output_to_operand_aliasing={{}: (9, {})} | custom-call | flops 1024 | bytes 1024 | tf_op jit(solution)/shard_map/pallas_call | solution.py:403
  (80 shorter events, 15.8 us)
Async XLA Ops:
  7.2 40.8 %copy-start = (bf16[4096,128]{1,0:T(8,128)(2,1)S(1)}, bf16[4096,128]{1,0:T(8,128)(2,1)}, u32[]{:S(2)}) copy-start(bf16[4096,128]{1,0:T(8,128)(2,1)} %param.26) | copy-start | bytes 3145732
  7.2 75.6 %all-gather.5.cloned.1.call-start = ((), (), s32[]{:S(2)}) async-start(), calls=%async_computation | async-start | bytes 2621440 | tf_op jit(solution)/shard_map/all_gather | solution.py:498
  8.2 15.2 %collective-permute-start = (bf16[16,4096]{1,0:T(8,128)(2,1)S(1)}, bf16[16,4096]{1,0:T(8,128)(2,1)S(1)}, u32[]{:S(2)}, u32[]{:S(2)}) collective-permute-start(bf16[16,4096]{1,0:T(8,128)(2,1)S(1)} %constant_dynamic-slice_fusion), channel_id=1, source_target_pairs={{0,1},{1,2},{2,3},{4,5},{5,6},{6,7},{8,9},{9,10},{10,11},{12,13},{... | collective-permute-start | bytes 393224 | tf_op jit(solution)/shard_map/ppermute | solution.py:466
  18.1 20.0 %collective-permute-start.1 = (bf16[3,256,256]{2,1,0:T(8,128)(2,1)}, bf16[3,256,256]{2,1,0:T(8,128)(2,1)S(1)}, u32[]{:S(2)}, u32[]{:S(2)}) collective-permute-start(bf16[3,256,256]{2,1,0:T(8,128)(2,1)} %get-tuple-element.152), channel_id=1, source_target_pairs={{0,1},{1,0},{2,3},{3,2},{4,5},{5,4},{6,7},{7,6},{8,9},{9,8},{10,11... | collective-permute-start | bytes 1179656 | tf_op jit(solution)/shard_map/ppermute | solution.py:38
  19.6 18.9 %collective-permute-start.2 = (bf16[3,256,256]{2,1,0:T(8,128)(2,1)}, bf16[3,256,256]{2,1,0:T(8,128)(2,1)S(1)}, u32[]{:S(2)}, u32[]{:S(2)}) collective-permute-start(bf16[3,256,256]{2,1,0:T(8,128)(2,1)} %get-tuple-element.151), channel_id=1, source_target_pairs={{0,2},{1,3},{2,0},{3,1},{4,6},{5,7},{6,4},{7,5},{8,10},{9,11},{10,... | collective-permute-start | bytes 1179656 | tf_op jit(solution)/shard_map/ppermute | solution.py:38
  19.6 18.9 %collective-permute-start.3 = (bf16[3,256,256]{2,1,0:T(8,128)(2,1)S(1)}, bf16[3,256,256]{2,1,0:T(8,128)(2,1)S(1)}, u32[]{:S(2)}, u32[]{:S(2)}) collective-permute-start(bf16[3,256,256]{2,1,0:T(8,128)(2,1)S(1)} %get-tuple-element.150), channel_id=1, source_target_pairs={{0,3},{1,2},{2,1},{3,0},{4,7},{5,6},{6,5},{7,4},{8,11},{9,10},{10,... | collective-permute-start | bytes 1179656 | tf_op jit(solution)/shard_map/ppermute | solution.py:38
  21.6 1.8 copy-start.9
  21.6 118.8 %all-gather.7.cloned.1.call-start = ((), (), s32[]{:S(2)}) async-start(), calls=%async_computation.1 | async-start | bytes 6684672 | tf_op jit(solution)/shard_map/all_gather | solution.py:545
  23.4 0.7 copy-start.7
  23.5 0.7 copy-start.8
  38.5 29.8 %collective-permute-start.6 = (bf16[272,4096]{1,0:T(8,128)(2,1)}, bf16[272,4096]{1,0:T(8,128)(2,1)}, u32[]{:S(2)}, u32[]{:S(2)}) collective-permute-start(bf16[272,4096]{1,0:T(8,128)(2,1)} %get-tuple-element.80.act_ref), channel_id=1, source_target_pairs={{0,16},{16,0},{1,17},{17,1},{2,18},{18,2},{3,19},{19,3},{4,20},{20... | collective-permute-start | bytes 6684680 | tf_op jit(solution)/shard_map/ppermute | solution.py:38
  38.5 61.6 %collective-permute-start.4 = (bf16[272,4096]{1,0:T(8,128)(2,1)}, bf16[272,4096]{1,0:T(8,128)(2,1)}, u32[]{:S(2)}, u32[]{:S(2)}) collective-permute-start(bf16[272,4096]{1,0:T(8,128)(2,1)} %get-tuple-element.80.act_ref), channel_id=1, source_target_pairs={{0,1},{1,0},{2,3},{3,2},{4,5},{5,4},{6,7},{7,6},{8,9},{9,8},{10,11... | collective-permute-start | bytes 6684680 | tf_op jit(solution)/shard_map/ppermute | solution.py:38
  39.8 60.3 %collective-permute-start.5 = (bf16[272,4096]{1,0:T(8,128)(2,1)}, bf16[272,4096]{1,0:T(8,128)(2,1)}, u32[]{:S(2)}, u32[]{:S(2)}) collective-permute-start(bf16[272,4096]{1,0:T(8,128)(2,1)} %get-tuple-element.80.act_ref), channel_id=1, source_target_pairs={{0,2},{1,3},{2,0},{3,1},{4,6},{5,7},{6,4},{7,5},{8,10},{9,11},{10,... | collective-permute-start | bytes 6684680 | tf_op jit(solution)/shard_map/ppermute | solution.py:38
  40.6 124.1 %copy-start.5 = (s32[3]{0:T(128)}, s32[3]{0:T(128)S(1)}, u32[]{:S(2)}) copy-start(s32[3]{0:T(128)S(1)} %pad_add_fusion.where_ref) | copy-start | bytes 40
  42.0 56.1 %collective-permute-start.8 = (bf16[4,3,256,256]{3,2,1,0:T(8,128)(2,1)}, bf16[4,3,256,256]{3,2,1,0:T(8,128)(2,1)}, u32[]{:S(2)}, u32[]{:S(2)}) collective-permute-start(bf16[4,3,256,256]{3,2,1,0:T(8,128)(2,1)} %pad_maximum_fusion.2.refs_3_), channel_id=1, source_target_pairs={{0,4},{4,8},{8,12},{1,5},{5,9},{9,13},{2,6},{6,10},{10,14},{3,7},{... | collective-permute-start | bytes 4718600 | tf_op jit(solution)/shard_map/ppermute | solution.py:466
  46.6 53.5 %collective-permute-start.9 = (bf16[4,3,256,256]{3,2,1,0:T(8,128)(2,1)}, bf16[4,3,256,256]{3,2,1,0:T(8,128)(2,1)}, u32[]{:S(2)}, u32[]{:S(2)}) collective-permute-start(bf16[4,3,256,256]{3,2,1,0:T(8,128)(2,1)} %pad_maximum_fusion.2.refs_3_), channel_id=1, source_target_pairs={{4,0},{8,4},{12,8},{5,1},{9,5},{13,9},{6,2},{10,6},{14,10},{7,3},{... | collective-permute-start | bytes 4718600 | tf_op jit(solution)/shard_map/ppermute | solution.py:466
  84.5 5.5 %collective-permute-start.7 = (bf16[2,1024,256]{2,1,0:T(8,128)(2,1)S(1)}, bf16[2,1024,256]{2,1,0:T(8,128)(2,1)S(1)}, u32[]{:S(2)}, u32[]{:S(2)}) collective-permute-start(bf16[2,1024,256]{2,1,0:T(8,128)(2,1)S(1)} %get-tuple-element.155), channel_id=1, source_target_pairs={{0,16},{16,0},{1,17},{17,1},{2,18},{18,2},{3,19},{19,3},{4,20},{20... | collective-permute-start | bytes 3145736 | tf_op jit(solution)/shard_map/ppermute | solution.py:38
  100.1 28.8 %collective-permute-start.10 = (bf16[272,4096]{1,0:T(8,128)(2,1)}, bf16[272,4096]{1,0:T(8,128)(2,1)}, u32[]{:S(2)}, u32[]{:S(2)}) collective-permute-start(bf16[272,4096]{1,0:T(8,128)(2,1)} %collective-permute-done.4.act_ref), channel_id=1, source_target_pairs={{0,16},{16,0},{1,17},{17,1},{2,18},{18,2},{3,19},{19,3},{4,20},{20... | collective-permute-start | bytes 6684680 | tf_op jit(solution)/shard_map/ppermute | solution.py:38
  101.5 35.7 %collective-permute-start.12 = (bf16[144,4096]{1,0:T(8,128)(2,1)S(1)}, bf16[144,4096]{1,0:T(8,128)(2,1)S(1)}, u32[]{:S(2)}, u32[]{:S(2)}) collective-permute-start(bf16[144,4096]{1,0:T(8,128)(2,1)S(1)} %slice.17), channel_id=1, source_target_pairs={{0,1},{1,0},{2,3},{3,2},{4,5},{5,4},{6,7},{7,6},{8,9},{9,8},{10,11... | collective-permute-start | bytes 3538952 | tf_op jit(solution)/shard_map/ppermute | solution.py:38
  104.3 32.8 %collective-permute-start.11 = (bf16[128,4096]{1,0:T(8,128)(2,1)S(1)}, bf16[128,4096]{1,0:T(8,128)(2,1)S(1)}, u32[]{:S(2)}, u32[]{:S(2)}) collective-permute-start(bf16[128,4096]{1,0:T(8,128)(2,1)S(1)} %slice.16), channel_id=1, source_target_pairs={{0,2},{1,3},{2,0},{3,1},{4,6},{5,7},{6,4},{7,5},{8,10},{9,11},{10,... | collective-permute-start | bytes 3145736 | tf_op jit(solution)/shard_map/ppermute | solution.py:38
  105.9 51.2 %collective-permute-start.14 = (bf16[4,3,256,256]{3,2,1,0:T(8,128)(2,1)}, bf16[4,3,256,256]{3,2,1,0:T(8,128)(2,1)}, u32[]{:S(2)}, u32[]{:S(2)}) collective-permute-start(bf16[4,3,256,256]{3,2,1,0:T(8,128)(2,1)} %collective-permute-done.8.refs_4_), channel_id=1, source_target_pairs={{0,4},{4,8},{8,12},{1,5},{5,9},{9,13},{2,6},{6,10},{10,14},{3,7},{... | collective-permute-start | bytes 4718600 | tf_op jit(solution)/shard_map/ppermute | solution.py:466
  111.0 46.1 %collective-permute-start.15 = (bf16[4,3,256,256]{3,2,1,0:T(8,128)(2,1)}, bf16[4,3,256,256]{3,2,1,0:T(8,128)(2,1)}, u32[]{:S(2)}, u32[]{:S(2)}) collective-permute-start(bf16[4,3,256,256]{3,2,1,0:T(8,128)(2,1)} %collective-permute-done.9.refs_5_), channel_id=1, source_target_pairs={{4,0},{8,4},{12,8},{5,1},{9,5},{13,9},{6,2},{10,6},{14,10},{7,3},{... | collective-permute-start | bytes 4718600 | tf_op jit(solution)/shard_map/ppermute | solution.py:466
  139.4 25.3 %collective-permute-start.13 = (bf16[272,4096]{1,0:T(8,128)(2,1)}, bf16[272,4096]{1,0:T(8,128)(2,1)}, u32[]{:S(2)}, u32[]{:S(2)}) collective-permute-start(bf16[272,4096]{1,0:T(8,128)(2,1)} %constant_dynamic-update-slice_fusion.act_ref), channel_id=1, source_target_pairs={{0,16},{16,0},{1,17},{17,1},{2,18},{18,2},{3,19},{19,3},{4,20},{20... | collective-permute-start | bytes 6684680 | tf_op jit(solution)/shard_map/ppermute | solution.py:38
  139.4 55.2 %collective-permute-start.18 = (bf16[2,2,1024,256]{3,2,1,0:T(8,128)(2,1)}, bf16[2,2,1024,256]{3,2,1,0:T(8,128)(2,1)}, u32[]{:S(2)}, u32[]{:S(2)}) collective-permute-start(bf16[2,2,1024,256]{3,2,1,0:T(8,128)(2,1)} %pad_maximum_fusion.1.refs_0_), channel_id=1, source_target_pairs={{0,1},{1,0},{2,3},{3,2},{4,5},{5,4},{6,7},{7,6},{8,9},{9,8},{10,11... | collective-permute-start | bytes 6291464 | tf_op jit(solution)/shard_map/ppermute | solution.py:38
  139.8 54.9 %collective-permute-start.19 = (bf16[2,2,1024,256]{3,2,1,0:T(8,128)(2,1)}, bf16[2,2,1024,256]{3,2,1,0:T(8,128)(2,1)}, u32[]{:S(2)}, u32[]{:S(2)}) collective-permute-start(bf16[2,2,1024,256]{3,2,1,0:T(8,128)(2,1)} %pad_maximum_fusion.1.refs_0_), channel_id=1, source_target_pairs={{0,2},{1,3},{2,0},{3,1},{4,6},{5,7},{6,4},{7,5},{8,10},{9,11},{10,... | collective-permute-start | bytes 6291464 | tf_op jit(solution)/shard_map/ppermute | solution.py:38
  140.4 2.3 copy-start.3
  157.1 45.1 %collective-permute-start.16 = (bf16[4,3,256,256]{3,2,1,0:T(8,128)(2,1)}, bf16[4,3,256,256]{3,2,1,0:T(8,128)(2,1)}, u32[]{:S(2)}, u32[]{:S(2)}) collective-permute-start(bf16[4,3,256,256]{3,2,1,0:T(8,128)(2,1)} %collective-permute-done.15.refs_7_.refs_2_), channel_id=1, source_target_pairs={{4,0},{8,4},{12,8},{5,1},{9,5},{13,9},{6,2},{10,6},{14,10},{7,3},{... | collective-permute-start | bytes 4718600 | tf_op jit(solution)/shard_map/ppermute | solution.py:466
  158.4 43.8 %collective-permute-start.17 = (bf16[4,3,256,256]{3,2,1,0:T(8,128)(2,1)}, bf16[4,3,256,256]{3,2,1,0:T(8,128)(2,1)}, u32[]{:S(2)}, u32[]{:S(2)}) collective-permute-start(bf16[4,3,256,256]{3,2,1,0:T(8,128)(2,1)} %collective-permute-done.14.refs_6_.refs_3_), channel_id=1, source_target_pairs={{0,4},{4,8},{8,12},{1,5},{5,9},{9,13},{2,6},{6,10},{10,14},{3,7},{... | collective-permute-start | bytes 4718600 | tf_op jit(solution)/shard_map/ppermute | solution.py:466
  173.1 21.6 %copy-start.2 = (bf16[2,4,256,128]{3,2,1,0:T(8,128)(2,1)}, bf16[2,4,256,128]{3,2,1,0:T(8,128)(2,1)S(1)}, u32[]{:S(2)}) copy-start(bf16[2,4,256,128]{3,2,1,0:T(8,128)(2,1)S(1)} %get-tuple-element.128.refs_6_) | copy-start | bytes 1572868
  196.9 43.7 %collective-permute-start.23 = (bf16[1,2,1024,256]{3,2,1,0:T(8,128)(2,1)}, bf16[1,2,1024,256]{3,2,1,0:T(8,128)(2,1)S(1)}, u32[]{:S(2)}, u32[]{:S(2)}) collective-permute-start(bf16[1,2,1024,256]{3,2,1,0:T(8,128)(2,1)} %slice.18), channel_id=1, source_target_pairs={{0,2},{1,3},{2,0},{3,1},{4,6},{5,7},{6,4},{7,5},{8,10},{9,11},{10,... | collective-permute-start | bytes 3145736 | tf_op jit(solution)/shard_map/ppermute | solution.py:38
  200.5 40.1 %collective-permute-start.24 = (bf16[1,2,1024,256]{3,2,1,0:T(8,128)(2,1)}, bf16[1,2,1024,256]{3,2,1,0:T(8,128)(2,1)S(1)}, u32[]{:S(2)}, u32[]{:S(2)}) collective-permute-start(bf16[1,2,1024,256]{3,2,1,0:T(8,128)(2,1)} %slice.19), channel_id=1, source_target_pairs={{0,1},{1,0},{2,3},{3,2},{4,5},{5,4},{6,7},{7,6},{8,9},{9,8},{10,11... | collective-permute-start | bytes 3145736 | tf_op jit(solution)/shard_map/ppermute | solution.py:38
  220.3 20.4 %collective-permute-start.20 = (bf16[320,256]{1,0:T(8,128)(2,1)S(1)}, bf16[320,256]{1,0:T(8,128)(2,1)S(1)}, u32[]{:S(2)}, u32[]{:S(2)}) collective-permute-start(bf16[320,256]{1,0:T(8,128)(2,1)S(1)} %get-tuple-element.162), channel_id=1, source_target_pairs={{0,1},{1,0},{2,3},{3,2},{4,5},{5,4},{6,7},{7,6},{8,9},{9,8},{10,11... | collective-permute-start | bytes 491528 | tf_op jit(solution)/shard_map/ppermute | solution.py:38
  220.7 20.0 %collective-permute-start.21 = (bf16[320,256]{1,0:T(8,128)(2,1)S(1)}, bf16[320,256]{1,0:T(8,128)(2,1)S(1)}, u32[]{:S(2)}, u32[]{:S(2)}) collective-permute-start(bf16[320,256]{1,0:T(8,128)(2,1)S(1)} %get-tuple-element.161), channel_id=1, source_target_pairs={{0,2},{1,3},{2,0},{3,1},{4,6},{5,7},{6,4},{7,5},{8,10},{9,11},{10,... | collective-permute-start | bytes 491528 | tf_op jit(solution)/shard_map/ppermute | solution.py:38
  221.4 19.3 %collective-permute-start.22 = (bf16[320,256]{1,0:T(8,128)(2,1)S(1)}, bf16[320,256]{1,0:T(8,128)(2,1)S(1)}, u32[]{:S(2)}, u32[]{:S(2)}) collective-permute-start(bf16[320,256]{1,0:T(8,128)(2,1)S(1)} %get-tuple-element.160), channel_id=1, source_target_pairs={{0,3},{1,2},{2,1},{3,0},{4,7},{5,6},{6,5},{7,4},{8,11},{9,10},{10,... | collective-permute-start | bytes 491528 | tf_op jit(solution)/shard_map/ppermute | solution.py:38
  240.6 5.0 %copy-start.4 = (bf16[256,256]{1,0:T(8,128)(2,1)S(1)}, bf16[256,256]{1,0:T(8,128)(2,1)}, u32[]{:S(2)}) copy-start(bf16[256,256]{1,0:T(8,128)(2,1)} %constant.63.clone.pick_ref) | copy-start | bytes 393220
  240.6 5.0 %copy-start.6 = (s32[3]{0:T(128)S(1)}, s32[3]{0:T(128)}, u32[]{:S(2)}) copy-start(s32[3]{0:T(128)} %copy-done.5) | copy-start | bytes 40
  240.8 6.5 %collective-permute-start.25 = (bf16[4,320,256]{2,1,0:T(8,128)(2,1)S(1)}, bf16[4,320,256]{2,1,0:T(8,128)(2,1)S(1)}, u32[]{:S(2)}, u32[]{:S(2)}) collective-permute-start(bf16[4,320,256]{2,1,0:T(8,128)(2,1)S(1)} %pad_maximum_fusion.3.own_ref.blocks_ref), channel_id=1, source_target_pairs={{0,16},{16,0},{1,17},{17,1},{2,18},{18,2},{3,19},{19,3},{4,20},{20... | collective-permute-start | bytes 1966088 | tf_op jit(solution)/shard_map/ppermute | solution.py:38
  242.1 11.2 %collective-permute-start.26 = (bf16[320,256]{1,0:T(8,128)(2,1)S(1)}, bf16[320,256]{1,0:T(8,128)(2,1)S(1)}, u32[]{:S(2)}, u32[]{:S(2)}) collective-permute-start(bf16[320,256]{1,0:T(8,128)(2,1)S(1)} %get-tuple-element.158), channel_id=1, source_target_pairs={{0,1},{1,0},{2,3},{3,2},{4,5},{5,4},{6,7},{7,6},{8,9},{9,8},{10,11... | collective-permute-start | bytes 491528 | tf_op jit(solution)/shard_map/ppermute | solution.py:38
  242.5 10.8 %collective-permute-start.27 = (bf16[320,256]{1,0:T(8,128)(2,1)S(1)}, bf16[320,256]{1,0:T(8,128)(2,1)S(1)}, u32[]{:S(2)}, u32[]{:S(2)}) collective-permute-start(bf16[320,256]{1,0:T(8,128)(2,1)S(1)} %get-tuple-element.157), channel_id=1, source_target_pairs={{0,2},{1,3},{2,0},{3,1},{4,6},{5,7},{6,4},{7,5},{8,10},{9,11},{10,... | collective-permute-start | bytes 491528 | tf_op jit(solution)/shard_map/ppermute | solution.py:38
  243.2 10.0 %collective-permute-start.28 = (bf16[320,256]{1,0:T(8,128)(2,1)S(1)}, bf16[320,256]{1,0:T(8,128)(2,1)S(1)}, u32[]{:S(2)}, u32[]{:S(2)}) collective-permute-start(bf16[320,256]{1,0:T(8,128)(2,1)S(1)} %get-tuple-element.156), channel_id=1, source_target_pairs={{0,3},{1,2},{2,1},{3,0},{4,7},{5,6},{6,5},{7,4},{8,11},{9,10},{10,... | collective-permute-start | bytes 491528 | tf_op jit(solution)/shard_map/ppermute | solution.py:38
  253.4 2.2 collective-permute-start.29
  255.5 6.0 %copy-start.1 = (bf16[4096,128]{1,0:T(8,128)(2,1)S(1)}, bf16[4096,128]{1,0:T(8,128)(2,1)}, u32[]{:S(2)}) copy-start(bf16[4096,128]{1,0:T(8,128)(2,1)} %param.26) | copy-start | bytes 3145732
Sparse Core Ops, SparseCore 0:
  21.7 61.0 all-gather.4
  100.2 14.4 all-gather.6
